TPU v7x, 32 devices: a whole 2x2x4 slice. The times are simulated.
32 devices in a mesh: dev: 32 (over z, y, x, core).
Axes of the slice: x: 2, y: 2, z: 4, core: 2. Of those that a mesh axis runs over, the one named last changes fastest.
Arguments:
- peripheral: bfloat16 [131072, 256], P('dev'), may hold values from -6 to 6
- hubs: bfloat16 [2048, 256], P('dev'), may hold values from -6 to 6
- tiles: bfloat16 [4608, 128, 128], P('dev'), may hold values from -0.5 to 0.5
- tile_rows: int32 [4608], P('dev'), may hold values from 0 to 1039, as said below
- local_cols: int32 [3584], P('dev'), may hold values from 0 to 1039, as said below
- tile_count: int32 [32], P('dev'), may hold values from 32 to 144, as said below
- send_list: int32 [32, 32], P('dev'), may hold values from 0 to 31
- hub_place: int32 [2048], replicated, may hold values from 0 to 2047, each once
- w_in: bfloat16 [2, 256, 2048], replicated, may hold values from -0.375 to 0.375
- w_out: bfloat16 [2, 2048, 256], replicated, may hold values from -0.125 to 0.125
Outputs:
- peripheral_out: bfloat16 [131072, 256], P('dev')
- hubs_out: bfloat16 [2048, 256], P('dev')
Inputs may be any that keep to these rules, and one draw needn't show every extreme that they name: `tile_rows`: row blocks of device d's slots are hub blocks (below 16) or d's own blocks 16 + d * 32 to 16 + d * 32 + 31; slots below 32 always name an own block. `local_cols`: column blocks of device d's slots from 32 on are hub blocks or d's own blocks. `tile_count`: every device holds at least 32 live slots; some device is full in every draw.
All inputs are finite; a program needn't handle non-finite values.
Results may differ from a plain program's by a relative error of at most 0.005.
Values may be sent and summed in bfloat16 or wider, within the bound.
No kernel may reach another device: no remote copies, remote signals or barrier semaphores. Data moves between devices by JAX's collectives and lax.ppermute only.
A program may use at most 128 MiB of HBM per device.

v0:
```python
import functools

import jax
import jax.numpy as jnp
from jax import lax
from jax.experimental import pallas as pl
from jax.experimental.pallas import tpu as pltpu
from jax.sharding import PartitionSpec as P

epsilon = 1e-06
f32 = jnp.float32
bf16 = jnp.bfloat16
MIB = 1024 * 1024
VMEM = pl.BlockSpec(memory_space=pltpu.VMEM)
SMEM = pl.BlockSpec(memory_space=pltpu.SMEM)
ANY = pl.BlockSpec(memory_space=pl.ANY)
GROUP = 4


def dot(a, b):
    return jnp.dot(a, b, preferred_element_type=f32)


def shape_of(shape, dtype):
    return jax.ShapeDtypeStruct(tuple(shape), dtype)


def call(kernel, name, mib, flops, moved, out_shape, in_specs, out_specs, scratch, args):
    return pl.pallas_call(
        kernel,
        out_shape=out_shape,
        in_specs=in_specs,
        out_specs=out_specs,
        scratch_shapes=scratch,
        compiler_params=pltpu.CompilerParams(vmem_limit_bytes=mib * MIB),
        cost_estimate=pl.CostEstimate(flops=flops, bytes_accessed=moved, transcendentals=0),
        name=name,
    )(*args)


def normalise(u):
    return (u * lax.rsqrt(jnp.mean(u * u, axis=-1, keepdims=True) + epsilon)).astype(bf16)


def network(u, first, second, hidden_step):
    normed = normalise(u)
    total = u
    for start in range(0, first.shape[-1], hidden_step):
        cut = slice(start, start + hidden_step)
        hidden = jnp.maximum(dot(normed, first[:, cut]), 0.0).astype(bf16)
        total = total + dot(hidden, second[cut, :])
    return total.astype(bf16)


def list_slots(rows, count, picked, begin, hub_count, want_hub):
    def step(slot, found):
        picked[found] = slot
        is_hub = (rows[slot] < hub_count).astype(jnp.int32)
        return found + (is_hub if want_hub else 1 - is_hub)

    return lax.fori_loop(begin, count[0], step, jnp.int32(0))


def add_products(rows, cols, picked, found, begin, tiles, hubs, own, total, shift, spare):
    hub_count = hubs.shape[0]

    def step(number, unused):
        where, products = [], []
        for lane in range(GROUP):
            place = number * GROUP + lane
            live = place < found
            slot = picked[jnp.minimum(place, found - 1)]
            where.append(jnp.where(live, rows[slot] - shift, spare))
            col = cols[slot - begin]
            of_hub = hubs[jnp.minimum(col, hub_count - 1)]
            of_own = own[jnp.maximum(col - hub_count, 0)]
            products.append(dot(tiles[slot - begin], jnp.where(col < hub_count, of_hub, of_own)))
        for row, product in zip(where, products):
            total[row] += product
        return unused

    lax.fori_loop(0, (found + GROUP - 1) // GROUP, step, 0)


def list_blocks(rows, remote, own_count, hub_count, marks, listed, want_remote):
    def clear(block, unused):
        marks[block] = 0
        return unused

    def mark(slot, unused):
        marks[rows[slot] - hub_count] = 1
        return unused

    def take(block, found):
        listed[found] = block
        return found + (marks[block] if want_remote else 1 - marks[block])

    lax.fori_loop(0, own_count, clear, 0)
    lax.fori_loop(0, remote, mark, 0)
    return lax.fori_loop(0, own_count, take, jnp.int32(0))


def network_blocks(listed, found, u, first, second, result):
    def step(number, unused):
        blocks = [
            listed[jnp.minimum(number * GROUP + lane, found - 1)] for lane in range(GROUP)
        ]
        values = jnp.concatenate([u[block] for block in blocks], axis=0)
        values = network(values, first, second, 512)
        size = u.shape[1]
        for lane, block in enumerate(blocks):
            result[block] = values[lane * size : (lane + 1) * size]
        return unused

    lax.fori_loop(0, (found + GROUP - 1) // GROUP, step, 0)


def pack_kernel(chosen, blocks, outgoing, held, sems):
    load = pltpu.make_async_copy(blocks, held, sems.at[0])
    load.start()
    load.wait()
    copies = []
    for number in range(outgoing.shape[0]):
        copy = pltpu.make_async_copy(
            held.at[chosen[0, number]], outgoing.at[number], sems.at[number]
        )
        copy.start()
        copies.append(copy)
    for copy in copies:
        copy.wait()


def pack(chosen, blocks):
    devices = chosen.shape[1]
    return call(
        pack_kernel,
        "pack",
        58,
        0,
        2 * blocks.size * 2,
        shape_of((devices,) + blocks.shape[1:], bf16),
        [SMEM, ANY],
        ANY,
        [pltpu.VMEM(blocks.shape, bf16), pltpu.SemaphoreType.DMA((devices,))],
        (chosen, blocks),
    )


def slot_place(slot, digits):
    place, weight = 0, 1
    for bit, radix in digits[:0:-1]:
        place += weight * ((slot // bit) % radix)
        weight *= radix
    return slot % 2, place


def place_shards(me, halves, table, digits, local):
    for slot in range(table.shape[0] // local):
        half, place = slot_place(slot, digits)
        start = pl.multiple_of((me ^ slot) * local, local)
        table[pl.ds(start, local), :] = halves[half][place * local : (place + 1) * local, :]


def split_sums(me, sums, local, kept, sent):
    odd = me % 2
    width = sums.shape[-1]
    pairs = sums.reshape(-1, 2, local, width)
    kept[...] = jnp.where(odd == 1, pairs[:, 1], pairs[:, 0]).reshape(kept.shape).astype(kept.dtype)
    sent[...] = jnp.where(odd == 1, pairs[:, 0], pairs[:, 1]).reshape(sent.shape).astype(sent.dtype)


def hub_first_kernel(
    digits, rows, cols, count, position, place_col, half0, half1, own_hbm, tiles_hbm,
    hubs, mine, kept, sent, own, tiles, table, total, picked, sems,
):
    hub_count, block_size, width = hubs.shape
    hub_rows = hub_count * block_size
    local = mine.shape[0]
    begin = rows.shape[0] - cols.shape[0]
    loads = [
        pltpu.make_async_copy(own_hbm, own, sems.at[0]),
        pltpu.make_async_copy(tiles_hbm.at[pl.ds(begin, cols.shape[0])], tiles, sems.at[1]),
    ]
    for load in loads:
        load.start()
    me = position[0]
    place_shards(me, (half0, half1), table, digits, local)
    total[...] = jnp.zeros_like(total)
    found = list_slots(rows, count, picked, begin, hub_count, True)
    step = 2 * block_size

    def rows_step(number, unused):
        cut = pl.ds(pl.multiple_of(number * step, step), step)
        lanes = lax.broadcasted_iota(jnp.int32, (step, hub_rows), 1)
        unit = jnp.where(place_col[cut, :] == lanes, 1.0, 0.0).astype(bf16)
        placed = dot(unit, table[...]).astype(bf16)
        hubs[pl.ds(number * 2, 2)] = placed.reshape(2, block_size, width)
        return unused

    lax.fori_loop(0, hub_rows // step, rows_step, 0)
    for load in loads:
        load.wait()
    add_products(rows, cols, picked, found, begin, tiles, hubs, own, total, 0, hub_count)
    split_sums(me, total[:hub_count], local, kept, sent)
    flat = hubs.reshape(hub_rows, width)
    mine[...] = flat[pl.ds(pl.multiple_of(me * local, local), local), :]


def hub_first(digits, rows, cols, count, position, place_col, halves, own, tiles, local):
    block_size, width = own.shape[1:]
    hub_rows = place_col.shape[0]
    hub_count = hub_rows // block_size
    half = shape_of((hub_rows // 2, width), f32)
    return call(
        functools.partial(hub_first_kernel, digits),
        "hub_first",
        54,
        2 * hub_rows * hub_rows * width,
        14 * MIB,
        (
            shape_of((hub_count, block_size, width), bf16),
            shape_of((local, width), bf16),
            half,
            half,
        ),
        [SMEM] * 4 + [VMEM] * 3 + [ANY] * 2,
        (VMEM,) * 4,
        [
            pltpu.VMEM(own.shape, bf16),
            pltpu.VMEM((cols.shape[0],) + tiles.shape[1:], bf16),
            pltpu.VMEM((hub_rows, width), bf16),
            pltpu.VMEM((hub_count + 1, block_size, width), f32),
            pltpu.SMEM((rows.shape[0],), jnp.int32),
            pltpu.SemaphoreType.DMA((2,)),
        ],
        (rows, cols, count, position, place_col) + tuple(halves) + (own, tiles),
    )


def hub_second_kernel(
    digits, rows, cols, count, position, place_row, half0, half1, own_hbm, tiles_hbm,
    hubs, mine, kept, sent, own, tiles, total, placed, picked, sems,
):
    hub_count, block_size, width = hubs.shape
    hub_rows = hub_count * block_size
    local = mine.shape[0]
    begin = rows.shape[0] - cols.shape[0]
    loads = [
        pltpu.make_async_copy(own_hbm, own, sems.at[0]),
        pltpu.make_async_copy(tiles_hbm.at[pl.ds(begin, cols.shape[0])], tiles, sems.at[1]),
    ]
    for load in loads:
        load.start()
    me = position[0]
    flat = hubs.reshape(hub_rows, width)
    place_shards(me, (half0, half1), flat, digits, local)
    total[...] = jnp.zeros_like(total)
    found = list_slots(rows, count, picked, begin, hub_count, True)

    def unit_rows(start, step):
        down = lax.broadcasted_iota(jnp.int32, (step, hub_rows), 0) + start
        return jnp.where(place_row[...] == down, 1.0, 0.0).astype(bf16)

    mine[...] = dot(unit_rows(me * local, local), flat[...]).astype(bf16)
    for load in loads:
        load.wait()
    add_products(rows, cols, picked, found, begin, tiles, hubs, own, total, 0, hub_count)
    sums = total[:hub_count].astype(bf16).reshape(hub_rows, width)
    step = 2 * block_size

    def rows_step(number, unused):
        start = number * step
        placed[pl.ds(pl.multiple_of(start, step), step), :] = dot(unit_rows(start, step), sums)
        return unused

    lax.fori_loop(0, hub_rows // step, rows_step, 0)
    split_sums(me, placed[...], local, kept, sent)


def hub_second(digits, rows, cols, count, position, place_row, halves, own, tiles, local):
    block_size, width = own.shape[1:]
    hub_rows = place_row.shape[1]
    hub_count = hub_rows // block_size
    return call(
        functools.partial(hub_second_kernel, digits),
        "hub_second",
        54,
        2 * hub_rows * hub_rows * width,
        14 * MIB,
        (
            shape_of((hub_count, block_size, width), bf16),
            shape_of((local, width), bf16),
            shape_of((hub_rows // 2, width), f32),
            shape_of((hub_rows // 2, width), bf16),
        ),
        [SMEM] * 4 + [VMEM] * 3 + [ANY] * 2,
        (VMEM,) * 4,
        [
            pltpu.VMEM(own.shape, bf16),
            pltpu.VMEM((cols.shape[0],) + tiles.shape[1:], bf16),
            pltpu.VMEM((hub_count + 1, block_size, width), f32),
            pltpu.VMEM((hub_rows, width), f32),
            pltpu.SMEM((rows.shape[0],), jnp.int32),
            pltpu.SemaphoreType.DMA((2,)),
        ],
        (rows, cols, count, position, place_row) + tuple(halves) + (own, tiles),
    )


def combine(position, kept, received, bit, radix, local, sent_type):
    rows = kept.shape[0] // radix
    width = kept.shape[1]

    def kernel(position, kept_in, *refs):
        received, outs = refs[: -radix], refs[-radix:]
        total = kept_in[...].astype(f32)
        for part in received:
            total = total + part[...].astype(f32)
        digit = (position[0] // bit) % radix
        parts = total.reshape(rows // local, radix, local, width)
        for offset, out in enumerate(outs):
            value = parts[:, 0]
            for number in range(1, radix):
                value = jnp.where((digit ^ offset) == number, parts[:, number], value)
            out[...] = value.reshape(rows, width).astype(out.dtype)

    shapes = [shape_of((rows, width), f32)] + [shape_of((rows, width), sent_type)] * (radix - 1)
    return call(
        kernel,
        "combine",
        16,
        kept.size,
        12 * kept.size,
        tuple(shapes),
        [SMEM] + [VMEM] * (1 + len(received)),
        (VMEM,) * radix,
        [],
        (position, kept) + tuple(received),
    )


def load_weights(layer, first_in, second_in, first, second, sems):
    loads = [
        pltpu.make_async_copy(first_in.at[layer], first, sems.at[0]),
        pltpu.make_async_copy(second_in.at[layer], second, sems.at[1]),
    ]
    for load in loads:
        load.start()
    return loads


def hub_network_kernel(layer, rows_in, *refs):
    parts, (first_in, second_in, out, first, second, sems) = refs[:-6], refs[-6:]
    loads = load_weights(layer, first_in, second_in, first, second, sems)
    u = rows_in[...].astype(f32)
    for part in parts:
        u = u + part[...].astype(f32)
    for load in loads:
        load.wait()
    out[...] = network(u, first, second, first.shape[-1])


def hub_network(layer, rows_in, parts, first, second):
    return call(
        functools.partial(hub_network_kernel, layer),
        "hub_network",
        58,
        4 * rows_in.size * first.shape[-1],
        2 * first.size,
        shape_of(rows_in.shape, bf16),
        [VMEM] * (1 + len(parts)) + [ANY] * 2,
        VMEM,
        [
            pltpu.VMEM(first.shape[1:], bf16),
            pltpu.VMEM(second.shape[1:], bf16),
            pltpu.SemaphoreType.DMA((2,)),
        ],
        (rows_in,) + tuple(parts) + (first, second),
    )


def before_kernel(
    layer, rows, cols, count, hubs_in, own_in, tiles_in, first_in, second_in, base, out,
    hubs, own, tiles, first, second, u, result, picked, marks, sems,
):
    own_count, block_size, width = own.shape
    hub_count = hubs.shape[0]
    begin = rows.shape[0] - cols.shape[0]
    loads = [
        pltpu.make_async_copy(own_in, own, sems.at[0]),
        pltpu.make_async_copy(hubs_in, hubs, sems.at[1]),
        pltpu.make_async_copy(tiles_in.at[pl.ds(begin, cols.shape[0])], tiles, sems.at[2]),
        pltpu.make_async_copy(first_in.at[layer], first, sems.at[3]),
        pltpu.make_async_copy(second_in.at[layer], second, sems.at[4]),
    ]
    for load in loads:
        load.start()
    found = list_slots(rows, count, picked, begin, hub_count, False)
    loads[0].wait()
    u[:own_count] = own[...].astype(f32)
    loads[1].wait()
    loads[2].wait()
    add_products(rows, cols, picked, found, begin, tiles, hubs, own, u, hub_count, own_count)
    store = pltpu.make_async_copy(u.at[pl.ds(0, own_count)], base, sems.at[5])
    store.start()
    found = list_blocks(rows, begin, own_count, hub_count, marks, picked, False)
    loads[3].wait()
    loads[4].wait()
    network_blocks(picked, found, u, first, second, result)
    last = pltpu.make_async_copy(result, out, sems.at[6])
    last.start()
    store.wait()
    last.wait()


def before(layer, rows, cols, count, hubs, own, tiles, first, second):
    own_count, block_size, width = own.shape
    return call(
        functools.partial(before_kernel, layer),
        "before",
        58,
        4 * own.size * first.shape[-1] // 3,
        18 * MIB,
        (shape_of(own.shape, f32), shape_of(own.shape, bf16)),
        [SMEM] * 3 + [ANY] * 5,
        (ANY, ANY),
        [
            pltpu.VMEM(hubs.shape, bf16),
            pltpu.VMEM(own.shape, bf16),
            pltpu.VMEM((cols.shape[0],) + tiles.shape[1:], bf16),
            pltpu.VMEM(first.shape[1:], bf16),
            pltpu.VMEM(second.shape[1:], bf16),
            pltpu.VMEM((own_count + 1, block_size, width), f32),
            pltpu.VMEM(own.shape, bf16),
            pltpu.SMEM((max(rows.shape[0], own_count),), jnp.int32),
            pltpu.SMEM((own_count,), jnp.int32),
            pltpu.SemaphoreType.DMA((7,)),
        ],
        (rows, cols, count, hubs, own, tiles, first, second),
    )


def after_kernel(
    layer, with_send, hub_count, rows, chosen, base, done, incoming, tiles, first_in, second_in, *refs
):
    out, refs = refs[0], refs[1:]
    if with_send:
        outgoing, refs = refs[0], refs[1:]
    u, inc, adj, first, second, result, listed, marks, sems = refs
    own_count = u.shape[0]
    remote = incoming.shape[0]
    loads = [
        pltpu.make_async_copy(incoming, inc, sems.at[0]),
        pltpu.make_async_copy(tiles.at[pl.ds(0, remote)], adj, sems.at[1]),
        pltpu.make_async_copy(base, u, sems.at[2]),
        pltpu.make_async_copy(first_in.at[layer], first, sems.at[3]),
        pltpu.make_async_copy(second_in.at[layer], second, sems.at[4]),
        pltpu.make_async_copy(done, result, sems.at[5]),
    ]
    for load in loads[:3]:
        load.start()
    found = list_blocks(rows, remote, own_count, hub_count, marks, listed, True)
    for load in loads[:3]:
        load.wait()
    for load in loads[3:]:
        load.start()
    group = 2 * GROUP

    def slots_step(number, unused):
        slots = [number * group + lane for lane in range(group)]
        products = [dot(adj[slot], inc[slot]) for slot in slots]
        for slot, product in zip(slots, products):
            u[rows[slot] - hub_count] += product
        return unused

    lax.fori_loop(0, remote // group, slots_step, 0)
    for load in loads[3:]:
        load.wait()
    network_blocks(listed, found, u, first, second, result)
    copies = []
    if with_send:
        for number in range(remote):
            copies.append(
                pltpu.make_async_copy(
                    result.at[chosen[0, number]], outgoing.at[number], sems.at[number]
                )
            )
    copies.append(pltpu.make_async_copy(result, out, sems.at[remote]))
    for copy in copies:
        copy.start()
    for copy in copies:
        copy.wait()


def after(layer, rows, chosen, base, done, incoming, tiles, first, second, hub_count, with_send):
    own_count, block_size, width = base.shape
    remote = incoming.shape[0]
    shapes = [shape_of(base.shape, bf16)]
    if with_send:
        shapes.append(shape_of(incoming.shape, bf16))
    return call(
        functools.partial(after_kernel, layer, with_send, hub_count),
        "after",
        58,
        4 * base.size * first.shape[-1],
        16 * MIB,
        tuple(shapes),
        [SMEM, SMEM] + [ANY] * 6,
        (ANY,) * len(shapes),
        [
            pltpu.VMEM(base.shape, f32),
            pltpu.VMEM(incoming.shape, bf16),
            pltpu.VMEM((remote,) + tiles.shape[1:], bf16),
            pltpu.VMEM(first.shape[1:], bf16),
            pltpu.VMEM(second.shape[1:], bf16),
            pltpu.VMEM(base.shape, bf16),
            pltpu.SMEM((own_count,), jnp.int32),
            pltpu.SMEM((own_count,), jnp.int32),
            pltpu.SemaphoreType.DMA((max(6, 1 + remote),)),
        ],
        (rows, chosen, base, done, incoming, tiles, first, second),
    )


def exchange(x, bit):
    devices = lax.axis_size("dev")
    return lax.ppermute(x, "dev", [(i, i ^ bit) for i in range(devices)])


def all_digits():
    devices = lax.axis_size("dev")
    digits, bit = [(1, 2)], 2
    while bit < devices:
        radix = 4 if 4 * bit <= devices else 2
        digits.append((bit, radix))
        bit *= radix
    return digits


def gather_step(x, bit, radix):
    return [x] + [exchange(x, bit * offset) for offset in range(1, radix)]


def gather_far(x, digits):
    return gather_step(x, *digits[-1])


def gather_near(pieces, digits):
    for digit in digits[-2:0:-1]:
        pieces = gather_step(jnp.concatenate(pieces, axis=0), *digit)
    x = jnp.concatenate(pieces, axis=0)
    return x, exchange(x, digits[0][0])


def scatter_near(position, kept, sent, digits, local):
    received = [exchange(sent, digits[0][0])]
    for bit, radix in digits[1:-1]:
        kept, *sent = combine(position, kept, received, bit, radix, local, bf16)
        received = [exchange(part, bit * (1 + number)) for number, part in enumerate(sent)]
    return kept, received


def scatter_far(position, kept, received, digits, local):
    bit, radix = digits[-1]
    kept, *sent = combine(position, kept, received, bit, radix, local, f32)
    return [kept] + [exchange(part, bit * (1 + number)) for number, part in enumerate(sent)]


def body(
    peripheral, hubs, tiles, tile_rows, local_cols, tile_count, send_list, hub_place, w_in, w_out
):
    position = lax.axis_index("dev")
    digits = all_digits()
    block_size = tiles.shape[1]
    width = peripheral.shape[1]
    own_count = peripheral.shape[0] // block_size
    hub_rows = hub_place.shape[0]
    hub_count = hub_rows // block_size
    local = hubs.shape[0]
    rows = jnp.where(tile_rows < hub_count, tile_rows, tile_rows - position * own_count)
    cols = jnp.where(local_cols < hub_count, local_cols, local_cols - position * own_count)
    place_col = hub_place.reshape(hub_rows, 1)
    place_row = hub_place.reshape(1, hub_rows)
    me = position.astype(jnp.int32).reshape(1)
    own = peripheral.reshape(own_count, block_size, width)
    all_to_all = functools.partial(
        lax.all_to_all, axis_name="dev", split_axis=0, concat_axis=0, tiled=True
    )

    outgoing = pack(send_list, own)
    pieces = gather_far(hubs, digits)
    outgoing, *pieces = lax.optimization_barrier((outgoing, *pieces))
    incoming = all_to_all(outgoing)
    halves = gather_near(pieces, digits)
    hub_table, mine, kept, sent = hub_first(
        digits, rows, cols, tile_count, me, place_col, halves, own, tiles, local
    )
    base, done = before(0, rows, cols, tile_count, hub_table, own, tiles, w_in, w_out)
    kept, received = scatter_near(me, kept, sent, digits, local)
    base, done, *received = lax.optimization_barrier((base, done, *received))
    parts = scatter_far(me, kept, received, digits, local)
    hub_new = hub_network(0, mine, parts, w_in, w_out)
    own, outgoing = after(
        0, rows, send_list, base, done, incoming, tiles, w_in, w_out, hub_count, True
    )

    pieces = gather_far(hub_new, digits)
    outgoing, *pieces = lax.optimization_barrier((outgoing, *pieces))
    incoming = all_to_all(outgoing)
    halves = gather_near(pieces, digits)
    hub_table, mine, kept, sent = hub_second(
        digits, rows, cols, tile_count, me, place_row, halves, own, tiles, local
    )
    base, done = before(1, rows, cols, tile_count, hub_table, own, tiles, w_in, w_out)
    kept, received = scatter_near(me, kept, sent, digits, local)
    base, done, *received = lax.optimization_barrier((base, done, *received))
    parts = scatter_far(me, kept, received, digits, local)
    hub_out = hub_network(1, mine, parts, w_in, w_out)
    (peri_out,) = after(
        1, rows, send_list, base, done, incoming, tiles, w_in, w_out, hub_count, False
    )
    return (peri_out.reshape(peripheral.shape), hub_out)


def solution(mesh):
    in_specs = (
        P("dev", None),
        P("dev", None),
        P("dev", None, None),
        P("dev"),
        P("dev"),
        P("dev"),
        P("dev", None),
        P(),
        P(),
        P(),
    )
    out_specs = (P("dev", None), P("dev", None))
    return jax.shard_map(body, mesh=mesh, in_specs=in_specs, out_specs=out_specs, check_vma=False)
```

profile of v0, /device:TPU:0, one launch (start us, length us, event | category | flops | bytes accessed | tf_op | source)
XLA Modules:
  0.0 211.4 jit_solution(2697304205087359180)
XLA Ops:
  0.6 3.1 %collective-permute-start = (bf16[64,256]{1,0:T(8,128)(2,1)}, bf16[64,256]{1,0:T(8,128)(2,1)S(1)}, u32[]{:S(2)}, u32[]{:S(2)}) collective-permute-start(bf16[64,256]{1,0:T(8,128)(2,1)} %param.11), channel_id=1, source_target_pairs={{0,8},{1,9},{2,10},{3,11},{4,12},{5,13},{6,14},{7,15},{8,0},{9,1},... | collective-permute-start | bytes 98312 | tf_op jit(solution)/shard_map/ppermute | solution.py:527
  3.7 2.6 %collective-permute-start.1 = (bf16[64,256]{1,0:T(8,128)(2,1)}, bf16[64,256]{1,0:T(8,128)(2,1)S(1)}, u32[]{:S(2)}, u32[]{:S(2)}) collective-permute-start(bf16[64,256]{1,0:T(8,128)(2,1)} %param.11), channel_id=1, source_target_pairs={{0,16},{1,17},{2,18},{3,19},{4,20},{5,21},{6,22},{7,23},{8,24},{9,... | collective-permute-start | bytes 98312 | tf_op jit(solution)/shard_map/ppermute | solution.py:527
  6.3 3.9 %pack.1 = bf16[32,128,256]{2,1,0:T(8,128)(2,1)} custom-call(s32[1,32]{1,0:T(1,128)} %chosen.5, bf16[32,128,256]{2,1,0:T(8,128)(2,1)} %bitcast.5), custom_call_target="tpu_custom_call" | custom-call | bytes 4194304 | tf_op jit(solution)/shard_map/pack/pallas_call | solution.py:29
  12.2 4.1 %all-to-all-start = ((bf16[32,128,256]{2,1,0:T(8,128)(2,1)}), bf16[32,128,256]{2,1,0:T(8,128)(2,1)S(1)}, u32[]{:S(2)}, u32[]{:S(2)}) async-start(bf16[32,128,256]{2,1,0:T(8,128)(2,1)} %pack.1), calls=%async_computation | async-start | bytes 4194304 | tf_op jit(solution)/shard_map/all_to_all | solution.py:593
  20.0 15.8 %collective-permute-done.3 = bf16[256,256]{1,0:T(8,128)(2,1)S(1)} collective-permute-done((bf16[256,256]{1,0:T(8,128)(2,1)S(1)}, bf16[256,256]{1,0:T(8,128)(2,1)S(1)}, u32[]{:S(2)}, u32[]{:S(2)}) %collective-permute-start.3) | collective-permute-done | bytes 131104 | tf_op jit(solution)/shard_map/ppermute | solution.py:527
  35.8 8.9 %collective-permute-done.5 = bf16[256,256]{1,0:T(8,128)(2,1)S(1)} collective-permute-done((bf16[256,256]{1,0:T(8,128)(2,1)S(1)}, bf16[256,256]{1,0:T(8,128)(2,1)S(1)}, u32[]{:S(2)}, u32[]{:S(2)}) %collective-permute-start.5) | collective-permute-done | bytes 131104 | tf_op jit(solution)/shard_map/ppermute | solution.py:527
  48.8 8.1 %hub_first.1 = (bf16[16,128,256]{2,1,0:T(8,128)(2,1)}, bf16[64,256]{1,0:T(8,128)(2,1)}, f32[1024,256]{1,0:T(8,128)}, f32[1024,256]{1,0:T(8,128)}) custom-call(s32[144]{0:T(256)} %compare_select_fusion.rows, s32[112]{0:T(128)} %compare_select_fusion.1.cols, s32[1]{0:T(128)S(6)} %copy.31.count, s32[1]{0:T(128)} %bitcast.position, s32[2048,1]{1,0:T(8,128)} %copy.12.place_col, ...), custom_call_target="tpu_custom_call" | custom-call | flops 2147483648 | bytes 14680064 | tf_op jit(solution)/shard_map/hub_first/pallas_call | solution.py:29
  57.0 2.9 %collective-permute-done.7.refs_0_ = f32[1024,256]{1,0:T(8,128)S(1)} collective-permute-done((f32[1024,256]{1,0:T(8,128)}, f32[1024,256]{1,0:T(8,128)S(1)}, u32[]{:S(2)}, u32[]{:S(2)}) %collective-permute-start.7) | collective-permute-done | bytes 1048608 | tf_op jit(solution)/shard_map/ppermute | solution.py:527
  61.3 3.1 %collective-permute-start.10 = (bf16[256,256]{1,0:T(8,128)(2,1)S(1)}, bf16[256,256]{1,0:T(8,128)(2,1)S(1)}, u32[]{:S(2)}, u32[]{:S(2)}) collective-permute-start(bf16[256,256]{1,0:T(8,128)(2,1)S(1)} %get-tuple-element.63), channel_id=1, source_target_pairs={{0,6},{1,7},{2,4},{3,5},{4,2},{5,3},{6,0},{7,1},{8,14},{9,15},{10,... | collective-permute-start | bytes 393224 | tf_op jit(solution)/shard_map/ppermute | solution.py:527
  66.9 10.4 %before.2 = (f32[32,128,256]{2,1,0:T(8,128)}, bf16[32,128,256]{2,1,0:T(8,128)(2,1)}) custom-call(s32[144]{0:T(256)} %compare_select_fusion.rows, s32[112]{0:T(128)} %compare_select_fusion.1.cols, s32[1]{0:T(128)S(6)} %copy.31.count, bf16[16,128,256]{2,1,0:T(8,128)(2,1)} %get-tuple-element.56.hubs_in, bf16[32,128,256]{2,1,0:T(8,128)(2,1)} %bitcast.7, ...), custom_call_target="tpu_custom_call" | custom-call | flops 2863311616 | bytes 18874368 | tf_op jit(solution)/shard_map/before/pallas_call | solution.py:29
  78.2 4.3 %collective-permute-start.13 = (f32[64,256]{1,0:T(8,128)S(1)}, f32[64,256]{1,0:T(8,128)S(1)}, u32[]{:S(2)}, u32[]{:S(2)}) collective-permute-start(f32[64,256]{1,0:T(8,128)S(1)} %get-tuple-element.76), channel_id=1, source_target_pairs={{0,24},{1,25},{2,26},{3,27},{4,28},{5,29},{6,30},{7,31},{8,16},{9,... | collective-permute-start | bytes 196616 | tf_op jit(solution)/shard_map/ppermute | solution.py:527
  84.2 2.5 %collective-permute-done.12.refs_2_ = f32[64,256]{1,0:T(8,128)S(1)} collective-permute-done((f32[64,256]{1,0:T(8,128)S(1)}, f32[64,256]{1,0:T(8,128)S(1)}, u32[]{:S(2)}, u32[]{:S(2)}) %collective-permute-start.12) | collective-permute-done | bytes 65568 | tf_op jit(solution)/shard_map/ppermute | solution.py:527
  87.4 3.7 %hub_network.2 = bf16[64,256]{1,0:T(8,128)(2,1)} custom-call(bf16[64,256]{1,0:T(8,128)(2,1)} %get-tuple-element.68.rows_in, f32[64,256]{1,0:T(8,128)} %copy-done.3, f32[64,256]{1,0:T(8,128)} %copy-done.9, f32[64,256]{1,0:T(8,128)} %copy-done.11, f32[64,256]{1,0:T(8,128)} %copy-done.13, bf16[2,256,2048]{2,1,0:T(8,128)(2,1)} %refs_4_.3, ...), custom_call_target="tpu_custom_call" | custom-call | flops 134217728 | bytes 2097152 | tf_op jit(solution)/shard_map/hub_network/pallas_call | solution.py:29
  96.9 16.9 %after.2 = (bf16[32,128,256]{2,1,0:T(8,128)(2,1)}, bf16[32,128,256]{2,1,0:T(8,128)(2,1)}) custom-call(s32[144]{0:T(256)} %compare_select_fusion.rows, s32[1,32]{1,0:T(1,128)} %chosen.5, f32[32,128,256]{2,1,0:T(8,128)} %get-tuple-element.64.base, bf16[32,128,256]{2,1,0:T(8,128)(2,1)} %get-tuple-element.65.done, bf16[32,128,256]{2,1,0:T(8,128)(2,1)} %copy-done.4, ...), custom_call_target="tpu_custom_call" | custom-call | flops 8589934592 | bytes 16777216 | tf_op jit(solution)/shard_map/after/pallas_call | solution.py:29
  113.9 6.0 %all-to-all-start.1 = ((bf16[32,128,256]{2,1,0:T(8,128)(2,1)}), bf16[32,128,256]{2,1,0:T(8,128)(2,1)S(1)}, u32[]{:S(2)}, u32[]{:S(2)}) async-start(bf16[32,128,256]{2,1,0:T(8,128)(2,1)} %get-tuple-element.92), calls=%async_computation.1 | async-start | bytes 4194304 | tf_op jit(solution)/shard_map/all_to_all | solution.py:609
  123.5 15.8 %collective-permute-done.17 = bf16[256,256]{1,0:T(8,128)(2,1)S(1)} collective-permute-done((bf16[256,256]{1,0:T(8,128)(2,1)S(1)}, bf16[256,256]{1,0:T(8,128)(2,1)S(1)}, u32[]{:S(2)}, u32[]{:S(2)}) %collective-permute-start.17) | collective-permute-done | bytes 131104 | tf_op jit(solution)/shard_map/ppermute | solution.py:527
  139.3 8.9 %collective-permute-done.19 = bf16[256,256]{1,0:T(8,128)(2,1)S(1)} collective-permute-done((bf16[256,256]{1,0:T(8,128)(2,1)S(1)}, bf16[256,256]{1,0:T(8,128)(2,1)S(1)}, u32[]{:S(2)}, u32[]{:S(2)}) %collective-permute-start.19) | collective-permute-done | bytes 131104 | tf_op jit(solution)/shard_map/ppermute | solution.py:527
  151.0 9.7 %hub_second.1 = (bf16[16,128,256]{2,1,0:T(8,128)(2,1)}, bf16[64,256]{1,0:T(8,128)(2,1)}, f32[1024,256]{1,0:T(8,128)}, bf16[1024,256]{1,0:T(8,128)(2,1)}) custom-call(s32[144]{0:T(256)} %compare_select_fusion.rows, s32[112]{0:T(128)} %compare_select_fusion.1.cols, s32[1]{0:T(128)S(6)} %copy.31.count, s32[1]{0:T(128)} %bitcast.position, s32[1,2048]{1,0:T(1,128)} %bitcast.8, ...), custom_call_target="tpu_custom_call" | custom-call | flops 2147483648 | bytes 14680064 | tf_op jit(solution)/shard_map/hub_second/pallas_call | solution.py:29
  164.4 3.2 %collective-permute-start.22 = (bf16[256,256]{1,0:T(8,128)(2,1)S(1)}, bf16[256,256]{1,0:T(8,128)(2,1)S(1)}, u32[]{:S(2)}, u32[]{:S(2)}) collective-permute-start(bf16[256,256]{1,0:T(8,128)(2,1)S(1)} %get-tuple-element.87), channel_id=1, source_target_pairs={{0,2},{1,3},{2,0},{3,1},{4,6},{5,7},{6,4},{7,5},{8,10},{9,11},{10,... | collective-permute-start | bytes 393224 | tf_op jit(solution)/shard_map/ppermute | solution.py:527
  169.2 10.6 %before.3 = (f32[32,128,256]{2,1,0:T(8,128)}, bf16[32,128,256]{2,1,0:T(8,128)(2,1)}) custom-call(s32[144]{0:T(256)} %compare_select_fusion.rows, s32[112]{0:T(128)} %compare_select_fusion.1.cols, s32[1]{0:T(128)S(6)} %copy.31.count, bf16[16,128,256]{2,1,0:T(8,128)(2,1)} %get-tuple-element.82.hubs_in, bf16[32,128,256]{2,1,0:T(8,128)(2,1)} %get-tuple-element.81.own_hbm.own_in, ...), custom_call_target="tpu_custom_call" | custom-call | flops 2863311616 | bytes 18874368 | tf_op jit(solution)/shard_map/before/pallas_call | solution.py:29
  181.5 3.4 %collective-permute-start.27 = (f32[64,256]{1,0:T(8,128)S(1)}, f32[64,256]{1,0:T(8,128)S(1)}, u32[]{:S(2)}, u32[]{:S(2)}) collective-permute-start(f32[64,256]{1,0:T(8,128)S(1)} %get-tuple-element.101), channel_id=1, source_target_pairs={{0,24},{1,25},{2,26},{3,27},{4,28},{5,29},{6,30},{7,31},{8,16},{9,... | collective-permute-start | bytes 196616 | tf_op jit(solution)/shard_map/ppermute | solution.py:527
  186.8 2.5 %collective-permute-done.26.refs_2_ = f32[64,256]{1,0:T(8,128)S(1)} collective-permute-done((f32[64,256]{1,0:T(8,128)S(1)}, f32[64,256]{1,0:T(8,128)S(1)}, u32[]{:S(2)}, u32[]{:S(2)}) %collective-permute-start.26) | collective-permute-done | bytes 65568 | tf_op jit(solution)/shard_map/ppermute | solution.py:527
  189.9 3.7 %hub_network.3 = bf16[64,256]{1,0:T(8,128)(2,1)} custom-call(bf16[64,256]{1,0:T(8,128)(2,1)} %get-tuple-element.93.rows_in, f32[64,256]{1,0:T(8,128)} %copy-done.2, f32[64,256]{1,0:T(8,128)} %copy-done.10, f32[64,256]{1,0:T(8,128)} %copy-done.12, f32[64,256]{1,0:T(8,128)} %copy-done.14, bf16[2,256,2048]{2,1,0:T(8,128)(2,1)} %refs_4_.3, ...), custom_call_target="tpu_custom_call" | custom-call | flops 134217728 | bytes 2097152 | tf_op jit(solution)/shard_map/hub_network/pallas_call | solution.py:29
  195.0 16.2 %after.3 = bf16[32,128,256]{2,1,0:T(8,128)(2,1)} custom-call(s32[144]{0:T(256)} %compare_select_fusion.rows, s32[1,32]{1,0:T(1,128)} %chosen.5, f32[32,128,256]{2,1,0:T(8,128)} %get-tuple-element.90.base, bf16[32,128,256]{2,1,0:T(8,128)(2,1)} %get-tuple-element.91.done, bf16[32,128,256]{2,1,0:T(8,128)(2,1)} %copy-done.5, bf16[144,128,128]{2,1,0:T(8,128)(2,1)} %tiles.3, ...), custom_call_target="tpu_custom_call" | custom-call | flops 8589934592 | bytes 16777216 | tf_op jit(solution)/shard_map/after/pallas_call | solution.py:29
  (108 shorter events, 39.1 us)
Async XLA Ops:
  0.6 9.6 %collective-permute-start = (bf16[64,256]{1,0:T(8,128)(2,1)}, bf16[64,256]{1,0:T(8,128)(2,1)S(1)}, u32[]{:S(2)}, u32[]{:S(2)}) collective-permute-start(bf16[64,256]{1,0:T(8,128)(2,1)} %param.11), channel_id=1, source_target_pairs={{0,8},{1,9},{2,10},{3,11},{4,12},{5,13},{6,14},{7,15},{8,0},{9,1},... | collective-permute-start | bytes 98312 | tf_op jit(solution)/shard_map/ppermute | solution.py:527
  3.7 6.5 %collective-permute-start.1 = (bf16[64,256]{1,0:T(8,128)(2,1)}, bf16[64,256]{1,0:T(8,128)(2,1)S(1)}, u32[]{:S(2)}, u32[]{:S(2)}) collective-permute-start(bf16[64,256]{1,0:T(8,128)(2,1)} %param.11), channel_id=1, source_target_pairs={{0,16},{1,17},{2,18},{3,19},{4,20},{5,21},{6,22},{7,23},{8,24},{9,... | collective-permute-start | bytes 98312 | tf_op jit(solution)/shard_map/ppermute | solution.py:527
  12.2 83.4 %all-to-all-start = ((bf16[32,128,256]{2,1,0:T(8,128)(2,1)}), bf16[32,128,256]{2,1,0:T(8,128)(2,1)S(1)}, u32[]{:S(2)}, u32[]{:S(2)}) async-start(bf16[32,128,256]{2,1,0:T(8,128)(2,1)} %pack.1), calls=%async_computation | async-start | bytes 4194304 | tf_op jit(solution)/shard_map/all_to_all | solution.py:593
  16.5 19.3 %collective-permute-start.3 = (bf16[256,256]{1,0:T(8,128)(2,1)S(1)}, bf16[256,256]{1,0:T(8,128)(2,1)S(1)}, u32[]{:S(2)}, u32[]{:S(2)}) collective-permute-start(bf16[256,256]{1,0:T(8,128)(2,1)S(1)} %get-tuple-element.110), channel_id=1, source_target_pairs={{0,2},{1,3},{2,0},{3,1},{4,6},{5,7},{6,4},{7,5},{8,10},{9,11},{10,... | collective-permute-start | bytes 393224 | tf_op jit(solution)/shard_map/ppermute | solution.py:527
  18.3 17.5 %collective-permute-start.4 = (bf16[256,256]{1,0:T(8,128)(2,1)S(1)}, bf16[256,256]{1,0:T(8,128)(2,1)S(1)}, u32[]{:S(2)}, u32[]{:S(2)}) collective-permute-start(bf16[256,256]{1,0:T(8,128)(2,1)S(1)} %get-tuple-element.110), channel_id=1, source_target_pairs={{0,4},{1,5},{2,6},{3,7},{4,0},{5,1},{6,2},{7,3},{8,12},{9,13},{10,... | collective-permute-start | bytes 393224 | tf_op jit(solution)/shard_map/ppermute | solution.py:527
  19.8 25.0 %collective-permute-start.5 = (bf16[256,256]{1,0:T(8,128)(2,1)S(1)}, bf16[256,256]{1,0:T(8,128)(2,1)S(1)}, u32[]{:S(2)}, u32[]{:S(2)}) collective-permute-start(bf16[256,256]{1,0:T(8,128)(2,1)S(1)} %get-tuple-element.110), channel_id=1, source_target_pairs={{0,6},{1,7},{2,4},{3,5},{4,2},{5,3},{6,0},{7,1},{8,14},{9,15},{10,... | collective-permute-start | bytes 393224 | tf_op jit(solution)/shard_map/ppermute | solution.py:527
  61.3 16.0 %collective-permute-start.10 = (bf16[256,256]{1,0:T(8,128)(2,1)S(1)}, bf16[256,256]{1,0:T(8,128)(2,1)S(1)}, u32[]{:S(2)}, u32[]{:S(2)}) collective-permute-start(bf16[256,256]{1,0:T(8,128)(2,1)S(1)} %get-tuple-element.63), channel_id=1, source_target_pairs={{0,6},{1,7},{2,4},{3,5},{4,2},{5,3},{6,0},{7,1},{8,14},{9,15},{10,... | collective-permute-start | bytes 393224 | tf_op jit(solution)/shard_map/ppermute | solution.py:527
  64.4 13.0 %collective-permute-start.8 = (bf16[256,256]{1,0:T(8,128)(2,1)S(1)}, bf16[256,256]{1,0:T(8,128)(2,1)S(1)}, u32[]{:S(2)}, u32[]{:S(2)}) collective-permute-start(bf16[256,256]{1,0:T(8,128)(2,1)S(1)} %get-tuple-element.61), channel_id=1, source_target_pairs={{0,2},{1,3},{2,0},{3,1},{4,6},{5,7},{6,4},{7,5},{8,10},{9,11},{10,... | collective-permute-start | bytes 393224 | tf_op jit(solution)/shard_map/ppermute | solution.py:527
  66.9 10.4 %collective-permute-start.9 = (bf16[256,256]{1,0:T(8,128)(2,1)S(1)}, bf16[256,256]{1,0:T(8,128)(2,1)S(1)}, u32[]{:S(2)}, u32[]{:S(2)}) collective-permute-start(bf16[256,256]{1,0:T(8,128)(2,1)S(1)} %get-tuple-element.62), channel_id=1, source_target_pairs={{0,4},{1,5},{2,6},{3,7},{4,0},{5,1},{6,2},{7,3},{8,12},{9,13},{10,... | collective-permute-start | bytes 393224 | tf_op jit(solution)/shard_map/ppermute | solution.py:527
  78.0 6.2 %collective-permute-start.11 = (f32[64,256]{1,0:T(8,128)S(1)}, f32[64,256]{1,0:T(8,128)S(1)}, u32[]{:S(2)}, u32[]{:S(2)}) collective-permute-start(f32[64,256]{1,0:T(8,128)S(1)} %get-tuple-element.74), channel_id=1, source_target_pairs={{0,8},{1,9},{2,10},{3,11},{4,12},{5,13},{6,14},{7,15},{8,0},{9,1},... | collective-permute-start | bytes 196616 | tf_op jit(solution)/shard_map/ppermute | solution.py:527
  78.1 8.7 %collective-permute-start.12 = (f32[64,256]{1,0:T(8,128)S(1)}, f32[64,256]{1,0:T(8,128)S(1)}, u32[]{:S(2)}, u32[]{:S(2)}) collective-permute-start(f32[64,256]{1,0:T(8,128)S(1)} %get-tuple-element.75), channel_id=1, source_target_pairs={{0,16},{1,17},{2,18},{3,19},{4,20},{5,21},{6,22},{7,23},{8,24},{9,... | collective-permute-start | bytes 196616 | tf_op jit(solution)/shard_map/ppermute | solution.py:527
  78.2 8.6 %collective-permute-start.13 = (f32[64,256]{1,0:T(8,128)S(1)}, f32[64,256]{1,0:T(8,128)S(1)}, u32[]{:S(2)}, u32[]{:S(2)}) collective-permute-start(f32[64,256]{1,0:T(8,128)S(1)} %get-tuple-element.76), channel_id=1, source_target_pairs={{0,24},{1,25},{2,26},{3,27},{4,28},{5,29},{6,30},{7,31},{8,16},{9,... | collective-permute-start | bytes 196616 | tf_op jit(solution)/shard_map/ppermute | solution.py:527
  91.1 22.7 %collective-permute-start.14 = (bf16[64,256]{1,0:T(8,128)(2,1)}, bf16[64,256]{1,0:T(8,128)(2,1)S(1)}, u32[]{:S(2)}, u32[]{:S(2)}) collective-permute-start(bf16[64,256]{1,0:T(8,128)(2,1)} %hub_network.2), channel_id=1, source_target_pairs={{0,8},{1,9},{2,10},{3,11},{4,12},{5,13},{6,14},{7,15},{8,0},{9,1},... | collective-permute-start | bytes 98312 | tf_op jit(solution)/shard_map/ppermute | solution.py:527
  93.1 20.7 %collective-permute-start.15 = (bf16[64,256]{1,0:T(8,128)(2,1)}, bf16[64,256]{1,0:T(8,128)(2,1)S(1)}, u32[]{:S(2)}, u32[]{:S(2)}) collective-permute-start(bf16[64,256]{1,0:T(8,128)(2,1)} %hub_network.2), channel_id=1, source_target_pairs={{0,16},{1,17},{2,18},{3,19},{4,20},{5,21},{6,22},{7,23},{8,24},{9,... | collective-permute-start | bytes 98312 | tf_op jit(solution)/shard_map/ppermute | solution.py:527
  93.7 20.1 %collective-permute-start.16 = (bf16[64,256]{1,0:T(8,128)(2,1)}, bf16[64,256]{1,0:T(8,128)(2,1)S(1)}, u32[]{:S(2)}, u32[]{:S(2)}) collective-permute-start(bf16[64,256]{1,0:T(8,128)(2,1)} %hub_network.2), channel_id=1, source_target_pairs={{0,24},{1,25},{2,26},{3,27},{4,28},{5,29},{6,30},{7,31},{8,16},{9,... | collective-permute-start | bytes 98312 | tf_op jit(solution)/shard_map/ppermute | solution.py:527
  113.9 79.8 %all-to-all-start.1 = ((bf16[32,128,256]{2,1,0:T(8,128)(2,1)}), bf16[32,128,256]{2,1,0:T(8,128)(2,1)S(1)}, u32[]{:S(2)}, u32[]{:S(2)}) async-start(bf16[32,128,256]{2,1,0:T(8,128)(2,1)} %get-tuple-element.92), calls=%async_computation.1 | async-start | bytes 4194304 | tf_op jit(solution)/shard_map/all_to_all | solution.py:609
  119.9 19.3 %collective-permute-start.17 = (bf16[256,256]{1,0:T(8,128)(2,1)S(1)}, bf16[256,256]{1,0:T(8,128)(2,1)S(1)}, u32[]{:S(2)}, u32[]{:S(2)}) collective-permute-start(bf16[256,256]{1,0:T(8,128)(2,1)S(1)} %get-tuple-element.102), channel_id=1, source_target_pairs={{0,2},{1,3},{2,0},{3,1},{4,6},{5,7},{6,4},{7,5},{8,10},{9,11},{10,... | collective-permute-start | bytes 393224 | tf_op jit(solution)/shard_map/ppermute | solution.py:527
  121.8 17.5 %collective-permute-start.18 = (bf16[256,256]{1,0:T(8,128)(2,1)S(1)}, bf16[256,256]{1,0:T(8,128)(2,1)S(1)}, u32[]{:S(2)}, u32[]{:S(2)}) collective-permute-start(bf16[256,256]{1,0:T(8,128)(2,1)S(1)} %get-tuple-element.102), channel_id=1, source_target_pairs={{0,4},{1,5},{2,6},{3,7},{4,0},{5,1},{6,2},{7,3},{8,12},{9,13},{10,... | collective-permute-start | bytes 393224 | tf_op jit(solution)/shard_map/ppermute | solution.py:527
  123.2 25.0 %collective-permute-start.19 = (bf16[256,256]{1,0:T(8,128)(2,1)S(1)}, bf16[256,256]{1,0:T(8,128)(2,1)S(1)}, u32[]{:S(2)}, u32[]{:S(2)}) collective-permute-start(bf16[256,256]{1,0:T(8,128)(2,1)S(1)} %get-tuple-element.102), channel_id=1, source_target_pairs={{0,6},{1,7},{2,4},{3,5},{4,2},{5,3},{6,0},{7,1},{8,14},{9,15},{10,... | collective-permute-start | bytes 393224 | tf_op jit(solution)/shard_map/ppermute | solution.py:527
  164.4 15.4 %collective-permute-start.22 = (bf16[256,256]{1,0:T(8,128)(2,1)S(1)}, bf16[256,256]{1,0:T(8,128)(2,1)S(1)}, u32[]{:S(2)}, u32[]{:S(2)}) collective-permute-start(bf16[256,256]{1,0:T(8,128)(2,1)S(1)} %get-tuple-element.87), channel_id=1, source_target_pairs={{0,2},{1,3},{2,0},{3,1},{4,6},{5,7},{6,4},{7,5},{8,10},{9,11},{10,... | collective-permute-start | bytes 393224 | tf_op jit(solution)/shard_map/ppermute | solution.py:527
  167.6 12.2 %collective-permute-start.23 = (bf16[256,256]{1,0:T(8,128)(2,1)S(1)}, bf16[256,256]{1,0:T(8,128)(2,1)S(1)}, u32[]{:S(2)}, u32[]{:S(2)}) collective-permute-start(bf16[256,256]{1,0:T(8,128)(2,1)S(1)} %get-tuple-element.88), channel_id=1, source_target_pairs={{0,4},{1,5},{2,6},{3,7},{4,0},{5,1},{6,2},{7,3},{8,12},{9,13},{10,... | collective-permute-start | bytes 393224 | tf_op jit(solution)/shard_map/ppermute | solution.py:527
  167.8 12.0 %collective-permute-start.24 = (bf16[256,256]{1,0:T(8,128)(2,1)S(1)}, bf16[256,256]{1,0:T(8,128)(2,1)S(1)}, u32[]{:S(2)}, u32[]{:S(2)}) collective-permute-start(bf16[256,256]{1,0:T(8,128)(2,1)S(1)} %get-tuple-element.89), channel_id=1, source_target_pairs={{0,6},{1,7},{2,4},{3,5},{4,2},{5,3},{6,0},{7,1},{8,14},{9,15},{10,... | collective-permute-start | bytes 393224 | tf_op jit(solution)/shard_map/ppermute | solution.py:527
  180.6 8.7 %collective-permute-start.26 = (f32[64,256]{1,0:T(8,128)S(1)}, f32[64,256]{1,0:T(8,128)S(1)}, u32[]{:S(2)}, u32[]{:S(2)}) collective-permute-start(f32[64,256]{1,0:T(8,128)S(1)} %get-tuple-element.100), channel_id=1, source_target_pairs={{0,16},{1,17},{2,18},{3,19},{4,20},{5,21},{6,22},{7,23},{8,24},{9,... | collective-permute-start | bytes 196616 | tf_op jit(solution)/shard_map/ppermute | solution.py:527
  181.5 7.8 %collective-permute-start.27 = (f32[64,256]{1,0:T(8,128)S(1)}, f32[64,256]{1,0:T(8,128)S(1)}, u32[]{:S(2)}, u32[]{:S(2)}) collective-permute-start(f32[64,256]{1,0:T(8,128)S(1)} %get-tuple-element.101), channel_id=1, source_target_pairs={{0,24},{1,25},{2,26},{3,27},{4,28},{5,29},{6,30},{7,31},{8,16},{9,... | collective-permute-start | bytes 196616 | tf_op jit(solution)/shard_map/ppermute | solution.py:527
  (27 other events, 152.2 us)
where the time goes:
time: 214 us; the launch traced here: 211 us
  Pallas kernels  84 us (39%)
  waiting for transfers between devices  66.9 us (31%)
  starting transfers between devices  46.8 us (22%)
  local copies, waits for them, and re-layouts  10.7 us (5%)
    pallas_call x13, Pallas kernels, call(): pl.pallas_call(kernel, out_shape=out_shape, in_specs=in_specs, out_specs=...  84 us
    ppermute x28, waiting for transfers between devices, exchange(): return lax.ppermute(x, 'dev', [(i, i ^ bit) for i in range(devices)])  66.9 us
    ppermute x28, starting transfers between devices, exchange(): return lax.ppermute(x, 'dev', [(i, i ^ bit) for i in range(devices)])  36.7 us
    all_to_all x2, starting transfers between devices, body(): incoming = all_to_all(outgoing)  10.1 us
    unnamed x52, local copies, waits for them, and re-layouts  9.34 us
  transfers between devices with their start and end apart: 30, of which 12 were waited for; matrix products, arithmetic and copies ran while one was open for 1% of the time, Pallas kernels for 32%

commit v1 on v0

--- a/solution.py
+++ b/solution.py
@@ -61,6 +61,22 @@
     return lax.fori_loop(begin, count[0], step, jnp.int32(0))
 
 
+def start_tiles(picked, found, source, tiles, sems):
+    def step(place, unused):
+        pltpu.make_async_copy(source.at[picked[place]], tiles.at[place], sems.at[place]).start()
+        return unused
+
+    lax.fori_loop(0, found, step, 0)
+
+
+def wait_tiles(picked, found, source, tiles, sems):
+    def step(place, unused):
+        pltpu.make_async_copy(source.at[picked[place]], tiles.at[place], sems.at[place]).wait()
+        return unused
+
+    lax.fori_loop(0, found, step, 0)
+
+
 def add_products(rows, cols, picked, found, begin, tiles, hubs, own, total, shift, spare):
     hub_count = hubs.shape[0]
 
@@ -69,12 +85,13 @@
         for lane in range(GROUP):
             place = number * GROUP + lane
             live = place < found
-            slot = picked[jnp.minimum(place, found - 1)]
+            place = jnp.minimum(place, found - 1)
+            slot = picked[place]
             where.append(jnp.where(live, rows[slot] - shift, spare))
             col = cols[slot - begin]
             of_hub = hubs[jnp.minimum(col, hub_count - 1)]
             of_own = own[jnp.maximum(col - hub_count, 0)]
-            products.append(dot(tiles[slot - begin], jnp.where(col < hub_count, of_hub, of_own)))
+            products.append(dot(tiles[place], jnp.where(col < hub_count, of_hub, of_own)))
         for row, product in zip(where, products):
             total[row] += product
         return unused
@@ -82,7 +99,23 @@
     lax.fori_loop(0, (found + GROUP - 1) // GROUP, step, 0)
 
 
-def list_blocks(rows, remote, own_count, hub_count, marks, listed, want_remote):
+def each_block(listed, found, copy_of, act):
+    def step(number, unused):
+        act(copy_of(listed[number]))
+        return unused
+
+    lax.fori_loop(0, found, step, 0)
+
+
+def start(copy):
+    copy.start()
+
+
+def wait(copy):
+    copy.wait()
+
+
+def list_blocks(rows, remote, own_count, hub_count, marks, fed, free):
     def clear(block, unused):
         marks[block] = 0
         return unused
@@ -92,24 +125,33 @@
         return unused
 
     def take(block, found):
-        listed[found] = block
-        return found + (marks[block] if want_remote else 1 - marks[block])
+        fed[found] = block
+        free[block - found] = block
+        return found + marks[block]
 
     lax.fori_loop(0, own_count, clear, 0)
     lax.fori_loop(0, remote, mark, 0)
-    return lax.fori_loop(0, own_count, take, jnp.int32(0))
-
-
-def network_blocks(listed, found, u, first, second, result):
+    found = lax.fori_loop(0, own_count, take, jnp.int32(0))
+    return found, own_count - found
+
+
+def network_blocks(listed, found, read, first, second, result, finish):
+    size = result.shape[1]
+
     def step(number, unused):
         blocks = [
             listed[jnp.minimum(number * GROUP + lane, found - 1)] for lane in range(GROUP)
         ]
-        values = jnp.concatenate([u[block] for block in blocks], axis=0)
+        values = jnp.concatenate([read(block) for block in blocks], axis=0)
         values = network(values, first, second, 512)
-        size = u.shape[1]
         for lane, block in enumerate(blocks):
             result[block] = values[lane * size : (lane + 1) * size]
+        for lane, block in enumerate(blocks):
+
+            @pl.when(number * GROUP + lane < found)
+            def _(block=block):
+                finish(block).start()
+
         return unused
 
     lax.fori_loop(0, (found + GROUP - 1) // GROUP, step, 0)
@@ -177,16 +219,13 @@
     hub_rows = hub_count * block_size
     local = mine.shape[0]
     begin = rows.shape[0] - cols.shape[0]
-    loads = [
-        pltpu.make_async_copy(own_hbm, own, sems.at[0]),
-        pltpu.make_async_copy(tiles_hbm.at[pl.ds(begin, cols.shape[0])], tiles, sems.at[1]),
-    ]
-    for load in loads:
-        load.start()
+    found = list_slots(rows, count, picked, begin, hub_count, True)
+    start_tiles(picked, found, tiles_hbm, tiles, sems)
+    load = pltpu.make_async_copy(own_hbm, own, sems.at[cols.shape[0]])
+    load.start()
     me = position[0]
     place_shards(me, (half0, half1), table, digits, local)
     total[...] = jnp.zeros_like(total)
-    found = list_slots(rows, count, picked, begin, hub_count, True)
     step = 2 * block_size
 
     def rows_step(number, unused):
@@ -198,8 +237,8 @@
         return unused
 
     lax.fori_loop(0, hub_rows // step, rows_step, 0)
-    for load in loads:
-        load.wait()
+    load.wait()
+    wait_tiles(picked, found, tiles_hbm, tiles, sems)
     add_products(rows, cols, picked, found, begin, tiles, hubs, own, total, 0, hub_count)
     split_sums(me, total[:hub_count], local, kept, sent)
     flat = hubs.reshape(hub_rows, width)
@@ -231,7 +270,7 @@
             pltpu.VMEM((hub_rows, width), bf16),
             pltpu.VMEM((hub_count + 1, block_size, width), f32),
             pltpu.SMEM((rows.shape[0],), jnp.int32),
-            pltpu.SemaphoreType.DMA((2,)),
+            pltpu.SemaphoreType.DMA((cols.shape[0] + 1,)),
         ],
         (rows, cols, count, position, place_col) + tuple(halves) + (own, tiles),
     )
@@ -245,25 +284,22 @@
     hub_rows = hub_count * block_size
     local = mine.shape[0]
     begin = rows.shape[0] - cols.shape[0]
-    loads = [
-        pltpu.make_async_copy(own_hbm, own, sems.at[0]),
-        pltpu.make_async_copy(tiles_hbm.at[pl.ds(begin, cols.shape[0])], tiles, sems.at[1]),
-    ]
-    for load in loads:
-        load.start()
+    found = list_slots(rows, count, picked, begin, hub_count, True)
+    start_tiles(picked, found, tiles_hbm, tiles, sems)
+    load = pltpu.make_async_copy(own_hbm, own, sems.at[cols.shape[0]])
+    load.start()
     me = position[0]
     flat = hubs.reshape(hub_rows, width)
     place_shards(me, (half0, half1), flat, digits, local)
     total[...] = jnp.zeros_like(total)
-    found = list_slots(rows, count, picked, begin, hub_count, True)
 
     def unit_rows(start, step):
         down = lax.broadcasted_iota(jnp.int32, (step, hub_rows), 0) + start
         return jnp.where(place_row[...] == down, 1.0, 0.0).astype(bf16)
 
     mine[...] = dot(unit_rows(me * local, local), flat[...]).astype(bf16)
-    for load in loads:
-        load.wait()
+    load.wait()
+    wait_tiles(picked, found, tiles_hbm, tiles, sems)
     add_products(rows, cols, picked, found, begin, tiles, hubs, own, total, 0, hub_count)
     sums = total[:hub_count].astype(bf16).reshape(hub_rows, width)
     step = 2 * block_size
@@ -301,7 +337,7 @@
             pltpu.VMEM((hub_count + 1, block_size, width), f32),
             pltpu.VMEM((hub_rows, width), f32),
             pltpu.SMEM((rows.shape[0],), jnp.int32),
-            pltpu.SemaphoreType.DMA((2,)),
+            pltpu.SemaphoreType.DMA((cols.shape[0] + 1,)),
         ],
         (rows, cols, count, position, place_row) + tuple(halves) + (own, tiles),
     )
@@ -364,7 +400,7 @@
     return call(
         functools.partial(hub_network_kernel, layer),
         "hub_network",
-        58,
+        24,
         4 * rows_in.size * first.shape[-1],
         2 * first.size,
         shape_of(rows_in.shape, bf16),
@@ -381,36 +417,37 @@
 
 def before_kernel(
     layer, rows, cols, count, hubs_in, own_in, tiles_in, first_in, second_in, base, out,
-    hubs, own, tiles, first, second, u, result, picked, marks, sems,
+    hubs, own, tiles, first, second, u, result, picked, marks, fed, free, sems, block_sems, sem,
 ):
-    own_count, block_size, width = own.shape
+    own_count = own.shape[0]
     hub_count = hubs.shape[0]
     begin = rows.shape[0] - cols.shape[0]
-    loads = [
-        pltpu.make_async_copy(own_in, own, sems.at[0]),
-        pltpu.make_async_copy(hubs_in, hubs, sems.at[1]),
-        pltpu.make_async_copy(tiles_in.at[pl.ds(begin, cols.shape[0])], tiles, sems.at[2]),
-        pltpu.make_async_copy(first_in.at[layer], first, sems.at[3]),
-        pltpu.make_async_copy(second_in.at[layer], second, sems.at[4]),
-    ]
+    load_own = pltpu.make_async_copy(own_in, own, sem.at[0])
+    load_hubs = pltpu.make_async_copy(hubs_in, hubs, sem.at[1])
+    load_own.start()
+    load_hubs.start()
+    found = list_slots(rows, count, picked, begin, hub_count, False)
+    start_tiles(picked, found, tiles_in, tiles, sems)
+    n_fed, n_free = list_blocks(rows, begin, own_count, hub_count, marks, fed, free)
+    load_own.wait()
+    u[:own_count] = own[...].astype(f32)
+    load_hubs.wait()
+    wait_tiles(picked, found, tiles_in, tiles, sems)
+    loads = load_weights(layer, first_in, second_in, first, second, sem.at[pl.ds(2, 2)])
+    add_products(rows, cols, picked, found, begin, tiles, hubs, own, u, hub_count, own_count)
     for load in loads:
-        load.start()
-    found = list_slots(rows, count, picked, begin, hub_count, False)
-    loads[0].wait()
-    u[:own_count] = own[...].astype(f32)
-    loads[1].wait()
-    loads[2].wait()
-    add_products(rows, cols, picked, found, begin, tiles, hubs, own, u, hub_count, own_count)
-    store = pltpu.make_async_copy(u.at[pl.ds(0, own_count)], base, sems.at[5])
-    store.start()
-    found = list_blocks(rows, begin, own_count, hub_count, marks, picked, False)
-    loads[3].wait()
-    loads[4].wait()
-    network_blocks(picked, found, u, first, second, result)
-    last = pltpu.make_async_copy(result, out, sems.at[6])
-    last.start()
-    store.wait()
-    last.wait()
+        load.wait()
+
+    def save(block):
+        return pltpu.make_async_copy(u.at[block], base.at[block], block_sems.at[block])
+
+    def finish(block):
+        return pltpu.make_async_copy(result.at[block], out.at[block], block_sems.at[block])
+
+    each_block(fed, n_fed, save, start)
+    network_blocks(free, n_free, lambda block: u[block], first, second, result, finish)
+    each_block(fed, n_fed, save, wait)
+    each_block(free, n_free, finish, wait)
 
 
 def before(layer, rows, cols, count, hubs, own, tiles, first, second):
@@ -432,9 +469,13 @@
             pltpu.VMEM(second.shape[1:], bf16),
             pltpu.VMEM((own_count + 1, block_size, width), f32),
             pltpu.VMEM(own.shape, bf16),
-            pltpu.SMEM((max(rows.shape[0], own_count),), jnp.int32),
+            pltpu.SMEM((rows.shape[0],), jnp.int32),
             pltpu.SMEM((own_count,), jnp.int32),
-            pltpu.SemaphoreType.DMA((7,)),
+            pltpu.SMEM((own_count,), jnp.int32),
+            pltpu.SMEM((own_count,), jnp.int32),
+            pltpu.SemaphoreType.DMA((cols.shape[0],)),
+            pltpu.SemaphoreType.DMA((own_count,)),
+            pltpu.SemaphoreType.DMA((4,)),
         ],
         (rows, cols, count, hubs, own, tiles, first, second),
     )
@@ -446,68 +487,78 @@
     out, refs = refs[0], refs[1:]
     if with_send:
         outgoing, refs = refs[0], refs[1:]
-    u, inc, adj, first, second, result, listed, marks, sems = refs
+    u, extra, inc, adj, first, second, result, marks, fed, free, block_sems, out_sems, sem = refs
     own_count = u.shape[0]
     remote = incoming.shape[0]
-    loads = [
-        pltpu.make_async_copy(incoming, inc, sems.at[0]),
-        pltpu.make_async_copy(tiles.at[pl.ds(0, remote)], adj, sems.at[1]),
-        pltpu.make_async_copy(base, u, sems.at[2]),
-        pltpu.make_async_copy(first_in.at[layer], first, sems.at[3]),
-        pltpu.make_async_copy(second_in.at[layer], second, sems.at[4]),
-        pltpu.make_async_copy(done, result, sems.at[5]),
-    ]
-    for load in loads[:3]:
-        load.start()
-    found = list_blocks(rows, remote, own_count, hub_count, marks, listed, True)
-    for load in loads[:3]:
+    parts = 4
+    size = remote // parts
+    loads = []
+    for part in range(parts):
+        cut = pl.ds(part * size, size)
+        loads.append(
+            (
+                pltpu.make_async_copy(tiles.at[cut], adj.at[cut], sem.at[2 + 2 * part]),
+                pltpu.make_async_copy(incoming.at[cut], inc.at[cut], sem.at[3 + 2 * part]),
+            )
+        )
+        for load in loads[-1]:
+            load.start()
+
+    def load_base(block):
+        return pltpu.make_async_copy(base.at[block], u.at[block], block_sems.at[block])
+
+    def load_done(block):
+        return pltpu.make_async_copy(done.at[block], result.at[block], block_sems.at[block])
+
+    def finish(block):
+        return pltpu.make_async_copy(result.at[block], out.at[block], out_sems.at[block])
+
+    extra[...] = jnp.zeros_like(extra)
+    n_fed, n_free = list_blocks(rows, remote, own_count, hub_count, marks, fed, free)
+    for part in range(parts):
+        for load in loads[part]:
+            load.wait()
+        if part == 0:
+            weights = load_weights(layer, first_in, second_in, first, second, sem.at[pl.ds(0, 2)])
+            each_block(fed, n_fed, load_base, start)
+            if with_send:
+                each_block(free, n_free, load_done, start)
+        products = [dot(adj[slot], inc[slot]) for slot in range(part * size, (part + 1) * size)]
+        for lane, product in enumerate(products):
+            extra[rows[part * size + lane] - hub_count] += product
+    each_block(fed, n_fed, load_base, wait)
+    for load in weights:
         load.wait()
-    for load in loads[3:]:
-        load.start()
-    group = 2 * GROUP
-
-    def slots_step(number, unused):
-        slots = [number * group + lane for lane in range(group)]
-        products = [dot(adj[slot], inc[slot]) for slot in slots]
-        for slot, product in zip(slots, products):
-            u[rows[slot] - hub_count] += product
-        return unused
-
-    lax.fori_loop(0, remote // group, slots_step, 0)
-    for load in loads[3:]:
-        load.wait()
-    network_blocks(listed, found, u, first, second, result)
+    network_blocks(
+        fed, n_fed, lambda block: u[block] + extra[block], first, second, result, finish
+    )
     copies = []
     if with_send:
+        each_block(free, n_free, load_done, wait)
         for number in range(remote):
-            copies.append(
-                pltpu.make_async_copy(
-                    result.at[chosen[0, number]], outgoing.at[number], sems.at[number]
-                )
+            copy = pltpu.make_async_copy(
+                result.at[chosen[0, number]], outgoing.at[number], sem.at[number]
             )
-    copies.append(pltpu.make_async_copy(result, out, sems.at[remote]))
-    for copy in copies:
-        copy.start()
+            copy.start()
+            copies.append(copy)
+    each_block(fed, n_fed, finish, wait)
     for copy in copies:
         copy.wait()
 
 
 def after(layer, rows, chosen, base, done, incoming, tiles, first, second, hub_count, with_send):
-    own_count, block_size, width = base.shape
+    own_count = base.shape[0]
     remote = incoming.shape[0]
     shapes = [shape_of(base.shape, bf16)]
     if with_send:
         shapes.append(shape_of(incoming.shape, bf16))
-    return call(
+    return pl.pallas_call(
         functools.partial(after_kernel, layer, with_send, hub_count),
-        "after",
-        58,
-        4 * base.size * first.shape[-1],
-        16 * MIB,
-        tuple(shapes),
-        [SMEM, SMEM] + [ANY] * 6,
-        (ANY,) * len(shapes),
-        [
+        out_shape=tuple(shapes),
+        in_specs=[SMEM, SMEM] + [ANY] * 6,
+        out_specs=(ANY,) * len(shapes),
+        scratch_shapes=[
+            pltpu.VMEM(base.shape, f32),
             pltpu.VMEM(base.shape, f32),
             pltpu.VMEM(incoming.shape, bf16),
             pltpu.VMEM((remote,) + tiles.shape[1:], bf16),
@@ -516,10 +567,18 @@
             pltpu.VMEM(base.shape, bf16),
             pltpu.SMEM((own_count,), jnp.int32),
             pltpu.SMEM((own_count,), jnp.int32),
-            pltpu.SemaphoreType.DMA((max(6, 1 + remote),)),
+            pltpu.SMEM((own_count,), jnp.int32),
+            pltpu.SemaphoreType.DMA((own_count,)),
+            pltpu.SemaphoreType.DMA((own_count,)),
+            pltpu.SemaphoreType.DMA((max(10, remote),)),
         ],
-        (rows, chosen, base, done, incoming, tiles, first, second),
-    )
+        input_output_aliases={3: 0},
+        compiler_params=pltpu.CompilerParams(vmem_limit_bytes=58 * MIB),
+        cost_estimate=pl.CostEstimate(
+            flops=4 * base.size * first.shape[-1], bytes_accessed=16 * MIB, transcendentals=0
+        ),
+        name="after",
+    )(rows, chosen, base, done, incoming, tiles, first, second)
 
 
 def exchange(x, bit):
@@ -548,6 +607,10 @@
 def gather_near(pieces, digits):
     for digit in digits[-2:0:-1]:
         pieces = gather_step(jnp.concatenate(pieces, axis=0), *digit)
+    return pieces
+
+
+def gather_last(pieces, digits):
     x = jnp.concatenate(pieces, axis=0)
     return x, exchange(x, digits[0][0])
 
@@ -591,7 +654,9 @@
     pieces = gather_far(hubs, digits)
     outgoing, *pieces = lax.optimization_barrier((outgoing, *pieces))
     incoming = all_to_all(outgoing)
-    halves = gather_near(pieces, digits)
+    pieces = gather_near(pieces, digits)
+    rows, cols, place_col, *pieces = lax.optimization_barrier((rows, cols, place_col, *pieces))
+    halves = gather_last(pieces, digits)
     hub_table, mine, kept, sent = hub_first(
         digits, rows, cols, tile_count, me, place_col, halves, own, tiles, local
     )
@@ -607,7 +672,7 @@
     pieces = gather_far(hub_new, digits)
     outgoing, *pieces = lax.optimization_barrier((outgoing, *pieces))
     incoming = all_to_all(outgoing)
-    halves = gather_near(pieces, digits)
+    halves = gather_last(gather_near(pieces, digits), digits)
     hub_table, mine, kept, sent = hub_second(
         digits, rows, cols, tile_count, me, place_row, halves, own, tiles, local
     )

time: 214 us -> 204 us (0.953)
  Pallas kernels: 84 us -> 73.3 us
  local copies, waits for them, and re-layouts: 10.7 us -> 5.61 us
  starting transfers between devices: 46.8 us -> 51.6 us
    pallas_call x13 -> x11, Pallas kernels: 84 us -> 46.6 us  [call(): pl.pallas_call(kernel, out_shape=out_shape, in_specs=in_specs, out_specs=...]
    pallas_call x0 -> x2, Pallas kernels: none -> 26.7 us  [after(): pl.pallas_call(functools.partial(after_kernel, layer, with_send, hub_coun...]
    unnamed x52 -> x43, local copies, waits for them, and re-layouts: 9.34 us -> 4.19 us
    ppermute x28, starting transfers between devices: 36.7 us -> 41.7 us  [exchange(): return lax.ppermute(x, 'dev', [(i, i ^ bit) for i in range(devices)])]
  transfers between devices with their start and end apart: 30 -> 30, of which waited for: 12 -> 14; matrix products, arithmetic and copies ran while one was open for 1% -> 1% of each run, Pallas kernels for 32% -> 30%
where the time goes in v1:
time: 204 us; the launch traced here: 201 us
  Pallas kernels  73.3 us (36%)
  waiting for transfers between devices  67.9 us (33%)
  starting transfers between devices  51.6 us (25%)
  local copies, waits for them, and re-layouts  5.61 us (3%)
    ppermute x28, waiting for transfers between devices, exchange(): return lax.ppermute(x, 'dev', [(i, i ^ bit) for i in range(devices)])  67.9 us
    pallas_call x11, Pallas kernels, call(): pl.pallas_call(kernel, out_shape=out_shape, in_specs=in_specs, out_specs=...  46.6 us
    ppermute x28, starting transfers between devices, exchange(): return lax.ppermute(x, 'dev', [(i, i ^ bit) for i in range(devices)])  41.7 us
    pallas_call x2, Pallas kernels, after(): pl.pallas_call(functools.partial(after_kernel, layer, with_send, hub_coun...  26.7 us
    all_to_all x2, starting transfers between devices, body(): incoming = all_to_all(outgoing)  9.97 us
    unnamed x43, local copies, waits for them, and re-layouts  4.19 us
  transfers between devices with their start and end apart: 30, of which 14 were waited for; matrix products, arithmetic and copies ran while one was open for 1% of the time, Pallas kernels for 30%

profile of v1, /device:TPU:0, one launch (start us, length us, event | category | flops | bytes accessed | tf_op | source)
XLA Modules:
  0.0 201.4 jit_solution(8620915367559300132)
XLA Ops:
  0.6 3.1 %collective-permute-start = (bf16[64,256]{1,0:T(8,128)(2,1)}, bf16[64,256]{1,0:T(8,128)(2,1)S(1)}, u32[]{:S(2)}, u32[]{:S(2)}) collective-permute-start(bf16[64,256]{1,0:T(8,128)(2,1)} %param.11), channel_id=1, source_target_pairs={{0,8},{1,9},{2,10},{3,11},{4,12},{5,13},{6,14},{7,15},{8,0},{9,1},... | collective-permute-start | bytes 98312 | tf_op jit(solution)/shard_map/ppermute | solution.py:586
  3.7 2.6 %collective-permute-start.1 = (bf16[64,256]{1,0:T(8,128)(2,1)}, bf16[64,256]{1,0:T(8,128)(2,1)S(1)}, u32[]{:S(2)}, u32[]{:S(2)}) collective-permute-start(bf16[64,256]{1,0:T(8,128)(2,1)} %param.11), channel_id=1, source_target_pairs={{0,16},{1,17},{2,18},{3,19},{4,20},{5,21},{6,22},{7,23},{8,24},{9,... | collective-permute-start | bytes 98312 | tf_op jit(solution)/shard_map/ppermute | solution.py:586
  6.3 3.8 %pack.1 = bf16[32,128,256]{2,1,0:T(8,128)(2,1)} custom-call(s32[1,32]{1,0:T(1,128)} %chosen.5, bf16[32,128,256]{2,1,0:T(8,128)(2,1)} %bitcast.5), custom_call_target="tpu_custom_call" | custom-call | bytes 4194304 | tf_op jit(solution)/shard_map/pack/pallas_call | solution.py:29
  12.2 4.2 %all-to-all-start = ((bf16[32,128,256]{2,1,0:T(8,128)(2,1)}), bf16[32,128,256]{2,1,0:T(8,128)(2,1)}, u32[]{:S(2)}, u32[]{:S(2)}) async-start(bf16[32,128,256]{2,1,0:T(8,128)(2,1)} %pack.1), calls=%async_computation | async-start | bytes 4194304 | tf_op jit(solution)/shard_map/all_to_all | solution.py:656
  21.1 14.5 %collective-permute-done.3 = bf16[256,256]{1,0:T(8,128)(2,1)S(1)} collective-permute-done((bf16[256,256]{1,0:T(8,128)(2,1)S(1)}, bf16[256,256]{1,0:T(8,128)(2,1)S(1)}, u32[]{:S(2)}, u32[]{:S(2)}) %collective-permute-start.3) | collective-permute-done | bytes 131104 | tf_op jit(solution)/shard_map/ppermute | solution.py:586
  35.7 9.0 %collective-permute-done.5 = bf16[256,256]{1,0:T(8,128)(2,1)S(1)} collective-permute-done((bf16[256,256]{1,0:T(8,128)(2,1)S(1)}, bf16[256,256]{1,0:T(8,128)(2,1)S(1)}, u32[]{:S(2)}, u32[]{:S(2)}) %collective-permute-start.5) | collective-permute-done | bytes 131104 | tf_op jit(solution)/shard_map/ppermute | solution.py:586
  47.7 8.6 %hub_first.1 = (bf16[16,128,256]{2,1,0:T(8,128)(2,1)}, bf16[64,256]{1,0:T(8,128)(2,1)}, f32[1024,256]{1,0:T(8,128)}, f32[1024,256]{1,0:T(8,128)}) custom-call(s32[144]{0:T(256)} %compare_select_fusion.rows, s32[112]{0:T(128)} %compare_select_fusion.1.cols, s32[1]{0:T(128)S(6)} %copy.32.count, s32[1]{0:T(128)} %bitcast.2.position, s32[2048,1]{1,0:T(8,128)} %copy.14.place_col, ...), custom_call_target="tpu_custom_call" | custom-call | flops 2147483648 | bytes 14680064 | tf_op jit(solution)/shard_map/hub_first/pallas_call | solution.py:29
  57.3 2.5 %collective-permute-done.7.refs_0_ = f32[1024,256]{1,0:T(8,128)S(1)} collective-permute-done((f32[1024,256]{1,0:T(8,128)}, f32[1024,256]{1,0:T(8,128)S(1)}, u32[]{:S(2)}, u32[]{:S(2)}) %collective-permute-start.7) | collective-permute-done | bytes 1048608 | tf_op jit(solution)/shard_map/ppermute | solution.py:586
  61.9 5.8 %collective-permute-start.8 = (bf16[256,256]{1,0:T(8,128)(2,1)S(1)}, bf16[256,256]{1,0:T(8,128)(2,1)S(1)}, u32[]{:S(2)}, u32[]{:S(2)}) collective-permute-start(bf16[256,256]{1,0:T(8,128)(2,1)S(1)} %get-tuple-element.75), channel_id=1, source_target_pairs={{0,2},{1,3},{2,0},{3,1},{4,6},{5,7},{6,4},{7,5},{8,10},{9,11},{10,... | collective-permute-start | bytes 393224 | tf_op jit(solution)/shard_map/ppermute | solution.py:586
  67.7 11.0 %before.2 = (f32[32,128,256]{2,1,0:T(8,128)}, bf16[32,128,256]{2,1,0:T(8,128)(2,1)}) custom-call(s32[144]{0:T(256)} %compare_select_fusion.rows, s32[112]{0:T(128)} %compare_select_fusion.1.cols, s32[1]{0:T(128)S(6)} %copy.32.count, bf16[16,128,256]{2,1,0:T(8,128)(2,1)} %get-tuple-element.70.hubs_in, bf16[32,128,256]{2,1,0:T(8,128)(2,1)} %bitcast.7, ...), custom_call_target="tpu_custom_call" | custom-call | flops 2863311616 | bytes 18874368 | tf_op jit(solution)/shard_map/before/pallas_call | solution.py:29
  78.9 4.2 %collective-permute-start.12 = (f32[64,256]{1,0:T(8,128)S(1)}, f32[64,256]{1,0:T(8,128)S(1)}, u32[]{:S(2)}, u32[]{:S(2)}) collective-permute-start(f32[64,256]{1,0:T(8,128)S(1)} %get-tuple-element.89), channel_id=1, source_target_pairs={{0,16},{1,17},{2,18},{3,19},{4,20},{5,21},{6,22},{7,23},{8,24},{9,... | collective-permute-start | bytes 196616 | tf_op jit(solution)/shard_map/ppermute | solution.py:586
  83.5 3.6 %collective-permute-done.12.refs_2_ = f32[64,256]{1,0:T(8,128)S(1)} collective-permute-done((f32[64,256]{1,0:T(8,128)S(1)}, f32[64,256]{1,0:T(8,128)S(1)}, u32[]{:S(2)}, u32[]{:S(2)}) %collective-permute-start.12) | collective-permute-done | bytes 65568 | tf_op jit(solution)/shard_map/ppermute | solution.py:586
  91.8 2.6 %collective-permute-start.16 = (bf16[64,256]{1,0:T(8,128)(2,1)S(1)}, bf16[64,256]{1,0:T(8,128)(2,1)S(1)}, u32[]{:S(2)}, u32[]{:S(2)}) collective-permute-start(bf16[64,256]{1,0:T(8,128)(2,1)S(1)} %hub_network.2), channel_id=1, source_target_pairs={{0,24},{1,25},{2,26},{3,27},{4,28},{5,29},{6,30},{7,31},{8,16},{9,... | collective-permute-start | bytes 98312 | tf_op jit(solution)/shard_map/ppermute | solution.py:586
  94.4 13.7 %after.2 = (bf16[32,128,256]{2,1,0:T(8,128)(2,1)}, bf16[32,128,256]{2,1,0:T(8,128)(2,1)}) custom-call(s32[144]{0:T(256)} %compare_select_fusion.rows, s32[1,32]{1,0:T(1,128)} %chosen.5, f32[32,128,256]{2,1,0:T(8,128)} %get-tuple-element.78.base, bf16[32,128,256]{2,1,0:T(8,128)(2,1)} %get-tuple-element.79.done, ...), custom_call_target="tpu_custom_call", output_to_operand_aliasing={{0}: (3, {})} | custom-call | flops 8589934592 | bytes 16777216 | tf_op jit(solution)/shard_map/after/pallas_call | solution.py:555
  108.2 5.8 %all-to-all-start.1 = ((bf16[32,128,256]{2,1,0:T(8,128)(2,1)}), bf16[32,128,256]{2,1,0:T(8,128)(2,1)}, u32[]{:S(2)}, u32[]{:S(2)}) async-start(bf16[32,128,256]{2,1,0:T(8,128)(2,1)} %get-tuple-element.106), calls=%async_computation.1 | async-start | bytes 4194304 | tf_op jit(solution)/shard_map/all_to_all | solution.py:674
  117.7 15.5 %collective-permute-done.17 = bf16[256,256]{1,0:T(8,128)(2,1)S(1)} collective-permute-done((bf16[256,256]{1,0:T(8,128)(2,1)S(1)}, bf16[256,256]{1,0:T(8,128)(2,1)S(1)}, u32[]{:S(2)}, u32[]{:S(2)}) %collective-permute-start.17) | collective-permute-done | bytes 131104 | tf_op jit(solution)/shard_map/ppermute | solution.py:586
  133.3 9.0 %collective-permute-done.19 = bf16[256,256]{1,0:T(8,128)(2,1)S(1)} collective-permute-done((bf16[256,256]{1,0:T(8,128)(2,1)S(1)}, bf16[256,256]{1,0:T(8,128)(2,1)S(1)}, u32[]{:S(2)}, u32[]{:S(2)}) %collective-permute-start.19) | collective-permute-done | bytes 131104 | tf_op jit(solution)/shard_map/ppermute | solution.py:586
  145.0 9.4 %hub_second.1 = (bf16[16,128,256]{2,1,0:T(8,128)(2,1)}, bf16[64,256]{1,0:T(8,128)(2,1)}, f32[1024,256]{1,0:T(8,128)}, bf16[1024,256]{1,0:T(8,128)(2,1)}) custom-call(s32[144]{0:T(256)} %compare_select_fusion.rows, s32[112]{0:T(128)} %compare_select_fusion.1.cols, s32[1]{0:T(128)S(6)} %copy.32.count, s32[1]{0:T(128)} %bitcast.2.position, s32[1,2048]{1,0:T(1,128)} %bitcast.8, ...), custom_call_target="tpu_custom_call" | custom-call | flops 2147483648 | bytes 14680064 | tf_op jit(solution)/shard_map/hub_second/pallas_call | solution.py:29
  158.2 4.6 %collective-permute-start.22 = (bf16[256,256]{1,0:T(8,128)(2,1)S(1)}, bf16[256,256]{1,0:T(8,128)(2,1)S(1)}, u32[]{:S(2)}, u32[]{:S(2)}) collective-permute-start(bf16[256,256]{1,0:T(8,128)(2,1)S(1)} %get-tuple-element.101), channel_id=1, source_target_pairs={{0,2},{1,3},{2,0},{3,1},{4,6},{5,7},{6,4},{7,5},{8,10},{9,11},{10,... | collective-permute-start | bytes 393224 | tf_op jit(solution)/shard_map/ppermute | solution.py:586
  165.5 10.9 %before.3 = (f32[32,128,256]{2,1,0:T(8,128)}, bf16[32,128,256]{2,1,0:T(8,128)(2,1)}) custom-call(s32[144]{0:T(256)} %compare_select_fusion.rows, s32[112]{0:T(128)} %compare_select_fusion.1.cols, s32[1]{0:T(128)S(6)} %copy.32.count, bf16[16,128,256]{2,1,0:T(8,128)(2,1)} %get-tuple-element.96.hubs_in, bf16[32,128,256]{2,1,0:T(8,128)(2,1)} %get-tuple-element.95.own_hbm.own_in, ...), custom_call_target="tpu_custom_call" | custom-call | flops 2863311616 | bytes 18874368 | tf_op jit(solution)/shard_map/before/pallas_call | solution.py:29
  176.7 4.2 %collective-permute-start.26 = (f32[64,256]{1,0:T(8,128)S(1)}, f32[64,256]{1,0:T(8,128)S(1)}, u32[]{:S(2)}, u32[]{:S(2)}) collective-permute-start(f32[64,256]{1,0:T(8,128)S(1)} %get-tuple-element.114), channel_id=1, source_target_pairs={{0,16},{1,17},{2,18},{3,19},{4,20},{5,21},{6,22},{7,23},{8,24},{9,... | collective-permute-start | bytes 196616 | tf_op jit(solution)/shard_map/ppermute | solution.py:586
  181.2 3.3 %collective-permute-done.26.refs_2_ = f32[64,256]{1,0:T(8,128)S(1)} collective-permute-done((f32[64,256]{1,0:T(8,128)S(1)}, f32[64,256]{1,0:T(8,128)S(1)}, u32[]{:S(2)}, u32[]{:S(2)}) %collective-permute-start.26) | collective-permute-done | bytes 65568 | tf_op jit(solution)/shard_map/ppermute | solution.py:586
  184.6 2.3 %collective-permute-done.27.refs_3_ = f32[64,256]{1,0:T(8,128)S(1)} collective-permute-done((f32[64,256]{1,0:T(8,128)S(1)}, f32[64,256]{1,0:T(8,128)S(1)}, u32[]{:S(2)}, u32[]{:S(2)}) %collective-permute-start.27) | collective-permute-done | bytes 65568 | tf_op jit(solution)/shard_map/ppermute | solution.py:586
  188.3 13.0 %after.3 = bf16[32,128,256]{2,1,0:T(8,128)(2,1)} custom-call(s32[144]{0:T(256)} %compare_select_fusion.rows, s32[1,32]{1,0:T(1,128)} %chosen.5, f32[32,128,256]{2,1,0:T(8,128)} %get-tuple-element.104.base, bf16[32,128,256]{2,1,0:T(8,128)(2,1)} %get-tuple-element.105.done, ...), custom_call_target="tpu_custom_call", output_to_operand_aliasing={{}: (3, {})} | custom-call | flops 8589934592 | bytes 16777216 | tf_op jit(solution)/shard_map/after/pallas_call | solution.py:555
  (99 shorter events, 32.3 us)
Async XLA Ops:
  0.6 9.6 %collective-permute-start = (bf16[64,256]{1,0:T(8,128)(2,1)}, bf16[64,256]{1,0:T(8,128)(2,1)S(1)}, u32[]{:S(2)}, u32[]{:S(2)}) collective-permute-start(bf16[64,256]{1,0:T(8,128)(2,1)} %param.11), channel_id=1, source_target_pairs={{0,8},{1,9},{2,10},{3,11},{4,12},{5,13},{6,14},{7,15},{8,0},{9,1},... | collective-permute-start | bytes 98312 | tf_op jit(solution)/shard_map/ppermute | solution.py:586
  3.7 6.5 %collective-permute-start.1 = (bf16[64,256]{1,0:T(8,128)(2,1)}, bf16[64,256]{1,0:T(8,128)(2,1)S(1)}, u32[]{:S(2)}, u32[]{:S(2)}) collective-permute-start(bf16[64,256]{1,0:T(8,128)(2,1)} %param.11), channel_id=1, source_target_pairs={{0,16},{1,17},{2,18},{3,19},{4,20},{5,21},{6,22},{7,23},{8,24},{9,... | collective-permute-start | bytes 98312 | tf_op jit(solution)/shard_map/ppermute | solution.py:586
  6.3 5.9 %collective-permute-start.2 = (bf16[64,256]{1,0:T(8,128)(2,1)}, bf16[64,256]{1,0:T(8,128)(2,1)S(1)}, u32[]{:S(2)}, u32[]{:S(2)}) collective-permute-start(bf16[64,256]{1,0:T(8,128)(2,1)} %param.11), channel_id=1, source_target_pairs={{0,24},{1,25},{2,26},{3,27},{4,28},{5,29},{6,30},{7,31},{8,16},{9,... | collective-permute-start | bytes 98312 | tf_op jit(solution)/shard_map/ppermute | solution.py:586
  12.2 82.2 %all-to-all-start = ((bf16[32,128,256]{2,1,0:T(8,128)(2,1)}), bf16[32,128,256]{2,1,0:T(8,128)(2,1)}, u32[]{:S(2)}, u32[]{:S(2)}) async-start(bf16[32,128,256]{2,1,0:T(8,128)(2,1)} %pack.1), calls=%async_computation | async-start | bytes 4194304 | tf_op jit(solution)/shard_map/all_to_all | solution.py:656
  17.0 18.7 %collective-permute-start.3 = (bf16[256,256]{1,0:T(8,128)(2,1)S(1)}, bf16[256,256]{1,0:T(8,128)(2,1)S(1)}, u32[]{:S(2)}, u32[]{:S(2)}) collective-permute-start(bf16[256,256]{1,0:T(8,128)(2,1)S(1)} %constant_dynamic-update-slice_fusion), channel_id=1, source_target_pairs={{0,2},{1,3},{2,0},{3,1},{4,6},{5,7},{6,4},{7,5},{8,10},{9,11},{10,... | collective-permute-start | bytes 393224 | tf_op jit(solution)/shard_map/ppermute | solution.py:586
  18.8 16.9 %collective-permute-start.4 = (bf16[256,256]{1,0:T(8,128)(2,1)S(1)}, bf16[256,256]{1,0:T(8,128)(2,1)S(1)}, u32[]{:S(2)}, u32[]{:S(2)}) collective-permute-start(bf16[256,256]{1,0:T(8,128)(2,1)S(1)} %constant_dynamic-update-slice_fusion), channel_id=1, source_target_pairs={{0,4},{1,5},{2,6},{3,7},{4,0},{5,1},{6,2},{7,3},{8,12},{9,13},{10,... | collective-permute-start | bytes 393224 | tf_op jit(solution)/shard_map/ppermute | solution.py:586
  20.2 24.4 %collective-permute-start.5 = (bf16[256,256]{1,0:T(8,128)(2,1)S(1)}, bf16[256,256]{1,0:T(8,128)(2,1)S(1)}, u32[]{:S(2)}, u32[]{:S(2)}) collective-permute-start(bf16[256,256]{1,0:T(8,128)(2,1)S(1)} %constant_dynamic-update-slice_fusion), channel_id=1, source_target_pairs={{0,6},{1,7},{2,4},{3,5},{4,2},{5,3},{6,0},{7,1},{8,14},{9,15},{10,... | collective-permute-start | bytes 393224 | tf_op jit(solution)/shard_map/ppermute | solution.py:586
  61.2 17.5 %collective-permute-start.10 = (bf16[256,256]{1,0:T(8,128)(2,1)S(1)}, bf16[256,256]{1,0:T(8,128)(2,1)S(1)}, u32[]{:S(2)}, u32[]{:S(2)}) collective-permute-start(bf16[256,256]{1,0:T(8,128)(2,1)S(1)} %get-tuple-element.77), channel_id=1, source_target_pairs={{0,6},{1,7},{2,4},{3,5},{4,2},{5,3},{6,0},{7,1},{8,14},{9,15},{10,... | collective-permute-start | bytes 393224 | tf_op jit(solution)/shard_map/ppermute | solution.py:586
  61.9 16.8 %collective-permute-start.8 = (bf16[256,256]{1,0:T(8,128)(2,1)S(1)}, bf16[256,256]{1,0:T(8,128)(2,1)S(1)}, u32[]{:S(2)}, u32[]{:S(2)}) collective-permute-start(bf16[256,256]{1,0:T(8,128)(2,1)S(1)} %get-tuple-element.75), channel_id=1, source_target_pairs={{0,2},{1,3},{2,0},{3,1},{4,6},{5,7},{6,4},{7,5},{8,10},{9,11},{10,... | collective-permute-start | bytes 393224 | tf_op jit(solution)/shard_map/ppermute | solution.py:586
  67.7 11.0 %collective-permute-start.9 = (bf16[256,256]{1,0:T(8,128)(2,1)S(1)}, bf16[256,256]{1,0:T(8,128)(2,1)S(1)}, u32[]{:S(2)}, u32[]{:S(2)}) collective-permute-start(bf16[256,256]{1,0:T(8,128)(2,1)S(1)} %get-tuple-element.76), channel_id=1, source_target_pairs={{0,4},{1,5},{2,6},{3,7},{4,0},{5,1},{6,2},{7,3},{8,12},{9,13},{10,... | collective-permute-start | bytes 393224 | tf_op jit(solution)/shard_map/ppermute | solution.py:586
  78.9 8.1 %collective-permute-start.12 = (f32[64,256]{1,0:T(8,128)S(1)}, f32[64,256]{1,0:T(8,128)S(1)}, u32[]{:S(2)}, u32[]{:S(2)}) collective-permute-start(f32[64,256]{1,0:T(8,128)S(1)} %get-tuple-element.89), channel_id=1, source_target_pairs={{0,16},{1,17},{2,18},{3,19},{4,20},{5,21},{6,22},{7,23},{8,24},{9,... | collective-permute-start | bytes 196616 | tf_op jit(solution)/shard_map/ppermute | solution.py:586
  83.1 6.1 %collective-permute-start.13 = (f32[64,256]{1,0:T(8,128)S(1)}, f32[64,256]{1,0:T(8,128)S(1)}, u32[]{:S(2)}, u32[]{:S(2)}) collective-permute-start(f32[64,256]{1,0:T(8,128)S(1)} %get-tuple-element.90), channel_id=1, source_target_pairs={{0,24},{1,25},{2,26},{3,27},{4,28},{5,29},{6,30},{7,31},{8,16},{9,... | collective-permute-start | bytes 196616 | tf_op jit(solution)/shard_map/ppermute | solution.py:586
  89.9 18.2 %collective-permute-start.14 = (bf16[64,256]{1,0:T(8,128)(2,1)S(1)}, bf16[64,256]{1,0:T(8,128)(2,1)S(1)}, u32[]{:S(2)}, u32[]{:S(2)}) collective-permute-start(bf16[64,256]{1,0:T(8,128)(2,1)S(1)} %hub_network.2), channel_id=1, source_target_pairs={{0,8},{1,9},{2,10},{3,11},{4,12},{5,13},{6,14},{7,15},{8,0},{9,1},... | collective-permute-start | bytes 98312 | tf_op jit(solution)/shard_map/ppermute | solution.py:586
  90.0 18.1 %collective-permute-start.15 = (bf16[64,256]{1,0:T(8,128)(2,1)S(1)}, bf16[64,256]{1,0:T(8,128)(2,1)S(1)}, u32[]{:S(2)}, u32[]{:S(2)}) collective-permute-start(bf16[64,256]{1,0:T(8,128)(2,1)S(1)} %hub_network.2), channel_id=1, source_target_pairs={{0,16},{1,17},{2,18},{3,19},{4,20},{5,21},{6,22},{7,23},{8,24},{9,... | collective-permute-start | bytes 98312 | tf_op jit(solution)/shard_map/ppermute | solution.py:586
  91.8 16.4 %collective-permute-start.16 = (bf16[64,256]{1,0:T(8,128)(2,1)S(1)}, bf16[64,256]{1,0:T(8,128)(2,1)S(1)}, u32[]{:S(2)}, u32[]{:S(2)}) collective-permute-start(bf16[64,256]{1,0:T(8,128)(2,1)S(1)} %hub_network.2), channel_id=1, source_target_pairs={{0,24},{1,25},{2,26},{3,27},{4,28},{5,29},{6,30},{7,31},{8,16},{9,... | collective-permute-start | bytes 98312 | tf_op jit(solution)/shard_map/ppermute | solution.py:586
  108.2 80.1 %all-to-all-start.1 = ((bf16[32,128,256]{2,1,0:T(8,128)(2,1)}), bf16[32,128,256]{2,1,0:T(8,128)(2,1)}, u32[]{:S(2)}, u32[]{:S(2)}) async-start(bf16[32,128,256]{2,1,0:T(8,128)(2,1)} %get-tuple-element.106), calls=%async_computation.1 | async-start | bytes 4194304 | tf_op jit(solution)/shard_map/all_to_all | solution.py:674
  114.0 19.2 %collective-permute-start.17 = (bf16[256,256]{1,0:T(8,128)(2,1)S(1)}, bf16[256,256]{1,0:T(8,128)(2,1)S(1)}, u32[]{:S(2)}, u32[]{:S(2)}) collective-permute-start(bf16[256,256]{1,0:T(8,128)(2,1)S(1)} %get-tuple-element.116), channel_id=1, source_target_pairs={{0,2},{1,3},{2,0},{3,1},{4,6},{5,7},{6,4},{7,5},{8,10},{9,11},{10,... | collective-permute-start | bytes 393224 | tf_op jit(solution)/shard_map/ppermute | solution.py:586
  115.8 17.5 %collective-permute-start.18 = (bf16[256,256]{1,0:T(8,128)(2,1)S(1)}, bf16[256,256]{1,0:T(8,128)(2,1)S(1)}, u32[]{:S(2)}, u32[]{:S(2)}) collective-permute-start(bf16[256,256]{1,0:T(8,128)(2,1)S(1)} %get-tuple-element.116), channel_id=1, source_target_pairs={{0,4},{1,5},{2,6},{3,7},{4,0},{5,1},{6,2},{7,3},{8,12},{9,13},{10,... | collective-permute-start | bytes 393224 | tf_op jit(solution)/shard_map/ppermute | solution.py:586
  117.2 25.0 %collective-permute-start.19 = (bf16[256,256]{1,0:T(8,128)(2,1)S(1)}, bf16[256,256]{1,0:T(8,128)(2,1)S(1)}, u32[]{:S(2)}, u32[]{:S(2)}) collective-permute-start(bf16[256,256]{1,0:T(8,128)(2,1)S(1)} %get-tuple-element.116), channel_id=1, source_target_pairs={{0,6},{1,7},{2,4},{3,5},{4,2},{5,3},{6,0},{7,1},{8,14},{9,15},{10,... | collective-permute-start | bytes 393224 | tf_op jit(solution)/shard_map/ppermute | solution.py:586
  158.2 18.2 %collective-permute-start.22 = (bf16[256,256]{1,0:T(8,128)(2,1)S(1)}, bf16[256,256]{1,0:T(8,128)(2,1)S(1)}, u32[]{:S(2)}, u32[]{:S(2)}) collective-permute-start(bf16[256,256]{1,0:T(8,128)(2,1)S(1)} %get-tuple-element.101), channel_id=1, source_target_pairs={{0,2},{1,3},{2,0},{3,1},{4,6},{5,7},{6,4},{7,5},{8,10},{9,11},{10,... | collective-permute-start | bytes 393224 | tf_op jit(solution)/shard_map/ppermute | solution.py:586
  162.9 13.6 %collective-permute-start.23 = (bf16[256,256]{1,0:T(8,128)(2,1)S(1)}, bf16[256,256]{1,0:T(8,128)(2,1)S(1)}, u32[]{:S(2)}, u32[]{:S(2)}) collective-permute-start(bf16[256,256]{1,0:T(8,128)(2,1)S(1)} %get-tuple-element.102), channel_id=1, source_target_pairs={{0,4},{1,5},{2,6},{3,7},{4,0},{5,1},{6,2},{7,3},{8,12},{9,13},{10,... | collective-permute-start | bytes 393224 | tf_op jit(solution)/shard_map/ppermute | solution.py:586
  164.1 12.4 %collective-permute-start.24 = (bf16[256,256]{1,0:T(8,128)(2,1)S(1)}, bf16[256,256]{1,0:T(8,128)(2,1)S(1)}, u32[]{:S(2)}, u32[]{:S(2)}) collective-permute-start(bf16[256,256]{1,0:T(8,128)(2,1)S(1)} %get-tuple-element.103), channel_id=1, source_target_pairs={{0,6},{1,7},{2,4},{3,5},{4,2},{5,3},{6,0},{7,1},{8,14},{9,15},{10,... | collective-permute-start | bytes 393224 | tf_op jit(solution)/shard_map/ppermute | solution.py:586
  176.7 7.9 %collective-permute-start.26 = (f32[64,256]{1,0:T(8,128)S(1)}, f32[64,256]{1,0:T(8,128)S(1)}, u32[]{:S(2)}, u32[]{:S(2)}) collective-permute-start(f32[64,256]{1,0:T(8,128)S(1)} %get-tuple-element.114), channel_id=1, source_target_pairs={{0,16},{1,17},{2,18},{3,19},{4,20},{5,21},{6,22},{7,23},{8,24},{9,... | collective-permute-start | bytes 196616 | tf_op jit(solution)/shard_map/ppermute | solution.py:586
  180.8 6.1 %collective-permute-start.27 = (f32[64,256]{1,0:T(8,128)S(1)}, f32[64,256]{1,0:T(8,128)S(1)}, u32[]{:S(2)}, u32[]{:S(2)}) collective-permute-start(f32[64,256]{1,0:T(8,128)S(1)} %get-tuple-element.115), channel_id=1, source_target_pairs={{0,24},{1,25},{2,26},{3,27},{4,28},{5,29},{6,30},{7,31},{8,16},{9,... | collective-permute-start | bytes 196616 | tf_op jit(solution)/shard_map/ppermute | solution.py:586
  (22 other events, 214.7 us)

commit v2 on v1

--- a/solution.py
+++ b/solution.py
@@ -253,7 +253,7 @@
     return call(
         functools.partial(hub_first_kernel, digits),
         "hub_first",
-        54,
+        48,
         2 * hub_rows * hub_rows * width,
         14 * MIB,
         (
@@ -320,7 +320,7 @@
     return call(
         functools.partial(hub_second_kernel, digits),
         "hub_second",
-        54,
+        48,
         2 * hub_rows * hub_rows * width,
         14 * MIB,
         (
@@ -651,11 +651,11 @@
     )
 
     outgoing = pack(send_list, own)
-    pieces = gather_far(hubs, digits)
-    outgoing, *pieces = lax.optimization_barrier((outgoing, *pieces))
+    pieces = gather_near(gather_far(hubs, digits), digits)
+    outgoing, rows, cols, place_col, *pieces = lax.optimization_barrier(
+        (outgoing, rows, cols, place_col, *pieces)
+    )
     incoming = all_to_all(outgoing)
-    pieces = gather_near(pieces, digits)
-    rows, cols, place_col, *pieces = lax.optimization_barrier((rows, cols, place_col, *pieces))
     halves = gather_last(pieces, digits)
     hub_table, mine, kept, sent = hub_first(
         digits, rows, cols, tile_count, me, place_col, halves, own, tiles, local
@@ -665,14 +665,16 @@
     base, done, *received = lax.optimization_barrier((base, done, *received))
     parts = scatter_far(me, kept, received, digits, local)
     hub_new = hub_network(0, mine, parts, w_in, w_out)
+    pieces = gather_far(hub_new, digits)
+    base, *pieces = lax.optimization_barrier((base, *pieces))
     own, outgoing = after(
         0, rows, send_list, base, done, incoming, tiles, w_in, w_out, hub_count, True
     )
 
-    pieces = gather_far(hub_new, digits)
+    pieces = gather_near(pieces, digits)
     outgoing, *pieces = lax.optimization_barrier((outgoing, *pieces))
     incoming = all_to_all(outgoing)
-    halves = gather_last(gather_near(pieces, digits), digits)
+    halves = gather_last(pieces, digits)
     hub_table, mine, kept, sent = hub_second(
         digits, rows, cols, tile_count, me, place_row, halves, own, tiles, local
     )

time: 204 us -> 179 us (0.88); the launches traced: 201 us -> 179 us
  waiting for transfers between devices: 67.9 us -> 52 us
  local copies, waits for them, and re-layouts: 5.61 us -> 1.29 us
    ppermute x28, waiting for transfers between devices: 67.9 us -> 52 us  [exchange(): return lax.ppermute(x, 'dev', [(i, i ^ bit) for i in range(devices)])]
    pallas_call x11, Pallas kernels: 46.6 us -> 42.1 us  [call(): pl.pallas_call(kernel, out_shape=out_shape, in_specs=in_specs, out_specs=...]
    unnamed x43 -> x38, local copies, waits for them, and re-layouts: 4.19 us -> 0.9 us
    pallas_call x2, Pallas kernels: 26.7 us -> 29.5 us  [after(): pl.pallas_call(functools.partial(after_kernel, layer, with_send, hub_coun...]
  transfers between devices with their start and end apart: 30 -> 30, of which waited for: 14 -> 17; matrix products, arithmetic and copies ran while one was open for 1% -> 1% of each run, Pallas kernels for 30% -> 32%
where the time goes in v2:
time: 179 us
  Pallas kernels  71.7 us (40%)
  waiting for transfers between devices  52 us (29%)
  starting transfers between devices  51.1 us (29%)
  between operations  1.81 us (1%)
    ppermute x28, waiting for transfers between devices, exchange(): return lax.ppermute(x, 'dev', [(i, i ^ bit) for i in range(devices)])  52 us
    ppermute x28, starting transfers between devices, exchange(): return lax.ppermute(x, 'dev', [(i, i ^ bit) for i in range(devices)])  42.3 us
    pallas_call x11, Pallas kernels, call(): pl.pallas_call(kernel, out_shape=out_shape, in_specs=in_specs, out_specs=...  42.1 us
    pallas_call x2, Pallas kernels, after(): pl.pallas_call(functools.partial(after_kernel, layer, with_send, hub_coun...  29.5 us
    all_to_all x2, starting transfers between devices, body(): incoming = all_to_all(outgoing)  8.82 us
  transfers between devices with their start and end apart: 30, of which 17 were waited for; matrix products, arithmetic and copies ran while one was open for 1% of the time, Pallas kernels for 32%

profile of v2, /device:TPU:0, one launch (start us, length us, event | category | flops | bytes accessed | tf_op | source)
XLA Modules:
  0.0 178.6 jit_solution(9237861332762475651)
XLA Ops:
  0.6 4.1 %collective-permute-start.1 = (bf16[64,256]{1,0:T(8,128)(2,1)}, bf16[64,256]{1,0:T(8,128)(2,1)S(1)}, u32[]{:S(2)}, u32[]{:S(2)}) collective-permute-start(bf16[64,256]{1,0:T(8,128)(2,1)} %param.11), channel_id=1, source_target_pairs={{0,16},{1,17},{2,18},{3,19},{4,20},{5,21},{6,22},{7,23},{8,24},{9,... | collective-permute-start | bytes 98312 | tf_op jit(solution)/shard_map/ppermute | solution.py:586
  7.8 4.0 %pack.1 = bf16[32,128,256]{2,1,0:T(8,128)(2,1)} custom-call(s32[1,32]{1,0:T(1,128)} %chosen.5, bf16[32,128,256]{2,1,0:T(8,128)(2,1)} %bitcast.7), custom_call_target="tpu_custom_call" | custom-call | bytes 4194304 | tf_op jit(solution)/shard_map/pack/pallas_call | solution.py:29
  12.2 2.4 %collective-permute-start.5 = (bf16[256,256]{1,0:T(8,128)(2,1)S(1)}, bf16[256,256]{1,0:T(8,128)(2,1)S(1)}, u32[]{:S(2)}, u32[]{:S(2)}) collective-permute-start(bf16[256,256]{1,0:T(8,128)(2,1)S(1)} %constant_dynamic-update-slice_fusion), channel_id=1, source_target_pairs={{0,6},{1,7},{2,4},{3,5},{4,2},{5,3},{6,0},{7,1},{8,14},{9,15},{10,... | collective-permute-start | bytes 393224 | tf_op jit(solution)/shard_map/ppermute | solution.py:586
  15.7 3.5 %collective-permute-done.5 = bf16[256,256]{1,0:T(8,128)(2,1)S(1)} collective-permute-done((bf16[256,256]{1,0:T(8,128)(2,1)S(1)}, bf16[256,256]{1,0:T(8,128)(2,1)S(1)}, u32[]{:S(2)}, u32[]{:S(2)}) %collective-permute-start.5) | collective-permute-done | bytes 131104 | tf_op jit(solution)/shard_map/ppermute | solution.py:586
  20.3 5.1 %all-to-all-start = ((bf16[32,128,256]{2,1,0:T(8,128)(2,1)}), bf16[32,128,256]{2,1,0:T(8,128)(2,1)}, u32[]{:S(2)}, u32[]{:S(2)}) async-start(bf16[32,128,256]{2,1,0:T(8,128)(2,1)} %pack.1), calls=%async_computation | async-start | bytes 4194304 | tf_op jit(solution)/shard_map/all_to_all | solution.py:658
  27.5 6.4 %hub_first.1 = (bf16[16,128,256]{2,1,0:T(8,128)(2,1)S(1)}, bf16[64,256]{1,0:T(8,128)(2,1)S(1)}, f32[1024,256]{1,0:T(8,128)S(1)}, f32[1024,256]{1,0:T(8,128)S(1)}) custom-call(s32[144]{0:T(256)S(1)} %compare_select_fusion.rows, s32[112]{0:T(128)S(1)} %compare_select_fusion.1.cols, s32[1]{0:T(128)S(6)} %copy.29.count, s32[1]{0:T(128)} %bitcast.2.position, ...), custom_call_target="tpu_custom_call" | custom-call | flops 2147483648 | bytes 14680064 | tf_op jit(solution)/shard_map/hub_first/pallas_call | solution.py:29
  34.9 2.3 %collective-permute-done.7.refs_0_ = f32[1024,256]{1,0:T(8,128)S(1)} collective-permute-done((f32[1024,256]{1,0:T(8,128)S(1)}, f32[1024,256]{1,0:T(8,128)S(1)}, u32[]{:S(2)}, u32[]{:S(2)}) %collective-permute-start.7) | collective-permute-done | bytes 1048608 | tf_op jit(solution)/shard_map/ppermute | solution.py:586
  39.1 3.9 %collective-permute-start.9 = (bf16[256,256]{1,0:T(8,128)(2,1)S(1)}, bf16[256,256]{1,0:T(8,128)(2,1)S(1)}, u32[]{:S(2)}, u32[]{:S(2)}) collective-permute-start(bf16[256,256]{1,0:T(8,128)(2,1)S(1)} %get-tuple-element.73), channel_id=1, source_target_pairs={{0,4},{1,5},{2,6},{3,7},{4,0},{5,1},{6,2},{7,3},{8,12},{9,13},{10,... | collective-permute-start | bytes 393224 | tf_op jit(solution)/shard_map/ppermute | solution.py:586
  44.3 11.0 %before.2 = (f32[32,128,256]{2,1,0:T(8,128)}, bf16[32,128,256]{2,1,0:T(8,128)(2,1)}) custom-call(s32[144]{0:T(256)} %copy-done.7, s32[112]{0:T(128)} %copy-done.10, s32[1]{0:T(128)S(6)} %copy.29.count, bf16[16,128,256]{2,1,0:T(8,128)(2,1)} %copy-done.6, bf16[32,128,256]{2,1,0:T(8,128)(2,1)} %bitcast.9, bf16[144,128,128]{2,1,0:T(8,128)(2,1)} %tiles.3, ...), custom_call_target="tpu_custom_call" | custom-call | flops 2863311616 | bytes 18874368 | tf_op jit(solution)/shard_map/before/pallas_call | solution.py:29
  55.3 1.6 collective-permute-done.10.refs_2_
  57.0 2.0 %collective-permute-start.11 = (f32[64,256]{1,0:T(8,128)S(1)}, f32[64,256]{1,0:T(8,128)S(1)}, u32[]{:S(2)}, u32[]{:S(2)}) collective-permute-start(f32[64,256]{1,0:T(8,128)S(1)} %get-tuple-element.82), channel_id=1, source_target_pairs={{0,8},{1,9},{2,10},{3,11},{4,12},{5,13},{6,14},{7,15},{8,0},{9,1},... | collective-permute-start | bytes 196616 | tf_op jit(solution)/shard_map/ppermute | solution.py:586
  62.6 16.3 %collective-permute-done.12.refs_2_ = f32[64,256]{1,0:T(8,128)S(1)} collective-permute-done((f32[64,256]{1,0:T(8,128)S(1)}, f32[64,256]{1,0:T(8,128)S(1)}, u32[]{:S(2)}, u32[]{:S(2)}) %collective-permute-start.12) | collective-permute-done | bytes 65568 | tf_op jit(solution)/shard_map/ppermute | solution.py:586
  81.1 1.6 collective-permute-start.15
  86.7 2.3 %collective-permute-start.19 = (bf16[256,256]{1,0:T(8,128)(2,1)S(1)}, bf16[256,256]{1,0:T(8,128)(2,1)S(1)}, u32[]{:S(2)}, u32[]{:S(2)}) collective-permute-start(bf16[256,256]{1,0:T(8,128)(2,1)S(1)} %constant_dynamic-update-slice_fusion.8), channel_id=1, source_target_pairs={{0,6},{1,7},{2,4},{3,5},{4,2},{5,3},{6,0},{7,1},{8,14},{9,15},{10,... | collective-permute-start | bytes 393224 | tf_op jit(solution)/shard_map/ppermute | solution.py:586
  90.2 15.2 %after.2 = (bf16[32,128,256]{2,1,0:T(8,128)(2,1)}, bf16[32,128,256]{2,1,0:T(8,128)(2,1)}) custom-call(s32[144]{0:T(256)} %copy-done.7, s32[1,32]{1,0:T(1,128)} %chosen.5, f32[32,128,256]{2,1,0:T(8,128)} %get-tuple-element.85.base, bf16[32,128,256]{2,1,0:T(8,128)(2,1)} %get-tuple-element.86.done, ...), custom_call_target="tpu_custom_call", output_to_operand_aliasing={{0}: (3, {})} | custom-call | flops 8589934592 | bytes 16777216 | tf_op jit(solution)/shard_map/after/pallas_call | solution.py:555
  105.5 3.7 %all-to-all-start.1 = ((bf16[32,128,256]{2,1,0:T(8,128)(2,1)}), bf16[32,128,256]{2,1,0:T(8,128)(2,1)}, u32[]{:S(2)}, u32[]{:S(2)}) async-start(bf16[32,128,256]{2,1,0:T(8,128)(2,1)} %get-tuple-element.108), calls=%async_computation.1 | async-start | bytes 4194304 | tf_op jit(solution)/shard_map/all_to_all | solution.py:676
  109.5 1.7 collective-permute-done.20.half1
  111.2 7.0 %hub_second.1 = (bf16[16,128,256]{2,1,0:T(8,128)(2,1)S(1)}, bf16[64,256]{1,0:T(8,128)(2,1)S(1)}, f32[1024,256]{1,0:T(8,128)S(1)}, bf16[1024,256]{1,0:T(8,128)(2,1)S(1)}) custom-call(s32[144]{0:T(256)S(1)} %copy-done.8, s32[112]{0:T(128)S(1)} %copy-done.11, s32[1]{0:T(128)S(6)} %copy.29.count, s32[1]{0:T(128)} %bitcast.2.position, s32[1,2048]{1,0:T(1,128)S(1)} %bitcast.6, ...), custom_call_target="tpu_custom_call" | custom-call | flops 2147483648 | bytes 14680064 | tf_op jit(solution)/shard_map/hub_second/pallas_call | solution.py:29
  122.6 4.0 %collective-permute-start.23 = (bf16[256,256]{1,0:T(8,128)(2,1)S(1)}, bf16[256,256]{1,0:T(8,128)(2,1)S(1)}, u32[]{:S(2)}, u32[]{:S(2)}) collective-permute-start(bf16[256,256]{1,0:T(8,128)(2,1)S(1)} %get-tuple-element.104), channel_id=1, source_target_pairs={{0,4},{1,5},{2,6},{3,7},{4,0},{5,1},{6,2},{7,3},{8,12},{9,13},{10,... | collective-permute-start | bytes 393224 | tf_op jit(solution)/shard_map/ppermute | solution.py:586
  127.9 11.0 %before.3 = (f32[32,128,256]{2,1,0:T(8,128)}, bf16[32,128,256]{2,1,0:T(8,128)(2,1)}) custom-call(s32[144]{0:T(256)} %copy-done.7, s32[112]{0:T(128)} %copy-done.10, s32[1]{0:T(128)S(6)} %copy.29.count, bf16[16,128,256]{2,1,0:T(8,128)(2,1)} %copy-done.5, bf16[32,128,256]{2,1,0:T(8,128)(2,1)} %get-tuple-element.97.own_hbm.own_in, ...), custom_call_target="tpu_custom_call" | custom-call | flops 2863311616 | bytes 18874368 | tf_op jit(solution)/shard_map/before/pallas_call | solution.py:29
  138.9 1.7 collective-permute-done.24.refs_2_
  140.7 1.9 %collective-permute-start.25 = (f32[64,256]{1,0:T(8,128)S(1)}, f32[64,256]{1,0:T(8,128)S(1)}, u32[]{:S(2)}, u32[]{:S(2)}) collective-permute-start(f32[64,256]{1,0:T(8,128)S(1)} %get-tuple-element.115), channel_id=1, source_target_pairs={{0,8},{1,9},{2,10},{3,11},{4,12},{5,13},{6,14},{7,15},{8,0},{9,1},... | collective-permute-start | bytes 196616 | tf_op jit(solution)/shard_map/ppermute | solution.py:586
  146.3 16.3 %collective-permute-done.26.refs_2_ = f32[64,256]{1,0:T(8,128)S(1)} collective-permute-done((f32[64,256]{1,0:T(8,128)S(1)}, f32[64,256]{1,0:T(8,128)S(1)}, u32[]{:S(2)}, u32[]{:S(2)}) %collective-permute-start.26) | collective-permute-done | bytes 65568 | tf_op jit(solution)/shard_map/ppermute | solution.py:586
  164.1 14.4 %after.3 = bf16[32,128,256]{2,1,0:T(8,128)(2,1)} custom-call(s32[144]{0:T(256)} %copy-done.7, s32[1,32]{1,0:T(1,128)} %chosen.5, f32[32,128,256]{2,1,0:T(8,128)} %get-tuple-element.106.base, bf16[32,128,256]{2,1,0:T(8,128)(2,1)} %get-tuple-element.107.done, bf16[32,128,256]{2,1,0:T(8,128)(2,1)} %all-to-all-done.1.incoming, ...), custom_call_target="tpu_custom_call", output_to_operand_aliasing={{}: (3, {})} | custom-call | flops 8589934592 | bytes 16777216 | tf_op jit(solution)/shard_map/after/pallas_call | solution.py:555
  (94 shorter events, 33.4 us)
Async XLA Ops:
  0.6 11.1 %collective-permute-start.1 = (bf16[64,256]{1,0:T(8,128)(2,1)}, bf16[64,256]{1,0:T(8,128)(2,1)S(1)}, u32[]{:S(2)}, u32[]{:S(2)}) collective-permute-start(bf16[64,256]{1,0:T(8,128)(2,1)} %param.11), channel_id=1, source_target_pairs={{0,16},{1,17},{2,18},{3,19},{4,20},{5,21},{6,22},{7,23},{8,24},{9,... | collective-permute-start | bytes 98312 | tf_op jit(solution)/shard_map/ppermute | solution.py:586
  4.7 7.0 %collective-permute-start = (bf16[64,256]{1,0:T(8,128)(2,1)}, bf16[64,256]{1,0:T(8,128)(2,1)S(1)}, u32[]{:S(2)}, u32[]{:S(2)}) collective-permute-start(bf16[64,256]{1,0:T(8,128)(2,1)} %param.11), channel_id=1, source_target_pairs={{0,8},{1,9},{2,10},{3,11},{4,12},{5,13},{6,14},{7,15},{8,0},{9,1},... | collective-permute-start | bytes 98312 | tf_op jit(solution)/shard_map/ppermute | solution.py:586
  6.3 5.9 %collective-permute-start.2 = (bf16[64,256]{1,0:T(8,128)(2,1)}, bf16[64,256]{1,0:T(8,128)(2,1)S(1)}, u32[]{:S(2)}, u32[]{:S(2)}) collective-permute-start(bf16[64,256]{1,0:T(8,128)(2,1)} %param.11), channel_id=1, source_target_pairs={{0,24},{1,25},{2,26},{3,27},{4,28},{5,29},{6,30},{7,31},{8,16},{9,... | collective-permute-start | bytes 98312 | tf_op jit(solution)/shard_map/ppermute | solution.py:586
  12.2 7.0 %collective-permute-start.5 = (bf16[256,256]{1,0:T(8,128)(2,1)S(1)}, bf16[256,256]{1,0:T(8,128)(2,1)S(1)}, u32[]{:S(2)}, u32[]{:S(2)}) collective-permute-start(bf16[256,256]{1,0:T(8,128)(2,1)S(1)} %constant_dynamic-update-slice_fusion), channel_id=1, source_target_pairs={{0,6},{1,7},{2,4},{3,5},{4,2},{5,3},{6,0},{7,1},{8,14},{9,15},{10,... | collective-permute-start | bytes 393224 | tf_op jit(solution)/shard_map/ppermute | solution.py:586
  14.7 5.6 %collective-permute-start.4 = (bf16[256,256]{1,0:T(8,128)(2,1)S(1)}, bf16[256,256]{1,0:T(8,128)(2,1)S(1)}, u32[]{:S(2)}, u32[]{:S(2)}) collective-permute-start(bf16[256,256]{1,0:T(8,128)(2,1)S(1)} %constant_dynamic-update-slice_fusion), channel_id=1, source_target_pairs={{0,4},{1,5},{2,6},{3,7},{4,0},{5,1},{6,2},{7,3},{8,12},{9,13},{10,... | collective-permute-start | bytes 393224 | tf_op jit(solution)/shard_map/ppermute | solution.py:586
  15.2 5.1 %collective-permute-start.3 = (bf16[256,256]{1,0:T(8,128)(2,1)S(1)}, bf16[256,256]{1,0:T(8,128)(2,1)S(1)}, u32[]{:S(2)}, u32[]{:S(2)}) collective-permute-start(bf16[256,256]{1,0:T(8,128)(2,1)S(1)} %constant_dynamic-update-slice_fusion), channel_id=1, source_target_pairs={{0,2},{1,3},{2,0},{3,1},{4,6},{5,7},{6,4},{7,5},{8,10},{9,11},{10,... | collective-permute-start | bytes 393224 | tf_op jit(solution)/shard_map/ppermute | solution.py:586
  20.3 69.9 %all-to-all-start = ((bf16[32,128,256]{2,1,0:T(8,128)(2,1)}), bf16[32,128,256]{2,1,0:T(8,128)(2,1)}, u32[]{:S(2)}, u32[]{:S(2)}) async-start(bf16[32,128,256]{2,1,0:T(8,128)(2,1)} %pack.1), calls=%async_computation | async-start | bytes 4194304 | tf_op jit(solution)/shard_map/all_to_all | solution.py:658
  37.5 17.9 %collective-permute-start.8 = (bf16[256,256]{1,0:T(8,128)(2,1)S(1)}, bf16[256,256]{1,0:T(8,128)(2,1)S(1)}, u32[]{:S(2)}, u32[]{:S(2)}) collective-permute-start(bf16[256,256]{1,0:T(8,128)(2,1)S(1)} %get-tuple-element.72), channel_id=1, source_target_pairs={{0,2},{1,3},{2,0},{3,1},{4,6},{5,7},{6,4},{7,5},{8,10},{9,11},{10,... | collective-permute-start | bytes 393224 | tf_op jit(solution)/shard_map/ppermute | solution.py:586
  39.1 16.3 %collective-permute-start.9 = (bf16[256,256]{1,0:T(8,128)(2,1)S(1)}, bf16[256,256]{1,0:T(8,128)(2,1)S(1)}, u32[]{:S(2)}, u32[]{:S(2)}) collective-permute-start(bf16[256,256]{1,0:T(8,128)(2,1)S(1)} %get-tuple-element.73), channel_id=1, source_target_pairs={{0,4},{1,5},{2,6},{3,7},{4,0},{5,1},{6,2},{7,3},{8,12},{9,13},{10,... | collective-permute-start | bytes 393224 | tf_op jit(solution)/shard_map/ppermute | solution.py:586
  42.9 14.0 %collective-permute-start.10 = (bf16[256,256]{1,0:T(8,128)(2,1)S(1)}, bf16[256,256]{1,0:T(8,128)(2,1)S(1)}, u32[]{:S(2)}, u32[]{:S(2)}) collective-permute-start(bf16[256,256]{1,0:T(8,128)(2,1)S(1)} %get-tuple-element.74), channel_id=1, source_target_pairs={{0,6},{1,7},{2,4},{3,5},{4,2},{5,3},{6,0},{7,1},{8,14},{9,15},{10,... | collective-permute-start | bytes 393224 | tf_op jit(solution)/shard_map/ppermute | solution.py:586
  57.0 5.6 %collective-permute-start.11 = (f32[64,256]{1,0:T(8,128)S(1)}, f32[64,256]{1,0:T(8,128)S(1)}, u32[]{:S(2)}, u32[]{:S(2)}) collective-permute-start(f32[64,256]{1,0:T(8,128)S(1)} %get-tuple-element.82), channel_id=1, source_target_pairs={{0,8},{1,9},{2,10},{3,11},{4,12},{5,13},{6,14},{7,15},{8,0},{9,1},... | collective-permute-start | bytes 196616 | tf_op jit(solution)/shard_map/ppermute | solution.py:586
  59.1 19.9 %collective-permute-start.12 = (f32[64,256]{1,0:T(8,128)S(1)}, f32[64,256]{1,0:T(8,128)S(1)}, u32[]{:S(2)}, u32[]{:S(2)}) collective-permute-start(f32[64,256]{1,0:T(8,128)S(1)} %get-tuple-element.83), channel_id=1, source_target_pairs={{0,16},{1,17},{2,18},{3,19},{4,20},{5,21},{6,22},{7,23},{8,24},{9,... | collective-permute-start | bytes 196616 | tf_op jit(solution)/shard_map/ppermute | solution.py:586
  60.0 18.9 %collective-permute-start.13 = (f32[64,256]{1,0:T(8,128)S(1)}, f32[64,256]{1,0:T(8,128)S(1)}, u32[]{:S(2)}, u32[]{:S(2)}) collective-permute-start(f32[64,256]{1,0:T(8,128)S(1)} %get-tuple-element.84), channel_id=1, source_target_pairs={{0,24},{1,25},{2,26},{3,27},{4,28},{5,29},{6,30},{7,31},{8,16},{9,... | collective-permute-start | bytes 196616 | tf_op jit(solution)/shard_map/ppermute | solution.py:586
  79.7 5.9 %collective-permute-start.16 = (bf16[64,256]{1,0:T(8,128)(2,1)S(1)}, bf16[64,256]{1,0:T(8,128)(2,1)S(1)}, u32[]{:S(2)}, u32[]{:S(2)}) collective-permute-start(bf16[64,256]{1,0:T(8,128)(2,1)S(1)} %hub_network.2), channel_id=1, source_target_pairs={{0,24},{1,25},{2,26},{3,27},{4,28},{5,29},{6,30},{7,31},{8,16},{9,... | collective-permute-start | bytes 98312 | tf_op jit(solution)/shard_map/ppermute | solution.py:586
  86.7 18.8 %collective-permute-start.19 = (bf16[256,256]{1,0:T(8,128)(2,1)S(1)}, bf16[256,256]{1,0:T(8,128)(2,1)S(1)}, u32[]{:S(2)}, u32[]{:S(2)}) collective-permute-start(bf16[256,256]{1,0:T(8,128)(2,1)S(1)} %constant_dynamic-update-slice_fusion.8), channel_id=1, source_target_pairs={{0,6},{1,7},{2,4},{3,5},{4,2},{5,3},{6,0},{7,1},{8,14},{9,15},{10,... | collective-permute-start | bytes 393224 | tf_op jit(solution)/shard_map/ppermute | solution.py:586
  89.0 16.4 %collective-permute-start.18 = (bf16[256,256]{1,0:T(8,128)(2,1)S(1)}, bf16[256,256]{1,0:T(8,128)(2,1)S(1)}, u32[]{:S(2)}, u32[]{:S(2)}) collective-permute-start(bf16[256,256]{1,0:T(8,128)(2,1)S(1)} %constant_dynamic-update-slice_fusion.8), channel_id=1, source_target_pairs={{0,4},{1,5},{2,6},{3,7},{4,0},{5,1},{6,2},{7,3},{8,12},{9,13},{10,... | collective-permute-start | bytes 393224 | tf_op jit(solution)/shard_map/ppermute | solution.py:586
  89.7 15.8 %collective-permute-start.17 = (bf16[256,256]{1,0:T(8,128)(2,1)S(1)}, bf16[256,256]{1,0:T(8,128)(2,1)S(1)}, u32[]{:S(2)}, u32[]{:S(2)}) collective-permute-start(bf16[256,256]{1,0:T(8,128)(2,1)S(1)} %constant_dynamic-update-slice_fusion.8), channel_id=1, source_target_pairs={{0,2},{1,3},{2,0},{3,1},{4,6},{5,7},{6,4},{7,5},{8,10},{9,11},{10,... | collective-permute-start | bytes 393224 | tf_op jit(solution)/shard_map/ppermute | solution.py:586
  105.5 58.6 %all-to-all-start.1 = ((bf16[32,128,256]{2,1,0:T(8,128)(2,1)}), bf16[32,128,256]{2,1,0:T(8,128)(2,1)}, u32[]{:S(2)}, u32[]{:S(2)}) async-start(bf16[32,128,256]{2,1,0:T(8,128)(2,1)} %get-tuple-element.108), calls=%async_computation.1 | async-start | bytes 4194304 | tf_op jit(solution)/shard_map/all_to_all | solution.py:676
  121.0 17.9 %collective-permute-start.22 = (bf16[256,256]{1,0:T(8,128)(2,1)S(1)}, bf16[256,256]{1,0:T(8,128)(2,1)S(1)}, u32[]{:S(2)}, u32[]{:S(2)}) collective-permute-start(bf16[256,256]{1,0:T(8,128)(2,1)S(1)} %get-tuple-element.103), channel_id=1, source_target_pairs={{0,2},{1,3},{2,0},{3,1},{4,6},{5,7},{6,4},{7,5},{8,10},{9,11},{10,... | collective-permute-start | bytes 393224 | tf_op jit(solution)/shard_map/ppermute | solution.py:586
  122.6 16.4 %collective-permute-start.23 = (bf16[256,256]{1,0:T(8,128)(2,1)S(1)}, bf16[256,256]{1,0:T(8,128)(2,1)S(1)}, u32[]{:S(2)}, u32[]{:S(2)}) collective-permute-start(bf16[256,256]{1,0:T(8,128)(2,1)S(1)} %get-tuple-element.104), channel_id=1, source_target_pairs={{0,4},{1,5},{2,6},{3,7},{4,0},{5,1},{6,2},{7,3},{8,12},{9,13},{10,... | collective-permute-start | bytes 393224 | tf_op jit(solution)/shard_map/ppermute | solution.py:586
  126.6 14.1 %collective-permute-start.24 = (bf16[256,256]{1,0:T(8,128)(2,1)S(1)}, bf16[256,256]{1,0:T(8,128)(2,1)S(1)}, u32[]{:S(2)}, u32[]{:S(2)}) collective-permute-start(bf16[256,256]{1,0:T(8,128)(2,1)S(1)} %get-tuple-element.105), channel_id=1, source_target_pairs={{0,6},{1,7},{2,4},{3,5},{4,2},{5,3},{6,0},{7,1},{8,14},{9,15},{10,... | collective-permute-start | bytes 393224 | tf_op jit(solution)/shard_map/ppermute | solution.py:586
  140.7 5.6 %collective-permute-start.25 = (f32[64,256]{1,0:T(8,128)S(1)}, f32[64,256]{1,0:T(8,128)S(1)}, u32[]{:S(2)}, u32[]{:S(2)}) collective-permute-start(f32[64,256]{1,0:T(8,128)S(1)} %get-tuple-element.115), channel_id=1, source_target_pairs={{0,8},{1,9},{2,10},{3,11},{4,12},{5,13},{6,14},{7,15},{8,0},{9,1},... | collective-permute-start | bytes 196616 | tf_op jit(solution)/shard_map/ppermute | solution.py:586
  142.6 20.0 %collective-permute-start.26 = (f32[64,256]{1,0:T(8,128)S(1)}, f32[64,256]{1,0:T(8,128)S(1)}, u32[]{:S(2)}, u32[]{:S(2)}) collective-permute-start(f32[64,256]{1,0:T(8,128)S(1)} %get-tuple-element.116), channel_id=1, source_target_pairs={{0,16},{1,17},{2,18},{3,19},{4,20},{5,21},{6,22},{7,23},{8,24},{9,... | collective-permute-start | bytes 196616 | tf_op jit(solution)/shard_map/ppermute | solution.py:586
  143.6 19.0 %collective-permute-start.27 = (f32[64,256]{1,0:T(8,128)S(1)}, f32[64,256]{1,0:T(8,128)S(1)}, u32[]{:S(2)}, u32[]{:S(2)}) collective-permute-start(f32[64,256]{1,0:T(8,128)S(1)} %get-tuple-element.117), channel_id=1, source_target_pairs={{0,24},{1,25},{2,26},{3,27},{4,28},{5,29},{6,30},{7,31},{8,16},{9,... | collective-permute-start | bytes 196616 | tf_op jit(solution)/shard_map/ppermute | solution.py:586
  (19 other events, 240.9 us)

commit v3 on v2

--- a/solution.py
+++ b/solution.py
@@ -15,6 +15,7 @@
 SMEM = pl.BlockSpec(memory_space=pltpu.SMEM)
 ANY = pl.BlockSpec(memory_space=pl.ANY)
 GROUP = 4
+SLOTS = 8
 
 
 def dot(a, b):
@@ -82,8 +83,8 @@
 
     def step(number, unused):
         where, products = [], []
-        for lane in range(GROUP):
-            place = number * GROUP + lane
+        for lane in range(SLOTS):
+            place = number * SLOTS + lane
             live = place < found
             place = jnp.minimum(place, found - 1)
             slot = picked[place]
@@ -96,12 +97,12 @@
             total[row] += product
         return unused
 
-    lax.fori_loop(0, (found + GROUP - 1) // GROUP, step, 0)
-
-
-def each_block(listed, found, copy_of, act):
+    lax.fori_loop(0, (found + SLOTS - 1) // SLOTS, step, 0)
+
+
+def each_block(pick, found, copy_of, act):
     def step(number, unused):
-        act(copy_of(listed[number]))
+        act(copy_of(pick(number)))
         return unused
 
     lax.fori_loop(0, found, step, 0)
@@ -115,33 +116,38 @@
     copy.wait()
 
 
-def list_blocks(rows, remote, own_count, hub_count, marks, fed, free):
+def list_blocks(rows, remote, own_count, hub_count, chosen, marks, fed, free):
     def clear(block, unused):
-        marks[block] = 0
+        marks[block] = 0 if chosen is not None else 1
+        marks[own_count + block] = 0
         return unused
 
     def mark(slot, unused):
-        marks[rows[slot] - hub_count] = 1
+        if chosen is not None:
+            marks[chosen[0, slot]] = 1
+        marks[own_count + rows[slot] - hub_count] = 1
         return unused
 
     def take(block, found):
-        fed[found] = block
-        free[block - found] = block
-        return found + marks[block]
+        n_now, n_later, n_free = found
+        is_fed, is_now = marks[own_count + block], marks[block]
+        now = is_fed * is_now
+        later = is_fed * (1 - is_now)
+        fed[jnp.where(is_now == 1, n_now, own_count - 1 - n_later)] = block
+        free[n_free] = block
+        return n_now + now, n_later + later, n_free + 1 - is_fed
 
     lax.fori_loop(0, own_count, clear, 0)
     lax.fori_loop(0, remote, mark, 0)
-    found = lax.fori_loop(0, own_count, take, jnp.int32(0))
-    return found, own_count - found
-
-
-def network_blocks(listed, found, read, first, second, result, finish):
+    zero = jnp.int32(0)
+    return lax.fori_loop(0, own_count, take, (zero, zero, zero))
+
+
+def network_blocks(pick, found, read, first, second, result, finish):
     size = result.shape[1]
 
     def step(number, unused):
-        blocks = [
-            listed[jnp.minimum(number * GROUP + lane, found - 1)] for lane in range(GROUP)
-        ]
+        blocks = [pick(jnp.minimum(number * GROUP + lane, found - 1)) for lane in range(GROUP)]
         values = jnp.concatenate([read(block) for block in blocks], axis=0)
         values = network(values, first, second, 512)
         for lane, block in enumerate(blocks):
@@ -301,12 +307,15 @@
     load.wait()
     wait_tiles(picked, found, tiles_hbm, tiles, sems)
     add_products(rows, cols, picked, found, begin, tiles, hubs, own, total, 0, hub_count)
-    sums = total[:hub_count].astype(bf16).reshape(hub_rows, width)
+    sums = total[:hub_count].reshape(hub_rows, width)
+    high = sums.astype(bf16)
+    low = (sums - high.astype(f32)).astype(bf16)
     step = 2 * block_size
 
     def rows_step(number, unused):
         start = number * step
-        placed[pl.ds(pl.multiple_of(start, step), step), :] = dot(unit_rows(start, step), sums)
+        unit = unit_rows(start, step)
+        placed[pl.ds(pl.multiple_of(start, step), step), :] = dot(unit, high) + dot(unit, low)
         return unused
 
     lax.fori_loop(0, hub_rows // step, rows_step, 0)
@@ -327,7 +336,7 @@
             shape_of((hub_count, block_size, width), bf16),
             shape_of((local, width), bf16),
             shape_of((hub_rows // 2, width), f32),
-            shape_of((hub_rows // 2, width), bf16),
+            shape_of((hub_rows // 2, width), f32),
         ),
         [SMEM] * 4 + [VMEM] * 3 + [ANY] * 2,
         (VMEM,) * 4,
@@ -428,7 +437,7 @@
     load_hubs.start()
     found = list_slots(rows, count, picked, begin, hub_count, False)
     start_tiles(picked, found, tiles_in, tiles, sems)
-    n_fed, n_free = list_blocks(rows, begin, own_count, hub_count, marks, fed, free)
+    n_fed, none, n_free = list_blocks(rows, begin, own_count, hub_count, None, marks, fed, free)
     load_own.wait()
     u[:own_count] = own[...].astype(f32)
     load_hubs.wait()
@@ -444,10 +453,10 @@
     def finish(block):
         return pltpu.make_async_copy(result.at[block], out.at[block], block_sems.at[block])
 
-    each_block(fed, n_fed, save, start)
-    network_blocks(free, n_free, lambda block: u[block], first, second, result, finish)
-    each_block(fed, n_fed, save, wait)
-    each_block(free, n_free, finish, wait)
+    each_block(lambda i: fed[i], n_fed, save, start)
+    network_blocks(lambda i: free[i], n_free, lambda block: u[block], first, second, result, finish)
+    each_block(lambda i: fed[i], n_fed, save, wait)
+    each_block(lambda i: free[i], n_free, finish, wait)
 
 
 def before(layer, rows, cols, count, hubs, own, tiles, first, second):
@@ -470,7 +479,7 @@
             pltpu.VMEM((own_count + 1, block_size, width), f32),
             pltpu.VMEM(own.shape, bf16),
             pltpu.SMEM((rows.shape[0],), jnp.int32),
-            pltpu.SMEM((own_count,), jnp.int32),
+            pltpu.SMEM((2 * own_count,), jnp.int32),
             pltpu.SMEM((own_count,), jnp.int32),
             pltpu.SMEM((own_count,), jnp.int32),
             pltpu.SemaphoreType.DMA((cols.shape[0],)),
@@ -486,7 +495,7 @@
 ):
     out, refs = refs[0], refs[1:]
     if with_send:
-        outgoing, refs = refs[0], refs[1:]
+        (sums, outgoing), refs = refs[:2], refs[2:]
     u, extra, inc, adj, first, second, result, marks, fed, free, block_sems, out_sems, sem = refs
     own_count = u.shape[0]
     remote = incoming.shape[0]
@@ -504,6 +513,12 @@
         for load in loads[-1]:
             load.start()
 
+    def now(number):
+        return fed[number]
+
+    def later(number):
+        return fed[own_count - 1 - number]
+
     def load_base(block):
         return pltpu.make_async_copy(base.at[block], u.at[block], block_sems.at[block])
 
@@ -514,34 +529,50 @@
         return pltpu.make_async_copy(result.at[block], out.at[block], out_sems.at[block])
 
     extra[...] = jnp.zeros_like(extra)
-    n_fed, n_free = list_blocks(rows, remote, own_count, hub_count, marks, fed, free)
+    n_now, n_later, n_free = list_blocks(
+        rows, remote, own_count, hub_count, chosen if with_send else None, marks, fed, free
+    )
     for part in range(parts):
         for load in loads[part]:
             load.wait()
         if part == 0:
             weights = load_weights(layer, first_in, second_in, first, second, sem.at[pl.ds(0, 2)])
-            each_block(fed, n_fed, load_base, start)
+            each_block(now, n_now, load_base, start)
             if with_send:
-                each_block(free, n_free, load_done, start)
+                each_block(later, n_later, load_base, start)
+                each_block(lambda i: free[i], n_free, load_done, start)
         products = [dot(adj[slot], inc[slot]) for slot in range(part * size, (part + 1) * size)]
         for lane, product in enumerate(products):
             extra[rows[part * size + lane] - hub_count] += product
-    each_block(fed, n_fed, load_base, wait)
+    each_block(now, n_now, load_base, wait)
     for load in weights:
         load.wait()
     network_blocks(
-        fed, n_fed, lambda block: u[block] + extra[block], first, second, result, finish
+        now, n_now, lambda block: u[block] + extra[block], first, second, result, finish
     )
     copies = []
     if with_send:
-        each_block(free, n_free, load_done, wait)
+        each_block(lambda i: free[i], n_free, load_done, wait)
         for number in range(remote):
             copy = pltpu.make_async_copy(
                 result.at[chosen[0, number]], outgoing.at[number], sem.at[number]
             )
             copy.start()
             copies.append(copy)
-    each_block(fed, n_fed, finish, wait)
+
+        def save(block):
+            return pltpu.make_async_copy(u.at[block], sums.at[block], block_sems.at[block])
+
+        def keep(number, unused):
+            block = later(number)
+            load_base(block).wait()
+            u[block] += extra[block]
+            save(block).start()
+            return unused
+
+        lax.fori_loop(0, n_later, keep, 0)
+        each_block(later, n_later, save, wait)
+    each_block(now, n_now, finish, wait)
     for copy in copies:
         copy.wait()
 
@@ -551,7 +582,7 @@
     remote = incoming.shape[0]
     shapes = [shape_of(base.shape, bf16)]
     if with_send:
-        shapes.append(shape_of(incoming.shape, bf16))
+        shapes += [shape_of(base.shape, f32), shape_of(incoming.shape, bf16)]
     return pl.pallas_call(
         functools.partial(after_kernel, layer, with_send, hub_count),
         out_shape=tuple(shapes),
@@ -565,20 +596,72 @@
             pltpu.VMEM(first.shape[1:], bf16),
             pltpu.VMEM(second.shape[1:], bf16),
             pltpu.VMEM(base.shape, bf16),
-            pltpu.SMEM((own_count,), jnp.int32),
+            pltpu.SMEM((2 * own_count,), jnp.int32),
             pltpu.SMEM((own_count,), jnp.int32),
             pltpu.SMEM((own_count,), jnp.int32),
             pltpu.SemaphoreType.DMA((own_count,)),
             pltpu.SemaphoreType.DMA((own_count,)),
             pltpu.SemaphoreType.DMA((max(10, remote),)),
         ],
-        input_output_aliases={3: 0},
+        input_output_aliases={3: 0, 2: 1} if with_send else {3: 0},
         compiler_params=pltpu.CompilerParams(vmem_limit_bytes=58 * MIB),
         cost_estimate=pl.CostEstimate(
             flops=4 * base.size * first.shape[-1], bytes_accessed=16 * MIB, transcendentals=0
         ),
         name="after",
     )(rows, chosen, base, done, incoming, tiles, first, second)
+
+
+def late_kernel(
+    layer, remote, hub_count, rows, chosen, sums, done, first_in, second_in, out,
+    u, first, second, result, marks, fed, free, block_sems, sem,
+):
+    own_count = u.shape[0]
+    weights = load_weights(layer, first_in, second_in, first, second, sem)
+    n_later = list_blocks(rows, remote, own_count, hub_count, chosen, marks, fed, free)[1]
+
+    def later(number):
+        return fed[own_count - 1 - number]
+
+    def load(block):
+        return pltpu.make_async_copy(sums.at[block], u.at[block], block_sems.at[block])
+
+    def finish(block):
+        return pltpu.make_async_copy(result.at[block], out.at[block], block_sems.at[block])
+
+    each_block(later, n_later, load, start)
+    each_block(later, n_later, load, wait)
+    for part in weights:
+        part.wait()
+    network_blocks(later, n_later, lambda block: u[block], first, second, result, finish)
+    each_block(later, n_later, finish, wait)
+
+
+def late(layer, rows, chosen, sums, done, first, second, hub_count):
+    own_count = sums.shape[0]
+    return pl.pallas_call(
+        functools.partial(late_kernel, layer, chosen.shape[1], hub_count),
+        out_shape=shape_of(done.shape, bf16),
+        in_specs=[SMEM, SMEM] + [ANY] * 4,
+        out_specs=ANY,
+        scratch_shapes=[
+            pltpu.VMEM(sums.shape, f32),
+            pltpu.VMEM(first.shape[1:], bf16),
+            pltpu.VMEM(second.shape[1:], bf16),
+            pltpu.VMEM(sums.shape, bf16),
+            pltpu.SMEM((2 * own_count,), jnp.int32),
+            pltpu.SMEM((own_count,), jnp.int32),
+            pltpu.SMEM((own_count,), jnp.int32),
+            pltpu.SemaphoreType.DMA((own_count,)),
+            pltpu.SemaphoreType.DMA((2,)),
+        ],
+        input_output_aliases={3: 0},
+        compiler_params=pltpu.CompilerParams(vmem_limit_bytes=58 * MIB),
+        cost_estimate=pl.CostEstimate(
+            flops=sums.size * first.shape[-1], bytes_accessed=5 * MIB, transcendentals=0
+        ),
+        name="late",
+    )(rows, chosen, sums, done, first, second)
 
 
 def exchange(x, bit):
@@ -623,9 +706,9 @@
     return kept, received
 
 
-def scatter_far(position, kept, received, digits, local):
+def scatter_far(position, kept, received, digits, local, sent_type):
     bit, radix = digits[-1]
-    kept, *sent = combine(position, kept, received, bit, radix, local, f32)
+    kept, *sent = combine(position, kept, received, bit, radix, local, sent_type)
     return [kept] + [exchange(part, bit * (1 + number)) for number, part in enumerate(sent)]
 
 
@@ -650,8 +733,10 @@
         lax.all_to_all, axis_name="dev", split_axis=0, concat_axis=0, tiled=True
     )
 
+    pieces = gather_far(hubs, digits)
+    own, *pieces = lax.optimization_barrier((own, *pieces))
     outgoing = pack(send_list, own)
-    pieces = gather_near(gather_far(hubs, digits), digits)
+    pieces = gather_near(pieces, digits)
     outgoing, rows, cols, place_col, *pieces = lax.optimization_barrier(
         (outgoing, rows, cols, place_col, *pieces)
     )
@@ -663,17 +748,18 @@
     base, done = before(0, rows, cols, tile_count, hub_table, own, tiles, w_in, w_out)
     kept, received = scatter_near(me, kept, sent, digits, local)
     base, done, *received = lax.optimization_barrier((base, done, *received))
-    parts = scatter_far(me, kept, received, digits, local)
+    parts = scatter_far(me, kept, received, digits, local, bf16)
     hub_new = hub_network(0, mine, parts, w_in, w_out)
     pieces = gather_far(hub_new, digits)
     base, *pieces = lax.optimization_barrier((base, *pieces))
-    own, outgoing = after(
+    done, sums, outgoing = after(
         0, rows, send_list, base, done, incoming, tiles, w_in, w_out, hub_count, True
     )
 
     pieces = gather_near(pieces, digits)
     outgoing, *pieces = lax.optimization_barrier((outgoing, *pieces))
     incoming = all_to_all(outgoing)
+    own = late(0, rows, send_list, sums, done, w_in, w_out, hub_count)
     halves = gather_last(pieces, digits)
     hub_table, mine, kept, sent = hub_second(
         digits, rows, cols, tile_count, me, place_row, halves, own, tiles, local
@@ -681,11 +767,12 @@
     base, done = before(1, rows, cols, tile_count, hub_table, own, tiles, w_in, w_out)
     kept, received = scatter_near(me, kept, sent, digits, local)
     base, done, *received = lax.optimization_barrier((base, done, *received))
-    parts = scatter_far(me, kept, received, digits, local)
-    hub_out = hub_network(1, mine, parts, w_in, w_out)
+    parts = scatter_far(me, kept, received, digits, local, f32)
     (peri_out,) = after(
         1, rows, send_list, base, done, incoming, tiles, w_in, w_out, hub_count, False
     )
+    peri_out, *parts = lax.optimization_barrier((peri_out, *parts))
+    hub_out = hub_network(1, mine, parts, w_in, w_out)
     return (peri_out.reshape(peripheral.shape), hub_out)
 
 

time: 179 us -> 172 us (0.961)
  waiting for transfers between devices: 52 us -> 35.8 us
  Pallas kernels: 71.7 us -> 78.1 us
    ppermute x28, waiting for transfers between devices: 52 us -> 29.3 us  [exchange(): return lax.ppermute(x, 'dev', [(i, i ^ bit) for i in range(devices)])]
    pallas_call x0 -> x1, Pallas kernels: none -> 8.38 us  [late(): pl.pallas_call(functools.partial(late_kernel, layer, chosen.shape[1], hub...]
    all_to_all x2, waiting for transfers between devices: 0.01 us -> 6.46 us  [body(): incoming = all_to_all(outgoing)]
    pallas_call x2, Pallas kernels: 29.5 us -> 24 us  [after(): pl.pallas_call(functools.partial(after_kernel, layer, with_send, hub_coun...]
    pallas_call x11, Pallas kernels: 42.1 us -> 45.7 us  [call(): pl.pallas_call(kernel, out_shape=out_shape, in_specs=in_specs, out_specs=...]
  transfers between devices with their start and end apart: 30 -> 30, of which waited for: 17 -> 13; matrix products, arithmetic and copies ran while one was open for 1% -> 1% of each run, Pallas kernels for 32% -> 45%
where the time goes in v3:
time: 172 us; the launch traced here: 170 us
  Pallas kernels  78.1 us (45%)
  starting transfers between devices  51.1 us (30%)
  waiting for transfers between devices  35.8 us (21%)
  local copies, waits for them, and re-layouts  2.22 us (1%)
  between operations  1.84 us (1%)
    pallas_call x11, Pallas kernels, call(): pl.pallas_call(kernel, out_shape=out_shape, in_specs=in_specs, out_specs=...  45.7 us
    ppermute x28, starting transfers between devices, exchange(): return lax.ppermute(x, 'dev', [(i, i ^ bit) for i in range(devices)])  42 us
    ppermute x28, waiting for transfers between devices, exchange(): return lax.ppermute(x, 'dev', [(i, i ^ bit) for i in range(devices)])  29.3 us
    pallas_call x2, Pallas kernels, after(): pl.pallas_call(functools.partial(after_kernel, layer, with_send, hub_coun...  24 us
    all_to_all x2, starting transfers between devices, body(): incoming = all_to_all(outgoing)  9.13 us
    pallas_call x1, Pallas kernels, late(): pl.pallas_call(functools.partial(late_kernel, layer, chosen.shape[1], hub...  8.38 us
    all_to_all x2, waiting for transfers between devices, body(): incoming = all_to_all(outgoing)  6.46 us
  transfers between devices with their start and end apart: 30, of which 13 were waited for; matrix products, arithmetic and copies ran while one was open for 1% of the time, Pallas kernels for 45%

profile of v3, /device:TPU:0, one launch (start us, length us, event | category | flops | bytes accessed | tf_op | source)
XLA Modules:
  0.0 170.4 jit_solution(14736388432940983424)
XLA Ops:
  0.6 4.1 %collective-permute-start.1 = (bf16[64,256]{1,0:T(8,128)(2,1)}, bf16[64,256]{1,0:T(8,128)(2,1)S(1)}, u32[]{:S(2)}, u32[]{:S(2)}) collective-permute-start(bf16[64,256]{1,0:T(8,128)(2,1)} %param.11), channel_id=1, source_target_pairs={{0,16},{1,17},{2,18},{3,19},{4,20},{5,21},{6,22},{7,23},{8,24},{9,... | collective-permute-start | bytes 98312 | tf_op jit(solution)/shard_map/ppermute | solution.py:669
  8.9 3.4 %collective-permute-done.2 = bf16[64,256]{1,0:T(8,128)(2,1)S(1)} collective-permute-done((bf16[64,256]{1,0:T(8,128)(2,1)}, bf16[64,256]{1,0:T(8,128)(2,1)S(1)}, u32[]{:S(2)}, u32[]{:S(2)}) %collective-permute-start.2) | collective-permute-done | bytes 32800 | tf_op jit(solution)/shard_map/ppermute | solution.py:669
  13.0 2.5 %collective-permute-start.5 = (bf16[256,256]{1,0:T(8,128)(2,1)S(1)}, bf16[256,256]{1,0:T(8,128)(2,1)S(1)}, u32[]{:S(2)}, u32[]{:S(2)}) collective-permute-start(bf16[256,256]{1,0:T(8,128)(2,1)S(1)} %constant_dynamic-update-slice_fusion), channel_id=1, source_target_pairs={{0,6},{1,7},{2,4},{3,5},{4,2},{5,3},{6,0},{7,1},{8,14},{9,15},{10,... | collective-permute-start | bytes 393224 | tf_op jit(solution)/shard_map/ppermute | solution.py:669
  17.2 3.8 %pack.1 = bf16[32,128,256]{2,1,0:T(8,128)(2,1)} custom-call(s32[1,32]{1,0:T(1,128)} %chosen.7, bf16[32,128,256]{2,1,0:T(8,128)(2,1)} %bitcast.7), custom_call_target="tpu_custom_call" | custom-call | bytes 4194304 | tf_op jit(solution)/shard_map/pack/pallas_call | solution.py:30
  21.1 3.6 %all-to-all-start = ((bf16[32,128,256]{2,1,0:T(8,128)(2,1)}), bf16[32,128,256]{2,1,0:T(8,128)(2,1)}, u32[]{:S(2)}, u32[]{:S(2)}) async-start(bf16[32,128,256]{2,1,0:T(8,128)(2,1)} %pack.1), calls=%async_computation | async-start | bytes 4194304 | tf_op jit(solution)/shard_map/all_to_all | solution.py:743
  26.8 6.8 %hub_first.1 = (bf16[16,128,256]{2,1,0:T(8,128)(2,1)S(1)}, bf16[64,256]{1,0:T(8,128)(2,1)S(1)}, f32[1024,256]{1,0:T(8,128)S(1)}, f32[1024,256]{1,0:T(8,128)S(1)}) custom-call(s32[144]{0:T(256)S(1)} %compare_select_fusion.rows, s32[112]{0:T(128)S(1)} %compare_select_fusion.1.cols, s32[1]{0:T(128)S(6)} %copy.33.count, s32[1]{0:T(128)} %bitcast.2.position, ...), custom_call_target="tpu_custom_call" | custom-call | flops 2147483648 | bytes 14680064 | tf_op jit(solution)/shard_map/hub_first/pallas_call | solution.py:30
  33.6 3.8 %collective-permute-start.7 = (f32[1024,256]{1,0:T(8,128)S(1)}, f32[1024,256]{1,0:T(8,128)S(1)}, u32[]{:S(2)}, u32[]{:S(2)}) collective-permute-start(f32[1024,256]{1,0:T(8,128)S(1)} %get-tuple-element.87), channel_id=1, source_target_pairs={{0,1},{1,0},{2,3},{3,2},{4,5},{5,4},{6,7},{7,6},{8,9},{9,8},{10,11... | collective-permute-start | bytes 3145736 | tf_op jit(solution)/shard_map/ppermute | solution.py:669
  37.4 2.3 %collective-permute-done.7.refs_0_ = f32[1024,256]{1,0:T(8,128)S(1)} collective-permute-done((f32[1024,256]{1,0:T(8,128)S(1)}, f32[1024,256]{1,0:T(8,128)S(1)}, u32[]{:S(2)}, u32[]{:S(2)}) %collective-permute-start.7) | collective-permute-done | bytes 1048608 | tf_op jit(solution)/shard_map/ppermute | solution.py:669
  43.5 11.1 %before.2 = (f32[32,128,256]{2,1,0:T(8,128)}, bf16[32,128,256]{2,1,0:T(8,128)(2,1)}) custom-call(s32[144]{0:T(256)} %copy-done.6, s32[112]{0:T(128)} %copy-done.9, s32[1]{0:T(128)S(6)} %copy.33.count, bf16[16,128,256]{2,1,0:T(8,128)(2,1)} %copy-done.5, bf16[32,128,256]{2,1,0:T(8,128)(2,1)} %bitcast.9, bf16[144,128,128]{2,1,0:T(8,128)(2,1)} %tiles.3, ...), custom_call_target="tpu_custom_call" | custom-call | flops 2863311616 | bytes 18874368 | tf_op jit(solution)/shard_map/before/pallas_call | solution.py:30
  55.1 2.4 %collective-permute-start.11 = (bf16[64,256]{1,0:T(8,128)(2,1)S(1)}, bf16[64,256]{1,0:T(8,128)(2,1)S(1)}, u32[]{:S(2)}, u32[]{:S(2)}) collective-permute-start(bf16[64,256]{1,0:T(8,128)(2,1)S(1)} %get-tuple-element.98), channel_id=1, source_target_pairs={{0,8},{1,9},{2,10},{3,11},{4,12},{5,13},{6,14},{7,15},{8,0},{9,1},... | collective-permute-start | bytes 98312 | tf_op jit(solution)/shard_map/ppermute | solution.py:669
  57.5 2.4 %collective-permute-start.13 = (bf16[64,256]{1,0:T(8,128)(2,1)S(1)}, bf16[64,256]{1,0:T(8,128)(2,1)S(1)}, u32[]{:S(2)}, u32[]{:S(2)}) collective-permute-start(bf16[64,256]{1,0:T(8,128)(2,1)S(1)} %get-tuple-element.100), channel_id=1, source_target_pairs={{0,24},{1,25},{2,26},{3,27},{4,28},{5,29},{6,30},{7,31},{8,16},{9,... | collective-permute-start | bytes 98312 | tf_op jit(solution)/shard_map/ppermute | solution.py:669
  61.2 14.8 %collective-permute-done.12.refs_2_ = bf16[64,256]{1,0:T(8,128)(2,1)S(1)} collective-permute-done((bf16[64,256]{1,0:T(8,128)(2,1)S(1)}, bf16[64,256]{1,0:T(8,128)(2,1)S(1)}, u32[]{:S(2)}, u32[]{:S(2)}) %collective-permute-start.12) | collective-permute-done | bytes 32800 | tf_op jit(solution)/shard_map/ppermute | solution.py:669
  83.4 2.4 %collective-permute-start.19 = (bf16[256,256]{1,0:T(8,128)(2,1)S(1)}, bf16[256,256]{1,0:T(8,128)(2,1)S(1)}, u32[]{:S(2)}, u32[]{:S(2)}) collective-permute-start(bf16[256,256]{1,0:T(8,128)(2,1)S(1)} %constant_dynamic-update-slice_fusion.8), channel_id=1, source_target_pairs={{0,6},{1,7},{2,4},{3,5},{4,2},{5,3},{6,0},{7,1},{8,14},{9,15},{10,... | collective-permute-start | bytes 393224 | tf_op jit(solution)/shard_map/ppermute | solution.py:669
  87.0 11.0 %after.2 = (bf16[32,128,256]{2,1,0:T(8,128)(2,1)}, f32[32,128,256]{2,1,0:T(8,128)}, bf16[32,128,256]{2,1,0:T(8,128)(2,1)}) custom-call(s32[144]{0:T(256)} %copy-done.6, s32[1,32]{1,0:T(1,128)} %chosen.7, f32[32,128,256]{2,1,0:T(8,128)} %get-tuple-element.101.base, ...), custom_call_target="tpu_custom_call", output_to_operand_aliasing={{0}: (3, {}), {1}: (2, {})} | custom-call | flops 8589934592 | bytes 16777216 | tf_op jit(solution)/shard_map/after/pallas_call | solution.py:586
  98.0 5.5 %all-to-all-start.1 = ((bf16[32,128,256]{2,1,0:T(8,128)(2,1)}), bf16[32,128,256]{2,1,0:T(8,128)(2,1)}, u32[]{:S(2)}, u32[]{:S(2)}) async-start(bf16[32,128,256]{2,1,0:T(8,128)(2,1)} %get-tuple-element.125), calls=%async_computation.1 | async-start | bytes 4194304 | tf_op jit(solution)/shard_map/all_to_all | solution.py:761
  103.8 8.4 %late.1.own_hbm.own_in = bf16[32,128,256]{2,1,0:T(8,128)(2,1)} custom-call(s32[144]{0:T(256)} %copy-done.6, s32[1,32]{1,0:T(1,128)} %chosen.7, f32[32,128,256]{2,1,0:T(8,128)} %get-tuple-element.113.sums, bf16[32,128,256]{2,1,0:T(8,128)(2,1)} %get-tuple-element.114.done, bf16[2,256,2048]{2,1,0:T(8,128)(2,1)} %refs_4_.3, ...), custom_call_target="tpu_custom_call", output_to_operand_aliasing={{}: (3, {})} | custom-call | flops 2147483648 | bytes 5242880 | tf_op jit(solution)/shard_map/late/pallas_call | solution.py:642
  112.3 10.7 %hub_second.1 = (bf16[16,128,256]{2,1,0:T(8,128)(2,1)S(1)}, bf16[64,256]{1,0:T(8,128)(2,1)S(1)}, f32[1024,256]{1,0:T(8,128)S(1)}, f32[1024,256]{1,0:T(8,128)S(1)}) custom-call(s32[144]{0:T(256)S(1)} %copy-done.7, s32[112]{0:T(128)S(1)} %copy-done.10, s32[1]{0:T(128)S(6)} %copy.33.count, s32[1]{0:T(128)} %bitcast.2.position, s32[1,2048]{1,0:T(1,128)S(1)} %bitcast.6, ...), custom_call_target="tpu_custom_call" | custom-call | flops 2147483648 | bytes 14680064 | tf_op jit(solution)/shard_map/hub_second/pallas_call | solution.py:30
  123.9 2.3 %collective-permute-start.21 = (f32[1024,256]{1,0:T(8,128)S(1)}, f32[1024,256]{1,0:T(8,128)S(1)}, u32[]{:S(2)}, u32[]{:S(2)}) collective-permute-start(f32[1024,256]{1,0:T(8,128)S(1)} %get-tuple-element.119), channel_id=1, source_target_pairs={{0,1},{1,0},{2,3},{3,2},{4,5},{5,4},{6,7},{7,6},{8,9},{9,8},{10,11... | collective-permute-start | bytes 3145736 | tf_op jit(solution)/shard_map/ppermute | solution.py:669
  128.7 2.4 %collective-permute-start.22 = (bf16[256,256]{1,0:T(8,128)(2,1)S(1)}, bf16[256,256]{1,0:T(8,128)(2,1)S(1)}, u32[]{:S(2)}, u32[]{:S(2)}) collective-permute-start(bf16[256,256]{1,0:T(8,128)(2,1)S(1)} %get-tuple-element.120), channel_id=1, source_target_pairs={{0,2},{1,3},{2,0},{3,1},{4,6},{5,7},{6,4},{7,5},{8,10},{9,11},{10,... | collective-permute-start | bytes 393224 | tf_op jit(solution)/shard_map/ppermute | solution.py:669
  132.6 10.5 %before.3 = (f32[32,128,256]{2,1,0:T(8,128)}, bf16[32,128,256]{2,1,0:T(8,128)(2,1)}) custom-call(s32[144]{0:T(256)} %copy-done.6, s32[112]{0:T(128)} %copy-done.9, s32[1]{0:T(128)S(6)} %copy.33.count, bf16[16,128,256]{2,1,0:T(8,128)(2,1)} %copy-done.4, bf16[32,128,256]{2,1,0:T(8,128)(2,1)} %late.1.own_hbm.own_in, bf16[144,128,128]{2,1,0:T(8,128)(2,1)} %tiles.3, ...), custom_call_target="tpu_custom_call" | custom-call | flops 2863311616 | bytes 18874368 | tf_op jit(solution)/shard_map/before/pallas_call | solution.py:30
  143.3 3.5 %collective-permute-start.25 = (f32[64,256]{1,0:T(8,128)S(1)}, f32[64,256]{1,0:T(8,128)S(1)}, u32[]{:S(2)}, u32[]{:S(2)}) collective-permute-start(f32[64,256]{1,0:T(8,128)S(1)} %get-tuple-element.131), channel_id=1, source_target_pairs={{0,8},{1,9},{2,10},{3,11},{4,12},{5,13},{6,14},{7,15},{8,0},{9,1},... | collective-permute-start | bytes 196616 | tf_op jit(solution)/shard_map/ppermute | solution.py:669
  146.8 2.4 %collective-permute-start.27 = (f32[64,256]{1,0:T(8,128)S(1)}, f32[64,256]{1,0:T(8,128)S(1)}, u32[]{:S(2)}, u32[]{:S(2)}) collective-permute-start(f32[64,256]{1,0:T(8,128)S(1)} %get-tuple-element.133), channel_id=1, source_target_pairs={{0,24},{1,25},{2,26},{3,27},{4,28},{5,29},{6,30},{7,31},{8,16},{9,... | collective-permute-start | bytes 196616 | tf_op jit(solution)/shard_map/ppermute | solution.py:669
  149.3 6.5 %all-to-all-done.1.incoming = bf16[32,128,256]{2,1,0:T(8,128)(2,1)} async-done(((bf16[32,128,256]{2,1,0:T(8,128)(2,1)}), bf16[32,128,256]{2,1,0:T(8,128)(2,1)}, u32[]{:S(2)}, u32[]{:S(2)}) %all-to-all-start.1) | async-done | bytes 2097184 | tf_op jit(solution)/shard_map/all_to_all | solution.py:761
  155.7 13.1 %after.3 = bf16[32,128,256]{2,1,0:T(8,128)(2,1)} custom-call(s32[144]{0:T(256)} %copy-done.6, s32[1,32]{1,0:T(1,128)} %chosen.7, f32[32,128,256]{2,1,0:T(8,128)} %get-tuple-element.123.base, bf16[32,128,256]{2,1,0:T(8,128)(2,1)} %get-tuple-element.124.done, bf16[32,128,256]{2,1,0:T(8,128)(2,1)} %all-to-all-done.1.incoming, ...), custom_call_target="tpu_custom_call", output_to_operand_aliasing={{}: (3, {})} | custom-call | flops 8589934592 | bytes 16777216 | tf_op jit(solution)/shard_map/after/pallas_call | solution.py:586
  (91 shorter events, 29.0 us)
Async XLA Ops:
  0.6 6.7 %collective-permute-start.1 = (bf16[64,256]{1,0:T(8,128)(2,1)}, bf16[64,256]{1,0:T(8,128)(2,1)S(1)}, u32[]{:S(2)}, u32[]{:S(2)}) collective-permute-start(bf16[64,256]{1,0:T(8,128)(2,1)} %param.11), channel_id=1, source_target_pairs={{0,16},{1,17},{2,18},{3,19},{4,20},{5,21},{6,22},{7,23},{8,24},{9,... | collective-permute-start | bytes 98312 | tf_op jit(solution)/shard_map/ppermute | solution.py:669
  6.3 5.9 %collective-permute-start.2 = (bf16[64,256]{1,0:T(8,128)(2,1)}, bf16[64,256]{1,0:T(8,128)(2,1)S(1)}, u32[]{:S(2)}, u32[]{:S(2)}) collective-permute-start(bf16[64,256]{1,0:T(8,128)(2,1)} %param.11), channel_id=1, source_target_pairs={{0,24},{1,25},{2,26},{3,27},{4,28},{5,29},{6,30},{7,31},{8,16},{9,... | collective-permute-start | bytes 98312 | tf_op jit(solution)/shard_map/ppermute | solution.py:669
  13.0 8.0 %collective-permute-start.5 = (bf16[256,256]{1,0:T(8,128)(2,1)S(1)}, bf16[256,256]{1,0:T(8,128)(2,1)S(1)}, u32[]{:S(2)}, u32[]{:S(2)}) collective-permute-start(bf16[256,256]{1,0:T(8,128)(2,1)S(1)} %constant_dynamic-update-slice_fusion), channel_id=1, source_target_pairs={{0,6},{1,7},{2,4},{3,5},{4,2},{5,3},{6,0},{7,1},{8,14},{9,15},{10,... | collective-permute-start | bytes 393224 | tf_op jit(solution)/shard_map/ppermute | solution.py:669
  15.5 5.6 %collective-permute-start.4 = (bf16[256,256]{1,0:T(8,128)(2,1)S(1)}, bf16[256,256]{1,0:T(8,128)(2,1)S(1)}, u32[]{:S(2)}, u32[]{:S(2)}) collective-permute-start(bf16[256,256]{1,0:T(8,128)(2,1)S(1)} %constant_dynamic-update-slice_fusion), channel_id=1, source_target_pairs={{0,4},{1,5},{2,6},{3,7},{4,0},{5,1},{6,2},{7,3},{8,12},{9,13},{10,... | collective-permute-start | bytes 393224 | tf_op jit(solution)/shard_map/ppermute | solution.py:669
  21.1 65.9 %all-to-all-start = ((bf16[32,128,256]{2,1,0:T(8,128)(2,1)}), bf16[32,128,256]{2,1,0:T(8,128)(2,1)}, u32[]{:S(2)}, u32[]{:S(2)}) async-start(bf16[32,128,256]{2,1,0:T(8,128)(2,1)} %pack.1), calls=%async_computation | async-start | bytes 4194304 | tf_op jit(solution)/shard_map/all_to_all | solution.py:743
  33.6 6.1 %collective-permute-start.7 = (f32[1024,256]{1,0:T(8,128)S(1)}, f32[1024,256]{1,0:T(8,128)S(1)}, u32[]{:S(2)}, u32[]{:S(2)}) collective-permute-start(f32[1024,256]{1,0:T(8,128)S(1)} %get-tuple-element.87), channel_id=1, source_target_pairs={{0,1},{1,0},{2,3},{3,2},{4,5},{5,4},{6,7},{7,6},{8,9},{9,8},{10,11... | collective-permute-start | bytes 3145736 | tf_op jit(solution)/shard_map/ppermute | solution.py:669
  39.9 14.7 %collective-permute-start.8 = (bf16[256,256]{1,0:T(8,128)(2,1)S(1)}, bf16[256,256]{1,0:T(8,128)(2,1)S(1)}, u32[]{:S(2)}, u32[]{:S(2)}) collective-permute-start(bf16[256,256]{1,0:T(8,128)(2,1)S(1)} %get-tuple-element.88), channel_id=1, source_target_pairs={{0,2},{1,3},{2,0},{3,1},{4,6},{5,7},{6,4},{7,5},{8,10},{9,11},{10,... | collective-permute-start | bytes 393224 | tf_op jit(solution)/shard_map/ppermute | solution.py:669
  40.7 13.9 %collective-permute-start.9 = (bf16[256,256]{1,0:T(8,128)(2,1)S(1)}, bf16[256,256]{1,0:T(8,128)(2,1)S(1)}, u32[]{:S(2)}, u32[]{:S(2)}) collective-permute-start(bf16[256,256]{1,0:T(8,128)(2,1)S(1)} %get-tuple-element.89), channel_id=1, source_target_pairs={{0,4},{1,5},{2,6},{3,7},{4,0},{5,1},{6,2},{7,3},{8,12},{9,13},{10,... | collective-permute-start | bytes 393224 | tf_op jit(solution)/shard_map/ppermute | solution.py:669
  42.2 12.8 %collective-permute-start.10 = (bf16[256,256]{1,0:T(8,128)(2,1)S(1)}, bf16[256,256]{1,0:T(8,128)(2,1)S(1)}, u32[]{:S(2)}, u32[]{:S(2)}) collective-permute-start(bf16[256,256]{1,0:T(8,128)(2,1)S(1)} %get-tuple-element.90), channel_id=1, source_target_pairs={{0,6},{1,7},{2,4},{3,5},{4,2},{5,3},{6,0},{7,1},{8,14},{9,15},{10,... | collective-permute-start | bytes 393224 | tf_op jit(solution)/shard_map/ppermute | solution.py:669
  55.1 6.1 %collective-permute-start.11 = (bf16[64,256]{1,0:T(8,128)(2,1)S(1)}, bf16[64,256]{1,0:T(8,128)(2,1)S(1)}, u32[]{:S(2)}, u32[]{:S(2)}) collective-permute-start(bf16[64,256]{1,0:T(8,128)(2,1)S(1)} %get-tuple-element.98), channel_id=1, source_target_pairs={{0,8},{1,9},{2,10},{3,11},{4,12},{5,13},{6,14},{7,15},{8,0},{9,1},... | collective-permute-start | bytes 98312 | tf_op jit(solution)/shard_map/ppermute | solution.py:669
  57.5 18.5 %collective-permute-start.12 = (bf16[64,256]{1,0:T(8,128)(2,1)S(1)}, bf16[64,256]{1,0:T(8,128)(2,1)S(1)}, u32[]{:S(2)}, u32[]{:S(2)}) collective-permute-start(bf16[64,256]{1,0:T(8,128)(2,1)S(1)} %get-tuple-element.99), channel_id=1, source_target_pairs={{0,16},{1,17},{2,18},{3,19},{4,20},{5,21},{6,22},{7,23},{8,24},{9,... | collective-permute-start | bytes 98312 | tf_op jit(solution)/shard_map/ppermute | solution.py:669
  57.5 18.5 %collective-permute-start.13 = (bf16[64,256]{1,0:T(8,128)(2,1)S(1)}, bf16[64,256]{1,0:T(8,128)(2,1)S(1)}, u32[]{:S(2)}, u32[]{:S(2)}) collective-permute-start(bf16[64,256]{1,0:T(8,128)(2,1)S(1)} %get-tuple-element.100), channel_id=1, source_target_pairs={{0,24},{1,25},{2,26},{3,27},{4,28},{5,29},{6,30},{7,31},{8,16},{9,... | collective-permute-start | bytes 98312 | tf_op jit(solution)/shard_map/ppermute | solution.py:669
  76.8 5.8 %collective-permute-start.16 = (bf16[64,256]{1,0:T(8,128)(2,1)S(1)}, bf16[64,256]{1,0:T(8,128)(2,1)S(1)}, u32[]{:S(2)}, u32[]{:S(2)}) collective-permute-start(bf16[64,256]{1,0:T(8,128)(2,1)S(1)} %hub_network.2), channel_id=1, source_target_pairs={{0,24},{1,25},{2,26},{3,27},{4,28},{5,29},{6,30},{7,31},{8,16},{9,... | collective-permute-start | bytes 98312 | tf_op jit(solution)/shard_map/ppermute | solution.py:669
  83.4 14.5 %collective-permute-start.19 = (bf16[256,256]{1,0:T(8,128)(2,1)S(1)}, bf16[256,256]{1,0:T(8,128)(2,1)S(1)}, u32[]{:S(2)}, u32[]{:S(2)}) collective-permute-start(bf16[256,256]{1,0:T(8,128)(2,1)S(1)} %constant_dynamic-update-slice_fusion.8), channel_id=1, source_target_pairs={{0,6},{1,7},{2,4},{3,5},{4,2},{5,3},{6,0},{7,1},{8,14},{9,15},{10,... | collective-permute-start | bytes 393224 | tf_op jit(solution)/shard_map/ppermute | solution.py:669
  85.8 12.2 %collective-permute-start.18 = (bf16[256,256]{1,0:T(8,128)(2,1)S(1)}, bf16[256,256]{1,0:T(8,128)(2,1)S(1)}, u32[]{:S(2)}, u32[]{:S(2)}) collective-permute-start(bf16[256,256]{1,0:T(8,128)(2,1)S(1)} %constant_dynamic-update-slice_fusion.8), channel_id=1, source_target_pairs={{0,4},{1,5},{2,6},{3,7},{4,0},{5,1},{6,2},{7,3},{8,12},{9,13},{10,... | collective-permute-start | bytes 393224 | tf_op jit(solution)/shard_map/ppermute | solution.py:669
  86.4 11.6 %collective-permute-start.17 = (bf16[256,256]{1,0:T(8,128)(2,1)S(1)}, bf16[256,256]{1,0:T(8,128)(2,1)S(1)}, u32[]{:S(2)}, u32[]{:S(2)}) collective-permute-start(bf16[256,256]{1,0:T(8,128)(2,1)S(1)} %constant_dynamic-update-slice_fusion.8), channel_id=1, source_target_pairs={{0,2},{1,3},{2,0},{3,1},{4,6},{5,7},{6,4},{7,5},{8,10},{9,11},{10,... | collective-permute-start | bytes 393224 | tf_op jit(solution)/shard_map/ppermute | solution.py:669
  98.0 57.7 %all-to-all-start.1 = ((bf16[32,128,256]{2,1,0:T(8,128)(2,1)}), bf16[32,128,256]{2,1,0:T(8,128)(2,1)}, u32[]{:S(2)}, u32[]{:S(2)}) async-start(bf16[32,128,256]{2,1,0:T(8,128)(2,1)} %get-tuple-element.125), calls=%async_computation.1 | async-start | bytes 4194304 | tf_op jit(solution)/shard_map/all_to_all | solution.py:761
  103.6 8.6 %collective-permute-start.20 = (bf16[1024,256]{1,0:T(8,128)(2,1)S(1)}, bf16[1024,256]{1,0:T(8,128)(2,1)S(1)}, u32[]{:S(2)}, u32[]{:S(2)}) collective-permute-start(bf16[1024,256]{1,0:T(8,128)(2,1)S(1)} %constant_dynamic-update-slice_fusion.12.half0), channel_id=1, source_target_pairs={{0,1},{1,0},{2,3},{3,2},{4,5},{5,4},{6,7},{7,6},{8,9},{9,8},{10,11... | collective-permute-start | bytes 1572872 | tf_op jit(solution)/shard_map/ppermute | solution.py:669
  128.7 14.4 %collective-permute-start.22 = (bf16[256,256]{1,0:T(8,128)(2,1)S(1)}, bf16[256,256]{1,0:T(8,128)(2,1)S(1)}, u32[]{:S(2)}, u32[]{:S(2)}) collective-permute-start(bf16[256,256]{1,0:T(8,128)(2,1)S(1)} %get-tuple-element.120), channel_id=1, source_target_pairs={{0,2},{1,3},{2,0},{3,1},{4,6},{5,7},{6,4},{7,5},{8,10},{9,11},{10,... | collective-permute-start | bytes 393224 | tf_op jit(solution)/shard_map/ppermute | solution.py:669
  131.1 12.1 %collective-permute-start.23 = (bf16[256,256]{1,0:T(8,128)(2,1)S(1)}, bf16[256,256]{1,0:T(8,128)(2,1)S(1)}, u32[]{:S(2)}, u32[]{:S(2)}) collective-permute-start(bf16[256,256]{1,0:T(8,128)(2,1)S(1)} %get-tuple-element.121), channel_id=1, source_target_pairs={{0,4},{1,5},{2,6},{3,7},{4,0},{5,1},{6,2},{7,3},{8,12},{9,13},{10,... | collective-permute-start | bytes 393224 | tf_op jit(solution)/shard_map/ppermute | solution.py:669
  132.6 10.6 %collective-permute-start.24 = (bf16[256,256]{1,0:T(8,128)(2,1)S(1)}, bf16[256,256]{1,0:T(8,128)(2,1)S(1)}, u32[]{:S(2)}, u32[]{:S(2)}) collective-permute-start(bf16[256,256]{1,0:T(8,128)(2,1)S(1)} %get-tuple-element.122), channel_id=1, source_target_pairs={{0,6},{1,7},{2,4},{3,5},{4,2},{5,3},{6,0},{7,1},{8,14},{9,15},{10,... | collective-permute-start | bytes 393224 | tf_op jit(solution)/shard_map/ppermute | solution.py:669
  143.3 25.5 %collective-permute-start.25 = (f32[64,256]{1,0:T(8,128)S(1)}, f32[64,256]{1,0:T(8,128)S(1)}, u32[]{:S(2)}, u32[]{:S(2)}) collective-permute-start(f32[64,256]{1,0:T(8,128)S(1)} %get-tuple-element.131), channel_id=1, source_target_pairs={{0,8},{1,9},{2,10},{3,11},{4,12},{5,13},{6,14},{7,15},{8,0},{9,1},... | collective-permute-start | bytes 196616 | tf_op jit(solution)/shard_map/ppermute | solution.py:669
  146.8 22.0 %collective-permute-start.26 = (f32[64,256]{1,0:T(8,128)S(1)}, f32[64,256]{1,0:T(8,128)S(1)}, u32[]{:S(2)}, u32[]{:S(2)}) collective-permute-start(f32[64,256]{1,0:T(8,128)S(1)} %get-tuple-element.132), channel_id=1, source_target_pairs={{0,16},{1,17},{2,18},{3,19},{4,20},{5,21},{6,22},{7,23},{8,24},{9,... | collective-permute-start | bytes 196616 | tf_op jit(solution)/shard_map/ppermute | solution.py:669
  146.8 22.0 %collective-permute-start.27 = (f32[64,256]{1,0:T(8,128)S(1)}, f32[64,256]{1,0:T(8,128)S(1)}, u32[]{:S(2)}, u32[]{:S(2)}) collective-permute-start(f32[64,256]{1,0:T(8,128)S(1)} %get-tuple-element.133), channel_id=1, source_target_pairs={{0,24},{1,25},{2,26},{3,27},{4,28},{5,29},{6,30},{7,31},{8,16},{9,... | collective-permute-start | bytes 196616 | tf_op jit(solution)/shard_map/ppermute | solution.py:669
  (17 other events, 186.8 us)

commit v4 on v3

--- a/solution.py
+++ b/solution.py
@@ -223,7 +223,7 @@
 ):
     hub_count, block_size, width = hubs.shape
     hub_rows = hub_count * block_size
-    local = mine.shape[0]
+    local = mine.shape[0] // digits[-1][1]
     begin = rows.shape[0] - cols.shape[0]
     found = list_slots(rows, count, picked, begin, hub_count, True)
     start_tiles(picked, found, tiles_hbm, tiles, sems)
@@ -248,7 +248,10 @@
     add_products(rows, cols, picked, found, begin, tiles, hubs, own, total, 0, hub_count)
     split_sums(me, total[:hub_count], local, kept, sent)
     flat = hubs.reshape(hub_rows, width)
-    mine[...] = flat[pl.ds(pl.multiple_of(me * local, local), local), :]
+    bit, radix = digits[-1]
+    for offset in range(radix):
+        first_row = pl.multiple_of((me ^ (bit * offset)) * local, local)
+        mine[offset * local : (offset + 1) * local, :] = flat[pl.ds(first_row, local), :]
 
 
 def hub_first(digits, rows, cols, count, position, place_col, halves, own, tiles, local):
@@ -264,7 +267,7 @@
         14 * MIB,
         (
             shape_of((hub_count, block_size, width), bf16),
-            shape_of((local, width), bf16),
+            shape_of((digits[-1][1] * local, width), bf16),
             half,
             half,
         ),
@@ -352,24 +355,31 @@
     )
 
 
-def combine(position, kept, received, bit, radix, local, sent_type):
+def combine(position, kept, received, bit, radix, local, sent_type, together=False):
     rows = kept.shape[0] // radix
     width = kept.shape[1]
+    if together:
+        shapes = [shape_of(kept.shape, sent_type)]
+    else:
+        shapes = [shape_of((rows, width), f32)] + [shape_of((rows, width), sent_type)] * (radix - 1)
 
     def kernel(position, kept_in, *refs):
-        received, outs = refs[: -radix], refs[-radix:]
+        received, outs = refs[: -len(shapes)], refs[-len(shapes) :]
         total = kept_in[...].astype(f32)
         for part in received:
             total = total + part[...].astype(f32)
         digit = (position[0] // bit) % radix
         parts = total.reshape(rows // local, radix, local, width)
-        for offset, out in enumerate(outs):
+        for offset in range(radix):
             value = parts[:, 0]
             for number in range(1, radix):
                 value = jnp.where((digit ^ offset) == number, parts[:, number], value)
-            out[...] = value.reshape(rows, width).astype(out.dtype)
-
-    shapes = [shape_of((rows, width), f32)] + [shape_of((rows, width), sent_type)] * (radix - 1)
+            value = value.reshape(rows, width)
+            if together:
+                outs[0][offset * rows : (offset + 1) * rows, :] = value.astype(sent_type)
+            else:
+                outs[offset][...] = value.astype(outs[offset].dtype)
+
     return call(
         kernel,
         "combine",
@@ -378,7 +388,7 @@
         12 * kept.size,
         tuple(shapes),
         [SMEM] + [VMEM] * (1 + len(received)),
-        (VMEM,) * radix,
+        (VMEM,) * len(shapes),
         [],
         (position, kept) + tuple(received),
     )
@@ -394,20 +404,24 @@
     return loads
 
 
-def hub_network_kernel(layer, rows_in, *refs):
+def hub_network_kernel(layer, local, rows_in, *refs):
     parts, (first_in, second_in, out, first, second, sems) = refs[:-6], refs[-6:]
     loads = load_weights(layer, first_in, second_in, first, second, sems)
     u = rows_in[...].astype(f32)
-    for part in parts:
-        u = u + part[...].astype(f32)
+    for mask, part in enumerate(parts):
+        if rows_in.shape[0] == local:
+            u = u + part[...].astype(f32)
+        else:
+            pieces = [part[(offset ^ mask) * local :][:local] for offset in range(len(parts))]
+            u = u + jnp.concatenate(pieces, axis=0).astype(f32)
     for load in loads:
         load.wait()
-    out[...] = network(u, first, second, first.shape[-1])
-
-
-def hub_network(layer, rows_in, parts, first, second):
+    out[...] = network(u, first, second, 512)
+
+
+def hub_network(layer, local, rows_in, parts, first, second):
     return call(
-        functools.partial(hub_network_kernel, layer),
+        functools.partial(hub_network_kernel, layer, local),
         "hub_network",
         24,
         4 * rows_in.size * first.shape[-1],
@@ -687,7 +701,8 @@
     return gather_step(x, *digits[-1])
 
 
-def gather_near(pieces, digits):
+def gather_near(x, digits):
+    pieces = [x]
     for digit in digits[-2:0:-1]:
         pieces = gather_step(jnp.concatenate(pieces, axis=0), *digit)
     return pieces
@@ -706,10 +721,16 @@
     return kept, received
 
 
-def scatter_far(position, kept, received, digits, local, sent_type):
+def scatter_far(position, kept, received, digits, local):
     bit, radix = digits[-1]
-    kept, *sent = combine(position, kept, received, bit, radix, local, sent_type)
+    kept, *sent = combine(position, kept, received, bit, radix, local, f32)
     return [kept] + [exchange(part, bit * (1 + number)) for number, part in enumerate(sent)]
+
+
+def share_far(position, kept, received, digits, local):
+    bit, radix = digits[-1]
+    (own,) = combine(position, kept, received, bit, radix, local, bf16, together=True)
+    return gather_step(own, bit, radix)
 
 
 def body(
@@ -734,12 +755,10 @@
     )
 
     pieces = gather_far(hubs, digits)
-    own, *pieces = lax.optimization_barrier((own, *pieces))
+    own, rows, cols, *pieces = lax.optimization_barrier((own, rows, cols, *pieces))
     outgoing = pack(send_list, own)
-    pieces = gather_near(pieces, digits)
-    outgoing, rows, cols, place_col, *pieces = lax.optimization_barrier(
-        (outgoing, rows, cols, place_col, *pieces)
-    )
+    pieces = gather_near(jnp.concatenate(pieces, axis=0), digits)
+    outgoing, place_col, *pieces = lax.optimization_barrier((outgoing, place_col, *pieces))
     incoming = all_to_all(outgoing)
     halves = gather_last(pieces, digits)
     hub_table, mine, kept, sent = hub_first(
@@ -748,15 +767,14 @@
     base, done = before(0, rows, cols, tile_count, hub_table, own, tiles, w_in, w_out)
     kept, received = scatter_near(me, kept, sent, digits, local)
     base, done, *received = lax.optimization_barrier((base, done, *received))
-    parts = scatter_far(me, kept, received, digits, local, bf16)
-    hub_new = hub_network(0, mine, parts, w_in, w_out)
-    pieces = gather_far(hub_new, digits)
-    base, *pieces = lax.optimization_barrier((base, *pieces))
+    parts = share_far(me, kept, received, digits, local)
     done, sums, outgoing = after(
         0, rows, send_list, base, done, incoming, tiles, w_in, w_out, hub_count, True
     )
-
-    pieces = gather_near(pieces, digits)
+    outgoing, *parts = lax.optimization_barrier((outgoing, *parts))
+    hub_new = hub_network(0, local, mine, parts, w_in, w_out)
+
+    pieces = gather_near(hub_new, digits)
     outgoing, *pieces = lax.optimization_barrier((outgoing, *pieces))
     incoming = all_to_all(outgoing)
     own = late(0, rows, send_list, sums, done, w_in, w_out, hub_count)
@@ -767,12 +785,12 @@
     base, done = before(1, rows, cols, tile_count, hub_table, own, tiles, w_in, w_out)
     kept, received = scatter_near(me, kept, sent, digits, local)
     base, done, *received = lax.optimization_barrier((base, done, *received))
-    parts = scatter_far(me, kept, received, digits, local, f32)
+    parts = scatter_far(me, kept, received, digits, local)
     (peri_out,) = after(
         1, rows, send_list, base, done, incoming, tiles, w_in, w_out, hub_count, False
     )
     peri_out, *parts = lax.optimization_barrier((peri_out, *parts))
-    hub_out = hub_network(1, mine, parts, w_in, w_out)
+    hub_out = hub_network(1, local, mine, parts, w_in, w_out)
     return (peri_out.reshape(peripheral.shape), hub_out)
 
 

time: 172 us -> 175 us (1.017)
  waiting for transfers between devices: 35.8 us -> 44.8 us
  starting transfers between devices: 51.1 us -> 43.5 us
    all_to_all x2, waiting for transfers between devices: 6.46 us -> 28.3 us  [body(): incoming = all_to_all(outgoing)]
    ppermute x28 -> x25, waiting for transfers between devices: 29.3 us -> 16.5 us  [exchange(): return lax.ppermute(x, 'dev', [(i, i ^ bit) for i in range(devices)])]
    ppermute x28 -> x25, starting transfers between devices: 42 us -> 36.4 us  [exchange(): return lax.ppermute(x, 'dev', [(i, i ^ bit) for i in range(devices)])]
    pallas_call x2, Pallas kernels: 24 us -> 28.6 us  [after(): pl.pallas_call(functools.partial(after_kernel, layer, with_send, hub_coun...]
    all_to_all x2, starting transfers between devices: 9.13 us -> 7.07 us  [body(): incoming = all_to_all(outgoing)]
  transfers between devices with their start and end apart: 30 -> 27, of which waited for: 13 -> 11; matrix products, arithmetic and copies ran while one was open for 1% -> 1% of each run, Pallas kernels for 45% -> 44%
where the time goes in v4:
time: 175 us; the launch traced here: 174 us
  Pallas kernels  79.6 us (45%)
  waiting for transfers between devices  44.8 us (26%)
  starting transfers between devices  43.5 us (25%)
  local copies, waits for them, and re-layouts  3.2 us (2%)
  between operations  1.84 us (1%)
    pallas_call x11, Pallas kernels, call(): pl.pallas_call(kernel, out_shape=out_shape, in_specs=in_specs, out_specs=...  44.4 us
    ppermute x25, starting transfers between devices, exchange(): return lax.ppermute(x, 'dev', [(i, i ^ bit) for i in range(devices)])  36.4 us
    pallas_call x2, Pallas kernels, after(): pl.pallas_call(functools.partial(after_kernel, layer, with_send, hub_coun...  28.6 us
    all_to_all x2, waiting for transfers between devices, body(): incoming = all_to_all(outgoing)  28.3 us
    ppermute x25, waiting for transfers between devices, exchange(): return lax.ppermute(x, 'dev', [(i, i ^ bit) for i in range(devices)])  16.5 us
    all_to_all x2, starting transfers between devices, body(): incoming = all_to_all(outgoing)  7.07 us
    pallas_call x1, Pallas kernels, late(): pl.pallas_call(functools.partial(late_kernel, layer, chosen.shape[1], hub...  6.63 us
  transfers between devices with their start and end apart: 27, of which 11 were waited for; matrix products, arithmetic and copies ran while one was open for 1% of the time, Pallas kernels for 44%

profile of v4, /device:TPU:0, one launch (start us, length us, event | category | flops | bytes accessed | tf_op | source)
XLA Modules:
  0.0 174.2 jit_solution(8901951640203245622)
XLA Ops:
  0.6 4.1 %collective-permute-start.1 = (bf16[64,256]{1,0:T(8,128)(2,1)}, bf16[64,256]{1,0:T(8,128)(2,1)S(1)}, u32[]{:S(2)}, u32[]{:S(2)}) collective-permute-start(bf16[64,256]{1,0:T(8,128)(2,1)} %param.11), channel_id=1, source_target_pairs={{0,16},{1,17},{2,18},{3,19},{4,20},{5,21},{6,22},{7,23},{8,24},{9,... | collective-permute-start | bytes 98312 | tf_op jit(solution)/shard_map/ppermute | solution.py:683
  8.9 3.4 %collective-permute-done.2 = bf16[64,256]{1,0:T(8,128)(2,1)S(1)} collective-permute-done((bf16[64,256]{1,0:T(8,128)(2,1)}, bf16[64,256]{1,0:T(8,128)(2,1)S(1)}, u32[]{:S(2)}, u32[]{:S(2)}) %collective-permute-start.2) | collective-permute-done | bytes 32800 | tf_op jit(solution)/shard_map/ppermute | solution.py:683
  13.0 2.5 %collective-permute-start.5 = (bf16[256,256]{1,0:T(8,128)(2,1)S(1)}, bf16[256,256]{1,0:T(8,128)(2,1)S(1)}, u32[]{:S(2)}, u32[]{:S(2)}) collective-permute-start(bf16[256,256]{1,0:T(8,128)(2,1)S(1)} %constant_dynamic-update-slice_fusion), channel_id=1, source_target_pairs={{0,6},{1,7},{2,4},{3,5},{4,2},{5,3},{6,0},{7,1},{8,14},{9,15},{10,... | collective-permute-start | bytes 393224 | tf_op jit(solution)/shard_map/ppermute | solution.py:683
  16.6 3.8 %pack.1 = bf16[32,128,256]{2,1,0:T(8,128)(2,1)} custom-call(s32[1,32]{1,0:T(1,128)} %chosen.7, bf16[32,128,256]{2,1,0:T(8,128)(2,1)} %bitcast.7), custom_call_target="tpu_custom_call" | custom-call | bytes 4194304 | tf_op jit(solution)/shard_map/pack/pallas_call | solution.py:30
  21.1 3.6 %all-to-all-start = ((bf16[32,128,256]{2,1,0:T(8,128)(2,1)}), bf16[32,128,256]{2,1,0:T(8,128)(2,1)}, u32[]{:S(2)}, u32[]{:S(2)}) async-start(bf16[32,128,256]{2,1,0:T(8,128)(2,1)} %pack.1), calls=%async_computation | async-start | bytes 4194304 | tf_op jit(solution)/shard_map/all_to_all | solution.py:762
  26.8 6.3 %hub_first.1 = (bf16[16,128,256]{2,1,0:T(8,128)(2,1)S(1)}, bf16[256,256]{1,0:T(8,128)(2,1)S(1)}, f32[1024,256]{1,0:T(8,128)S(1)}, f32[1024,256]{1,0:T(8,128)S(1)}) custom-call(s32[144]{0:T(256)S(1)} %compare_select_fusion.rows, s32[112]{0:T(128)S(1)} %compare_select_fusion.1.cols, s32[1]{0:T(128)S(6)} %copy.30.count, s32[1]{0:T(128)} %bitcast.1.position, ...), custom_call_target="tpu_custom_call" | custom-call | flops 2147483648 | bytes 14680064 | tf_op jit(solution)/shard_map/hub_first/pallas_call | solution.py:30
  34.7 2.3 %collective-permute-done.7.refs_0_ = f32[1024,256]{1,0:T(8,128)S(1)} collective-permute-done((f32[1024,256]{1,0:T(8,128)S(1)}, f32[1024,256]{1,0:T(8,128)S(1)}, u32[]{:S(2)}, u32[]{:S(2)}) %collective-permute-start.7) | collective-permute-done | bytes 1048608 | tf_op jit(solution)/shard_map/ppermute | solution.py:683
  38.5 5.2 %collective-permute-start.9 = (bf16[256,256]{1,0:T(8,128)(2,1)S(1)}, bf16[256,256]{1,0:T(8,128)(2,1)S(1)}, u32[]{:S(2)}, u32[]{:S(2)}) collective-permute-start(bf16[256,256]{1,0:T(8,128)(2,1)S(1)} %get-tuple-element.85), channel_id=1, source_target_pairs={{0,4},{1,5},{2,6},{3,7},{4,0},{5,1},{6,2},{7,3},{8,12},{9,13},{10,... | collective-permute-start | bytes 393224 | tf_op jit(solution)/shard_map/ppermute | solution.py:683
  43.7 10.4 %before.2 = (f32[32,128,256]{2,1,0:T(8,128)}, bf16[32,128,256]{2,1,0:T(8,128)(2,1)}) custom-call(s32[144]{0:T(256)} %copy-done.6, s32[112]{0:T(128)} %copy-done.9, s32[1]{0:T(128)S(6)} %copy.30.count, bf16[16,128,256]{2,1,0:T(8,128)(2,1)} %copy-done.5, bf16[32,128,256]{2,1,0:T(8,128)(2,1)} %bitcast.9, bf16[144,128,128]{2,1,0:T(8,128)(2,1)} %tiles.3, ...), custom_call_target="tpu_custom_call" | custom-call | flops 2863311616 | bytes 18874368 | tf_op jit(solution)/shard_map/before/pallas_call | solution.py:30
  57.8 2.9 %collective-permute-start.11 = (bf16[256,256]{1,0:T(8,128)(2,1)S(1)}, bf16[256,256]{1,0:T(8,128)(2,1)S(1)}, u32[]{:S(2)}, u32[]{:S(2)}) collective-permute-start(bf16[256,256]{1,0:T(8,128)(2,1)S(1)} %combine.5.refs_0_), channel_id=1, source_target_pairs={{0,8},{1,9},{2,10},{3,11},{4,12},{5,13},{6,14},{7,15},{8,0},{9,1},... | collective-permute-start | bytes 393224 | tf_op jit(solution)/shard_map/ppermute | solution.py:683
  60.8 19.1 %all-to-all-done.incoming = bf16[32,128,256]{2,1,0:T(8,128)(2,1)} async-done(((bf16[32,128,256]{2,1,0:T(8,128)(2,1)}), bf16[32,128,256]{2,1,0:T(8,128)(2,1)}, u32[]{:S(2)}, u32[]{:S(2)}) %all-to-all-start) | async-done | bytes 2097184 | tf_op jit(solution)/shard_map/all_to_all | solution.py:762
  79.9 14.0 %after.2 = (bf16[32,128,256]{2,1,0:T(8,128)(2,1)}, f32[32,128,256]{2,1,0:T(8,128)}, bf16[32,128,256]{2,1,0:T(8,128)(2,1)}) custom-call(s32[144]{0:T(256)} %copy-done.6, s32[1,32]{1,0:T(1,128)} %chosen.7, f32[32,128,256]{2,1,0:T(8,128)} %get-tuple-element.87.base, ...), custom_call_target="tpu_custom_call", output_to_operand_aliasing={{0}: (3, {}), {1}: (2, {})} | custom-call | flops 8589934592 | bytes 16777216 | tf_op jit(solution)/shard_map/after/pallas_call | solution.py:600
  96.0 2.7 %collective-permute-start.14 = (bf16[256,256]{1,0:T(8,128)(2,1)S(1)}, bf16[256,256]{1,0:T(8,128)(2,1)S(1)}, u32[]{:S(2)}, u32[]{:S(2)}) collective-permute-start(bf16[256,256]{1,0:T(8,128)(2,1)S(1)} %hub_network.2), channel_id=1, source_target_pairs={{0,2},{1,3},{2,0},{3,1},{4,6},{5,7},{6,4},{7,5},{8,10},{9,11},{10,... | collective-permute-start | bytes 393224 | tf_op jit(solution)/shard_map/ppermute | solution.py:683
  98.7 2.9 %collective-permute-done.16 = bf16[256,256]{1,0:T(8,128)(2,1)S(1)} collective-permute-done((bf16[256,256]{1,0:T(8,128)(2,1)S(1)}, bf16[256,256]{1,0:T(8,128)(2,1)S(1)}, u32[]{:S(2)}, u32[]{:S(2)}) %collective-permute-start.16) | collective-permute-done | bytes 131104 | tf_op jit(solution)/shard_map/ppermute | solution.py:683
  102.3 3.5 %all-to-all-start.1 = ((bf16[32,128,256]{2,1,0:T(8,128)(2,1)}), bf16[32,128,256]{2,1,0:T(8,128)(2,1)}, u32[]{:S(2)}, u32[]{:S(2)}) async-start(bf16[32,128,256]{2,1,0:T(8,128)(2,1)} %get-tuple-element.117), calls=%async_computation.1 | async-start | bytes 4194304 | tf_op jit(solution)/shard_map/all_to_all | solution.py:779
  106.0 6.6 %late.1.own_hbm.own_in = bf16[32,128,256]{2,1,0:T(8,128)(2,1)} custom-call(s32[144]{0:T(256)} %copy-done.6, s32[1,32]{1,0:T(1,128)} %chosen.7, f32[32,128,256]{2,1,0:T(8,128)} %get-tuple-element.105.sums, bf16[32,128,256]{2,1,0:T(8,128)(2,1)} %get-tuple-element.106.done, bf16[2,256,2048]{2,1,0:T(8,128)(2,1)} %refs_4_.3, ...), custom_call_target="tpu_custom_call", output_to_operand_aliasing={{}: (3, {})} | custom-call | flops 2147483648 | bytes 5242880 | tf_op jit(solution)/shard_map/late/pallas_call | solution.py:656
  112.7 10.2 %hub_second.1 = (bf16[16,128,256]{2,1,0:T(8,128)(2,1)S(1)}, bf16[64,256]{1,0:T(8,128)(2,1)S(1)}, f32[1024,256]{1,0:T(8,128)S(1)}, f32[1024,256]{1,0:T(8,128)S(1)}) custom-call(s32[144]{0:T(256)S(1)} %copy-done.7, s32[112]{0:T(128)S(1)} %copy-done.10, s32[1]{0:T(128)S(6)} %copy.30.count, s32[1]{0:T(128)} %bitcast.1.position, s32[1,2048]{1,0:T(1,128)S(1)} %bitcast.6, ...), custom_call_target="tpu_custom_call" | custom-call | flops 2147483648 | bytes 14680064 | tf_op jit(solution)/shard_map/hub_second/pallas_call | solution.py:30
  125.0 2.3 %collective-permute-done.18.refs_0_ = f32[1024,256]{1,0:T(8,128)S(1)} collective-permute-done((f32[1024,256]{1,0:T(8,128)S(1)}, f32[1024,256]{1,0:T(8,128)S(1)}, u32[]{:S(2)}, u32[]{:S(2)}) %collective-permute-start.18) | collective-permute-done | bytes 1048608 | tf_op jit(solution)/shard_map/ppermute | solution.py:683
  127.5 2.5 %collective-permute-start.19 = (bf16[256,256]{1,0:T(8,128)(2,1)S(1)}, bf16[256,256]{1,0:T(8,128)(2,1)S(1)}, u32[]{:S(2)}, u32[]{:S(2)}) collective-permute-start(bf16[256,256]{1,0:T(8,128)(2,1)S(1)} %get-tuple-element.112), channel_id=1, source_target_pairs={{0,2},{1,3},{2,0},{3,1},{4,6},{5,7},{6,4},{7,5},{8,10},{9,11},{10,... | collective-permute-start | bytes 393224 | tf_op jit(solution)/shard_map/ppermute | solution.py:683
  130.0 3.8 %collective-permute-start.20 = (bf16[256,256]{1,0:T(8,128)(2,1)S(1)}, bf16[256,256]{1,0:T(8,128)(2,1)S(1)}, u32[]{:S(2)}, u32[]{:S(2)}) collective-permute-start(bf16[256,256]{1,0:T(8,128)(2,1)S(1)} %get-tuple-element.113), channel_id=1, source_target_pairs={{0,4},{1,5},{2,6},{3,7},{4,0},{5,1},{6,2},{7,3},{8,12},{9,13},{10,... | collective-permute-start | bytes 393224 | tf_op jit(solution)/shard_map/ppermute | solution.py:683
  133.9 10.4 %before.3 = (f32[32,128,256]{2,1,0:T(8,128)}, bf16[32,128,256]{2,1,0:T(8,128)(2,1)}) custom-call(s32[144]{0:T(256)} %copy-done.6, s32[112]{0:T(128)} %copy-done.9, s32[1]{0:T(128)S(6)} %copy.30.count, bf16[16,128,256]{2,1,0:T(8,128)(2,1)} %copy-done.4, bf16[32,128,256]{2,1,0:T(8,128)(2,1)} %late.1.own_hbm.own_in, bf16[144,128,128]{2,1,0:T(8,128)(2,1)} %tiles.3, ...), custom_call_target="tpu_custom_call" | custom-call | flops 2863311616 | bytes 18874368 | tf_op jit(solution)/shard_map/before/pallas_call | solution.py:30
  145.9 2.8 %collective-permute-start.23 = (f32[64,256]{1,0:T(8,128)S(1)}, f32[64,256]{1,0:T(8,128)S(1)}, u32[]{:S(2)}, u32[]{:S(2)}) collective-permute-start(f32[64,256]{1,0:T(8,128)S(1)} %get-tuple-element.124), channel_id=1, source_target_pairs={{0,16},{1,17},{2,18},{3,19},{4,20},{5,21},{6,22},{7,23},{8,24},{9,... | collective-permute-start | bytes 196616 | tf_op jit(solution)/shard_map/ppermute | solution.py:683
  148.9 9.2 %all-to-all-done.1.incoming = bf16[32,128,256]{2,1,0:T(8,128)(2,1)} async-done(((bf16[32,128,256]{2,1,0:T(8,128)(2,1)}), bf16[32,128,256]{2,1,0:T(8,128)(2,1)}, u32[]{:S(2)}, u32[]{:S(2)}) %all-to-all-start.1) | async-done | bytes 2097184 | tf_op jit(solution)/shard_map/all_to_all | solution.py:779
  158.1 14.5 %after.3 = bf16[32,128,256]{2,1,0:T(8,128)(2,1)} custom-call(s32[144]{0:T(256)} %copy-done.6, s32[1,32]{1,0:T(1,128)} %chosen.7, f32[32,128,256]{2,1,0:T(8,128)} %get-tuple-element.115.base, bf16[32,128,256]{2,1,0:T(8,128)(2,1)} %get-tuple-element.116.done, bf16[32,128,256]{2,1,0:T(8,128)(2,1)} %all-to-all-done.1.incoming, ...), custom_call_target="tpu_custom_call", output_to_operand_aliasing={{}: (3, {})} | custom-call | flops 8589934592 | bytes 16777216 | tf_op jit(solution)/shard_map/after/pallas_call | solution.py:600
  (81 shorter events, 23.3 us)
Async XLA Ops:
  0.6 7.0 %collective-permute-start.1 = (bf16[64,256]{1,0:T(8,128)(2,1)}, bf16[64,256]{1,0:T(8,128)(2,1)S(1)}, u32[]{:S(2)}, u32[]{:S(2)}) collective-permute-start(bf16[64,256]{1,0:T(8,128)(2,1)} %param.11), channel_id=1, source_target_pairs={{0,16},{1,17},{2,18},{3,19},{4,20},{5,21},{6,22},{7,23},{8,24},{9,... | collective-permute-start | bytes 98312 | tf_op jit(solution)/shard_map/ppermute | solution.py:683
  4.7 4.1 %collective-permute-start = (bf16[64,256]{1,0:T(8,128)(2,1)}, bf16[64,256]{1,0:T(8,128)(2,1)S(1)}, u32[]{:S(2)}, u32[]{:S(2)}) collective-permute-start(bf16[64,256]{1,0:T(8,128)(2,1)} %param.11), channel_id=1, source_target_pairs={{0,8},{1,9},{2,10},{3,11},{4,12},{5,13},{6,14},{7,15},{8,0},{9,1},... | collective-permute-start | bytes 98312 | tf_op jit(solution)/shard_map/ppermute | solution.py:683
  6.3 5.9 %collective-permute-start.2 = (bf16[64,256]{1,0:T(8,128)(2,1)}, bf16[64,256]{1,0:T(8,128)(2,1)S(1)}, u32[]{:S(2)}, u32[]{:S(2)}) collective-permute-start(bf16[64,256]{1,0:T(8,128)(2,1)} %param.11), channel_id=1, source_target_pairs={{0,24},{1,25},{2,26},{3,27},{4,28},{5,29},{6,30},{7,31},{8,16},{9,... | collective-permute-start | bytes 98312 | tf_op jit(solution)/shard_map/ppermute | solution.py:683
  13.0 7.4 %collective-permute-start.5 = (bf16[256,256]{1,0:T(8,128)(2,1)S(1)}, bf16[256,256]{1,0:T(8,128)(2,1)S(1)}, u32[]{:S(2)}, u32[]{:S(2)}) collective-permute-start(bf16[256,256]{1,0:T(8,128)(2,1)S(1)} %constant_dynamic-update-slice_fusion), channel_id=1, source_target_pairs={{0,6},{1,7},{2,4},{3,5},{4,2},{5,3},{6,0},{7,1},{8,14},{9,15},{10,... | collective-permute-start | bytes 393224 | tf_op jit(solution)/shard_map/ppermute | solution.py:683
  15.5 5.6 %collective-permute-start.4 = (bf16[256,256]{1,0:T(8,128)(2,1)S(1)}, bf16[256,256]{1,0:T(8,128)(2,1)S(1)}, u32[]{:S(2)}, u32[]{:S(2)}) collective-permute-start(bf16[256,256]{1,0:T(8,128)(2,1)S(1)} %constant_dynamic-update-slice_fusion), channel_id=1, source_target_pairs={{0,4},{1,5},{2,6},{3,7},{4,0},{5,1},{6,2},{7,3},{8,12},{9,13},{10,... | collective-permute-start | bytes 393224 | tf_op jit(solution)/shard_map/ppermute | solution.py:683
  16.0 5.1 %collective-permute-start.3 = (bf16[256,256]{1,0:T(8,128)(2,1)S(1)}, bf16[256,256]{1,0:T(8,128)(2,1)S(1)}, u32[]{:S(2)}, u32[]{:S(2)}) collective-permute-start(bf16[256,256]{1,0:T(8,128)(2,1)S(1)} %constant_dynamic-update-slice_fusion), channel_id=1, source_target_pairs={{0,2},{1,3},{2,0},{3,1},{4,6},{5,7},{6,4},{7,5},{8,10},{9,11},{10,... | collective-permute-start | bytes 393224 | tf_op jit(solution)/shard_map/ppermute | solution.py:683
  21.1 58.7 %all-to-all-start = ((bf16[32,128,256]{2,1,0:T(8,128)(2,1)}), bf16[32,128,256]{2,1,0:T(8,128)(2,1)}, u32[]{:S(2)}, u32[]{:S(2)}) async-start(bf16[32,128,256]{2,1,0:T(8,128)(2,1)} %pack.1), calls=%async_computation | async-start | bytes 4194304 | tf_op jit(solution)/shard_map/all_to_all | solution.py:762
  37.2 16.9 %collective-permute-start.8 = (bf16[256,256]{1,0:T(8,128)(2,1)S(1)}, bf16[256,256]{1,0:T(8,128)(2,1)S(1)}, u32[]{:S(2)}, u32[]{:S(2)}) collective-permute-start(bf16[256,256]{1,0:T(8,128)(2,1)S(1)} %get-tuple-element.84), channel_id=1, source_target_pairs={{0,2},{1,3},{2,0},{3,1},{4,6},{5,7},{6,4},{7,5},{8,10},{9,11},{10,... | collective-permute-start | bytes 393224 | tf_op jit(solution)/shard_map/ppermute | solution.py:683
  38.5 15.6 %collective-permute-start.9 = (bf16[256,256]{1,0:T(8,128)(2,1)S(1)}, bf16[256,256]{1,0:T(8,128)(2,1)S(1)}, u32[]{:S(2)}, u32[]{:S(2)}) collective-permute-start(bf16[256,256]{1,0:T(8,128)(2,1)S(1)} %get-tuple-element.85), channel_id=1, source_target_pairs={{0,4},{1,5},{2,6},{3,7},{4,0},{5,1},{6,2},{7,3},{8,12},{9,13},{10,... | collective-permute-start | bytes 393224 | tf_op jit(solution)/shard_map/ppermute | solution.py:683
  43.7 12.5 %collective-permute-start.10 = (bf16[256,256]{1,0:T(8,128)(2,1)S(1)}, bf16[256,256]{1,0:T(8,128)(2,1)S(1)}, u32[]{:S(2)}, u32[]{:S(2)}) collective-permute-start(bf16[256,256]{1,0:T(8,128)(2,1)S(1)} %get-tuple-element.86), channel_id=1, source_target_pairs={{0,6},{1,7},{2,4},{3,5},{4,2},{5,3},{6,0},{7,1},{8,14},{9,15},{10,... | collective-permute-start | bytes 393224 | tf_op jit(solution)/shard_map/ppermute | solution.py:683
  56.3 37.6 %collective-permute-start.13 = (bf16[256,256]{1,0:T(8,128)(2,1)S(1)}, bf16[256,256]{1,0:T(8,128)(2,1)S(1)}, u32[]{:S(2)}, u32[]{:S(2)}) collective-permute-start(bf16[256,256]{1,0:T(8,128)(2,1)S(1)} %combine.5.refs_0_), channel_id=1, source_target_pairs={{0,24},{1,25},{2,26},{3,27},{4,28},{5,29},{6,30},{7,31},{8,16},{9,... | collective-permute-start | bytes 393224 | tf_op jit(solution)/shard_map/ppermute | solution.py:683
  56.5 37.4 %collective-permute-start.12 = (bf16[256,256]{1,0:T(8,128)(2,1)S(1)}, bf16[256,256]{1,0:T(8,128)(2,1)S(1)}, u32[]{:S(2)}, u32[]{:S(2)}) collective-permute-start(bf16[256,256]{1,0:T(8,128)(2,1)S(1)} %combine.5.refs_0_), channel_id=1, source_target_pairs={{0,16},{1,17},{2,18},{3,19},{4,20},{5,21},{6,22},{7,23},{8,24},{9,... | collective-permute-start | bytes 393224 | tf_op jit(solution)/shard_map/ppermute | solution.py:683
  57.8 36.1 %collective-permute-start.11 = (bf16[256,256]{1,0:T(8,128)(2,1)S(1)}, bf16[256,256]{1,0:T(8,128)(2,1)S(1)}, u32[]{:S(2)}, u32[]{:S(2)}) collective-permute-start(bf16[256,256]{1,0:T(8,128)(2,1)S(1)} %combine.5.refs_0_), channel_id=1, source_target_pairs={{0,8},{1,9},{2,10},{3,11},{4,12},{5,13},{6,14},{7,15},{8,0},{9,1},... | collective-permute-start | bytes 393224 | tf_op jit(solution)/shard_map/ppermute | solution.py:683
  95.1 6.4 %collective-permute-start.16 = (bf16[256,256]{1,0:T(8,128)(2,1)S(1)}, bf16[256,256]{1,0:T(8,128)(2,1)S(1)}, u32[]{:S(2)}, u32[]{:S(2)}) collective-permute-start(bf16[256,256]{1,0:T(8,128)(2,1)S(1)} %hub_network.2), channel_id=1, source_target_pairs={{0,6},{1,7},{2,4},{3,5},{4,2},{5,3},{6,0},{7,1},{8,14},{9,15},{10,... | collective-permute-start | bytes 393224 | tf_op jit(solution)/shard_map/ppermute | solution.py:683
  96.0 6.4 %collective-permute-start.15 = (bf16[256,256]{1,0:T(8,128)(2,1)S(1)}, bf16[256,256]{1,0:T(8,128)(2,1)S(1)}, u32[]{:S(2)}, u32[]{:S(2)}) collective-permute-start(bf16[256,256]{1,0:T(8,128)(2,1)S(1)} %hub_network.2), channel_id=1, source_target_pairs={{0,4},{1,5},{2,6},{3,7},{4,0},{5,1},{6,2},{7,3},{8,12},{9,13},{10,... | collective-permute-start | bytes 393224 | tf_op jit(solution)/shard_map/ppermute | solution.py:683
  96.0 6.4 %collective-permute-start.14 = (bf16[256,256]{1,0:T(8,128)(2,1)S(1)}, bf16[256,256]{1,0:T(8,128)(2,1)S(1)}, u32[]{:S(2)}, u32[]{:S(2)}) collective-permute-start(bf16[256,256]{1,0:T(8,128)(2,1)S(1)} %hub_network.2), channel_id=1, source_target_pairs={{0,2},{1,3},{2,0},{3,1},{4,6},{5,7},{6,4},{7,5},{8,10},{9,11},{10,... | collective-permute-start | bytes 393224 | tf_op jit(solution)/shard_map/ppermute | solution.py:683
  102.3 55.8 %all-to-all-start.1 = ((bf16[32,128,256]{2,1,0:T(8,128)(2,1)}), bf16[32,128,256]{2,1,0:T(8,128)(2,1)}, u32[]{:S(2)}, u32[]{:S(2)}) async-start(bf16[32,128,256]{2,1,0:T(8,128)(2,1)} %get-tuple-element.117), calls=%async_computation.1 | async-start | bytes 4194304 | tf_op jit(solution)/shard_map/all_to_all | solution.py:779
  105.9 6.7 %collective-permute-start.17 = (bf16[1024,256]{1,0:T(8,128)(2,1)S(1)}, bf16[1024,256]{1,0:T(8,128)(2,1)S(1)}, u32[]{:S(2)}, u32[]{:S(2)}) collective-permute-start(bf16[1024,256]{1,0:T(8,128)(2,1)S(1)} %constant_dynamic-update-slice_fusion.8.half0), channel_id=1, source_target_pairs={{0,1},{1,0},{2,3},{3,2},{4,5},{5,4},{6,7},{7,6},{8,9},{9,8},{10,11... | collective-permute-start | bytes 1572872 | tf_op jit(solution)/shard_map/ppermute | solution.py:683
  127.5 16.8 %collective-permute-start.19 = (bf16[256,256]{1,0:T(8,128)(2,1)S(1)}, bf16[256,256]{1,0:T(8,128)(2,1)S(1)}, u32[]{:S(2)}, u32[]{:S(2)}) collective-permute-start(bf16[256,256]{1,0:T(8,128)(2,1)S(1)} %get-tuple-element.112), channel_id=1, source_target_pairs={{0,2},{1,3},{2,0},{3,1},{4,6},{5,7},{6,4},{7,5},{8,10},{9,11},{10,... | collective-permute-start | bytes 393224 | tf_op jit(solution)/shard_map/ppermute | solution.py:683
  130.0 14.3 %collective-permute-start.20 = (bf16[256,256]{1,0:T(8,128)(2,1)S(1)}, bf16[256,256]{1,0:T(8,128)(2,1)S(1)}, u32[]{:S(2)}, u32[]{:S(2)}) collective-permute-start(bf16[256,256]{1,0:T(8,128)(2,1)S(1)} %get-tuple-element.113), channel_id=1, source_target_pairs={{0,4},{1,5},{2,6},{3,7},{4,0},{5,1},{6,2},{7,3},{8,12},{9,13},{10,... | collective-permute-start | bytes 393224 | tf_op jit(solution)/shard_map/ppermute | solution.py:683
  133.8 10.5 %collective-permute-start.21 = (bf16[256,256]{1,0:T(8,128)(2,1)S(1)}, bf16[256,256]{1,0:T(8,128)(2,1)S(1)}, u32[]{:S(2)}, u32[]{:S(2)}) collective-permute-start(bf16[256,256]{1,0:T(8,128)(2,1)S(1)} %get-tuple-element.114), channel_id=1, source_target_pairs={{0,6},{1,7},{2,4},{3,5},{4,2},{5,3},{6,0},{7,1},{8,14},{9,15},{10,... | collective-permute-start | bytes 393224 | tf_op jit(solution)/shard_map/ppermute | solution.py:683
  144.4 28.2 %collective-permute-start.22 = (f32[64,256]{1,0:T(8,128)S(1)}, f32[64,256]{1,0:T(8,128)S(1)}, u32[]{:S(2)}, u32[]{:S(2)}) collective-permute-start(f32[64,256]{1,0:T(8,128)S(1)} %get-tuple-element.123), channel_id=1, source_target_pairs={{0,8},{1,9},{2,10},{3,11},{4,12},{5,13},{6,14},{7,15},{8,0},{9,1},... | collective-permute-start | bytes 196616 | tf_op jit(solution)/shard_map/ppermute | solution.py:683
  145.9 26.8 %collective-permute-start.23 = (f32[64,256]{1,0:T(8,128)S(1)}, f32[64,256]{1,0:T(8,128)S(1)}, u32[]{:S(2)}, u32[]{:S(2)}) collective-permute-start(f32[64,256]{1,0:T(8,128)S(1)} %get-tuple-element.124), channel_id=1, source_target_pairs={{0,16},{1,17},{2,18},{3,19},{4,20},{5,21},{6,22},{7,23},{8,24},{9,... | collective-permute-start | bytes 196616 | tf_op jit(solution)/shard_map/ppermute | solution.py:683
  148.6 24.0 %collective-permute-start.24 = (f32[64,256]{1,0:T(8,128)S(1)}, f32[64,256]{1,0:T(8,128)S(1)}, u32[]{:S(2)}, u32[]{:S(2)}) collective-permute-start(f32[64,256]{1,0:T(8,128)S(1)} %get-tuple-element.125), channel_id=1, source_target_pairs={{0,24},{1,25},{2,26},{3,27},{4,28},{5,29},{6,30},{7,31},{8,16},{9,... | collective-permute-start | bytes 196616 | tf_op jit(solution)/shard_map/ppermute | solution.py:683
  (14 other events, 157.3 us)

commit v5 on v3

v5 whole, which is shorter than its diff:
```python
import functools

import jax
import jax.numpy as jnp
from jax import lax
from jax.experimental import pallas as pl
from jax.experimental.pallas import tpu as pltpu
from jax.sharding import PartitionSpec as P

epsilon = 1e-06
f32 = jnp.float32
bf16 = jnp.bfloat16
MIB = 1024 * 1024
VMEM = pl.BlockSpec(memory_space=pltpu.VMEM)
SMEM = pl.BlockSpec(memory_space=pltpu.SMEM)
ANY = pl.BlockSpec(memory_space=pl.ANY)
GROUP = 4
SLOTS = 8


def dot(a, b):
    return jnp.dot(a, b, preferred_element_type=f32)


def shape_of(shape, dtype):
    return jax.ShapeDtypeStruct(tuple(shape), dtype)


def call(kernel, name, mib, flops, moved, out_shape, in_specs, out_specs, scratch, args):
    return pl.pallas_call(
        kernel,
        out_shape=out_shape,
        in_specs=in_specs,
        out_specs=out_specs,
        scratch_shapes=scratch,
        compiler_params=pltpu.CompilerParams(vmem_limit_bytes=mib * MIB),
        cost_estimate=pl.CostEstimate(flops=flops, bytes_accessed=moved, transcendentals=0),
        name=name,
    )(*args)


def normalise(u):
    return (u * lax.rsqrt(jnp.mean(u * u, axis=-1, keepdims=True) + epsilon)).astype(bf16)


def network(u, first, second, hidden_step):
    normed = normalise(u)
    total = u
    for start in range(0, first.shape[-1], hidden_step):
        cut = slice(start, start + hidden_step)
        hidden = jnp.maximum(dot(normed, first[:, cut]), 0.0).astype(bf16)
        total = total + dot(hidden, second[cut, :])
    return total.astype(bf16)


SLOT, ROW, COL, BLOCK, REMOTE, GOING, COUNTS = range(7)
N_HUB, N_OWN, N_NOW, N_FED, N_HELD = range(5)


def ranked(key, size):
    down = lax.broadcasted_iota(jnp.int32, (size, size), 0)
    along = lax.broadcasted_iota(jnp.int32, (size, size), 1)
    wide = jnp.broadcast_to(key, (size, size))
    tall = jnp.sum(jnp.where(down == along, wide, 0), axis=1, keepdims=True)
    ahead = (wide < tall) | ((wide == tall) & (along < down))
    return jnp.sum(ahead.astype(jnp.int32), axis=1, keepdims=True)


def plan_kernel(hub_count, own_count, remote, position, count, rows_in, cols_in, chosen, plan):
    capacity = rows_in.shape[1]
    shift = position[0] * own_count
    rows = jnp.where(rows_in[...] < hub_count, rows_in[...], rows_in[...] - shift)
    cols = jnp.where(cols_in[...] < hub_count, cols_in[...], cols_in[...] - shift)
    plan[...] = jnp.zeros_like(plan)
    slot = lax.broadcasted_iota(jnp.int32, (1, capacity), 1)
    picked = (slot >= remote) & (slot < count[0])
    of_hub = picked & (rows < hub_count)
    of_own = picked & (rows >= hub_count)
    key = jnp.where(of_hub, 0, jnp.where(of_own, 1, 2))
    place = ranked(key, capacity)
    down = lax.broadcasted_iota(jnp.int32, (capacity, capacity), 0)
    along = lax.broadcasted_iota(jnp.int32, (capacity, capacity), 1)
    here = place == along

    def column(row):
        wide = jnp.broadcast_to(row, (capacity, capacity))
        return jnp.sum(jnp.where(down == along, wide, 0), axis=1, keepdims=True)

    def ordered(values):
        return jnp.sum(jnp.where(here, values, 0), axis=0, keepdims=True)

    plan[SLOT : SLOT + 1, :capacity] = ordered(down)
    plan[ROW : ROW + 1, :capacity] = ordered(column(rows))
    plan[COL : COL + 1, :capacity] = ordered(column(cols))

    block = lax.broadcasted_iota(jnp.int32, (own_count, remote), 0)
    target = rows[:, :remote] - hub_count
    fed = jnp.max((block == target).astype(jnp.int32), axis=1, keepdims=True)
    sent = jnp.max((block == chosen[...]).astype(jnp.int32), axis=1, keepdims=True)
    key = 3 - 2 * fed - sent
    down = lax.broadcasted_iota(jnp.int32, (own_count, own_count), 0)
    along = lax.broadcasted_iota(jnp.int32, (own_count, own_count), 1)
    row_key = jnp.sum(jnp.where(down == along, key, 0), axis=0, keepdims=True)
    place = ranked(row_key, own_count)
    plan[BLOCK : BLOCK + 1, :own_count] = jnp.sum(
        jnp.where(place == along, down, 0), axis=0, keepdims=True
    )
    plan[REMOTE : REMOTE + 1, :remote] = jnp.sum(
        jnp.where(block == target, place, 0), axis=0, keepdims=True
    )
    plan[GOING : GOING + 1, :remote] = jnp.sum(
        jnp.where(block == chosen[...], place, 0), axis=0, keepdims=True
    )
    numbers = [
        jnp.sum(of_hub.astype(jnp.int32), axis=1, keepdims=True),
        jnp.sum(of_own.astype(jnp.int32), axis=1, keepdims=True),
        jnp.sum((row_key < 1).astype(jnp.int32), axis=1, keepdims=True),
        jnp.sum((row_key < 2).astype(jnp.int32), axis=1, keepdims=True),
        jnp.sum((row_key < 3).astype(jnp.int32), axis=1, keepdims=True),
    ]
    lane = lax.broadcasted_iota(jnp.int32, (1, plan.shape[1]), 1)
    counts = jnp.zeros((1, plan.shape[1]), jnp.int32)
    for place, number in enumerate(numbers):
        counts = jnp.where(lane == place, number, counts)
    plan[COUNTS : COUNTS + 1, :] = counts


def make_plan(position, count, rows, cols, chosen, hub_count, own_count):
    capacity, remote = rows.shape[0], chosen.shape[1]
    wide = -(-max(capacity, own_count, remote) // 128) * 128
    cols = jnp.concatenate([jnp.zeros((remote,), jnp.int32), cols])
    return call(
        functools.partial(plan_kernel, hub_count, own_count, remote),
        "plan",
        24,
        10**6,
        10**4,
        shape_of((8, wide), jnp.int32),
        [SMEM, SMEM, VMEM, VMEM, VMEM],
        VMEM,
        [],
        (position, count, rows.reshape(1, capacity), cols.reshape(1, capacity), chosen),
    )


def tile_loads(source, tiles, sems):
    remote = source.shape[0] - tiles.shape[0]
    size = tiles.shape[0] // 4
    loads = []
    for part in range(4):
        cut = pl.ds(remote + part * size, size)
        copy = pltpu.make_async_copy(source.at[cut], tiles.at[pl.ds(part * size, size)], sems.at[part])
        loads.append((remote + part * size, copy))
    return loads


def for_live(count, loads, act):
    for first_slot, load in loads:

        @pl.when(count[0] > first_slot)
        def _(load=load):
            act(load)


def add_products(plan, begin, found, remote, tiles, hubs, own, total, shift, spare):
    hub_count = hubs.shape[0]

    def step(number, unused):
        where, products = [], []
        for lane in range(SLOTS):
            place = number * SLOTS + lane
            live = place < found
            place = begin + jnp.minimum(place, found - 1)
            where.append(jnp.where(live, plan[ROW, place] - shift, spare))
            col = plan[COL, place]
            of_hub = hubs[jnp.minimum(col, hub_count - 1)]
            of_own = own[jnp.maximum(col - hub_count, 0)]
            tile = tiles[plan[SLOT, place] - remote]
            products.append(dot(tile, jnp.where(col < hub_count, of_hub, of_own)))
        for row, product in zip(where, products):
            total[row] += product
        return unused

    lax.fori_loop(0, (found + SLOTS - 1) // SLOTS, step, 0)


def each_block(first_place, last_place, copy_of, act):
    def step(place, unused):
        act(copy_of(place))
        return unused

    lax.fori_loop(first_place, last_place, step, 0)


def start(copy):
    copy.start()


def wait(copy):
    copy.wait()


def rounded_up(number):
    return (number + GROUP - 1) // GROUP


def finish_group(first_place, begin, end, finish):
    for lane in range(GROUP):
        place = first_place + lane

        @pl.when((place >= begin) & (place < end))
        def _(place=place):
            finish(place).start()


def pack_kernel(chosen, blocks, outgoing, held, sems):
    load = pltpu.make_async_copy(blocks, held, sems.at[0])
    load.start()
    load.wait()
    copies = []
    for number in range(outgoing.shape[0]):
        copy = pltpu.make_async_copy(
            held.at[chosen[0, number]], outgoing.at[number], sems.at[number]
        )
        copy.start()
        copies.append(copy)
    for copy in copies:
        copy.wait()


def pack(chosen, blocks):
    devices = chosen.shape[1]
    return call(
        pack_kernel,
        "pack",
        58,
        0,
        2 * blocks.size * 2,
        shape_of((devices,) + blocks.shape[1:], bf16),
        [SMEM, ANY],
        ANY,
        [pltpu.VMEM(blocks.shape, bf16), pltpu.SemaphoreType.DMA((devices,))],
        (chosen, blocks),
    )


def slot_place(slot, digits):
    place, weight = 0, 1
    for bit, radix in digits[:0:-1]:
        place += weight * ((slot // bit) % radix)
        weight *= radix
    return slot % 2, place


def place_shards(me, halves, table, digits, local):
    for slot in range(table.shape[0] // local):
        half, place = slot_place(slot, digits)
        start = pl.multiple_of((me ^ slot) * local, local)
        table[pl.ds(start, local), :] = halves[half][place * local : (place + 1) * local, :]


def split_sums(me, sums, local, kept, sent):
    odd = me % 2
    width = sums.shape[-1]
    pairs = sums.reshape(-1, 2, local, width)
    kept[...] = jnp.where(odd == 1, pairs[:, 1], pairs[:, 0]).reshape(kept.shape).astype(kept.dtype)
    sent[...] = jnp.where(odd == 1, pairs[:, 0], pairs[:, 1]).reshape(sent.shape).astype(sent.dtype)


def hub_first_kernel(
    digits, plan, count, position, place_col, half0, half1, own_hbm, tiles_hbm,
    hubs, mine, kept, sent, own, tiles, table, total, sems,
):
    hub_count, block_size, width = hubs.shape
    hub_rows = hub_count * block_size
    local = mine.shape[0]
    remote = tiles_hbm.shape[0] - tiles.shape[0]
    loads = tile_loads(tiles_hbm, tiles, sems)
    load = pltpu.make_async_copy(own_hbm, own, sems.at[4])
    load.start()
    for_live(count, loads, start)
    me = position[0]
    place_shards(me, (half0, half1), table, digits, local)
    total[...] = jnp.zeros_like(total)
    step = 2 * block_size

    def rows_step(number, unused):
        cut = pl.ds(pl.multiple_of(number * step, step), step)
        lanes = lax.broadcasted_iota(jnp.int32, (step, hub_rows), 1)
        unit = jnp.where(place_col[cut, :] == lanes, 1.0, 0.0).astype(bf16)
        placed = dot(unit, table[...]).astype(bf16)
        hubs[pl.ds(number * 2, 2)] = placed.reshape(2, block_size, width)
        return unused

    lax.fori_loop(0, hub_rows // step, rows_step, 0)
    load.wait()
    for_live(count, loads, wait)
    add_products(plan, 0, plan[COUNTS, N_HUB], remote, tiles, hubs, own, total, 0, hub_count)
    split_sums(me, total[:hub_count], local, kept, sent)
    flat = hubs.reshape(hub_rows, width)
    mine[...] = flat[pl.ds(pl.multiple_of(me * local, local), local), :]


def hub_first(digits, plan, count, position, place_col, halves, own, tiles, local, remote):
    block_size, width = own.shape[1:]
    hub_rows = place_col.shape[0]
    hub_count = hub_rows // block_size
    half = shape_of((hub_rows // 2, width), f32)
    return call(
        functools.partial(hub_first_kernel, digits),
        "hub_first",
        48,
        2 * hub_rows * hub_rows * width,
        14 * MIB,
        (
            shape_of((hub_count, block_size, width), bf16),
            shape_of((local, width), bf16),
            half,
            half,
        ),
        [SMEM] * 3 + [VMEM] * 3 + [ANY] * 2,
        (VMEM,) * 4,
        [
            pltpu.VMEM(own.shape, bf16),
            pltpu.VMEM((tiles.shape[0] - remote,) + tiles.shape[1:], bf16),
            pltpu.VMEM((hub_rows, width), bf16),
            pltpu.VMEM((hub_count + 1, block_size, width), f32),
            pltpu.SemaphoreType.DMA((5,)),
        ],
        (plan, count, position, place_col) + tuple(halves) + (own, tiles),
    )


def hub_second_kernel(
    digits, plan, count, position, place_row, half0, half1, own_hbm, tiles_hbm,
    hubs, mine, kept, sent, own, tiles, total, placed, sems,
):
    hub_count, block_size, width = hubs.shape
    hub_rows = hub_count * block_size
    local = mine.shape[0]
    remote = tiles_hbm.shape[0] - tiles.shape[0]
    loads = tile_loads(tiles_hbm, tiles, sems)
    load = pltpu.make_async_copy(own_hbm, own, sems.at[4])
    load.start()
    for_live(count, loads, start)
    me = position[0]
    flat = hubs.reshape(hub_rows, width)
    place_shards(me, (half0, half1), flat, digits, local)
    total[...] = jnp.zeros_like(total)

    def unit_rows(start, step):
        down = lax.broadcasted_iota(jnp.int32, (step, hub_rows), 0) + start
        return jnp.where(place_row[...] == down, 1.0, 0.0).astype(bf16)

    mine[...] = dot(unit_rows(me * local, local), flat[...]).astype(bf16)
    load.wait()
    for_live(count, loads, wait)
    add_products(plan, 0, plan[COUNTS, N_HUB], remote, tiles, hubs, own, total, 0, hub_count)
    sums = total[:hub_count].reshape(hub_rows, width)
    high = sums.astype(bf16)
    low = (sums - high.astype(f32)).astype(bf16)
    step = 2 * block_size

    def rows_step(number, unused):
        start = number * step
        unit = unit_rows(start, step)
        placed[pl.ds(pl.multiple_of(start, step), step), :] = dot(unit, high) + dot(unit, low)
        return unused

    lax.fori_loop(0, hub_rows // step, rows_step, 0)
    split_sums(me, placed[...], local, kept, sent)


def hub_second(digits, plan, count, position, place_row, halves, own, tiles, local, remote):
    block_size, width = own.shape[1:]
    hub_rows = place_row.shape[1]
    hub_count = hub_rows // block_size
    return call(
        functools.partial(hub_second_kernel, digits),
        "hub_second",
        48,
        2 * hub_rows * hub_rows * width,
        14 * MIB,
        (
            shape_of((hub_count, block_size, width), bf16),
            shape_of((local, width), bf16),
            shape_of((hub_rows // 2, width), f32),
            shape_of((hub_rows // 2, width), f32),
        ),
        [SMEM] * 3 + [VMEM] * 3 + [ANY] * 2,
        (VMEM,) * 4,
        [
            pltpu.VMEM(own.shape, bf16),
            pltpu.VMEM((tiles.shape[0] - remote,) + tiles.shape[1:], bf16),
            pltpu.VMEM((hub_count + 1, block_size, width), f32),
            pltpu.VMEM((hub_rows, width), f32),
            pltpu.SemaphoreType.DMA((5,)),
        ],
        (plan, count, position, place_row) + tuple(halves) + (own, tiles),
    )


def combine(position, kept, received, bit, radix, local, sent_type):
    rows = kept.shape[0] // radix
    width = kept.shape[1]

    def kernel(position, kept_in, *refs):
        received, outs = refs[: -radix], refs[-radix:]
        total = kept_in[...].astype(f32)
        for part in received:
            total = total + part[...].astype(f32)
        digit = (position[0] // bit) % radix
        parts = total.reshape(rows // local, radix, local, width)
        for offset, out in enumerate(outs):
            value = parts[:, 0]
            for number in range(1, radix):
                value = jnp.where((digit ^ offset) == number, parts[:, number], value)
            out[...] = value.reshape(rows, width).astype(out.dtype)

    shapes = [shape_of((rows, width), f32)] + [shape_of((rows, width), sent_type)] * (radix - 1)
    return call(
        kernel,
        "combine",
        16,
        kept.size,
        12 * kept.size,
        tuple(shapes),
        [SMEM] + [VMEM] * (1 + len(received)),
        (VMEM,) * radix,
        [],
        (position, kept) + tuple(received),
    )


def load_weights(layer, first_in, second_in, first, second, sems):
    loads = [
        pltpu.make_async_copy(first_in.at[layer], first, sems.at[0]),
        pltpu.make_async_copy(second_in.at[layer], second, sems.at[1]),
    ]
    for load in loads:
        load.start()
    return loads


def hub_network_kernel(layer, rows_in, *refs):
    parts, (first_in, second_in, out, first, second, sems) = refs[:-6], refs[-6:]
    loads = load_weights(layer, first_in, second_in, first, second, sems)
    u = rows_in[...].astype(f32)
    for part in parts:
        u = u + part[...].astype(f32)
    for load in loads:
        load.wait()
    out[...] = network(u, first, second, first.shape[-1])


def hub_network(layer, rows_in, parts, first, second):
    return call(
        functools.partial(hub_network_kernel, layer),
        "hub_network",
        24,
        4 * rows_in.size * first.shape[-1],
        2 * first.size,
        shape_of(rows_in.shape, bf16),
        [VMEM] * (1 + len(parts)) + [ANY] * 2,
        VMEM,
        [
            pltpu.VMEM(first.shape[1:], bf16),
            pltpu.VMEM(second.shape[1:], bf16),
            pltpu.SemaphoreType.DMA((2,)),
        ],
        (rows_in,) + tuple(parts) + (first, second),
    )


def before_kernel(
    layer, plan, count, hubs_in, own_in, tiles_in, first_in, second_in, base, out,
    hubs, own, tiles, first, second, u, result, tile_sems, block_sems, sem,
):
    own_count = own.shape[0]
    hub_count = hubs.shape[0]
    remote = tiles_in.shape[0] - tiles.shape[0]
    load_own = pltpu.make_async_copy(own_in, own, sem.at[0])
    load_hubs = pltpu.make_async_copy(hubs_in, hubs, sem.at[1])
    loads = tile_loads(tiles_in, tiles, tile_sems)
    load_own.start()
    load_hubs.start()
    for_live(count, loads, start)
    load_own.wait()
    u[:own_count] = own[...].astype(f32)
    load_hubs.wait()
    for_live(count, loads, wait)
    weights = load_weights(layer, first_in, second_in, first, second, sem.at[pl.ds(2, 2)])
    n_fed = plan[COUNTS, N_FED]
    add_products(
        plan, plan[COUNTS, N_HUB], plan[COUNTS, N_OWN], remote, tiles, hubs, own, u, hub_count, own_count
    )

    def save(place):
        return pltpu.make_async_copy(u.at[plan[BLOCK, place]], base.at[place], block_sems.at[place])

    def finish(place):
        block = plan[BLOCK, place]
        return pltpu.make_async_copy(result.at[place], out.at[block], block_sems.at[place])

    each_block(0, n_fed, save, start)
    for load in weights:
        load.wait()

    def step(number, unused):
        first_place = number * GROUP
        places = [first_place + lane for lane in range(GROUP)]
        values = jnp.concatenate([u[plan[BLOCK, place]] for place in places], axis=0)
        values = network(values, first, second, 512)
        result[pl.ds(first_place, GROUP)] = values.reshape((GROUP,) + result.shape[1:])
        finish_group(first_place, n_fed, own_count, finish)
        return unused

    lax.fori_loop(n_fed // GROUP, own_count // GROUP, step, 0)
    each_block(0, n_fed, save, wait)
    each_block(n_fed, own_count, finish, wait)


def before(layer, plan, count, hubs, own, tiles, first, second, remote):
    own_count, block_size, width = own.shape
    return call(
        functools.partial(before_kernel, layer),
        "before",
        58,
        4 * own.size * first.shape[-1] // 3,
        18 * MIB,
        (shape_of(own.shape, f32), shape_of(own.shape, bf16)),
        [SMEM] * 2 + [ANY] * 5,
        (ANY, ANY),
        [
            pltpu.VMEM(hubs.shape, bf16),
            pltpu.VMEM(own.shape, bf16),
            pltpu.VMEM((tiles.shape[0] - remote,) + tiles.shape[1:], bf16),
            pltpu.VMEM(first.shape[1:], bf16),
            pltpu.VMEM(second.shape[1:], bf16),
            pltpu.VMEM((own_count + 1, block_size, width), f32),
            pltpu.VMEM(own.shape, bf16),
            pltpu.SemaphoreType.DMA((4,)),
            pltpu.SemaphoreType.DMA((own_count,)),
            pltpu.SemaphoreType.DMA((4,)),
        ],
        (plan, count, hubs, own, tiles, first, second),
    )


def after_kernel(
    layer, with_send, plan, base, done, incoming, tiles, first_in, second_in, *refs
):
    out, refs = refs[0], refs[1:]
    if with_send:
        (sums, outgoing), refs = refs[:2], refs[2:]
    u, extra, inc, adj, first, second, result, base_sems, block_sems, sem = refs
    own_count = u.shape[0]
    remote = incoming.shape[0]
    parts = 4
    size = remote // parts
    loads = []
    for part in range(parts):
        cut = pl.ds(part * size, size)
        loads.append(
            (
                pltpu.make_async_copy(tiles.at[cut], adj.at[cut], sem.at[2 + 2 * part]),
                pltpu.make_async_copy(incoming.at[cut], inc.at[cut], sem.at[3 + 2 * part]),
            )
        )
        for load in loads[-1]:
            load.start()
    n_fed, n_held = plan[COUNTS, N_FED], plan[COUNTS, N_HELD]
    groups = rounded_up(n_fed)
    groups_now = rounded_up(plan[COUNTS, N_NOW]) if with_send else groups
    apart = jnp.minimum(groups * GROUP, n_held)

    def cut_of(group):
        return pl.ds(group * GROUP, GROUP)

    def load_base(group):
        cut = cut_of(group)
        return pltpu.make_async_copy(base.at[cut], u.at[cut], base_sems.at[group])

    def load_done(place):
        block = plan[BLOCK, place]
        return pltpu.make_async_copy(done.at[block], result.at[place], block_sems.at[place])

    def finish(place):
        block = plan[BLOCK, place]
        return pltpu.make_async_copy(result.at[place], out.at[block], block_sems.at[place])

    extra[...] = jnp.zeros_like(extra)
    for part in range(parts):
        for load in loads[part]:
            load.wait()
        if part == 0:
            weights = load_weights(layer, first_in, second_in, first, second, sem.at[pl.ds(0, 2)])
            each_block(0, groups, load_base, start)
            if with_send:
                each_block(apart, n_held, load_done, start)
        products = [dot(adj[slot], inc[slot]) for slot in range(part * size, (part + 1) * size)]
        for lane, product in enumerate(products):
            extra[plan[REMOTE, part * size + lane]] += product
    for load in weights:
        load.wait()
    n_now = jnp.minimum(groups_now * GROUP, n_fed)

    def step(group, unused):
        load_base(group).wait()
        cut = cut_of(group)
        values = (u[cut] + extra[cut]).reshape(GROUP * u.shape[1], u.shape[2])
        values = network(values, first, second, 512)
        result[cut] = values.reshape((GROUP,) + result.shape[1:])
        finish_group(group * GROUP, 0, n_now, finish)
        return unused

    lax.fori_loop(0, groups_now, step, 0)
    copies = []
    if with_send:
        each_block(n_fed, apart, load_done, start)
        each_block(n_fed, n_held, load_done, wait)
        for number in range(remote):
            copy = pltpu.make_async_copy(
                result.at[plan[GOING, number]], outgoing.at[number], sem.at[number]
            )
            copy.start()
            copies.append(copy)

        def save(group):
            cut = cut_of(group)
            return pltpu.make_async_copy(u.at[cut], sums.at[cut], base_sems.at[group])

        def keep(group, unused):
            load_base(group).wait()
            cut = cut_of(group)
            u[cut] += extra[cut]
            save(group).start()
            return unused

        lax.fori_loop(groups_now, groups, keep, 0)
        each_block(groups_now, groups, save, wait)
    each_block(0, n_now, finish, wait)
    for copy in copies:
        copy.wait()


def after(layer, plan, base, done, incoming, tiles, first, second, with_send):
    own_count = base.shape[0]
    remote = incoming.shape[0]
    shapes = [shape_of(base.shape, bf16)]
    if with_send:
        shapes += [shape_of(base.shape, f32), shape_of(incoming.shape, bf16)]
    return pl.pallas_call(
        functools.partial(after_kernel, layer, with_send),
        out_shape=tuple(shapes),
        in_specs=[SMEM] + [ANY] * 6,
        out_specs=(ANY,) * len(shapes),
        scratch_shapes=[
            pltpu.VMEM(base.shape, f32),
            pltpu.VMEM(base.shape, f32),
            pltpu.VMEM(incoming.shape, bf16),
            pltpu.VMEM((remote,) + tiles.shape[1:], bf16),
            pltpu.VMEM(first.shape[1:], bf16),
            pltpu.VMEM(second.shape[1:], bf16),
            pltpu.VMEM(base.shape, bf16),
            pltpu.SemaphoreType.DMA((own_count // GROUP,)),
            pltpu.SemaphoreType.DMA((own_count,)),
            pltpu.SemaphoreType.DMA((max(10, remote),)),
        ],
        input_output_aliases={2: 0, 1: 1} if with_send else {2: 0},
        compiler_params=pltpu.CompilerParams(vmem_limit_bytes=58 * MIB),
        cost_estimate=pl.CostEstimate(
            flops=4 * base.size * first.shape[-1], bytes_accessed=16 * MIB, transcendentals=0
        ),
        name="after",
    )(plan, base, done, incoming, tiles, first, second)


def late_kernel(
    layer, plan, sums, done, first_in, second_in, out, u, first, second, result, base_sems, block_sems, sem
):
    weights = load_weights(layer, first_in, second_in, first, second, sem)
    n_fed = plan[COUNTS, N_FED]
    groups = rounded_up(n_fed)
    groups_now = rounded_up(plan[COUNTS, N_NOW])

    def load(group):
        cut = pl.ds(group * GROUP, GROUP)
        return pltpu.make_async_copy(sums.at[cut], u.at[cut], base_sems.at[group])

    def finish(place):
        block = plan[BLOCK, place]
        return pltpu.make_async_copy(result.at[place], out.at[block], block_sems.at[place])

    each_block(groups_now, groups, load, start)
    for part in weights:
        part.wait()

    def step(group, unused):
        load(group).wait()
        cut = pl.ds(group * GROUP, GROUP)
        values = network(u[cut].reshape(GROUP * u.shape[1], u.shape[2]), first, second, 512)
        result[cut] = values.reshape((GROUP,) + result.shape[1:])
        finish_group(group * GROUP, 0, n_fed, finish)
        return unused

    lax.fori_loop(groups_now, groups, step, 0)
    each_block(jnp.minimum(groups_now * GROUP, n_fed), n_fed, finish, wait)


def late(layer, plan, sums, done, first, second):
    own_count = sums.shape[0]
    return pl.pallas_call(
        functools.partial(late_kernel, layer),
        out_shape=shape_of(done.shape, bf16),
        in_specs=[SMEM] + [ANY] * 4,
        out_specs=ANY,
        scratch_shapes=[
            pltpu.VMEM(sums.shape, f32),
            pltpu.VMEM(first.shape[1:], bf16),
            pltpu.VMEM(second.shape[1:], bf16),
            pltpu.VMEM(sums.shape, bf16),
            pltpu.SemaphoreType.DMA((own_count // GROUP,)),
            pltpu.SemaphoreType.DMA((own_count,)),
            pltpu.SemaphoreType.DMA((2,)),
        ],
        input_output_aliases={2: 0},
        compiler_params=pltpu.CompilerParams(vmem_limit_bytes=58 * MIB),
        cost_estimate=pl.CostEstimate(
            flops=sums.size * first.shape[-1], bytes_accessed=5 * MIB, transcendentals=0
        ),
        name="late",
    )(plan, sums, done, first, second)


def exchange(x, bit):
    devices = lax.axis_size("dev")
    return lax.ppermute(x, "dev", [(i, i ^ bit) for i in range(devices)])


def all_digits():
    devices = lax.axis_size("dev")
    digits, bit = [(1, 2)], 2
    while bit < devices:
        radix = 4 if 4 * bit <= devices else 2
        digits.append((bit, radix))
        bit *= radix
    return digits


def gather_step(x, bit, radix):
    return [x] + [exchange(x, bit * offset) for offset in range(1, radix)]


def gather_far(x, digits):
    return gather_step(x, *digits[-1])


def gather_near(pieces, digits):
    for digit in digits[-2:0:-1]:
        pieces = gather_step(jnp.concatenate(pieces, axis=0), *digit)
    return pieces


def gather_last(pieces, digits):
    x = jnp.concatenate(pieces, axis=0)
    return x, exchange(x, digits[0][0])


def scatter_near(position, kept, sent, digits, local):
    received = [exchange(sent, digits[0][0])]
    for bit, radix in digits[1:-1]:
        kept, *sent = combine(position, kept, received, bit, radix, local, bf16)
        received = [exchange(part, bit * (1 + number)) for number, part in enumerate(sent)]
    return kept, received


def scatter_far(position, kept, received, digits, local, sent_type):
    bit, radix = digits[-1]
    kept, *sent = combine(position, kept, received, bit, radix, local, sent_type)
    return [kept] + [exchange(part, bit * (1 + number)) for number, part in enumerate(sent)]


def body(
    peripheral, hubs, tiles, tile_rows, local_cols, tile_count, send_list, hub_place, w_in, w_out
):
    position = lax.axis_index("dev")
    digits = all_digits()
    block_size = tiles.shape[1]
    width = peripheral.shape[1]
    own_count = peripheral.shape[0] // block_size
    hub_rows = hub_place.shape[0]
    hub_count = hub_rows // block_size
    local = hubs.shape[0]
    remote = send_list.shape[1]
    place_col = hub_place.reshape(hub_rows, 1)
    place_row = hub_place.reshape(1, hub_rows)
    me = position.astype(jnp.int32).reshape(1)
    own = peripheral.reshape(own_count, block_size, width)
    all_to_all = functools.partial(
        lax.all_to_all, axis_name="dev", split_axis=0, concat_axis=0, tiled=True
    )

    pieces = gather_far(hubs, digits)
    plan = make_plan(me, tile_count, tile_rows, local_cols, send_list, hub_count, own_count)
    own, plan, *pieces = lax.optimization_barrier((own, plan, *pieces))
    outgoing = pack(send_list, own)
    pieces = gather_near(pieces, digits)
    outgoing, place_col, *pieces = lax.optimization_barrier((outgoing, place_col, *pieces))
    incoming = all_to_all(outgoing)
    halves = gather_last(pieces, digits)
    hub_table, mine, kept, sent = hub_first(
        digits, plan, tile_count, me, place_col, halves, own, tiles, local, remote
    )
    base, done = before(0, plan, tile_count, hub_table, own, tiles, w_in, w_out, remote)
    kept, received = scatter_near(me, kept, sent, digits, local)
    base, done, *received = lax.optimization_barrier((base, done, *received))
    parts = scatter_far(me, kept, received, digits, local, bf16)
    hub_new = hub_network(0, mine, parts, w_in, w_out)
    pieces = gather_far(hub_new, digits)
    base, *pieces = lax.optimization_barrier((base, *pieces))
    done, sums, outgoing = after(0, plan, base, done, incoming, tiles, w_in, w_out, True)

    pieces = gather_near(pieces, digits)
    outgoing, *pieces = lax.optimization_barrier((outgoing, *pieces))
    incoming = all_to_all(outgoing)
    own = late(0, plan, sums, done, w_in, w_out)
    halves = gather_last(pieces, digits)
    hub_table, mine, kept, sent = hub_second(
        digits, plan, tile_count, me, place_row, halves, own, tiles, local, remote
    )
    base, done = before(1, plan, tile_count, hub_table, own, tiles, w_in, w_out, remote)
    kept, received = scatter_near(me, kept, sent, digits, local)
    base, done, *received = lax.optimization_barrier((base, done, *received))
    parts = scatter_far(me, kept, received, digits, local, f32)
    (peri_out,) = after(1, plan, base, done, incoming, tiles, w_in, w_out, False)
    peri_out, *parts = lax.optimization_barrier((peri_out, *parts))
    hub_out = hub_network(1, mine, parts, w_in, w_out)
    return (peri_out.reshape(peripheral.shape), hub_out)


def solution(mesh):
    in_specs = (
        P("dev", None),
        P("dev", None),
        P("dev", None, None),
        P("dev"),
        P("dev"),
        P("dev"),
        P("dev", None),
        P(),
        P(),
        P(),
    )
    out_specs = (P("dev", None), P("dev", None))
    return jax.shard_map(body, mesh=mesh, in_specs=in_specs, out_specs=out_specs, check_vma=False)
```

time: 172 us -> 172 us (level)
  waiting for transfers between devices: 35.8 us -> 43.3 us
  starting transfers between devices: 51.1 us -> 46.9 us
  Pallas kernels: 78.1 us -> 74.8 us
    ppermute x28, starting transfers between devices: 42 us -> 37.8 us  [exchange(): return lax.ppermute(x, 'dev', [(i, i ^ bit) for i in range(devices)])]
    all_to_all x2, waiting for transfers between devices: 6.46 us -> 10.4 us  [body(): incoming = all_to_all(outgoing)]
    ppermute x28, waiting for transfers between devices: 29.3 us -> 32.9 us  [exchange(): return lax.ppermute(x, 'dev', [(i, i ^ bit) for i in range(devices)])]
    pallas_call x3, Pallas kernels: 32.4 us -> 30.3 us  [the longest x2 23.8 us: after(): pl.pallas_call(functools.partial(after_kernel, layer, with_send), out_sha...]
    pallas_call x11 -> x12, Pallas kernels: 45.7 us -> 44.5 us  [call(): pl.pallas_call(kernel, out_shape=out_shape, in_specs=in_specs, out_specs=...]
  transfers between devices with their start and end apart: 30 -> 30, of which waited for: 13 -> 11; matrix products, arithmetic and copies ran while one was open for 1% -> 1% of each run, Pallas kernels for 45% -> 43%
where the time goes in v5:
time: 172 us; the launch traced here: 170 us
  Pallas kernels  74.8 us (43%)
  starting transfers between devices  46.9 us (27%)
  waiting for transfers between devices  43.3 us (25%)
  local copies, waits for them, and re-layouts  3.34 us (2%)
  between operations  1.87 us (1%)
    pallas_call x12, Pallas kernels, call(): pl.pallas_call(kernel, out_shape=out_shape, in_specs=in_specs, out_specs=...  44.5 us
    ppermute x28, starting transfers between devices, exchange(): return lax.ppermute(x, 'dev', [(i, i ^ bit) for i in range(devices)])  37.8 us
    ppermute x28, waiting for transfers between devices, exchange(): return lax.ppermute(x, 'dev', [(i, i ^ bit) for i in range(devices)])  32.9 us
    pallas_call x2, Pallas kernels, after(): pl.pallas_call(functools.partial(after_kernel, layer, with_send), out_sha...  23.8 us
    all_to_all x2, waiting for transfers between devices, body(): incoming = all_to_all(outgoing)  10.4 us
    all_to_all x2, starting transfers between devices, body(): incoming = all_to_all(outgoing)  9.13 us
    pallas_call x1, Pallas kernels, late(): pl.pallas_call(functools.partial(late_kernel, layer), out_shape=shape_of(...  6.47 us
  transfers between devices with their start and end apart: 30, of which 11 were waited for; matrix products, arithmetic and copies ran while one was open for 1% of the time, Pallas kernels for 43%

profile of v5, /device:TPU:0, one launch (start us, length us, event | category | flops | bytes accessed | tf_op | source)
XLA Modules:
  0.0 170.2 jit_solution(342911083838076553)
XLA Ops:
  0.6 4.1 %collective-permute-start.1 = (bf16[64,256]{1,0:T(8,128)(2,1)}, bf16[64,256]{1,0:T(8,128)(2,1)S(1)}, u32[]{:S(2)}, u32[]{:S(2)}) collective-permute-start(bf16[64,256]{1,0:T(8,128)(2,1)} %param.11), channel_id=1, source_target_pairs={{0,16},{1,17},{2,18},{3,19},{4,20},{5,21},{6,22},{7,23},{8,24},{9,... | collective-permute-start | bytes 98312 | tf_op jit(solution)/shard_map/ppermute | solution.py:738
  9.4 2.8 %collective-permute-done.2 = bf16[64,256]{1,0:T(8,128)(2,1)S(1)} collective-permute-done((bf16[64,256]{1,0:T(8,128)(2,1)}, bf16[64,256]{1,0:T(8,128)(2,1)S(1)}, u32[]{:S(2)}, u32[]{:S(2)}) %collective-permute-start.2) | collective-permute-done | bytes 32800 | tf_op jit(solution)/shard_map/ppermute | solution.py:738
  13.0 2.5 %collective-permute-start.5 = (bf16[256,256]{1,0:T(8,128)(2,1)S(1)}, bf16[256,256]{1,0:T(8,128)(2,1)S(1)}, u32[]{:S(2)}, u32[]{:S(2)}) collective-permute-start(bf16[256,256]{1,0:T(8,128)(2,1)S(1)} %constant_dynamic-update-slice_fusion), channel_id=1, source_target_pairs={{0,6},{1,7},{2,4},{3,5},{4,2},{5,3},{6,0},{7,1},{8,14},{9,15},{10,... | collective-permute-start | bytes 393224 | tf_op jit(solution)/shard_map/ppermute | solution.py:738
  16.6 3.8 %pack.1 = bf16[32,128,256]{2,1,0:T(8,128)(2,1)} custom-call(s32[1,32]{1,0:T(1,128)} %chosen.3, bf16[32,128,256]{2,1,0:T(8,128)(2,1)} %bitcast.11), custom_call_target="tpu_custom_call" | custom-call | bytes 4194304 | tf_op jit(solution)/shard_map/pack/pallas_call | solution.py:30
  21.1 3.6 %all-to-all-start = ((bf16[32,128,256]{2,1,0:T(8,128)(2,1)}), bf16[32,128,256]{2,1,0:T(8,128)(2,1)}, u32[]{:S(2)}, u32[]{:S(2)}) async-start(bf16[32,128,256]{2,1,0:T(8,128)(2,1)} %pack.1), calls=%async_computation | async-start | bytes 4194304 | tf_op jit(solution)/shard_map/all_to_all | solution.py:810
  26.8 5.3 %hub_first.1 = (bf16[16,128,256]{2,1,0:T(8,128)(2,1)S(1)}, bf16[64,256]{1,0:T(8,128)(2,1)S(1)}, f32[1024,256]{1,0:T(8,128)S(1)}, f32[1024,256]{1,0:T(8,128)S(1)}) custom-call(s32[8,256]{1,0:T(8,128)S(1)} %plan.1, s32[1]{0:T(128)S(6)} %copy.33.count, s32[1]{0:T(128)} %bitcast.1.position, s32[2048,1]{1,0:T(8,128)S(1)} %copy.16.place_col, ...), custom_call_target="tpu_custom_call" | custom-call | flops 2147483648 | bytes 14680064 | tf_op jit(solution)/shard_map/hub_first/pallas_call | solution.py:30
  32.7 2.3 %collective-permute-done.7.refs_0_ = f32[1024,256]{1,0:T(8,128)S(1)} collective-permute-done((f32[1024,256]{1,0:T(8,128)S(1)}, f32[1024,256]{1,0:T(8,128)S(1)}, u32[]{:S(2)}, u32[]{:S(2)}) %collective-permute-start.7) | collective-permute-done | bytes 1048608 | tf_op jit(solution)/shard_map/ppermute | solution.py:738
  38.8 11.7 %before.2 = (f32[32,128,256]{2,1,0:T(8,128)}, bf16[32,128,256]{2,1,0:T(8,128)(2,1)}) custom-call(s32[8,256]{1,0:T(8,128)} %copy-done.6, s32[1]{0:T(128)S(6)} %copy.33.count, bf16[16,128,256]{2,1,0:T(8,128)(2,1)} %copy-done.5, bf16[32,128,256]{2,1,0:T(8,128)(2,1)} %bitcast.13, bf16[144,128,128]{2,1,0:T(8,128)(2,1)} %tiles.3, bf16[2,256,2048]{2,1,0:T(8,128)(2,1)} %refs_4_.3, ...), custom_call_target="tpu_custom_call" | custom-call | flops 2863311616 | bytes 18874368 | tf_op jit(solution)/shard_map/before/pallas_call | solution.py:30
  50.6 2.2 %collective-permute-done.10.refs_2_ = bf16[256,256]{1,0:T(8,128)(2,1)S(1)} collective-permute-done((bf16[256,256]{1,0:T(8,128)(2,1)S(1)}, bf16[256,256]{1,0:T(8,128)(2,1)S(1)}, u32[]{:S(2)}, u32[]{:S(2)}) %collective-permute-start.10) | collective-permute-done | bytes 131104 | tf_op jit(solution)/shard_map/ppermute | solution.py:738
  53.6 2.9 %collective-permute-start.12 = (bf16[64,256]{1,0:T(8,128)(2,1)S(1)}, bf16[64,256]{1,0:T(8,128)(2,1)S(1)}, u32[]{:S(2)}, u32[]{:S(2)}) collective-permute-start(bf16[64,256]{1,0:T(8,128)(2,1)S(1)} %get-tuple-element.97), channel_id=1, source_target_pairs={{0,16},{1,17},{2,18},{3,19},{4,20},{5,21},{6,22},{7,23},{8,24},{9,... | collective-permute-start | bytes 98312 | tf_op jit(solution)/shard_map/ppermute | solution.py:738
  57.4 3.2 %collective-permute-done.11.refs_1_ = bf16[64,256]{1,0:T(8,128)(2,1)S(1)} collective-permute-done((bf16[64,256]{1,0:T(8,128)(2,1)S(1)}, bf16[64,256]{1,0:T(8,128)(2,1)S(1)}, u32[]{:S(2)}, u32[]{:S(2)}) %collective-permute-start.11) | collective-permute-done | bytes 32800 | tf_op jit(solution)/shard_map/ppermute | solution.py:738
  60.7 15.4 %collective-permute-done.12.refs_2_ = bf16[64,256]{1,0:T(8,128)(2,1)S(1)} collective-permute-done((bf16[64,256]{1,0:T(8,128)(2,1)S(1)}, bf16[64,256]{1,0:T(8,128)(2,1)S(1)}, u32[]{:S(2)}, u32[]{:S(2)}) %collective-permute-start.12) | collective-permute-done | bytes 32800 | tf_op jit(solution)/shard_map/ppermute | solution.py:738
  83.4 2.4 %collective-permute-start.19 = (bf16[256,256]{1,0:T(8,128)(2,1)S(1)}, bf16[256,256]{1,0:T(8,128)(2,1)S(1)}, u32[]{:S(2)}, u32[]{:S(2)}) collective-permute-start(bf16[256,256]{1,0:T(8,128)(2,1)S(1)} %constant_dynamic-update-slice_fusion.8), channel_id=1, source_target_pairs={{0,6},{1,7},{2,4},{3,5},{4,2},{5,3},{6,0},{7,1},{8,14},{9,15},{10,... | collective-permute-start | bytes 393224 | tf_op jit(solution)/shard_map/ppermute | solution.py:738
  87.0 11.5 %after.2 = (bf16[32,128,256]{2,1,0:T(8,128)(2,1)}, f32[32,128,256]{2,1,0:T(8,128)}, bf16[32,128,256]{2,1,0:T(8,128)(2,1)}) custom-call(s32[8,256]{1,0:T(8,128)} %copy-done.6, f32[32,128,256]{2,1,0:T(8,128)} %get-tuple-element.99.base, bf16[32,128,256]{2,1,0:T(8,128)(2,1)} %get-tuple-element.100.done, ...), custom_call_target="tpu_custom_call", output_to_operand_aliasing={{0}: (2, {}), {1}: (1, {})} | custom-call | flops 8589934592 | bytes 16777216 | tf_op jit(solution)/shard_map/after/pallas_call | solution.py:653
  98.5 5.5 %all-to-all-start.1 = ((bf16[32,128,256]{2,1,0:T(8,128)(2,1)}), bf16[32,128,256]{2,1,0:T(8,128)(2,1)}, u32[]{:S(2)}, u32[]{:S(2)}) async-start(bf16[32,128,256]{2,1,0:T(8,128)(2,1)} %get-tuple-element.123), calls=%async_computation.1 | async-start | bytes 4194304 | tf_op jit(solution)/shard_map/all_to_all | solution.py:826
  104.3 6.5 %late.1.own_hbm.own_in = bf16[32,128,256]{2,1,0:T(8,128)(2,1)} custom-call(s32[8,256]{1,0:T(8,128)} %copy-done.6, f32[32,128,256]{2,1,0:T(8,128)} %get-tuple-element.111.sums, bf16[32,128,256]{2,1,0:T(8,128)(2,1)} %get-tuple-element.112.done, bf16[2,256,2048]{2,1,0:T(8,128)(2,1)} %refs_4_.3, ...), custom_call_target="tpu_custom_call", output_to_operand_aliasing={{}: (2, {})} | custom-call | flops 2147483648 | bytes 5242880 | tf_op jit(solution)/shard_map/late/pallas_call | solution.py:713
  110.8 9.2 %hub_second.1 = (bf16[16,128,256]{2,1,0:T(8,128)(2,1)S(1)}, bf16[64,256]{1,0:T(8,128)(2,1)S(1)}, f32[1024,256]{1,0:T(8,128)S(1)}, f32[1024,256]{1,0:T(8,128)S(1)}) custom-call(s32[8,256]{1,0:T(8,128)S(1)} %copy-done.7, s32[1]{0:T(128)S(6)} %copy.33.count, s32[1]{0:T(128)} %bitcast.1.position, s32[1,2048]{1,0:T(1,128)S(1)} %bitcast.8, ...), custom_call_target="tpu_custom_call" | custom-call | flops 2147483648 | bytes 14680064 | tf_op jit(solution)/shard_map/hub_second/pallas_call | solution.py:30
  120.1 2.6 %collective-permute-done.21.refs_0_ = f32[1024,256]{1,0:T(8,128)S(1)} collective-permute-done((f32[1024,256]{1,0:T(8,128)S(1)}, f32[1024,256]{1,0:T(8,128)S(1)}, u32[]{:S(2)}, u32[]{:S(2)}) %collective-permute-start.21) | collective-permute-done | bytes 1048608 | tf_op jit(solution)/shard_map/ppermute | solution.py:738
  124.8 2.1 %collective-permute-start.23 = (bf16[256,256]{1,0:T(8,128)(2,1)S(1)}, bf16[256,256]{1,0:T(8,128)(2,1)S(1)}, u32[]{:S(2)}, u32[]{:S(2)}) collective-permute-start(bf16[256,256]{1,0:T(8,128)(2,1)S(1)} %get-tuple-element.119), channel_id=1, source_target_pairs={{0,4},{1,5},{2,6},{3,7},{4,0},{5,1},{6,2},{7,3},{8,12},{9,13},{10,... | collective-permute-start | bytes 393224 | tf_op jit(solution)/shard_map/ppermute | solution.py:738
  128.3 11.2 %before.3 = (f32[32,128,256]{2,1,0:T(8,128)}, bf16[32,128,256]{2,1,0:T(8,128)(2,1)}) custom-call(s32[8,256]{1,0:T(8,128)} %copy-done.6, s32[1]{0:T(128)S(6)} %copy.33.count, bf16[16,128,256]{2,1,0:T(8,128)(2,1)} %copy-done.4, bf16[32,128,256]{2,1,0:T(8,128)(2,1)} %late.1.own_hbm.own_in, bf16[144,128,128]{2,1,0:T(8,128)(2,1)} %tiles.3, ...), custom_call_target="tpu_custom_call" | custom-call | flops 2863311616 | bytes 18874368 | tf_op jit(solution)/shard_map/before/pallas_call | solution.py:30
  139.7 2.4 %collective-permute-start.25 = (f32[64,256]{1,0:T(8,128)S(1)}, f32[64,256]{1,0:T(8,128)S(1)}, u32[]{:S(2)}, u32[]{:S(2)}) collective-permute-start(f32[64,256]{1,0:T(8,128)S(1)} %get-tuple-element.129), channel_id=1, source_target_pairs={{0,8},{1,9},{2,10},{3,11},{4,12},{5,13},{6,14},{7,15},{8,0},{9,1},... | collective-permute-start | bytes 196616 | tf_op jit(solution)/shard_map/ppermute | solution.py:738
  142.1 2.4 %collective-permute-start.26 = (f32[64,256]{1,0:T(8,128)S(1)}, f32[64,256]{1,0:T(8,128)S(1)}, u32[]{:S(2)}, u32[]{:S(2)}) collective-permute-start(f32[64,256]{1,0:T(8,128)S(1)} %get-tuple-element.130), channel_id=1, source_target_pairs={{0,16},{1,17},{2,18},{3,19},{4,20},{5,21},{6,22},{7,23},{8,24},{9,... | collective-permute-start | bytes 196616 | tf_op jit(solution)/shard_map/ppermute | solution.py:738
  145.9 10.4 %all-to-all-done.1.incoming = bf16[32,128,256]{2,1,0:T(8,128)(2,1)} async-done(((bf16[32,128,256]{2,1,0:T(8,128)(2,1)}), bf16[32,128,256]{2,1,0:T(8,128)(2,1)}, u32[]{:S(2)}, u32[]{:S(2)}) %all-to-all-start.1) | async-done | bytes 2097184 | tf_op jit(solution)/shard_map/all_to_all | solution.py:826
  156.3 12.3 %after.3 = bf16[32,128,256]{2,1,0:T(8,128)(2,1)} custom-call(s32[8,256]{1,0:T(8,128)} %copy-done.6, f32[32,128,256]{2,1,0:T(8,128)} %get-tuple-element.121.base, bf16[32,128,256]{2,1,0:T(8,128)(2,1)} %get-tuple-element.122.done, bf16[32,128,256]{2,1,0:T(8,128)(2,1)} %all-to-all-done.1.incoming, ...), custom_call_target="tpu_custom_call", output_to_operand_aliasing={{}: (2, {})} | custom-call | flops 8589934592 | bytes 16777216 | tf_op jit(solution)/shard_map/after/pallas_call | solution.py:653
  (91 shorter events, 29.9 us)
Async XLA Ops:
  0.6 8.8 %collective-permute-start.1 = (bf16[64,256]{1,0:T(8,128)(2,1)}, bf16[64,256]{1,0:T(8,128)(2,1)S(1)}, u32[]{:S(2)}, u32[]{:S(2)}) collective-permute-start(bf16[64,256]{1,0:T(8,128)(2,1)} %param.11), channel_id=1, source_target_pairs={{0,16},{1,17},{2,18},{3,19},{4,20},{5,21},{6,22},{7,23},{8,24},{9,... | collective-permute-start | bytes 98312 | tf_op jit(solution)/shard_map/ppermute | solution.py:738
  6.3 5.9 %collective-permute-start.2 = (bf16[64,256]{1,0:T(8,128)(2,1)}, bf16[64,256]{1,0:T(8,128)(2,1)S(1)}, u32[]{:S(2)}, u32[]{:S(2)}) collective-permute-start(bf16[64,256]{1,0:T(8,128)(2,1)} %param.11), channel_id=1, source_target_pairs={{0,24},{1,25},{2,26},{3,27},{4,28},{5,29},{6,30},{7,31},{8,16},{9,... | collective-permute-start | bytes 98312 | tf_op jit(solution)/shard_map/ppermute | solution.py:738
  13.0 7.4 %collective-permute-start.5 = (bf16[256,256]{1,0:T(8,128)(2,1)S(1)}, bf16[256,256]{1,0:T(8,128)(2,1)S(1)}, u32[]{:S(2)}, u32[]{:S(2)}) collective-permute-start(bf16[256,256]{1,0:T(8,128)(2,1)S(1)} %constant_dynamic-update-slice_fusion), channel_id=1, source_target_pairs={{0,6},{1,7},{2,4},{3,5},{4,2},{5,3},{6,0},{7,1},{8,14},{9,15},{10,... | collective-permute-start | bytes 393224 | tf_op jit(solution)/shard_map/ppermute | solution.py:738
  15.5 5.6 %collective-permute-start.4 = (bf16[256,256]{1,0:T(8,128)(2,1)S(1)}, bf16[256,256]{1,0:T(8,128)(2,1)S(1)}, u32[]{:S(2)}, u32[]{:S(2)}) collective-permute-start(bf16[256,256]{1,0:T(8,128)(2,1)S(1)} %constant_dynamic-update-slice_fusion), channel_id=1, source_target_pairs={{0,4},{1,5},{2,6},{3,7},{4,0},{5,1},{6,2},{7,3},{8,12},{9,13},{10,... | collective-permute-start | bytes 393224 | tf_op jit(solution)/shard_map/ppermute | solution.py:738
  21.1 65.9 %all-to-all-start = ((bf16[32,128,256]{2,1,0:T(8,128)(2,1)}), bf16[32,128,256]{2,1,0:T(8,128)(2,1)}, u32[]{:S(2)}, u32[]{:S(2)}) async-start(bf16[32,128,256]{2,1,0:T(8,128)(2,1)} %pack.1), calls=%async_computation | async-start | bytes 4194304 | tf_op jit(solution)/shard_map/all_to_all | solution.py:810
  35.2 15.3 %collective-permute-start.8 = (bf16[256,256]{1,0:T(8,128)(2,1)S(1)}, bf16[256,256]{1,0:T(8,128)(2,1)S(1)}, u32[]{:S(2)}, u32[]{:S(2)}) collective-permute-start(bf16[256,256]{1,0:T(8,128)(2,1)S(1)} %get-tuple-element.86), channel_id=1, source_target_pairs={{0,2},{1,3},{2,0},{3,1},{4,6},{5,7},{6,4},{7,5},{8,10},{9,11},{10,... | collective-permute-start | bytes 393224 | tf_op jit(solution)/shard_map/ppermute | solution.py:738
  36.7 13.8 %collective-permute-start.9 = (bf16[256,256]{1,0:T(8,128)(2,1)S(1)}, bf16[256,256]{1,0:T(8,128)(2,1)S(1)}, u32[]{:S(2)}, u32[]{:S(2)}) collective-permute-start(bf16[256,256]{1,0:T(8,128)(2,1)S(1)} %get-tuple-element.87), channel_id=1, source_target_pairs={{0,4},{1,5},{2,6},{3,7},{4,0},{5,1},{6,2},{7,3},{8,12},{9,13},{10,... | collective-permute-start | bytes 393224 | tf_op jit(solution)/shard_map/ppermute | solution.py:738
  38.6 14.2 %collective-permute-start.10 = (bf16[256,256]{1,0:T(8,128)(2,1)S(1)}, bf16[256,256]{1,0:T(8,128)(2,1)S(1)}, u32[]{:S(2)}, u32[]{:S(2)}) collective-permute-start(bf16[256,256]{1,0:T(8,128)(2,1)S(1)} %get-tuple-element.88), channel_id=1, source_target_pairs={{0,6},{1,7},{2,4},{3,5},{4,2},{5,3},{6,0},{7,1},{8,14},{9,15},{10,... | collective-permute-start | bytes 393224 | tf_op jit(solution)/shard_map/ppermute | solution.py:738
  52.9 7.8 %collective-permute-start.11 = (bf16[64,256]{1,0:T(8,128)(2,1)S(1)}, bf16[64,256]{1,0:T(8,128)(2,1)S(1)}, u32[]{:S(2)}, u32[]{:S(2)}) collective-permute-start(bf16[64,256]{1,0:T(8,128)(2,1)S(1)} %get-tuple-element.96), channel_id=1, source_target_pairs={{0,8},{1,9},{2,10},{3,11},{4,12},{5,13},{6,14},{7,15},{8,0},{9,1},... | collective-permute-start | bytes 98312 | tf_op jit(solution)/shard_map/ppermute | solution.py:738
  53.6 22.4 %collective-permute-start.12 = (bf16[64,256]{1,0:T(8,128)(2,1)S(1)}, bf16[64,256]{1,0:T(8,128)(2,1)S(1)}, u32[]{:S(2)}, u32[]{:S(2)}) collective-permute-start(bf16[64,256]{1,0:T(8,128)(2,1)S(1)} %get-tuple-element.97), channel_id=1, source_target_pairs={{0,16},{1,17},{2,18},{3,19},{4,20},{5,21},{6,22},{7,23},{8,24},{9,... | collective-permute-start | bytes 98312 | tf_op jit(solution)/shard_map/ppermute | solution.py:738
  56.5 19.5 %collective-permute-start.13 = (bf16[64,256]{1,0:T(8,128)(2,1)S(1)}, bf16[64,256]{1,0:T(8,128)(2,1)S(1)}, u32[]{:S(2)}, u32[]{:S(2)}) collective-permute-start(bf16[64,256]{1,0:T(8,128)(2,1)S(1)} %get-tuple-element.98), channel_id=1, source_target_pairs={{0,24},{1,25},{2,26},{3,27},{4,28},{5,29},{6,30},{7,31},{8,16},{9,... | collective-permute-start | bytes 98312 | tf_op jit(solution)/shard_map/ppermute | solution.py:738
  76.8 5.8 %collective-permute-start.16 = (bf16[64,256]{1,0:T(8,128)(2,1)S(1)}, bf16[64,256]{1,0:T(8,128)(2,1)S(1)}, u32[]{:S(2)}, u32[]{:S(2)}) collective-permute-start(bf16[64,256]{1,0:T(8,128)(2,1)S(1)} %hub_network.2), channel_id=1, source_target_pairs={{0,24},{1,25},{2,26},{3,27},{4,28},{5,29},{6,30},{7,31},{8,16},{9,... | collective-permute-start | bytes 98312 | tf_op jit(solution)/shard_map/ppermute | solution.py:738
  78.2 5.2 %collective-permute-start.15 = (bf16[64,256]{1,0:T(8,128)(2,1)S(1)}, bf16[64,256]{1,0:T(8,128)(2,1)S(1)}, u32[]{:S(2)}, u32[]{:S(2)}) collective-permute-start(bf16[64,256]{1,0:T(8,128)(2,1)S(1)} %hub_network.2), channel_id=1, source_target_pairs={{0,16},{1,17},{2,18},{3,19},{4,20},{5,21},{6,22},{7,23},{8,24},{9,... | collective-permute-start | bytes 98312 | tf_op jit(solution)/shard_map/ppermute | solution.py:738
  83.4 15.0 %collective-permute-start.19 = (bf16[256,256]{1,0:T(8,128)(2,1)S(1)}, bf16[256,256]{1,0:T(8,128)(2,1)S(1)}, u32[]{:S(2)}, u32[]{:S(2)}) collective-permute-start(bf16[256,256]{1,0:T(8,128)(2,1)S(1)} %constant_dynamic-update-slice_fusion.8), channel_id=1, source_target_pairs={{0,6},{1,7},{2,4},{3,5},{4,2},{5,3},{6,0},{7,1},{8,14},{9,15},{10,... | collective-permute-start | bytes 393224 | tf_op jit(solution)/shard_map/ppermute | solution.py:738
  85.8 12.7 %collective-permute-start.18 = (bf16[256,256]{1,0:T(8,128)(2,1)S(1)}, bf16[256,256]{1,0:T(8,128)(2,1)S(1)}, u32[]{:S(2)}, u32[]{:S(2)}) collective-permute-start(bf16[256,256]{1,0:T(8,128)(2,1)S(1)} %constant_dynamic-update-slice_fusion.8), channel_id=1, source_target_pairs={{0,4},{1,5},{2,6},{3,7},{4,0},{5,1},{6,2},{7,3},{8,12},{9,13},{10,... | collective-permute-start | bytes 393224 | tf_op jit(solution)/shard_map/ppermute | solution.py:738
  86.4 12.1 %collective-permute-start.17 = (bf16[256,256]{1,0:T(8,128)(2,1)S(1)}, bf16[256,256]{1,0:T(8,128)(2,1)S(1)}, u32[]{:S(2)}, u32[]{:S(2)}) collective-permute-start(bf16[256,256]{1,0:T(8,128)(2,1)S(1)} %constant_dynamic-update-slice_fusion.8), channel_id=1, source_target_pairs={{0,2},{1,3},{2,0},{3,1},{4,6},{5,7},{6,4},{7,5},{8,10},{9,11},{10,... | collective-permute-start | bytes 393224 | tf_op jit(solution)/shard_map/ppermute | solution.py:738
  98.5 57.8 %all-to-all-start.1 = ((bf16[32,128,256]{2,1,0:T(8,128)(2,1)}), bf16[32,128,256]{2,1,0:T(8,128)(2,1)}, u32[]{:S(2)}, u32[]{:S(2)}) async-start(bf16[32,128,256]{2,1,0:T(8,128)(2,1)} %get-tuple-element.123), calls=%async_computation.1 | async-start | bytes 4194304 | tf_op jit(solution)/shard_map/all_to_all | solution.py:826
  104.1 6.7 %collective-permute-start.20 = (bf16[1024,256]{1,0:T(8,128)(2,1)S(1)}, bf16[1024,256]{1,0:T(8,128)(2,1)S(1)}, u32[]{:S(2)}, u32[]{:S(2)}) collective-permute-start(bf16[1024,256]{1,0:T(8,128)(2,1)S(1)} %constant_dynamic-update-slice_fusion.12.half0), channel_id=1, source_target_pairs={{0,1},{1,0},{2,3},{3,2},{4,5},{5,4},{6,7},{7,6},{8,9},{9,8},{10,11... | collective-permute-start | bytes 1572872 | tf_op jit(solution)/shard_map/ppermute | solution.py:738
  123.1 16.5 %collective-permute-start.22 = (bf16[256,256]{1,0:T(8,128)(2,1)S(1)}, bf16[256,256]{1,0:T(8,128)(2,1)S(1)}, u32[]{:S(2)}, u32[]{:S(2)}) collective-permute-start(bf16[256,256]{1,0:T(8,128)(2,1)S(1)} %get-tuple-element.118), channel_id=1, source_target_pairs={{0,2},{1,3},{2,0},{3,1},{4,6},{5,7},{6,4},{7,5},{8,10},{9,11},{10,... | collective-permute-start | bytes 393224 | tf_op jit(solution)/shard_map/ppermute | solution.py:738
  124.8 14.8 %collective-permute-start.23 = (bf16[256,256]{1,0:T(8,128)(2,1)S(1)}, bf16[256,256]{1,0:T(8,128)(2,1)S(1)}, u32[]{:S(2)}, u32[]{:S(2)}) collective-permute-start(bf16[256,256]{1,0:T(8,128)(2,1)S(1)} %get-tuple-element.119), channel_id=1, source_target_pairs={{0,4},{1,5},{2,6},{3,7},{4,0},{5,1},{6,2},{7,3},{8,12},{9,13},{10,... | collective-permute-start | bytes 393224 | tf_op jit(solution)/shard_map/ppermute | solution.py:738
  126.9 12.7 %collective-permute-start.24 = (bf16[256,256]{1,0:T(8,128)(2,1)S(1)}, bf16[256,256]{1,0:T(8,128)(2,1)S(1)}, u32[]{:S(2)}, u32[]{:S(2)}) collective-permute-start(bf16[256,256]{1,0:T(8,128)(2,1)S(1)} %get-tuple-element.120), channel_id=1, source_target_pairs={{0,6},{1,7},{2,4},{3,5},{4,2},{5,3},{6,0},{7,1},{8,14},{9,15},{10,... | collective-permute-start | bytes 393224 | tf_op jit(solution)/shard_map/ppermute | solution.py:738
  139.7 28.9 %collective-permute-start.25 = (f32[64,256]{1,0:T(8,128)S(1)}, f32[64,256]{1,0:T(8,128)S(1)}, u32[]{:S(2)}, u32[]{:S(2)}) collective-permute-start(f32[64,256]{1,0:T(8,128)S(1)} %get-tuple-element.129), channel_id=1, source_target_pairs={{0,8},{1,9},{2,10},{3,11},{4,12},{5,13},{6,14},{7,15},{8,0},{9,1},... | collective-permute-start | bytes 196616 | tf_op jit(solution)/shard_map/ppermute | solution.py:738
  142.1 26.5 %collective-permute-start.26 = (f32[64,256]{1,0:T(8,128)S(1)}, f32[64,256]{1,0:T(8,128)S(1)}, u32[]{:S(2)}, u32[]{:S(2)}) collective-permute-start(f32[64,256]{1,0:T(8,128)S(1)} %get-tuple-element.130), channel_id=1, source_target_pairs={{0,16},{1,17},{2,18},{3,19},{4,20},{5,21},{6,22},{7,23},{8,24},{9,... | collective-permute-start | bytes 196616 | tf_op jit(solution)/shard_map/ppermute | solution.py:738
  144.5 24.1 %collective-permute-start.27 = (f32[64,256]{1,0:T(8,128)S(1)}, f32[64,256]{1,0:T(8,128)S(1)}, u32[]{:S(2)}, u32[]{:S(2)}) collective-permute-start(f32[64,256]{1,0:T(8,128)S(1)} %get-tuple-element.131), channel_id=1, source_target_pairs={{0,24},{1,25},{2,26},{3,27},{4,28},{5,29},{6,30},{7,31},{8,16},{9,... | collective-permute-start | bytes 196616 | tf_op jit(solution)/shard_map/ppermute | solution.py:738
  (17 other events, 171.2 us)

commit v6 on v5

--- a/solution.py
+++ b/solution.py
@@ -200,12 +200,24 @@
     copy.wait()
 
 
+def run_groups(begin, end, step):
+    def pair(number, unused):
+        step(begin + 2 * number, 2)
+        return unused
+
+    lax.fori_loop(0, (end - begin) // 2, pair, 0)
+
+    @pl.when((end - begin) % 2 == 1)
+    def _():
+        step(end - 1, 1)
+
+
 def rounded_up(number):
     return (number + GROUP - 1) // GROUP
 
 
-def finish_group(first_place, begin, end, finish):
-    for lane in range(GROUP):
+def finish_group(first_place, number, begin, end, finish):
+    for lane in range(number):
         place = first_place + lane
 
         @pl.when((place >= begin) & (place < end))
@@ -506,16 +518,15 @@
     for load in weights:
         load.wait()
 
-    def step(number, unused):
-        first_place = number * GROUP
-        places = [first_place + lane for lane in range(GROUP)]
+    def step(group, many):
+        first_place, number = group * GROUP, many * GROUP
+        places = [first_place + lane for lane in range(number)]
         values = jnp.concatenate([u[plan[BLOCK, place]] for place in places], axis=0)
         values = network(values, first, second, 512)
-        result[pl.ds(first_place, GROUP)] = values.reshape((GROUP,) + result.shape[1:])
-        finish_group(first_place, n_fed, own_count, finish)
-        return unused
-
-    lax.fori_loop(n_fed // GROUP, own_count // GROUP, step, 0)
+        result[pl.ds(first_place, number)] = values.reshape((number,) + result.shape[1:])
+        finish_group(first_place, number, n_fed, own_count, finish)
+
+    run_groups(n_fed // GROUP, own_count // GROUP, step)
     each_block(0, n_fed, save, wait)
     each_block(n_fed, own_count, finish, wait)
 
@@ -573,6 +584,7 @@
     groups = rounded_up(n_fed)
     groups_now = rounded_up(plan[COUNTS, N_NOW]) if with_send else groups
     apart = jnp.minimum(groups * GROUP, n_held)
+    early = jnp.minimum(groups, 2)
 
     def cut_of(group):
         return pl.ds(group * GROUP, GROUP)
@@ -595,7 +607,9 @@
             load.wait()
         if part == 0:
             weights = load_weights(layer, first_in, second_in, first, second, sem.at[pl.ds(0, 2)])
-            each_block(0, groups, load_base, start)
+            each_block(0, early, load_base, start)
+        if part == 2:
+            each_block(early, groups, load_base, start)
             if with_send:
                 each_block(apart, n_held, load_done, start)
         products = [dot(adj[slot], inc[slot]) for slot in range(part * size, (part + 1) * size)]
@@ -605,16 +619,16 @@
         load.wait()
     n_now = jnp.minimum(groups_now * GROUP, n_fed)
 
-    def step(group, unused):
-        load_base(group).wait()
-        cut = cut_of(group)
-        values = (u[cut] + extra[cut]).reshape(GROUP * u.shape[1], u.shape[2])
+    def step(group, many):
+        for offset in range(many):
+            load_base(group + offset).wait()
+        cut = pl.ds(group * GROUP, many * GROUP)
+        values = (u[cut] + extra[cut]).reshape(many * GROUP * u.shape[1], u.shape[2])
         values = network(values, first, second, 512)
-        result[cut] = values.reshape((GROUP,) + result.shape[1:])
-        finish_group(group * GROUP, 0, n_now, finish)
-        return unused
-
-    lax.fori_loop(0, groups_now, step, 0)
+        result[cut] = values.reshape((many * GROUP,) + result.shape[1:])
+        finish_group(group * GROUP, many * GROUP, 0, n_now, finish)
+
+    run_groups(0, groups_now, step)
     copies = []
     if with_send:
         each_block(n_fed, apart, load_done, start)
@@ -696,15 +710,17 @@
     for part in weights:
         part.wait()
 
-    def step(group, unused):
-        load(group).wait()
-        cut = pl.ds(group * GROUP, GROUP)
-        values = network(u[cut].reshape(GROUP * u.shape[1], u.shape[2]), first, second, 512)
-        result[cut] = values.reshape((GROUP,) + result.shape[1:])
-        finish_group(group * GROUP, 0, n_fed, finish)
-        return unused
-
-    lax.fori_loop(groups_now, groups, step, 0)
+    def step(group, many):
+        for offset in range(many):
+            load(group + offset).wait()
+        cut = pl.ds(group * GROUP, many * GROUP)
+        values = network(
+            u[cut].reshape(many * GROUP * u.shape[1], u.shape[2]), first, second, 512
+        )
+        result[cut] = values.reshape((many * GROUP,) + result.shape[1:])
+        finish_group(group * GROUP, many * GROUP, 0, n_fed, finish)
+
+    run_groups(groups_now, groups, step)
     each_block(jnp.minimum(groups_now * GROUP, n_fed), n_fed, finish, wait)
 
 
@@ -770,7 +786,7 @@
 def scatter_near(position, kept, sent, digits, local):
     received = [exchange(sent, digits[0][0])]
     for bit, radix in digits[1:-1]:
-        kept, *sent = combine(position, kept, received, bit, radix, local, bf16)
+        kept, *sent = combine(position, kept, received, bit, radix, local, f32)
         received = [exchange(part, bit * (1 + number)) for number, part in enumerate(sent)]
     return kept, received
 
@@ -803,8 +819,8 @@
 
     pieces = gather_far(hubs, digits)
     plan = make_plan(me, tile_count, tile_rows, local_cols, send_list, hub_count, own_count)
-    own, plan, *pieces = lax.optimization_barrier((own, plan, *pieces))
     outgoing = pack(send_list, own)
+    plan, outgoing, *pieces = lax.optimization_barrier((plan, outgoing, *pieces))
     pieces = gather_near(pieces, digits)
     outgoing, place_col, *pieces = lax.optimization_barrier((outgoing, place_col, *pieces))
     incoming = all_to_all(outgoing)
@@ -832,7 +848,7 @@
     base, done = before(1, plan, tile_count, hub_table, own, tiles, w_in, w_out, remote)
     kept, received = scatter_near(me, kept, sent, digits, local)
     base, done, *received = lax.optimization_barrier((base, done, *received))
-    parts = scatter_far(me, kept, received, digits, local, f32)
+    parts = scatter_far(me, kept, received, digits, local, bf16)
     (peri_out,) = after(1, plan, base, done, incoming, tiles, w_in, w_out, False)
     peri_out, *parts = lax.optimization_barrier((peri_out, *parts))
     hub_out = hub_network(1, mine, parts, w_in, w_out)

time: 172 us -> 169 us (0.983)
  starting transfers between devices: 46.9 us -> 52.2 us
  Pallas kernels: 74.8 us -> 69.9 us
  local copies, waits for them, and re-layouts: 3.34 us -> 1.26 us
    all_to_all x2, waiting for transfers between devices: 10.4 us -> 1.94 us  [body(): incoming = all_to_all(outgoing)]
    ppermute x28, waiting for transfers between devices: 32.9 us -> 40.1 us  [exchange(): return lax.ppermute(x, 'dev', [(i, i ^ bit) for i in range(devices)])]
    ppermute x28, starting transfers between devices: 37.8 us -> 41.9 us  [exchange(): return lax.ppermute(x, 'dev', [(i, i ^ bit) for i in range(devices)])]
    pallas_call x12, Pallas kernels: 44.5 us -> 41.1 us  [call(): pl.pallas_call(kernel, out_shape=out_shape, in_specs=in_specs, out_specs=...]
    unnamed x34 -> x36, local copies, waits for them, and re-layouts: 2.21 us -> 0.14 us
  transfers between devices with their start and end apart: 30 -> 30, of which waited for: 11 -> 15; matrix products, arithmetic and copies ran while one was open for 1% -> 1% of each run, Pallas kernels for 43% -> 41%
where the time goes in v6:
time: 169 us; the launch traced here: 167 us
  Pallas kernels  69.9 us (41%)
  starting transfers between devices  52.2 us (31%)
  waiting for transfers between devices  42.1 us (25%)
  between operations  1.87 us (1%)
    ppermute x28, starting transfers between devices, exchange(): return lax.ppermute(x, 'dev', [(i, i ^ bit) for i in range(devices)])  41.9 us
    pallas_call x12, Pallas kernels, call(): pl.pallas_call(kernel, out_shape=out_shape, in_specs=in_specs, out_specs=...  41.1 us
    ppermute x28, waiting for transfers between devices, exchange(): return lax.ppermute(x, 'dev', [(i, i ^ bit) for i in range(devices)])  40.1 us
    pallas_call x2, Pallas kernels, after(): pl.pallas_call(functools.partial(after_kernel, layer, with_send), out_sha...  22.3 us
    all_to_all x2, starting transfers between devices, body(): incoming = all_to_all(outgoing)  10.3 us
    pallas_call x1, Pallas kernels, late(): pl.pallas_call(functools.partial(late_kernel, layer), out_shape=shape_of(...  6.48 us
  transfers between devices with their start and end apart: 30, of which 15 were waited for; matrix products, arithmetic and copies ran while one was open for 1% of the time, Pallas kernels for 41%

profile of v6, /device:TPU:0, one launch (start us, length us, event | category | flops | bytes accessed | tf_op | source)
XLA Modules:
  0.0 167.3 jit_solution(16830885784336190303)
XLA Ops:
  0.6 4.1 %collective-permute-start.1 = (bf16[64,256]{1,0:T(8,128)(2,1)}, bf16[64,256]{1,0:T(8,128)(2,1)S(1)}, u32[]{:S(2)}, u32[]{:S(2)}) collective-permute-start(bf16[64,256]{1,0:T(8,128)(2,1)} %param.11), channel_id=1, source_target_pairs={{0,16},{1,17},{2,18},{3,19},{4,20},{5,21},{6,22},{7,23},{8,24},{9,... | collective-permute-start | bytes 98312 | tf_op jit(solution)/shard_map/ppermute | solution.py:754
  7.7 4.0 %pack.1 = bf16[32,128,256]{2,1,0:T(8,128)(2,1)} custom-call(s32[1,32]{1,0:T(1,128)} %chosen.3, bf16[32,128,256]{2,1,0:T(8,128)(2,1)} %bitcast.11), custom_call_target="tpu_custom_call" | custom-call | bytes 4194304 | tf_op jit(solution)/shard_map/pack/pallas_call | solution.py:30
  12.3 2.6 %collective-permute-start.5 = (bf16[256,256]{1,0:T(8,128)(2,1)S(1)}, bf16[256,256]{1,0:T(8,128)(2,1)S(1)}, u32[]{:S(2)}, u32[]{:S(2)}) collective-permute-start(bf16[256,256]{1,0:T(8,128)(2,1)S(1)} %constant_dynamic-update-slice_fusion), channel_id=1, source_target_pairs={{0,6},{1,7},{2,4},{3,5},{4,2},{5,3},{6,0},{7,1},{8,14},{9,15},{10,... | collective-permute-start | bytes 393224 | tf_op jit(solution)/shard_map/ppermute | solution.py:754
  15.8 3.2 %collective-permute-done.5 = bf16[256,256]{1,0:T(8,128)(2,1)S(1)} collective-permute-done((bf16[256,256]{1,0:T(8,128)(2,1)S(1)}, bf16[256,256]{1,0:T(8,128)(2,1)S(1)}, u32[]{:S(2)}, u32[]{:S(2)}) %collective-permute-start.5) | collective-permute-done | bytes 131104 | tf_op jit(solution)/shard_map/ppermute | solution.py:754
  20.7 5.1 %all-to-all-start = ((bf16[32,128,256]{2,1,0:T(8,128)(2,1)}), bf16[32,128,256]{2,1,0:T(8,128)(2,1)}, u32[]{:S(2)}, u32[]{:S(2)}) async-start(bf16[32,128,256]{2,1,0:T(8,128)(2,1)} %pack.1), calls=%async_computation | async-start | bytes 4194304 | tf_op jit(solution)/shard_map/all_to_all | solution.py:826
  27.9 5.3 %hub_first.1 = (bf16[16,128,256]{2,1,0:T(8,128)(2,1)S(1)}, bf16[64,256]{1,0:T(8,128)(2,1)S(1)}, f32[1024,256]{1,0:T(8,128)S(1)}, f32[1024,256]{1,0:T(8,128)S(1)}) custom-call(s32[8,256]{1,0:T(8,128)S(1)} %plan.1, s32[1]{0:T(128)S(6)} %copy.33.count, s32[1]{0:T(128)} %bitcast.position, s32[2048,1]{1,0:T(8,128)S(1)} %copy.16.place_col, ...), custom_call_target="tpu_custom_call" | custom-call | flops 2147483648 | bytes 14680064 | tf_op jit(solution)/shard_map/hub_first/pallas_call | solution.py:30
  33.8 2.3 %collective-permute-done.7.refs_0_ = f32[1024,256]{1,0:T(8,128)S(1)} collective-permute-done((f32[1024,256]{1,0:T(8,128)S(1)}, f32[1024,256]{1,0:T(8,128)S(1)}, u32[]{:S(2)}, u32[]{:S(2)}) %collective-permute-start.7) | collective-permute-done | bytes 1048608 | tf_op jit(solution)/shard_map/ppermute | solution.py:754
  36.3 3.7 %collective-permute-start.8 = (f32[256,256]{1,0:T(8,128)S(1)}, f32[256,256]{1,0:T(8,128)S(1)}, u32[]{:S(2)}, u32[]{:S(2)}) collective-permute-start(f32[256,256]{1,0:T(8,128)S(1)} %get-tuple-element.86), channel_id=1, source_target_pairs={{0,2},{1,3},{2,0},{3,1},{4,6},{5,7},{6,4},{7,5},{8,10},{9,11},{10,... | collective-permute-start | bytes 786440 | tf_op jit(solution)/shard_map/ppermute | solution.py:754
  41.7 10.0 %before.2 = (f32[32,128,256]{2,1,0:T(8,128)}, bf16[32,128,256]{2,1,0:T(8,128)(2,1)}) custom-call(s32[8,256]{1,0:T(8,128)} %copy-done.6, s32[1]{0:T(128)S(6)} %copy.33.count, bf16[16,128,256]{2,1,0:T(8,128)(2,1)} %copy-done.5, bf16[32,128,256]{2,1,0:T(8,128)(2,1)} %bitcast.13, bf16[144,128,128]{2,1,0:T(8,128)(2,1)} %tiles.3, bf16[2,256,2048]{2,1,0:T(8,128)(2,1)} %refs_4_.3, ...), custom_call_target="tpu_custom_call" | custom-call | flops 2863311616 | bytes 18874368 | tf_op jit(solution)/shard_map/before/pallas_call | solution.py:30
  52.6 9.1 %collective-permute-done.9.refs_1_ = f32[256,256]{1,0:T(8,128)S(1)} collective-permute-done((f32[256,256]{1,0:T(8,128)S(1)}, f32[256,256]{1,0:T(8,128)S(1)}, u32[]{:S(2)}, u32[]{:S(2)}) %collective-permute-start.9) | collective-permute-done | bytes 262176 | tf_op jit(solution)/shard_map/ppermute | solution.py:754
  61.9 3.3 %collective-permute-start.11 = (bf16[64,256]{1,0:T(8,128)(2,1)S(1)}, bf16[64,256]{1,0:T(8,128)(2,1)S(1)}, u32[]{:S(2)}, u32[]{:S(2)}) collective-permute-start(bf16[64,256]{1,0:T(8,128)(2,1)S(1)} %get-tuple-element.96), channel_id=1, source_target_pairs={{0,8},{1,9},{2,10},{3,11},{4,12},{5,13},{6,14},{7,15},{8,0},{9,1},... | collective-permute-start | bytes 98312 | tf_op jit(solution)/shard_map/ppermute | solution.py:754
  67.6 9.5 %collective-permute-done.12.refs_2_ = bf16[64,256]{1,0:T(8,128)(2,1)S(1)} collective-permute-done((bf16[64,256]{1,0:T(8,128)(2,1)S(1)}, bf16[64,256]{1,0:T(8,128)(2,1)S(1)}, u32[]{:S(2)}, u32[]{:S(2)}) %collective-permute-start.12) | collective-permute-done | bytes 32800 | tf_op jit(solution)/shard_map/ppermute | solution.py:754
  80.4 2.0 %collective-permute-start.14 = (bf16[64,256]{1,0:T(8,128)(2,1)S(1)}, bf16[64,256]{1,0:T(8,128)(2,1)S(1)}, u32[]{:S(2)}, u32[]{:S(2)}) collective-permute-start(bf16[64,256]{1,0:T(8,128)(2,1)S(1)} %hub_network.2), channel_id=1, source_target_pairs={{0,8},{1,9},{2,10},{3,11},{4,12},{5,13},{6,14},{7,15},{8,0},{9,1},... | collective-permute-start | bytes 98312 | tf_op jit(solution)/shard_map/ppermute | solution.py:754
  84.6 2.3 %collective-permute-start.19 = (bf16[256,256]{1,0:T(8,128)(2,1)S(1)}, bf16[256,256]{1,0:T(8,128)(2,1)S(1)}, u32[]{:S(2)}, u32[]{:S(2)}) collective-permute-start(bf16[256,256]{1,0:T(8,128)(2,1)S(1)} %constant_dynamic-update-slice_fusion.8), channel_id=1, source_target_pairs={{0,6},{1,7},{2,4},{3,5},{4,2},{5,3},{6,0},{7,1},{8,14},{9,15},{10,... | collective-permute-start | bytes 393224 | tf_op jit(solution)/shard_map/ppermute | solution.py:754
  88.2 10.4 %after.2 = (bf16[32,128,256]{2,1,0:T(8,128)(2,1)}, f32[32,128,256]{2,1,0:T(8,128)}, bf16[32,128,256]{2,1,0:T(8,128)(2,1)}) custom-call(s32[8,256]{1,0:T(8,128)} %copy-done.6, f32[32,128,256]{2,1,0:T(8,128)} %get-tuple-element.99.base, bf16[32,128,256]{2,1,0:T(8,128)(2,1)} %get-tuple-element.100.done, ...), custom_call_target="tpu_custom_call", output_to_operand_aliasing={{0}: (2, {}), {1}: (1, {})} | custom-call | flops 8589934592 | bytes 16777216 | tf_op jit(solution)/shard_map/after/pallas_call | solution.py:667
  98.6 5.2 %all-to-all-start.1 = ((bf16[32,128,256]{2,1,0:T(8,128)(2,1)}), bf16[32,128,256]{2,1,0:T(8,128)(2,1)}, u32[]{:S(2)}, u32[]{:S(2)}) async-start(bf16[32,128,256]{2,1,0:T(8,128)(2,1)} %get-tuple-element.123), calls=%async_computation.1 | async-start | bytes 4194304 | tf_op jit(solution)/shard_map/all_to_all | solution.py:842
  104.1 6.5 %late.1.own_hbm.own_in = bf16[32,128,256]{2,1,0:T(8,128)(2,1)} custom-call(s32[8,256]{1,0:T(8,128)} %copy-done.6, f32[32,128,256]{2,1,0:T(8,128)} %get-tuple-element.111.sums, bf16[32,128,256]{2,1,0:T(8,128)(2,1)} %get-tuple-element.112.done, bf16[2,256,2048]{2,1,0:T(8,128)(2,1)} %refs_4_.3, ...), custom_call_target="tpu_custom_call", output_to_operand_aliasing={{}: (2, {})} | custom-call | flops 2147483648 | bytes 5242880 | tf_op jit(solution)/shard_map/late/pallas_call | solution.py:729
  110.6 9.2 %hub_second.1 = (bf16[16,128,256]{2,1,0:T(8,128)(2,1)S(1)}, bf16[64,256]{1,0:T(8,128)(2,1)S(1)}, f32[1024,256]{1,0:T(8,128)S(1)}, f32[1024,256]{1,0:T(8,128)S(1)}) custom-call(s32[8,256]{1,0:T(8,128)S(1)} %copy-done.7, s32[1]{0:T(128)S(6)} %copy.33.count, s32[1]{0:T(128)} %bitcast.position, s32[1,2048]{1,0:T(1,128)S(1)} %bitcast.8, ...), custom_call_target="tpu_custom_call" | custom-call | flops 2147483648 | bytes 14680064 | tf_op jit(solution)/shard_map/hub_second/pallas_call | solution.py:30
  119.9 2.6 %collective-permute-done.21.refs_0_ = f32[1024,256]{1,0:T(8,128)S(1)} collective-permute-done((f32[1024,256]{1,0:T(8,128)S(1)}, f32[1024,256]{1,0:T(8,128)S(1)}, u32[]{:S(2)}, u32[]{:S(2)}) %collective-permute-start.21) | collective-permute-done | bytes 1048608 | tf_op jit(solution)/shard_map/ppermute | solution.py:754
  122.8 3.4 %collective-permute-start.22 = (f32[256,256]{1,0:T(8,128)S(1)}, f32[256,256]{1,0:T(8,128)S(1)}, u32[]{:S(2)}, u32[]{:S(2)}) collective-permute-start(f32[256,256]{1,0:T(8,128)S(1)} %get-tuple-element.118), channel_id=1, source_target_pairs={{0,2},{1,3},{2,0},{3,1},{4,6},{5,7},{6,4},{7,5},{8,10},{9,11},{10,... | collective-permute-start | bytes 786440 | tf_op jit(solution)/shard_map/ppermute | solution.py:754
  128.2 9.5 %before.3 = (f32[32,128,256]{2,1,0:T(8,128)}, bf16[32,128,256]{2,1,0:T(8,128)(2,1)}) custom-call(s32[8,256]{1,0:T(8,128)} %copy-done.6, s32[1]{0:T(128)S(6)} %copy.33.count, bf16[16,128,256]{2,1,0:T(8,128)(2,1)} %copy-done.4, bf16[32,128,256]{2,1,0:T(8,128)(2,1)} %late.1.own_hbm.own_in, bf16[144,128,128]{2,1,0:T(8,128)(2,1)} %tiles.3, ...), custom_call_target="tpu_custom_call" | custom-call | flops 2863311616 | bytes 18874368 | tf_op jit(solution)/shard_map/before/pallas_call | solution.py:30
  137.8 6.8 %collective-permute-done.23.refs_1_ = f32[256,256]{1,0:T(8,128)S(1)} collective-permute-done((f32[256,256]{1,0:T(8,128)S(1)}, f32[256,256]{1,0:T(8,128)S(1)}, u32[]{:S(2)}, u32[]{:S(2)}) %collective-permute-start.23) | collective-permute-done | bytes 262176 | tf_op jit(solution)/shard_map/ppermute | solution.py:754
  144.7 4.0 %collective-permute-start.25 = (bf16[64,256]{1,0:T(8,128)(2,1)S(1)}, bf16[64,256]{1,0:T(8,128)(2,1)S(1)}, u32[]{:S(2)}, u32[]{:S(2)}) collective-permute-start(bf16[64,256]{1,0:T(8,128)(2,1)S(1)} %get-tuple-element.129), channel_id=1, source_target_pairs={{0,8},{1,9},{2,10},{3,11},{4,12},{5,13},{6,14},{7,15},{8,0},{9,1},... | collective-permute-start | bytes 98312 | tf_op jit(solution)/shard_map/ppermute | solution.py:754
  153.7 11.9 %after.3 = bf16[32,128,256]{2,1,0:T(8,128)(2,1)} custom-call(s32[8,256]{1,0:T(8,128)} %copy-done.6, f32[32,128,256]{2,1,0:T(8,128)} %get-tuple-element.121.base, bf16[32,128,256]{2,1,0:T(8,128)(2,1)} %get-tuple-element.122.done, bf16[32,128,256]{2,1,0:T(8,128)(2,1)} %all-to-all-done.1.incoming, ...), custom_call_target="tpu_custom_call", output_to_operand_aliasing={{}: (2, {})} | custom-call | flops 8589934592 | bytes 16777216 | tf_op jit(solution)/shard_map/after/pallas_call | solution.py:667
  (93 shorter events, 29.3 us)
Async XLA Ops:
  0.6 11.4 %collective-permute-start.1 = (bf16[64,256]{1,0:T(8,128)(2,1)}, bf16[64,256]{1,0:T(8,128)(2,1)S(1)}, u32[]{:S(2)}, u32[]{:S(2)}) collective-permute-start(bf16[64,256]{1,0:T(8,128)(2,1)} %param.11), channel_id=1, source_target_pairs={{0,16},{1,17},{2,18},{3,19},{4,20},{5,21},{6,22},{7,23},{8,24},{9,... | collective-permute-start | bytes 98312 | tf_op jit(solution)/shard_map/ppermute | solution.py:754
  4.7 7.3 %collective-permute-start = (bf16[64,256]{1,0:T(8,128)(2,1)}, bf16[64,256]{1,0:T(8,128)(2,1)S(1)}, u32[]{:S(2)}, u32[]{:S(2)}) collective-permute-start(bf16[64,256]{1,0:T(8,128)(2,1)} %param.11), channel_id=1, source_target_pairs={{0,8},{1,9},{2,10},{3,11},{4,12},{5,13},{6,14},{7,15},{8,0},{9,1},... | collective-permute-start | bytes 98312 | tf_op jit(solution)/shard_map/ppermute | solution.py:754
  6.3 5.9 %collective-permute-start.2 = (bf16[64,256]{1,0:T(8,128)(2,1)}, bf16[64,256]{1,0:T(8,128)(2,1)S(1)}, u32[]{:S(2)}, u32[]{:S(2)}) collective-permute-start(bf16[64,256]{1,0:T(8,128)(2,1)} %param.11), channel_id=1, source_target_pairs={{0,24},{1,25},{2,26},{3,27},{4,28},{5,29},{6,30},{7,31},{8,16},{9,... | collective-permute-start | bytes 98312 | tf_op jit(solution)/shard_map/ppermute | solution.py:754
  12.3 6.7 %collective-permute-start.5 = (bf16[256,256]{1,0:T(8,128)(2,1)S(1)}, bf16[256,256]{1,0:T(8,128)(2,1)S(1)}, u32[]{:S(2)}, u32[]{:S(2)}) collective-permute-start(bf16[256,256]{1,0:T(8,128)(2,1)S(1)} %constant_dynamic-update-slice_fusion), channel_id=1, source_target_pairs={{0,6},{1,7},{2,4},{3,5},{4,2},{5,3},{6,0},{7,1},{8,14},{9,15},{10,... | collective-permute-start | bytes 393224 | tf_op jit(solution)/shard_map/ppermute | solution.py:754
  14.9 5.7 %collective-permute-start.4 = (bf16[256,256]{1,0:T(8,128)(2,1)S(1)}, bf16[256,256]{1,0:T(8,128)(2,1)S(1)}, u32[]{:S(2)}, u32[]{:S(2)}) collective-permute-start(bf16[256,256]{1,0:T(8,128)(2,1)S(1)} %constant_dynamic-update-slice_fusion), channel_id=1, source_target_pairs={{0,4},{1,5},{2,6},{3,7},{4,0},{5,1},{6,2},{7,3},{8,12},{9,13},{10,... | collective-permute-start | bytes 393224 | tf_op jit(solution)/shard_map/ppermute | solution.py:754
  20.7 67.5 %all-to-all-start = ((bf16[32,128,256]{2,1,0:T(8,128)(2,1)}), bf16[32,128,256]{2,1,0:T(8,128)(2,1)}, u32[]{:S(2)}, u32[]{:S(2)}) async-start(bf16[32,128,256]{2,1,0:T(8,128)(2,1)} %pack.1), calls=%async_computation | async-start | bytes 4194304 | tf_op jit(solution)/shard_map/all_to_all | solution.py:826
  36.3 16.3 %collective-permute-start.8 = (f32[256,256]{1,0:T(8,128)S(1)}, f32[256,256]{1,0:T(8,128)S(1)}, u32[]{:S(2)}, u32[]{:S(2)}) collective-permute-start(f32[256,256]{1,0:T(8,128)S(1)} %get-tuple-element.86), channel_id=1, source_target_pairs={{0,2},{1,3},{2,0},{3,1},{4,6},{5,7},{6,4},{7,5},{8,10},{9,11},{10,... | collective-permute-start | bytes 786440 | tf_op jit(solution)/shard_map/ppermute | solution.py:754
  40.0 21.8 %collective-permute-start.9 = (f32[256,256]{1,0:T(8,128)S(1)}, f32[256,256]{1,0:T(8,128)S(1)}, u32[]{:S(2)}, u32[]{:S(2)}) collective-permute-start(f32[256,256]{1,0:T(8,128)S(1)} %get-tuple-element.87), channel_id=1, source_target_pairs={{0,4},{1,5},{2,6},{3,7},{4,0},{5,1},{6,2},{7,3},{8,12},{9,13},{10,... | collective-permute-start | bytes 786440 | tf_op jit(solution)/shard_map/ppermute | solution.py:754
  41.7 20.1 %collective-permute-start.10 = (f32[256,256]{1,0:T(8,128)S(1)}, f32[256,256]{1,0:T(8,128)S(1)}, u32[]{:S(2)}, u32[]{:S(2)}) collective-permute-start(f32[256,256]{1,0:T(8,128)S(1)} %get-tuple-element.88), channel_id=1, source_target_pairs={{0,6},{1,7},{2,4},{3,5},{4,2},{5,3},{6,0},{7,1},{8,14},{9,15},{10,... | collective-permute-start | bytes 786440 | tf_op jit(solution)/shard_map/ppermute | solution.py:754
  61.9 5.8 %collective-permute-start.11 = (bf16[64,256]{1,0:T(8,128)(2,1)S(1)}, bf16[64,256]{1,0:T(8,128)(2,1)S(1)}, u32[]{:S(2)}, u32[]{:S(2)}) collective-permute-start(bf16[64,256]{1,0:T(8,128)(2,1)S(1)} %get-tuple-element.96), channel_id=1, source_target_pairs={{0,8},{1,9},{2,10},{3,11},{4,12},{5,13},{6,14},{7,15},{8,0},{9,1},... | collective-permute-start | bytes 98312 | tf_op jit(solution)/shard_map/ppermute | solution.py:754
  65.2 12.0 %collective-permute-start.12 = (bf16[64,256]{1,0:T(8,128)(2,1)S(1)}, bf16[64,256]{1,0:T(8,128)(2,1)S(1)}, u32[]{:S(2)}, u32[]{:S(2)}) collective-permute-start(bf16[64,256]{1,0:T(8,128)(2,1)S(1)} %get-tuple-element.97), channel_id=1, source_target_pairs={{0,16},{1,17},{2,18},{3,19},{4,20},{5,21},{6,22},{7,23},{8,24},{9,... | collective-permute-start | bytes 98312 | tf_op jit(solution)/shard_map/ppermute | solution.py:754
  65.7 11.4 %collective-permute-start.13 = (bf16[64,256]{1,0:T(8,128)(2,1)S(1)}, bf16[64,256]{1,0:T(8,128)(2,1)S(1)}, u32[]{:S(2)}, u32[]{:S(2)}) collective-permute-start(bf16[64,256]{1,0:T(8,128)(2,1)S(1)} %get-tuple-element.98), channel_id=1, source_target_pairs={{0,24},{1,25},{2,26},{3,27},{4,28},{5,29},{6,30},{7,31},{8,16},{9,... | collective-permute-start | bytes 98312 | tf_op jit(solution)/shard_map/ppermute | solution.py:754
  77.9 5.8 %collective-permute-start.16 = (bf16[64,256]{1,0:T(8,128)(2,1)S(1)}, bf16[64,256]{1,0:T(8,128)(2,1)S(1)}, u32[]{:S(2)}, u32[]{:S(2)}) collective-permute-start(bf16[64,256]{1,0:T(8,128)(2,1)S(1)} %hub_network.2), channel_id=1, source_target_pairs={{0,24},{1,25},{2,26},{3,27},{4,28},{5,29},{6,30},{7,31},{8,16},{9,... | collective-permute-start | bytes 98312 | tf_op jit(solution)/shard_map/ppermute | solution.py:754
  84.6 14.0 %collective-permute-start.19 = (bf16[256,256]{1,0:T(8,128)(2,1)S(1)}, bf16[256,256]{1,0:T(8,128)(2,1)S(1)}, u32[]{:S(2)}, u32[]{:S(2)}) collective-permute-start(bf16[256,256]{1,0:T(8,128)(2,1)S(1)} %constant_dynamic-update-slice_fusion.8), channel_id=1, source_target_pairs={{0,6},{1,7},{2,4},{3,5},{4,2},{5,3},{6,0},{7,1},{8,14},{9,15},{10,... | collective-permute-start | bytes 393224 | tf_op jit(solution)/shard_map/ppermute | solution.py:754
  86.9 11.6 %collective-permute-start.18 = (bf16[256,256]{1,0:T(8,128)(2,1)S(1)}, bf16[256,256]{1,0:T(8,128)(2,1)S(1)}, u32[]{:S(2)}, u32[]{:S(2)}) collective-permute-start(bf16[256,256]{1,0:T(8,128)(2,1)S(1)} %constant_dynamic-update-slice_fusion.8), channel_id=1, source_target_pairs={{0,4},{1,5},{2,6},{3,7},{4,0},{5,1},{6,2},{7,3},{8,12},{9,13},{10,... | collective-permute-start | bytes 393224 | tf_op jit(solution)/shard_map/ppermute | solution.py:754
  87.5 11.1 %collective-permute-start.17 = (bf16[256,256]{1,0:T(8,128)(2,1)S(1)}, bf16[256,256]{1,0:T(8,128)(2,1)S(1)}, u32[]{:S(2)}, u32[]{:S(2)}) collective-permute-start(bf16[256,256]{1,0:T(8,128)(2,1)S(1)} %constant_dynamic-update-slice_fusion.8), channel_id=1, source_target_pairs={{0,2},{1,3},{2,0},{3,1},{4,6},{5,7},{6,4},{7,5},{8,10},{9,11},{10,... | collective-permute-start | bytes 393224 | tf_op jit(solution)/shard_map/ppermute | solution.py:754
  98.6 55.1 %all-to-all-start.1 = ((bf16[32,128,256]{2,1,0:T(8,128)(2,1)}), bf16[32,128,256]{2,1,0:T(8,128)(2,1)}, u32[]{:S(2)}, u32[]{:S(2)}) async-start(bf16[32,128,256]{2,1,0:T(8,128)(2,1)} %get-tuple-element.123), calls=%async_computation.1 | async-start | bytes 4194304 | tf_op jit(solution)/shard_map/all_to_all | solution.py:842
  103.9 6.7 %collective-permute-start.20 = (bf16[1024,256]{1,0:T(8,128)(2,1)S(1)}, bf16[1024,256]{1,0:T(8,128)(2,1)S(1)}, u32[]{:S(2)}, u32[]{:S(2)}) collective-permute-start(bf16[1024,256]{1,0:T(8,128)(2,1)S(1)} %constant_dynamic-update-slice_fusion.12.half0), channel_id=1, source_target_pairs={{0,1},{1,0},{2,3},{3,2},{4,5},{5,4},{6,7},{7,6},{8,9},{9,8},{10,11... | collective-permute-start | bytes 1572872 | tf_op jit(solution)/shard_map/ppermute | solution.py:754
  122.8 15.0 %collective-permute-start.22 = (f32[256,256]{1,0:T(8,128)S(1)}, f32[256,256]{1,0:T(8,128)S(1)}, u32[]{:S(2)}, u32[]{:S(2)}) collective-permute-start(f32[256,256]{1,0:T(8,128)S(1)} %get-tuple-element.118), channel_id=1, source_target_pairs={{0,2},{1,3},{2,0},{3,1},{4,6},{5,7},{6,4},{7,5},{8,10},{9,11},{10,... | collective-permute-start | bytes 786440 | tf_op jit(solution)/shard_map/ppermute | solution.py:754
  126.2 18.5 %collective-permute-start.23 = (f32[256,256]{1,0:T(8,128)S(1)}, f32[256,256]{1,0:T(8,128)S(1)}, u32[]{:S(2)}, u32[]{:S(2)}) collective-permute-start(f32[256,256]{1,0:T(8,128)S(1)} %get-tuple-element.119), channel_id=1, source_target_pairs={{0,4},{1,5},{2,6},{3,7},{4,0},{5,1},{6,2},{7,3},{8,12},{9,13},{10,... | collective-permute-start | bytes 786440 | tf_op jit(solution)/shard_map/ppermute | solution.py:754
  127.6 17.1 %collective-permute-start.24 = (f32[256,256]{1,0:T(8,128)S(1)}, f32[256,256]{1,0:T(8,128)S(1)}, u32[]{:S(2)}, u32[]{:S(2)}) collective-permute-start(f32[256,256]{1,0:T(8,128)S(1)} %get-tuple-element.120), channel_id=1, source_target_pairs={{0,6},{1,7},{2,4},{3,5},{4,2},{5,3},{6,0},{7,1},{8,14},{9,15},{10,... | collective-permute-start | bytes 786440 | tf_op jit(solution)/shard_map/ppermute | solution.py:754
  144.7 20.9 %collective-permute-start.25 = (bf16[64,256]{1,0:T(8,128)(2,1)S(1)}, bf16[64,256]{1,0:T(8,128)(2,1)S(1)}, u32[]{:S(2)}, u32[]{:S(2)}) collective-permute-start(bf16[64,256]{1,0:T(8,128)(2,1)S(1)} %get-tuple-element.129), channel_id=1, source_target_pairs={{0,8},{1,9},{2,10},{3,11},{4,12},{5,13},{6,14},{7,15},{8,0},{9,1},... | collective-permute-start | bytes 98312 | tf_op jit(solution)/shard_map/ppermute | solution.py:754
  148.8 16.9 %collective-permute-start.26 = (bf16[64,256]{1,0:T(8,128)(2,1)S(1)}, bf16[64,256]{1,0:T(8,128)(2,1)S(1)}, u32[]{:S(2)}, u32[]{:S(2)}) collective-permute-start(bf16[64,256]{1,0:T(8,128)(2,1)S(1)} %get-tuple-element.130), channel_id=1, source_target_pairs={{0,16},{1,17},{2,18},{3,19},{4,20},{5,21},{6,22},{7,23},{8,24},{9,... | collective-permute-start | bytes 98312 | tf_op jit(solution)/shard_map/ppermute | solution.py:754
  150.4 15.3 %collective-permute-start.27 = (bf16[64,256]{1,0:T(8,128)(2,1)S(1)}, bf16[64,256]{1,0:T(8,128)(2,1)S(1)}, u32[]{:S(2)}, u32[]{:S(2)}) collective-permute-start(bf16[64,256]{1,0:T(8,128)(2,1)S(1)} %get-tuple-element.131), channel_id=1, source_target_pairs={{0,24},{1,25},{2,26},{3,27},{4,28},{5,29},{6,30},{7,31},{8,16},{9,... | collective-permute-start | bytes 98312 | tf_op jit(solution)/shard_map/ppermute | solution.py:754
  (18 other events, 172.2 us)

commit v7 on v6

--- a/solution.py
+++ b/solution.py
@@ -264,11 +264,13 @@
     return slot % 2, place
 
 
-def place_shards(me, halves, table, digits, local):
+def place_shards(me, halves, table, digits, local, in_order):
+    bit = digits[-1][0]
     for slot in range(table.shape[0] // local):
         half, place = slot_place(slot, digits)
-        start = pl.multiple_of((me ^ slot) * local, local)
-        table[pl.ds(start, local), :] = halves[half][place * local : (place + 1) * local, :]
+        device = slot // bit * bit + (lax.rem(me, bit) ^ (slot % bit)) if in_order else me ^ slot
+        first_row = pl.multiple_of(device * local, local)
+        table[pl.ds(first_row, local), :] = halves[half][place * local : (place + 1) * local, :]
 
 
 def split_sums(me, sums, local, kept, sent):
@@ -285,14 +287,14 @@
 ):
     hub_count, block_size, width = hubs.shape
     hub_rows = hub_count * block_size
-    local = mine.shape[0]
+    local = mine.shape[0] // digits[-1][1]
     remote = tiles_hbm.shape[0] - tiles.shape[0]
     loads = tile_loads(tiles_hbm, tiles, sems)
     load = pltpu.make_async_copy(own_hbm, own, sems.at[4])
     load.start()
     for_live(count, loads, start)
     me = position[0]
-    place_shards(me, (half0, half1), table, digits, local)
+    place_shards(me, (half0, half1), table, digits, local, False)
     total[...] = jnp.zeros_like(total)
     step = 2 * block_size
 
@@ -310,7 +312,10 @@
     add_products(plan, 0, plan[COUNTS, N_HUB], remote, tiles, hubs, own, total, 0, hub_count)
     split_sums(me, total[:hub_count], local, kept, sent)
     flat = hubs.reshape(hub_rows, width)
-    mine[...] = flat[pl.ds(pl.multiple_of(me * local, local), local), :]
+    bit, radix = digits[-1]
+    for digit in range(radix):
+        first_row = pl.multiple_of((digit * bit + lax.rem(me, bit)) * local, local)
+        mine[digit * local : (digit + 1) * local, :] = flat[pl.ds(first_row, local), :]
 
 
 def hub_first(digits, plan, count, position, place_col, halves, own, tiles, local, remote):
@@ -326,7 +331,7 @@
         14 * MIB,
         (
             shape_of((hub_count, block_size, width), bf16),
-            shape_of((local, width), bf16),
+            shape_of((digits[-1][1] * local, width), bf16),
             half,
             half,
         ),
@@ -357,7 +362,7 @@
     for_live(count, loads, start)
     me = position[0]
     flat = hubs.reshape(hub_rows, width)
-    place_shards(me, (half0, half1), flat, digits, local)
+    place_shards(me, (half0, half1), flat, digits, local, True)
     total[...] = jnp.zeros_like(total)
 
     def unit_rows(start, step):
@@ -444,6 +449,28 @@
     )
 
 
+def total_kernel(*refs):
+    total = refs[0][...].astype(f32)
+    for part in refs[1:-1]:
+        total = total + part[...].astype(f32)
+    refs[-1][...] = total.astype(bf16)
+
+
+def total(parts):
+    return call(
+        total_kernel,
+        "total",
+        16,
+        parts[0].size,
+        8 * parts[0].size,
+        shape_of(parts[0].shape, bf16),
+        [VMEM] * len(parts),
+        VMEM,
+        [],
+        tuple(parts),
+    )
+
+
 def load_weights(layer, first_in, second_in, first, second, sems):
     loads = [
         pltpu.make_async_copy(first_in.at[layer], first, sems.at[0]),
@@ -462,7 +489,7 @@
         u = u + part[...].astype(f32)
     for load in loads:
         load.wait()
-    out[...] = network(u, first, second, first.shape[-1])
+    out[...] = network(u, first, second, 512)
 
 
 def hub_network(layer, rows_in, parts, first, second):
@@ -797,6 +824,16 @@
     return [kept] + [exchange(part, bit * (1 + number)) for number, part in enumerate(sent)]
 
 
+def share_far(kept, received, digits):
+    bit, radix = digits[-1]
+    parts = [kept] + received
+    while radix > 1:
+        mine = total(parts)
+        parts = [mine, exchange(mine, bit)]
+        bit, radix = 2 * bit, radix // 2
+    return parts
+
+
 def body(
     peripheral, hubs, tiles, tile_rows, local_cols, tile_count, send_list, hub_place, w_in, w_out
 ):
@@ -831,13 +868,12 @@
     base, done = before(0, plan, tile_count, hub_table, own, tiles, w_in, w_out, remote)
     kept, received = scatter_near(me, kept, sent, digits, local)
     base, done, *received = lax.optimization_barrier((base, done, *received))
-    parts = scatter_far(me, kept, received, digits, local, bf16)
+    parts = share_far(kept, received, digits)
     hub_new = hub_network(0, mine, parts, w_in, w_out)
-    pieces = gather_far(hub_new, digits)
-    base, *pieces = lax.optimization_barrier((base, *pieces))
+    base, hub_new = lax.optimization_barrier((base, hub_new))
     done, sums, outgoing = after(0, plan, base, done, incoming, tiles, w_in, w_out, True)
 
-    pieces = gather_near(pieces, digits)
+    pieces = gather_near([hub_new], digits)
     outgoing, *pieces = lax.optimization_barrier((outgoing, *pieces))
     incoming = all_to_all(outgoing)
     own = late(0, plan, sums, done, w_in, w_out)

time: 169 us -> 166 us (0.982)
  starting transfers between devices: 52.2 us -> 44.5 us
  Pallas kernels: 69.9 us -> 74.4 us
    ppermute x28 -> x24, starting transfers between devices: 41.9 us -> 34.1 us  [exchange(): return lax.ppermute(x, 'dev', [(i, i ^ bit) for i in range(devices)])]
    pallas_call x12 -> x13, Pallas kernels: 41.1 us -> 45 us  [call(): pl.pallas_call(kernel, out_shape=out_shape, in_specs=in_specs, out_specs=...]
    ppermute x28 -> x24, waiting for transfers between devices: 40.1 us -> 41.1 us  [exchange(): return lax.ppermute(x, 'dev', [(i, i ^ bit) for i in range(devices)])]
  transfers between devices with their start and end apart: 30 -> 26, of which waited for: 15 -> 14; matrix products, arithmetic and copies ran while one was open for 1% -> 1% of each run, Pallas kernels for 41% -> 44%
where the time goes in v7:
time: 166 us; the launch traced here: 165 us
  Pallas kernels  74.4 us (45%)
  starting transfers between devices  44.5 us (27%)
  waiting for transfers between devices  42.9 us (26%)
  between operations  1.83 us (1%)
    pallas_call x13, Pallas kernels, call(): pl.pallas_call(kernel, out_shape=out_shape, in_specs=in_specs, out_specs=...  45 us
    ppermute x24, waiting for transfers between devices, exchange(): return lax.ppermute(x, 'dev', [(i, i ^ bit) for i in range(devices)])  41.1 us
    ppermute x24, starting transfers between devices, exchange(): return lax.ppermute(x, 'dev', [(i, i ^ bit) for i in range(devices)])  34.1 us
    pallas_call x2, Pallas kernels, after(): pl.pallas_call(functools.partial(after_kernel, layer, with_send), out_sha...  23.1 us
    all_to_all x2, starting transfers between devices, body(): incoming = all_to_all(outgoing)  10.4 us
    pallas_call x1, Pallas kernels, late(): pl.pallas_call(functools.partial(late_kernel, layer), out_shape=shape_of(...  6.36 us
  transfers between devices with their start and end apart: 26, of which 14 were waited for; matrix products, arithmetic and copies ran while one was open for 1% of the time, Pallas kernels for 44%

profile of v7, /device:TPU:0, one launch (start us, length us, event | category | flops | bytes accessed | tf_op | source)
XLA Modules:
  0.0 164.9 jit_solution(3761825111022383760)
XLA Ops:
  0.6 4.1 %collective-permute-start.1 = (bf16[64,256]{1,0:T(8,128)(2,1)}, bf16[64,256]{1,0:T(8,128)(2,1)S(1)}, u32[]{:S(2)}, u32[]{:S(2)}) collective-permute-start(bf16[64,256]{1,0:T(8,128)(2,1)} %param.11), channel_id=1, source_target_pairs={{0,16},{1,17},{2,18},{3,19},{4,20},{5,21},{6,22},{7,23},{8,24},{9,... | collective-permute-start | bytes 98312 | tf_op jit(solution)/shard_map/ppermute | solution.py:781
  7.7 4.0 %pack.1 = bf16[32,128,256]{2,1,0:T(8,128)(2,1)} custom-call(s32[1,32]{1,0:T(1,128)} %chosen.3, bf16[32,128,256]{2,1,0:T(8,128)(2,1)} %bitcast.11), custom_call_target="tpu_custom_call" | custom-call | bytes 4194304 | tf_op jit(solution)/shard_map/pack/pallas_call | solution.py:30
  12.3 2.6 %collective-permute-start.5 = (bf16[256,256]{1,0:T(8,128)(2,1)S(1)}, bf16[256,256]{1,0:T(8,128)(2,1)S(1)}, u32[]{:S(2)}, u32[]{:S(2)}) collective-permute-start(bf16[256,256]{1,0:T(8,128)(2,1)S(1)} %constant_dynamic-update-slice_fusion), channel_id=1, source_target_pairs={{0,6},{1,7},{2,4},{3,5},{4,2},{5,3},{6,0},{7,1},{8,14},{9,15},{10,... | collective-permute-start | bytes 393224 | tf_op jit(solution)/shard_map/ppermute | solution.py:781
  15.8 3.2 %collective-permute-done.5 = bf16[256,256]{1,0:T(8,128)(2,1)S(1)} collective-permute-done((bf16[256,256]{1,0:T(8,128)(2,1)S(1)}, bf16[256,256]{1,0:T(8,128)(2,1)S(1)}, u32[]{:S(2)}, u32[]{:S(2)}) %collective-permute-start.5) | collective-permute-done | bytes 131104 | tf_op jit(solution)/shard_map/ppermute | solution.py:781
  20.7 5.1 %all-to-all-start = ((bf16[32,128,256]{2,1,0:T(8,128)(2,1)}), bf16[32,128,256]{2,1,0:T(8,128)(2,1)}, u32[]{:S(2)}, u32[]{:S(2)}) async-start(bf16[32,128,256]{2,1,0:T(8,128)(2,1)} %pack.1), calls=%async_computation | async-start | bytes 4194304 | tf_op jit(solution)/shard_map/all_to_all | solution.py:863
  27.9 5.6 %hub_first.1 = (bf16[16,128,256]{2,1,0:T(8,128)(2,1)S(1)}, bf16[256,256]{1,0:T(8,128)(2,1)S(1)}, f32[1024,256]{1,0:T(8,128)S(1)}, f32[1024,256]{1,0:T(8,128)S(1)}) custom-call(s32[8,256]{1,0:T(8,128)S(1)} %plan.1, s32[1]{0:T(128)S(6)} %copy.30.count, s32[1]{0:T(128)} %bitcast.position, s32[2048,1]{1,0:T(8,128)S(1)} %copy.16.place_col, ...), custom_call_target="tpu_custom_call" | custom-call | flops 2147483648 | bytes 14680064 | tf_op jit(solution)/shard_map/hub_first/pallas_call | solution.py:30
  33.8 2.5 %collective-permute-done.7.refs_0_ = f32[1024,256]{1,0:T(8,128)S(1)} collective-permute-done((f32[1024,256]{1,0:T(8,128)S(1)}, f32[1024,256]{1,0:T(8,128)S(1)}, u32[]{:S(2)}, u32[]{:S(2)}) %collective-permute-start.7) | collective-permute-done | bytes 1048608 | tf_op jit(solution)/shard_map/ppermute | solution.py:781
  40.6 11.1 %before.2 = (f32[32,128,256]{2,1,0:T(8,128)}, bf16[32,128,256]{2,1,0:T(8,128)(2,1)}) custom-call(s32[8,256]{1,0:T(8,128)} %copy-done.6, s32[1]{0:T(128)S(6)} %copy.30.count, bf16[16,128,256]{2,1,0:T(8,128)(2,1)} %copy-done.5, bf16[32,128,256]{2,1,0:T(8,128)(2,1)} %bitcast.13, bf16[144,128,128]{2,1,0:T(8,128)(2,1)} %tiles.3, bf16[2,256,2048]{2,1,0:T(8,128)(2,1)} %refs_4_.1, ...), custom_call_target="tpu_custom_call" | custom-call | flops 2863311616 | bytes 18874368 | tf_op jit(solution)/shard_map/before/pallas_call | solution.py:30
  52.4 8.6 %collective-permute-done.9.refs_2_ = f32[256,256]{1,0:T(8,128)S(1)} collective-permute-done((f32[256,256]{1,0:T(8,128)S(1)}, f32[256,256]{1,0:T(8,128)S(1)}, u32[]{:S(2)}, u32[]{:S(2)}) %collective-permute-start.9) | collective-permute-done | bytes 262176 | tf_op jit(solution)/shard_map/ppermute | solution.py:781
  61.0 1.8 %collective-permute-start.11 = (bf16[256,256]{1,0:T(8,128)(2,1)S(1)}, bf16[256,256]{1,0:T(8,128)(2,1)S(1)}, u32[]{:S(2)}, u32[]{:S(2)}) collective-permute-start(bf16[256,256]{1,0:T(8,128)(2,1)S(1)} %total.2.refs_0_), channel_id=1, source_target_pairs={{0,8},{1,9},{2,10},{3,11},{4,12},{5,13},{6,14},{7,15},{8,0},{9,1},... | collective-permute-start | bytes 393224 | tf_op jit(solution)/shard_map/ppermute | solution.py:781
  62.8 4.6 %collective-permute-done.11.refs_1_ = bf16[256,256]{1,0:T(8,128)(2,1)S(1)} collective-permute-done((bf16[256,256]{1,0:T(8,128)(2,1)S(1)}, bf16[256,256]{1,0:T(8,128)(2,1)S(1)}, u32[]{:S(2)}, u32[]{:S(2)}) %collective-permute-start.11) | collective-permute-done | bytes 131104 | tf_op jit(solution)/shard_map/ppermute | solution.py:781
  67.5 3.5 %collective-permute-start.12 = (bf16[256,256]{1,0:T(8,128)(2,1)S(1)}, bf16[256,256]{1,0:T(8,128)(2,1)S(1)}, u32[]{:S(2)}, u32[]{:S(2)}) collective-permute-start(bf16[256,256]{1,0:T(8,128)(2,1)S(1)} %total.3.refs_0_), channel_id=1, source_target_pairs={{0,16},{1,17},{2,18},{3,19},{4,20},{5,21},{6,22},{7,23},{8,24},{9,... | collective-permute-start | bytes 393224 | tf_op jit(solution)/shard_map/ppermute | solution.py:781
  71.0 9.3 %collective-permute-done.12.refs_1_ = bf16[256,256]{1,0:T(8,128)(2,1)S(1)} collective-permute-done((bf16[256,256]{1,0:T(8,128)(2,1)S(1)}, bf16[256,256]{1,0:T(8,128)(2,1)S(1)}, u32[]{:S(2)}, u32[]{:S(2)}) %collective-permute-start.12) | collective-permute-done | bytes 131104 | tf_op jit(solution)/shard_map/ppermute | solution.py:781
  81.4 2.3 %collective-permute-start.15 = (bf16[256,256]{1,0:T(8,128)(2,1)S(1)}, bf16[256,256]{1,0:T(8,128)(2,1)S(1)}, u32[]{:S(2)}, u32[]{:S(2)}) collective-permute-start(bf16[256,256]{1,0:T(8,128)(2,1)S(1)} %hub_network.2), channel_id=1, source_target_pairs={{0,6},{1,7},{2,4},{3,5},{4,2},{5,3},{6,0},{7,1},{8,14},{9,15},{10,... | collective-permute-start | bytes 393224 | tf_op jit(solution)/shard_map/ppermute | solution.py:781
  85.0 11.3 %after.2 = (bf16[32,128,256]{2,1,0:T(8,128)(2,1)}, f32[32,128,256]{2,1,0:T(8,128)}, bf16[32,128,256]{2,1,0:T(8,128)(2,1)}) custom-call(s32[8,256]{1,0:T(8,128)} %copy-done.6, f32[32,128,256]{2,1,0:T(8,128)} %get-tuple-element.88.base, bf16[32,128,256]{2,1,0:T(8,128)(2,1)} %get-tuple-element.89.done, ...), custom_call_target="tpu_custom_call", output_to_operand_aliasing={{0}: (2, {}), {1}: (1, {})} | custom-call | flops 8589934592 | bytes 16777216 | tf_op jit(solution)/shard_map/after/pallas_call | solution.py:694
  96.3 5.3 %all-to-all-start.1 = ((bf16[32,128,256]{2,1,0:T(8,128)(2,1)}), bf16[32,128,256]{2,1,0:T(8,128)(2,1)}, u32[]{:S(2)}, u32[]{:S(2)}) async-start(bf16[32,128,256]{2,1,0:T(8,128)(2,1)} %get-tuple-element.109), calls=%async_computation.1 | async-start | bytes 4194304 | tf_op jit(solution)/shard_map/all_to_all | solution.py:878
  101.9 6.4 %late.1.own_hbm.own_in = bf16[32,128,256]{2,1,0:T(8,128)(2,1)} custom-call(s32[8,256]{1,0:T(8,128)} %copy-done.6, f32[32,128,256]{2,1,0:T(8,128)} %get-tuple-element.97.sums, bf16[32,128,256]{2,1,0:T(8,128)(2,1)} %get-tuple-element.98.done, bf16[2,256,2048]{2,1,0:T(8,128)(2,1)} %refs_4_.1, bf16[2,2048,256]{2,1,0:T(8,128)(2,1)} %refs_5_.1), custom_call_target="tpu_custom_call", output_to_operand_aliasing={{}: (2, {})} | custom-call | flops 2147483648 | bytes 5242880 | tf_op jit(solution)/shard_map/late/pallas_call | solution.py:756
  108.3 9.5 %hub_second.1 = (bf16[16,128,256]{2,1,0:T(8,128)(2,1)S(1)}, bf16[64,256]{1,0:T(8,128)(2,1)S(1)}, f32[1024,256]{1,0:T(8,128)S(1)}, f32[1024,256]{1,0:T(8,128)S(1)}) custom-call(s32[8,256]{1,0:T(8,128)S(1)} %copy-done.7, s32[1]{0:T(128)S(6)} %copy.30.count, s32[1]{0:T(128)} %bitcast.position, s32[1,2048]{1,0:T(1,128)S(1)} %bitcast.8, ...), custom_call_target="tpu_custom_call" | custom-call | flops 2147483648 | bytes 14680064 | tf_op jit(solution)/shard_map/hub_second/pallas_call | solution.py:30
  118.2 2.3 %collective-permute-done.17.refs_0_ = f32[1024,256]{1,0:T(8,128)S(1)} collective-permute-done((f32[1024,256]{1,0:T(8,128)S(1)}, f32[1024,256]{1,0:T(8,128)S(1)}, u32[]{:S(2)}, u32[]{:S(2)}) %collective-permute-start.17) | collective-permute-done | bytes 1048608 | tf_op jit(solution)/shard_map/ppermute | solution.py:781
  124.4 10.6 %before.3 = (f32[32,128,256]{2,1,0:T(8,128)}, bf16[32,128,256]{2,1,0:T(8,128)(2,1)}) custom-call(s32[8,256]{1,0:T(8,128)} %copy-done.6, s32[1]{0:T(128)S(6)} %copy.30.count, bf16[16,128,256]{2,1,0:T(8,128)(2,1)} %copy-done.4, bf16[32,128,256]{2,1,0:T(8,128)(2,1)} %late.1.own_hbm.own_in, bf16[144,128,128]{2,1,0:T(8,128)(2,1)} %tiles.3, ...), custom_call_target="tpu_custom_call" | custom-call | flops 2863311616 | bytes 18874368 | tf_op jit(solution)/shard_map/before/pallas_call | solution.py:30
  135.6 6.2 %collective-permute-done.19.refs_1_ = f32[256,256]{1,0:T(8,128)S(1)} collective-permute-done((f32[256,256]{1,0:T(8,128)S(1)}, f32[256,256]{1,0:T(8,128)S(1)}, u32[]{:S(2)}, u32[]{:S(2)}) %collective-permute-start.19) | collective-permute-done | bytes 262176 | tf_op jit(solution)/shard_map/ppermute | solution.py:781
  141.8 4.7 %collective-permute-start.21 = (bf16[64,256]{1,0:T(8,128)(2,1)S(1)}, bf16[64,256]{1,0:T(8,128)(2,1)S(1)}, u32[]{:S(2)}, u32[]{:S(2)}) collective-permute-start(bf16[64,256]{1,0:T(8,128)(2,1)S(1)} %get-tuple-element.115), channel_id=1, source_target_pairs={{0,8},{1,9},{2,10},{3,11},{4,12},{5,13},{6,14},{7,15},{8,0},{9,1},... | collective-permute-start | bytes 98312 | tf_op jit(solution)/shard_map/ppermute | solution.py:781
  149.7 1.9 %all-to-all-done.1.incoming = bf16[32,128,256]{2,1,0:T(8,128)(2,1)} async-done(((bf16[32,128,256]{2,1,0:T(8,128)(2,1)}), bf16[32,128,256]{2,1,0:T(8,128)(2,1)}, u32[]{:S(2)}, u32[]{:S(2)}) %all-to-all-start.1) | async-done | bytes 2097184 | tf_op jit(solution)/shard_map/all_to_all | solution.py:878
  151.5 11.8 %after.3 = bf16[32,128,256]{2,1,0:T(8,128)(2,1)} custom-call(s32[8,256]{1,0:T(8,128)} %copy-done.6, f32[32,128,256]{2,1,0:T(8,128)} %get-tuple-element.107.base, bf16[32,128,256]{2,1,0:T(8,128)(2,1)} %get-tuple-element.108.done, bf16[32,128,256]{2,1,0:T(8,128)(2,1)} %all-to-all-done.1.incoming, ...), custom_call_target="tpu_custom_call", output_to_operand_aliasing={{}: (2, {})} | custom-call | flops 8589934592 | bytes 16777216 | tf_op jit(solution)/shard_map/after/pallas_call | solution.py:694
  (82 shorter events, 24.9 us)
Async XLA Ops:
  0.6 11.4 %collective-permute-start.1 = (bf16[64,256]{1,0:T(8,128)(2,1)}, bf16[64,256]{1,0:T(8,128)(2,1)S(1)}, u32[]{:S(2)}, u32[]{:S(2)}) collective-permute-start(bf16[64,256]{1,0:T(8,128)(2,1)} %param.11), channel_id=1, source_target_pairs={{0,16},{1,17},{2,18},{3,19},{4,20},{5,21},{6,22},{7,23},{8,24},{9,... | collective-permute-start | bytes 98312 | tf_op jit(solution)/shard_map/ppermute | solution.py:781
  4.7 7.3 %collective-permute-start = (bf16[64,256]{1,0:T(8,128)(2,1)}, bf16[64,256]{1,0:T(8,128)(2,1)S(1)}, u32[]{:S(2)}, u32[]{:S(2)}) collective-permute-start(bf16[64,256]{1,0:T(8,128)(2,1)} %param.11), channel_id=1, source_target_pairs={{0,8},{1,9},{2,10},{3,11},{4,12},{5,13},{6,14},{7,15},{8,0},{9,1},... | collective-permute-start | bytes 98312 | tf_op jit(solution)/shard_map/ppermute | solution.py:781
  6.3 5.9 %collective-permute-start.2 = (bf16[64,256]{1,0:T(8,128)(2,1)}, bf16[64,256]{1,0:T(8,128)(2,1)S(1)}, u32[]{:S(2)}, u32[]{:S(2)}) collective-permute-start(bf16[64,256]{1,0:T(8,128)(2,1)} %param.11), channel_id=1, source_target_pairs={{0,24},{1,25},{2,26},{3,27},{4,28},{5,29},{6,30},{7,31},{8,16},{9,... | collective-permute-start | bytes 98312 | tf_op jit(solution)/shard_map/ppermute | solution.py:781
  12.3 6.7 %collective-permute-start.5 = (bf16[256,256]{1,0:T(8,128)(2,1)S(1)}, bf16[256,256]{1,0:T(8,128)(2,1)S(1)}, u32[]{:S(2)}, u32[]{:S(2)}) collective-permute-start(bf16[256,256]{1,0:T(8,128)(2,1)S(1)} %constant_dynamic-update-slice_fusion), channel_id=1, source_target_pairs={{0,6},{1,7},{2,4},{3,5},{4,2},{5,3},{6,0},{7,1},{8,14},{9,15},{10,... | collective-permute-start | bytes 393224 | tf_op jit(solution)/shard_map/ppermute | solution.py:781
  14.9 5.7 %collective-permute-start.4 = (bf16[256,256]{1,0:T(8,128)(2,1)S(1)}, bf16[256,256]{1,0:T(8,128)(2,1)S(1)}, u32[]{:S(2)}, u32[]{:S(2)}) collective-permute-start(bf16[256,256]{1,0:T(8,128)(2,1)S(1)} %constant_dynamic-update-slice_fusion), channel_id=1, source_target_pairs={{0,4},{1,5},{2,6},{3,7},{4,0},{5,1},{6,2},{7,3},{8,12},{9,13},{10,... | collective-permute-start | bytes 393224 | tf_op jit(solution)/shard_map/ppermute | solution.py:781
  15.4 5.3 %collective-permute-start.3 = (bf16[256,256]{1,0:T(8,128)(2,1)S(1)}, bf16[256,256]{1,0:T(8,128)(2,1)S(1)}, u32[]{:S(2)}, u32[]{:S(2)}) collective-permute-start(bf16[256,256]{1,0:T(8,128)(2,1)S(1)} %constant_dynamic-update-slice_fusion), channel_id=1, source_target_pairs={{0,2},{1,3},{2,0},{3,1},{4,6},{5,7},{6,4},{7,5},{8,10},{9,11},{10,... | collective-permute-start | bytes 393224 | tf_op jit(solution)/shard_map/ppermute | solution.py:781
  20.7 64.3 %all-to-all-start = ((bf16[32,128,256]{2,1,0:T(8,128)(2,1)}), bf16[32,128,256]{2,1,0:T(8,128)(2,1)}, u32[]{:S(2)}, u32[]{:S(2)}) async-start(bf16[32,128,256]{2,1,0:T(8,128)(2,1)} %pack.1), calls=%async_computation | async-start | bytes 4194304 | tf_op jit(solution)/shard_map/all_to_all | solution.py:863
  33.5 2.7 %collective-permute-start.7 = (f32[1024,256]{1,0:T(8,128)S(1)}, f32[1024,256]{1,0:T(8,128)S(1)}, u32[]{:S(2)}, u32[]{:S(2)}) collective-permute-start(f32[1024,256]{1,0:T(8,128)S(1)} %get-tuple-element.78), channel_id=1, source_target_pairs={{0,1},{1,0},{2,3},{3,2},{4,5},{5,4},{6,7},{7,6},{8,9},{9,8},{10,11... | collective-permute-start | bytes 3145736 | tf_op jit(solution)/shard_map/ppermute | solution.py:781
  37.1 15.3 %collective-permute-start.8 = (f32[256,256]{1,0:T(8,128)}, f32[256,256]{1,0:T(8,128)S(1)}, u32[]{:S(2)}, u32[]{:S(2)}) collective-permute-start(f32[256,256]{1,0:T(8,128)} %get-tuple-element.79), channel_id=1, source_target_pairs={{0,2},{1,3},{2,0},{3,1},{4,6},{5,7},{6,4},{7,5},{8,10},{9,11},{10,... | collective-permute-start | bytes 786440 | tf_op jit(solution)/shard_map/ppermute | solution.py:781
  38.5 22.5 %collective-permute-start.9 = (f32[256,256]{1,0:T(8,128)S(1)}, f32[256,256]{1,0:T(8,128)S(1)}, u32[]{:S(2)}, u32[]{:S(2)}) collective-permute-start(f32[256,256]{1,0:T(8,128)S(1)} %get-tuple-element.80), channel_id=1, source_target_pairs={{0,4},{1,5},{2,6},{3,7},{4,0},{5,1},{6,2},{7,3},{8,12},{9,13},{10,... | collective-permute-start | bytes 786440 | tf_op jit(solution)/shard_map/ppermute | solution.py:781
  39.9 21.0 %collective-permute-start.10 = (f32[256,256]{1,0:T(8,128)S(1)}, f32[256,256]{1,0:T(8,128)S(1)}, u32[]{:S(2)}, u32[]{:S(2)}) collective-permute-start(f32[256,256]{1,0:T(8,128)S(1)} %get-tuple-element.81), channel_id=1, source_target_pairs={{0,6},{1,7},{2,4},{3,5},{4,2},{5,3},{6,0},{7,1},{8,14},{9,15},{10,... | collective-permute-start | bytes 786440 | tf_op jit(solution)/shard_map/ppermute | solution.py:781
  61.0 6.4 %collective-permute-start.11 = (bf16[256,256]{1,0:T(8,128)(2,1)S(1)}, bf16[256,256]{1,0:T(8,128)(2,1)S(1)}, u32[]{:S(2)}, u32[]{:S(2)}) collective-permute-start(bf16[256,256]{1,0:T(8,128)(2,1)S(1)} %total.2.refs_0_), channel_id=1, source_target_pairs={{0,8},{1,9},{2,10},{3,11},{4,12},{5,13},{6,14},{7,15},{8,0},{9,1},... | collective-permute-start | bytes 393224 | tf_op jit(solution)/shard_map/ppermute | solution.py:781
  67.5 12.8 %collective-permute-start.12 = (bf16[256,256]{1,0:T(8,128)(2,1)S(1)}, bf16[256,256]{1,0:T(8,128)(2,1)S(1)}, u32[]{:S(2)}, u32[]{:S(2)}) collective-permute-start(bf16[256,256]{1,0:T(8,128)(2,1)S(1)} %total.3.refs_0_), channel_id=1, source_target_pairs={{0,16},{1,17},{2,18},{3,19},{4,20},{5,21},{6,22},{7,23},{8,24},{9,... | collective-permute-start | bytes 393224 | tf_op jit(solution)/shard_map/ppermute | solution.py:781
  81.4 14.9 %collective-permute-start.15 = (bf16[256,256]{1,0:T(8,128)(2,1)S(1)}, bf16[256,256]{1,0:T(8,128)(2,1)S(1)}, u32[]{:S(2)}, u32[]{:S(2)}) collective-permute-start(bf16[256,256]{1,0:T(8,128)(2,1)S(1)} %hub_network.2), channel_id=1, source_target_pairs={{0,6},{1,7},{2,4},{3,5},{4,2},{5,3},{6,0},{7,1},{8,14},{9,15},{10,... | collective-permute-start | bytes 393224 | tf_op jit(solution)/shard_map/ppermute | solution.py:781
  83.7 12.6 %collective-permute-start.14 = (bf16[256,256]{1,0:T(8,128)(2,1)S(1)}, bf16[256,256]{1,0:T(8,128)(2,1)S(1)}, u32[]{:S(2)}, u32[]{:S(2)}) collective-permute-start(bf16[256,256]{1,0:T(8,128)(2,1)S(1)} %hub_network.2), channel_id=1, source_target_pairs={{0,4},{1,5},{2,6},{3,7},{4,0},{5,1},{6,2},{7,3},{8,12},{9,13},{10,... | collective-permute-start | bytes 393224 | tf_op jit(solution)/shard_map/ppermute | solution.py:781
  84.3 12.0 %collective-permute-start.13 = (bf16[256,256]{1,0:T(8,128)(2,1)S(1)}, bf16[256,256]{1,0:T(8,128)(2,1)S(1)}, u32[]{:S(2)}, u32[]{:S(2)}) collective-permute-start(bf16[256,256]{1,0:T(8,128)(2,1)S(1)} %hub_network.2), channel_id=1, source_target_pairs={{0,2},{1,3},{2,0},{3,1},{4,6},{5,7},{6,4},{7,5},{8,10},{9,11},{10,... | collective-permute-start | bytes 393224 | tf_op jit(solution)/shard_map/ppermute | solution.py:781
  96.3 55.2 %all-to-all-start.1 = ((bf16[32,128,256]{2,1,0:T(8,128)(2,1)}), bf16[32,128,256]{2,1,0:T(8,128)(2,1)}, u32[]{:S(2)}, u32[]{:S(2)}) async-start(bf16[32,128,256]{2,1,0:T(8,128)(2,1)} %get-tuple-element.109), calls=%async_computation.1 | async-start | bytes 4194304 | tf_op jit(solution)/shard_map/all_to_all | solution.py:878
  101.7 6.6 %collective-permute-start.16 = (bf16[1024,256]{1,0:T(8,128)(2,1)S(1)}, bf16[1024,256]{1,0:T(8,128)(2,1)S(1)}, u32[]{:S(2)}, u32[]{:S(2)}) collective-permute-start(bf16[1024,256]{1,0:T(8,128)(2,1)S(1)} %constant_dynamic-update-slice_fusion.8.half0), channel_id=1, source_target_pairs={{0,1},{1,0},{2,3},{3,2},{4,5},{5,4},{6,7},{7,6},{8,9},{9,8},{10,11... | collective-permute-start | bytes 1572872 | tf_op jit(solution)/shard_map/ppermute | solution.py:781
  120.8 14.8 %collective-permute-start.18 = (f32[256,256]{1,0:T(8,128)S(1)}, f32[256,256]{1,0:T(8,128)S(1)}, u32[]{:S(2)}, u32[]{:S(2)}) collective-permute-start(f32[256,256]{1,0:T(8,128)S(1)} %get-tuple-element.104), channel_id=1, source_target_pairs={{0,2},{1,3},{2,0},{3,1},{4,6},{5,7},{6,4},{7,5},{8,10},{9,11},{10,... | collective-permute-start | bytes 786440 | tf_op jit(solution)/shard_map/ppermute | solution.py:781
  122.3 19.5 %collective-permute-start.19 = (f32[256,256]{1,0:T(8,128)S(1)}, f32[256,256]{1,0:T(8,128)S(1)}, u32[]{:S(2)}, u32[]{:S(2)}) collective-permute-start(f32[256,256]{1,0:T(8,128)S(1)} %get-tuple-element.105), channel_id=1, source_target_pairs={{0,4},{1,5},{2,6},{3,7},{4,0},{5,1},{6,2},{7,3},{8,12},{9,13},{10,... | collective-permute-start | bytes 786440 | tf_op jit(solution)/shard_map/ppermute | solution.py:781
  123.8 18.0 %collective-permute-start.20 = (f32[256,256]{1,0:T(8,128)S(1)}, f32[256,256]{1,0:T(8,128)S(1)}, u32[]{:S(2)}, u32[]{:S(2)}) collective-permute-start(f32[256,256]{1,0:T(8,128)S(1)} %get-tuple-element.106), channel_id=1, source_target_pairs={{0,6},{1,7},{2,4},{3,5},{4,2},{5,3},{6,0},{7,1},{8,14},{9,15},{10,... | collective-permute-start | bytes 786440 | tf_op jit(solution)/shard_map/ppermute | solution.py:781
  141.8 21.5 %collective-permute-start.21 = (bf16[64,256]{1,0:T(8,128)(2,1)S(1)}, bf16[64,256]{1,0:T(8,128)(2,1)S(1)}, u32[]{:S(2)}, u32[]{:S(2)}) collective-permute-start(bf16[64,256]{1,0:T(8,128)(2,1)S(1)} %get-tuple-element.115), channel_id=1, source_target_pairs={{0,8},{1,9},{2,10},{3,11},{4,12},{5,13},{6,14},{7,15},{8,0},{9,1},... | collective-permute-start | bytes 98312 | tf_op jit(solution)/shard_map/ppermute | solution.py:781
  146.5 16.8 %collective-permute-start.22 = (bf16[64,256]{1,0:T(8,128)(2,1)S(1)}, bf16[64,256]{1,0:T(8,128)(2,1)S(1)}, u32[]{:S(2)}, u32[]{:S(2)}) collective-permute-start(bf16[64,256]{1,0:T(8,128)(2,1)S(1)} %get-tuple-element.116), channel_id=1, source_target_pairs={{0,16},{1,17},{2,18},{3,19},{4,20},{5,21},{6,22},{7,23},{8,24},{9,... | collective-permute-start | bytes 98312 | tf_op jit(solution)/shard_map/ppermute | solution.py:781
  148.3 15.1 %collective-permute-start.23 = (bf16[64,256]{1,0:T(8,128)(2,1)S(1)}, bf16[64,256]{1,0:T(8,128)(2,1)S(1)}, u32[]{:S(2)}, u32[]{:S(2)}) collective-permute-start(bf16[64,256]{1,0:T(8,128)(2,1)S(1)} %get-tuple-element.117), channel_id=1, source_target_pairs={{0,24},{1,25},{2,26},{3,27},{4,28},{5,29},{6,30},{7,31},{8,16},{9,... | collective-permute-start | bytes 98312 | tf_op jit(solution)/shard_map/ppermute | solution.py:781
  (14 other events, 161.3 us)

commit v8 on v7

--- a/solution.py
+++ b/solution.py
@@ -226,18 +226,17 @@
 
 
 def pack_kernel(chosen, blocks, outgoing, held, sems):
-    load = pltpu.make_async_copy(blocks, held, sems.at[0])
-    load.start()
-    load.wait()
-    copies = []
+    loads, stores = [], []
     for number in range(outgoing.shape[0]):
-        copy = pltpu.make_async_copy(
-            held.at[chosen[0, number]], outgoing.at[number], sems.at[number]
-        )
-        copy.start()
-        copies.append(copy)
-    for copy in copies:
-        copy.wait()
+        here = held.at[number]
+        loads.append(pltpu.make_async_copy(blocks.at[chosen[0, number]], here, sems.at[number]))
+        stores.append(pltpu.make_async_copy(here, outgoing.at[number], sems.at[number]))
+        loads[-1].start()
+    for load, store in zip(loads, stores):
+        load.wait()
+        store.start()
+    for store in stores:
+        store.wait()
 
 
 def pack(chosen, blocks):
@@ -251,7 +250,10 @@
         shape_of((devices,) + blocks.shape[1:], bf16),
         [SMEM, ANY],
         ANY,
-        [pltpu.VMEM(blocks.shape, bf16), pltpu.SemaphoreType.DMA((devices,))],
+        [
+            pltpu.VMEM((devices,) + blocks.shape[1:], bf16),
+            pltpu.SemaphoreType.DMA((devices,)),
+        ],
         (chosen, blocks),
     )
 
@@ -855,11 +857,13 @@
     )
 
     pieces = gather_far(hubs, digits)
+    outgoing = pack(send_list, own)
+    outgoing, *pieces = lax.optimization_barrier((outgoing, *pieces))
+    pieces = gather_near(pieces, digits)
+    outgoing, place_col, tile_rows, local_cols, *pieces = lax.optimization_barrier(
+        (outgoing, place_col, tile_rows, local_cols, *pieces)
+    )
     plan = make_plan(me, tile_count, tile_rows, local_cols, send_list, hub_count, own_count)
-    outgoing = pack(send_list, own)
-    plan, outgoing, *pieces = lax.optimization_barrier((plan, outgoing, *pieces))
-    pieces = gather_near(pieces, digits)
-    outgoing, place_col, *pieces = lax.optimization_barrier((outgoing, place_col, *pieces))
     incoming = all_to_all(outgoing)
     halves = gather_last(pieces, digits)
     hub_table, mine, kept, sent = hub_first(

time: 166 us -> 164 us (0.988)
  waiting for transfers between devices: 42.9 us -> 39.6 us
    ppermute x24, waiting for transfers between devices: 41.1 us -> 36.3 us  [exchange(): return lax.ppermute(x, 'dev', [(i, i ^ bit) for i in range(devices)])]
    pallas_call x13, Pallas kernels: 45 us -> 48.3 us  [call(): pl.pallas_call(kernel, out_shape=out_shape, in_specs=in_specs, out_specs=...]
    all_to_all x2, starting transfers between devices: 10.4 us -> 7.95 us  [body(): incoming = all_to_all(outgoing)]
    ppermute x24, starting transfers between devices: 34.1 us -> 36.4 us  [exchange(): return lax.ppermute(x, 'dev', [(i, i ^ bit) for i in range(devices)])]
  transfers between devices with their start and end apart: 26 -> 26, of which waited for: 14 -> 11; matrix products, arithmetic and copies ran while one was open for 1% -> 0% of each run, Pallas kernels for 44% -> 46%
where the time goes in v8:
time: 164 us; the launch traced here: 161 us
  Pallas kernels  74.9 us (46%)
  starting transfers between devices  44.4 us (27%)
  waiting for transfers between devices  39.6 us (24%)
  between operations  1.9 us (1%)
    pallas_call x13, Pallas kernels, call(): pl.pallas_call(kernel, out_shape=out_shape, in_specs=in_specs, out_specs=...  48.3 us
    ppermute x24, starting transfers between devices, exchange(): return lax.ppermute(x, 'dev', [(i, i ^ bit) for i in range(devices)])  36.4 us
    ppermute x24, waiting for transfers between devices, exchange(): return lax.ppermute(x, 'dev', [(i, i ^ bit) for i in range(devices)])  36.3 us
    pallas_call x2, Pallas kernels, after(): pl.pallas_call(functools.partial(after_kernel, layer, with_send), out_sha...  21.5 us
    all_to_all x2, starting transfers between devices, body(): incoming = all_to_all(outgoing)  7.95 us
    pallas_call x1, Pallas kernels, late(): pl.pallas_call(functools.partial(late_kernel, layer), out_shape=shape_of(...  5.07 us
    all_to_all x2, waiting for transfers between devices, body(): incoming = all_to_all(outgoing)  3.39 us
  transfers between devices with their start and end apart: 26, of which 11 were waited for; matrix products, arithmetic and copies ran while one was open for 0% of the time, Pallas kernels for 46%

profile of v8, /device:TPU:0, one launch (start us, length us, event | category | flops | bytes accessed | tf_op | source)
XLA Modules:
  0.0 161.4 jit_solution(16315982367138652676)
XLA Ops:
  0.6 4.1 %collective-permute-start.1 = (bf16[64,256]{1,0:T(8,128)(2,1)}, bf16[64,256]{1,0:T(8,128)(2,1)S(1)}, u32[]{:S(2)}, u32[]{:S(2)}) collective-permute-start(bf16[64,256]{1,0:T(8,128)(2,1)} %param.11), channel_id=1, source_target_pairs={{0,16},{1,17},{2,18},{3,19},{4,20},{5,21},{6,22},{7,23},{8,24},{9,... | collective-permute-start | bytes 98312 | tf_op jit(solution)/shard_map/ppermute | solution.py:783
  6.3 3.7 %pack.1 = bf16[32,128,256]{2,1,0:T(8,128)(2,1)} custom-call(s32[1,32]{1,0:T(1,128)} %chosen.3, bf16[32,128,256]{2,1,0:T(8,128)(2,1)} %bitcast.11), custom_call_target="tpu_custom_call" | custom-call | bytes 4194304 | tf_op jit(solution)/shard_map/pack/pallas_call | solution.py:30
  12.3 2.5 %collective-permute-start.5 = (bf16[256,256]{1,0:T(8,128)(2,1)S(1)}, bf16[256,256]{1,0:T(8,128)(2,1)S(1)}, u32[]{:S(2)}, u32[]{:S(2)}) collective-permute-start(bf16[256,256]{1,0:T(8,128)(2,1)S(1)} %constant_dynamic-update-slice_fusion), channel_id=1, source_target_pairs={{0,6},{1,7},{2,4},{3,5},{4,2},{5,3},{6,0},{7,1},{8,14},{9,15},{10,... | collective-permute-start | bytes 393224 | tf_op jit(solution)/shard_map/ppermute | solution.py:783
  15.8 3.6 %collective-permute-done.5 = bf16[256,256]{1,0:T(8,128)(2,1)S(1)} collective-permute-done((bf16[256,256]{1,0:T(8,128)(2,1)S(1)}, bf16[256,256]{1,0:T(8,128)(2,1)S(1)}, u32[]{:S(2)}, u32[]{:S(2)}) %collective-permute-start.5) | collective-permute-done | bytes 131104 | tf_op jit(solution)/shard_map/ppermute | solution.py:783
  20.4 3.6 %all-to-all-start = ((bf16[32,128,256]{2,1,0:T(8,128)(2,1)}), bf16[32,128,256]{2,1,0:T(8,128)(2,1)}, u32[]{:S(2)}, u32[]{:S(2)}) async-start(bf16[32,128,256]{2,1,0:T(8,128)(2,1)} %pack.1), calls=%async_computation | async-start | bytes 4194304 | tf_op jit(solution)/shard_map/all_to_all | solution.py:867
  26.1 5.7 %hub_first.1 = (bf16[16,128,256]{2,1,0:T(8,128)(2,1)S(1)}, bf16[256,256]{1,0:T(8,128)(2,1)S(1)}, f32[1024,256]{1,0:T(8,128)S(1)}, f32[1024,256]{1,0:T(8,128)S(1)}) custom-call(s32[8,256]{1,0:T(8,128)S(1)} %plan.1, s32[1]{0:T(128)S(6)} %copy.30.count, s32[1]{0:T(128)} %bitcast.position, s32[2048,1]{1,0:T(8,128)S(1)} %copy.16.place_col, ...), custom_call_target="tpu_custom_call" | custom-call | flops 2147483648 | bytes 14680064 | tf_op jit(solution)/shard_map/hub_first/pallas_call | solution.py:30
  31.9 2.6 %collective-permute-done.7.refs_0_ = f32[1024,256]{1,0:T(8,128)S(1)} collective-permute-done((f32[1024,256]{1,0:T(8,128)S(1)}, f32[1024,256]{1,0:T(8,128)S(1)}, u32[]{:S(2)}, u32[]{:S(2)}) %collective-permute-start.7) | collective-permute-done | bytes 1048608 | tf_op jit(solution)/shard_map/ppermute | solution.py:783
  40.1 12.8 %before.2 = (f32[32,128,256]{2,1,0:T(8,128)}, bf16[32,128,256]{2,1,0:T(8,128)(2,1)}) custom-call(s32[8,256]{1,0:T(8,128)} %copy-done.6, s32[1]{0:T(128)S(6)} %copy.30.count, bf16[16,128,256]{2,1,0:T(8,128)(2,1)} %copy-done.5, bf16[32,128,256]{2,1,0:T(8,128)(2,1)} %bitcast.13, bf16[144,128,128]{2,1,0:T(8,128)(2,1)} %tiles.3, bf16[2,256,2048]{2,1,0:T(8,128)(2,1)} %refs_4_.1, ...), custom_call_target="tpu_custom_call" | custom-call | flops 2863311616 | bytes 18874368 | tf_op jit(solution)/shard_map/before/pallas_call | solution.py:30
  52.9 6.8 %collective-permute-done.10.refs_3_ = f32[256,256]{1,0:T(8,128)S(1)} collective-permute-done((f32[256,256]{1,0:T(8,128)S(1)}, f32[256,256]{1,0:T(8,128)S(1)}, u32[]{:S(2)}, u32[]{:S(2)}) %collective-permute-start.10) | collective-permute-done | bytes 262176 | tf_op jit(solution)/shard_map/ppermute | solution.py:783
  59.8 4.8 %collective-permute-start.11 = (bf16[256,256]{1,0:T(8,128)(2,1)S(1)}, bf16[256,256]{1,0:T(8,128)(2,1)S(1)}, u32[]{:S(2)}, u32[]{:S(2)}) collective-permute-start(bf16[256,256]{1,0:T(8,128)(2,1)S(1)} %total.2.refs_0_), channel_id=1, source_target_pairs={{0,8},{1,9},{2,10},{3,11},{4,12},{5,13},{6,14},{7,15},{8,0},{9,1},... | collective-permute-start | bytes 393224 | tf_op jit(solution)/shard_map/ppermute | solution.py:783
  64.6 4.7 %collective-permute-done.11.refs_1_ = bf16[256,256]{1,0:T(8,128)(2,1)S(1)} collective-permute-done((bf16[256,256]{1,0:T(8,128)(2,1)S(1)}, bf16[256,256]{1,0:T(8,128)(2,1)S(1)}, u32[]{:S(2)}, u32[]{:S(2)}) %collective-permute-start.11) | collective-permute-done | bytes 131104 | tf_op jit(solution)/shard_map/ppermute | solution.py:783
  69.4 9.2 %collective-permute-done.12.refs_1_ = bf16[256,256]{1,0:T(8,128)(2,1)S(1)} collective-permute-done((bf16[256,256]{1,0:T(8,128)(2,1)S(1)}, bf16[256,256]{1,0:T(8,128)(2,1)S(1)}, u32[]{:S(2)}, u32[]{:S(2)}) %collective-permute-start.12) | collective-permute-done | bytes 131104 | tf_op jit(solution)/shard_map/ppermute | solution.py:783
  79.7 2.2 %collective-permute-start.15 = (bf16[256,256]{1,0:T(8,128)(2,1)S(1)}, bf16[256,256]{1,0:T(8,128)(2,1)S(1)}, u32[]{:S(2)}, u32[]{:S(2)}) collective-permute-start(bf16[256,256]{1,0:T(8,128)(2,1)S(1)} %hub_network.2), channel_id=1, source_target_pairs={{0,6},{1,7},{2,4},{3,5},{4,2},{5,3},{6,0},{7,1},{8,14},{9,15},{10,... | collective-permute-start | bytes 393224 | tf_op jit(solution)/shard_map/ppermute | solution.py:783
  83.2 11.0 %after.2 = (bf16[32,128,256]{2,1,0:T(8,128)(2,1)}, f32[32,128,256]{2,1,0:T(8,128)}, bf16[32,128,256]{2,1,0:T(8,128)(2,1)}) custom-call(s32[8,256]{1,0:T(8,128)} %copy-done.6, f32[32,128,256]{2,1,0:T(8,128)} %get-tuple-element.90.base, bf16[32,128,256]{2,1,0:T(8,128)(2,1)} %get-tuple-element.91.done, ...), custom_call_target="tpu_custom_call", output_to_operand_aliasing={{0}: (2, {}), {1}: (1, {})} | custom-call | flops 8589934592 | bytes 16777216 | tf_op jit(solution)/shard_map/after/pallas_call | solution.py:696
  94.3 4.3 %all-to-all-start.1 = ((bf16[32,128,256]{2,1,0:T(8,128)(2,1)}), bf16[32,128,256]{2,1,0:T(8,128)(2,1)}, u32[]{:S(2)}, u32[]{:S(2)}) async-start(bf16[32,128,256]{2,1,0:T(8,128)(2,1)} %get-tuple-element.111), calls=%async_computation.1 | async-start | bytes 4194304 | tf_op jit(solution)/shard_map/all_to_all | solution.py:882
  98.9 5.1 %late.1.own_hbm.own_in = bf16[32,128,256]{2,1,0:T(8,128)(2,1)} custom-call(s32[8,256]{1,0:T(8,128)} %copy-done.6, f32[32,128,256]{2,1,0:T(8,128)} %get-tuple-element.99.sums, bf16[32,128,256]{2,1,0:T(8,128)(2,1)} %get-tuple-element.100.done, bf16[2,256,2048]{2,1,0:T(8,128)(2,1)} %refs_4_.1, bf16[2,2048,256]{2,1,0:T(8,128)(2,1)} %refs_5_.1), custom_call_target="tpu_custom_call", output_to_operand_aliasing={{}: (2, {})} | custom-call | flops 2147483648 | bytes 5242880 | tf_op jit(solution)/shard_map/late/pallas_call | solution.py:758
  104.0 9.8 %hub_second.1 = (bf16[16,128,256]{2,1,0:T(8,128)(2,1)S(1)}, bf16[64,256]{1,0:T(8,128)(2,1)S(1)}, f32[1024,256]{1,0:T(8,128)S(1)}, f32[1024,256]{1,0:T(8,128)S(1)}) custom-call(s32[8,256]{1,0:T(8,128)S(1)} %copy-done.7, s32[1]{0:T(128)S(6)} %copy.30.count, s32[1]{0:T(128)} %bitcast.position, s32[1,2048]{1,0:T(1,128)S(1)} %bitcast.8, ...), custom_call_target="tpu_custom_call" | custom-call | flops 2147483648 | bytes 14680064 | tf_op jit(solution)/shard_map/hub_second/pallas_call | solution.py:30
  115.0 2.3 %collective-permute-done.17.refs_0_ = f32[1024,256]{1,0:T(8,128)S(1)} collective-permute-done((f32[1024,256]{1,0:T(8,128)S(1)}, f32[1024,256]{1,0:T(8,128)S(1)}, u32[]{:S(2)}, u32[]{:S(2)}) %collective-permute-start.17) | collective-permute-done | bytes 1048608 | tf_op jit(solution)/shard_map/ppermute | solution.py:783
  119.5 2.5 %collective-permute-start.19 = (f32[256,256]{1,0:T(8,128)S(1)}, f32[256,256]{1,0:T(8,128)S(1)}, u32[]{:S(2)}, u32[]{:S(2)}) collective-permute-start(f32[256,256]{1,0:T(8,128)S(1)} %get-tuple-element.107), channel_id=1, source_target_pairs={{0,4},{1,5},{2,6},{3,7},{4,0},{5,1},{6,2},{7,3},{8,12},{9,13},{10,... | collective-permute-start | bytes 786440 | tf_op jit(solution)/shard_map/ppermute | solution.py:783
  123.4 12.3 %before.3 = (f32[32,128,256]{2,1,0:T(8,128)}, bf16[32,128,256]{2,1,0:T(8,128)(2,1)}) custom-call(s32[8,256]{1,0:T(8,128)} %copy-done.6, s32[1]{0:T(128)S(6)} %copy.30.count, bf16[16,128,256]{2,1,0:T(8,128)(2,1)} %copy-done.4, bf16[32,128,256]{2,1,0:T(8,128)(2,1)} %late.1.own_hbm.own_in, bf16[144,128,128]{2,1,0:T(8,128)(2,1)} %tiles.3, ...), custom_call_target="tpu_custom_call" | custom-call | flops 2863311616 | bytes 18874368 | tf_op jit(solution)/shard_map/before/pallas_call | solution.py:30
  135.7 3.5 %collective-permute-done.19.refs_1_ = f32[256,256]{1,0:T(8,128)S(1)} collective-permute-done((f32[256,256]{1,0:T(8,128)S(1)}, f32[256,256]{1,0:T(8,128)S(1)}, u32[]{:S(2)}, u32[]{:S(2)}) %collective-permute-start.19) | collective-permute-done | bytes 262176 | tf_op jit(solution)/shard_map/ppermute | solution.py:783
  139.3 4.1 %collective-permute-start.21 = (bf16[64,256]{1,0:T(8,128)(2,1)S(1)}, bf16[64,256]{1,0:T(8,128)(2,1)S(1)}, u32[]{:S(2)}, u32[]{:S(2)}) collective-permute-start(bf16[64,256]{1,0:T(8,128)(2,1)S(1)} %get-tuple-element.117), channel_id=1, source_target_pairs={{0,8},{1,9},{2,10},{3,11},{4,12},{5,13},{6,14},{7,15},{8,0},{9,1},... | collective-permute-start | bytes 98312 | tf_op jit(solution)/shard_map/ppermute | solution.py:783
  145.9 3.4 %all-to-all-done.1.incoming = bf16[32,128,256]{2,1,0:T(8,128)(2,1)} async-done(((bf16[32,128,256]{2,1,0:T(8,128)(2,1)}), bf16[32,128,256]{2,1,0:T(8,128)(2,1)}, u32[]{:S(2)}, u32[]{:S(2)}) %all-to-all-start.1) | async-done | bytes 2097184 | tf_op jit(solution)/shard_map/all_to_all | solution.py:882
  149.3 10.5 %after.3 = bf16[32,128,256]{2,1,0:T(8,128)(2,1)} custom-call(s32[8,256]{1,0:T(8,128)} %copy-done.6, f32[32,128,256]{2,1,0:T(8,128)} %get-tuple-element.109.base, bf16[32,128,256]{2,1,0:T(8,128)(2,1)} %get-tuple-element.110.done, bf16[32,128,256]{2,1,0:T(8,128)(2,1)} %all-to-all-done.1.incoming, ...), custom_call_target="tpu_custom_call", output_to_operand_aliasing={{}: (2, {})} | custom-call | flops 8589934592 | bytes 16777216 | tf_op jit(solution)/shard_map/after/pallas_call | solution.py:696
  (84 shorter events, 24.4 us)
Async XLA Ops:
  0.6 9.4 %collective-permute-start.1 = (bf16[64,256]{1,0:T(8,128)(2,1)}, bf16[64,256]{1,0:T(8,128)(2,1)S(1)}, u32[]{:S(2)}, u32[]{:S(2)}) collective-permute-start(bf16[64,256]{1,0:T(8,128)(2,1)} %param.11), channel_id=1, source_target_pairs={{0,16},{1,17},{2,18},{3,19},{4,20},{5,21},{6,22},{7,23},{8,24},{9,... | collective-permute-start | bytes 98312 | tf_op jit(solution)/shard_map/ppermute | solution.py:783
  4.7 5.3 %collective-permute-start = (bf16[64,256]{1,0:T(8,128)(2,1)}, bf16[64,256]{1,0:T(8,128)(2,1)S(1)}, u32[]{:S(2)}, u32[]{:S(2)}) collective-permute-start(bf16[64,256]{1,0:T(8,128)(2,1)} %param.11), channel_id=1, source_target_pairs={{0,8},{1,9},{2,10},{3,11},{4,12},{5,13},{6,14},{7,15},{8,0},{9,1},... | collective-permute-start | bytes 98312 | tf_op jit(solution)/shard_map/ppermute | solution.py:783
  6.3 5.9 %collective-permute-start.2 = (bf16[64,256]{1,0:T(8,128)(2,1)}, bf16[64,256]{1,0:T(8,128)(2,1)S(1)}, u32[]{:S(2)}, u32[]{:S(2)}) collective-permute-start(bf16[64,256]{1,0:T(8,128)(2,1)} %param.11), channel_id=1, source_target_pairs={{0,24},{1,25},{2,26},{3,27},{4,28},{5,29},{6,30},{7,31},{8,16},{9,... | collective-permute-start | bytes 98312 | tf_op jit(solution)/shard_map/ppermute | solution.py:783
  12.3 7.2 %collective-permute-start.5 = (bf16[256,256]{1,0:T(8,128)(2,1)S(1)}, bf16[256,256]{1,0:T(8,128)(2,1)S(1)}, u32[]{:S(2)}, u32[]{:S(2)}) collective-permute-start(bf16[256,256]{1,0:T(8,128)(2,1)S(1)} %constant_dynamic-update-slice_fusion), channel_id=1, source_target_pairs={{0,6},{1,7},{2,4},{3,5},{4,2},{5,3},{6,0},{7,1},{8,14},{9,15},{10,... | collective-permute-start | bytes 393224 | tf_op jit(solution)/shard_map/ppermute | solution.py:783
  14.8 5.6 %collective-permute-start.4 = (bf16[256,256]{1,0:T(8,128)(2,1)S(1)}, bf16[256,256]{1,0:T(8,128)(2,1)S(1)}, u32[]{:S(2)}, u32[]{:S(2)}) collective-permute-start(bf16[256,256]{1,0:T(8,128)(2,1)S(1)} %constant_dynamic-update-slice_fusion), channel_id=1, source_target_pairs={{0,4},{1,5},{2,6},{3,7},{4,0},{5,1},{6,2},{7,3},{8,12},{9,13},{10,... | collective-permute-start | bytes 393224 | tf_op jit(solution)/shard_map/ppermute | solution.py:783
  15.3 5.1 %collective-permute-start.3 = (bf16[256,256]{1,0:T(8,128)(2,1)S(1)}, bf16[256,256]{1,0:T(8,128)(2,1)S(1)}, u32[]{:S(2)}, u32[]{:S(2)}) collective-permute-start(bf16[256,256]{1,0:T(8,128)(2,1)S(1)} %constant_dynamic-update-slice_fusion), channel_id=1, source_target_pairs={{0,2},{1,3},{2,0},{3,1},{4,6},{5,7},{6,4},{7,5},{8,10},{9,11},{10,... | collective-permute-start | bytes 393224 | tf_op jit(solution)/shard_map/ppermute | solution.py:783
  20.4 62.8 %all-to-all-start = ((bf16[32,128,256]{2,1,0:T(8,128)(2,1)}), bf16[32,128,256]{2,1,0:T(8,128)(2,1)}, u32[]{:S(2)}, u32[]{:S(2)}) async-start(bf16[32,128,256]{2,1,0:T(8,128)(2,1)} %pack.1), calls=%async_computation | async-start | bytes 4194304 | tf_op jit(solution)/shard_map/all_to_all | solution.py:867
  35.4 17.5 %collective-permute-start.8 = (f32[256,256]{1,0:T(8,128)}, f32[256,256]{1,0:T(8,128)S(1)}, u32[]{:S(2)}, u32[]{:S(2)}) collective-permute-start(f32[256,256]{1,0:T(8,128)} %get-tuple-element.81), channel_id=1, source_target_pairs={{0,2},{1,3},{2,0},{3,1},{4,6},{5,7},{6,4},{7,5},{8,10},{9,11},{10,... | collective-permute-start | bytes 786440 | tf_op jit(solution)/shard_map/ppermute | solution.py:783
  36.8 16.1 %collective-permute-start.9 = (f32[256,256]{1,0:T(8,128)S(1)}, f32[256,256]{1,0:T(8,128)S(1)}, u32[]{:S(2)}, u32[]{:S(2)}) collective-permute-start(f32[256,256]{1,0:T(8,128)S(1)} %get-tuple-element.82), channel_id=1, source_target_pairs={{0,4},{1,5},{2,6},{3,7},{4,0},{5,1},{6,2},{7,3},{8,12},{9,13},{10,... | collective-permute-start | bytes 786440 | tf_op jit(solution)/shard_map/ppermute | solution.py:783
  38.6 21.1 %collective-permute-start.10 = (f32[256,256]{1,0:T(8,128)S(1)}, f32[256,256]{1,0:T(8,128)S(1)}, u32[]{:S(2)}, u32[]{:S(2)}) collective-permute-start(f32[256,256]{1,0:T(8,128)S(1)} %get-tuple-element.83), channel_id=1, source_target_pairs={{0,6},{1,7},{2,4},{3,5},{4,2},{5,3},{6,0},{7,1},{8,14},{9,15},{10,... | collective-permute-start | bytes 786440 | tf_op jit(solution)/shard_map/ppermute | solution.py:783
  59.8 9.5 %collective-permute-start.11 = (bf16[256,256]{1,0:T(8,128)(2,1)S(1)}, bf16[256,256]{1,0:T(8,128)(2,1)S(1)}, u32[]{:S(2)}, u32[]{:S(2)}) collective-permute-start(bf16[256,256]{1,0:T(8,128)(2,1)S(1)} %total.2.refs_0_), channel_id=1, source_target_pairs={{0,8},{1,9},{2,10},{3,11},{4,12},{5,13},{6,14},{7,15},{8,0},{9,1},... | collective-permute-start | bytes 393224 | tf_op jit(solution)/shard_map/ppermute | solution.py:783
  69.3 9.2 %collective-permute-start.12 = (bf16[256,256]{1,0:T(8,128)(2,1)S(1)}, bf16[256,256]{1,0:T(8,128)(2,1)S(1)}, u32[]{:S(2)}, u32[]{:S(2)}) collective-permute-start(bf16[256,256]{1,0:T(8,128)(2,1)S(1)} %total.3.refs_0_), channel_id=1, source_target_pairs={{0,16},{1,17},{2,18},{3,19},{4,20},{5,21},{6,22},{7,23},{8,24},{9,... | collective-permute-start | bytes 393224 | tf_op jit(solution)/shard_map/ppermute | solution.py:783
  79.7 14.6 %collective-permute-start.15 = (bf16[256,256]{1,0:T(8,128)(2,1)S(1)}, bf16[256,256]{1,0:T(8,128)(2,1)S(1)}, u32[]{:S(2)}, u32[]{:S(2)}) collective-permute-start(bf16[256,256]{1,0:T(8,128)(2,1)S(1)} %hub_network.2), channel_id=1, source_target_pairs={{0,6},{1,7},{2,4},{3,5},{4,2},{5,3},{6,0},{7,1},{8,14},{9,15},{10,... | collective-permute-start | bytes 393224 | tf_op jit(solution)/shard_map/ppermute | solution.py:783
  81.9 12.3 %collective-permute-start.14 = (bf16[256,256]{1,0:T(8,128)(2,1)S(1)}, bf16[256,256]{1,0:T(8,128)(2,1)S(1)}, u32[]{:S(2)}, u32[]{:S(2)}) collective-permute-start(bf16[256,256]{1,0:T(8,128)(2,1)S(1)} %hub_network.2), channel_id=1, source_target_pairs={{0,4},{1,5},{2,6},{3,7},{4,0},{5,1},{6,2},{7,3},{8,12},{9,13},{10,... | collective-permute-start | bytes 393224 | tf_op jit(solution)/shard_map/ppermute | solution.py:783
  82.4 11.9 %collective-permute-start.13 = (bf16[256,256]{1,0:T(8,128)(2,1)S(1)}, bf16[256,256]{1,0:T(8,128)(2,1)S(1)}, u32[]{:S(2)}, u32[]{:S(2)}) collective-permute-start(bf16[256,256]{1,0:T(8,128)(2,1)S(1)} %hub_network.2), channel_id=1, source_target_pairs={{0,2},{1,3},{2,0},{3,1},{4,6},{5,7},{6,4},{7,5},{8,10},{9,11},{10,... | collective-permute-start | bytes 393224 | tf_op jit(solution)/shard_map/ppermute | solution.py:783
  94.3 55.1 %all-to-all-start.1 = ((bf16[32,128,256]{2,1,0:T(8,128)(2,1)}), bf16[32,128,256]{2,1,0:T(8,128)(2,1)}, u32[]{:S(2)}, u32[]{:S(2)}) async-start(bf16[32,128,256]{2,1,0:T(8,128)(2,1)} %get-tuple-element.111), calls=%async_computation.1 | async-start | bytes 4194304 | tf_op jit(solution)/shard_map/all_to_all | solution.py:882
  98.7 5.3 %collective-permute-start.16 = (bf16[1024,256]{1,0:T(8,128)(2,1)S(1)}, bf16[1024,256]{1,0:T(8,128)(2,1)S(1)}, u32[]{:S(2)}, u32[]{:S(2)}) collective-permute-start(bf16[1024,256]{1,0:T(8,128)(2,1)S(1)} %constant_dynamic-update-slice_fusion.8.half0), channel_id=1, source_target_pairs={{0,1},{1,0},{2,3},{3,2},{4,5},{5,4},{6,7},{7,6},{8,9},{9,8},{10,11... | collective-permute-start | bytes 1572872 | tf_op jit(solution)/shard_map/ppermute | solution.py:783
  113.8 3.5 %collective-permute-start.17 = (f32[1024,256]{1,0:T(8,128)S(1)}, f32[1024,256]{1,0:T(8,128)S(1)}, u32[]{:S(2)}, u32[]{:S(2)}) collective-permute-start(f32[1024,256]{1,0:T(8,128)S(1)} %get-tuple-element.105), channel_id=1, source_target_pairs={{0,1},{1,0},{2,3},{3,2},{4,5},{5,4},{6,7},{7,6},{8,9},{9,8},{10,11... | collective-permute-start | bytes 3145736 | tf_op jit(solution)/shard_map/ppermute | solution.py:783
  117.6 18.2 %collective-permute-start.18 = (f32[256,256]{1,0:T(8,128)S(1)}, f32[256,256]{1,0:T(8,128)S(1)}, u32[]{:S(2)}, u32[]{:S(2)}) collective-permute-start(f32[256,256]{1,0:T(8,128)S(1)} %get-tuple-element.106), channel_id=1, source_target_pairs={{0,2},{1,3},{2,0},{3,1},{4,6},{5,7},{6,4},{7,5},{8,10},{9,11},{10,... | collective-permute-start | bytes 786440 | tf_op jit(solution)/shard_map/ppermute | solution.py:783
  119.5 19.7 %collective-permute-start.19 = (f32[256,256]{1,0:T(8,128)S(1)}, f32[256,256]{1,0:T(8,128)S(1)}, u32[]{:S(2)}, u32[]{:S(2)}) collective-permute-start(f32[256,256]{1,0:T(8,128)S(1)} %get-tuple-element.107), channel_id=1, source_target_pairs={{0,4},{1,5},{2,6},{3,7},{4,0},{5,1},{6,2},{7,3},{8,12},{9,13},{10,... | collective-permute-start | bytes 786440 | tf_op jit(solution)/shard_map/ppermute | solution.py:783
  122.0 17.2 %collective-permute-start.20 = (f32[256,256]{1,0:T(8,128)S(1)}, f32[256,256]{1,0:T(8,128)S(1)}, u32[]{:S(2)}, u32[]{:S(2)}) collective-permute-start(f32[256,256]{1,0:T(8,128)S(1)} %get-tuple-element.108), channel_id=1, source_target_pairs={{0,6},{1,7},{2,4},{3,5},{4,2},{5,3},{6,0},{7,1},{8,14},{9,15},{10,... | collective-permute-start | bytes 786440 | tf_op jit(solution)/shard_map/ppermute | solution.py:783
  139.3 20.5 %collective-permute-start.21 = (bf16[64,256]{1,0:T(8,128)(2,1)S(1)}, bf16[64,256]{1,0:T(8,128)(2,1)S(1)}, u32[]{:S(2)}, u32[]{:S(2)}) collective-permute-start(bf16[64,256]{1,0:T(8,128)(2,1)S(1)} %get-tuple-element.117), channel_id=1, source_target_pairs={{0,8},{1,9},{2,10},{3,11},{4,12},{5,13},{6,14},{7,15},{8,0},{9,1},... | collective-permute-start | bytes 98312 | tf_op jit(solution)/shard_map/ppermute | solution.py:783
  143.5 16.3 %collective-permute-start.22 = (bf16[64,256]{1,0:T(8,128)(2,1)S(1)}, bf16[64,256]{1,0:T(8,128)(2,1)S(1)}, u32[]{:S(2)}, u32[]{:S(2)}) collective-permute-start(bf16[64,256]{1,0:T(8,128)(2,1)S(1)} %get-tuple-element.118), channel_id=1, source_target_pairs={{0,16},{1,17},{2,18},{3,19},{4,20},{5,21},{6,22},{7,23},{8,24},{9,... | collective-permute-start | bytes 98312 | tf_op jit(solution)/shard_map/ppermute | solution.py:783
  144.0 15.8 %collective-permute-start.23 = (bf16[64,256]{1,0:T(8,128)(2,1)S(1)}, bf16[64,256]{1,0:T(8,128)(2,1)S(1)}, u32[]{:S(2)}, u32[]{:S(2)}) collective-permute-start(bf16[64,256]{1,0:T(8,128)(2,1)S(1)} %get-tuple-element.119), channel_id=1, source_target_pairs={{0,24},{1,25},{2,26},{3,27},{4,28},{5,29},{6,30},{7,31},{8,16},{9,... | collective-permute-start | bytes 98312 | tf_op jit(solution)/shard_map/ppermute | solution.py:783
  (15 other events, 145.5 us)

commit v9 on v8

--- a/solution.py
+++ b/solution.py
@@ -14,7 +14,7 @@
 VMEM = pl.BlockSpec(memory_space=pltpu.VMEM)
 SMEM = pl.BlockSpec(memory_space=pltpu.SMEM)
 ANY = pl.BlockSpec(memory_space=pl.ANY)
-GROUP = 4
+GROUP = 2
 SLOTS = 8
 
 
@@ -201,13 +201,18 @@
 
 
 def run_groups(begin, end, step):
-    def pair(number, unused):
-        step(begin + 2 * number, 2)
+    def four(number, unused):
+        step(begin + 4 * number, 4)
         return unused
 
-    lax.fori_loop(0, (end - begin) // 2, pair, 0)
-
-    @pl.when((end - begin) % 2 == 1)
+    lax.fori_loop(0, (end - begin) // 4, four, 0)
+    rest = (end - begin) % 4
+
+    @pl.when(rest >= 2)
+    def _():
+        step(end - rest, 2)
+
+    @pl.when(rest % 2 == 1)
     def _():
         step(end - 1, 1)
 
@@ -613,7 +618,7 @@
     groups = rounded_up(n_fed)
     groups_now = rounded_up(plan[COUNTS, N_NOW]) if with_send else groups
     apart = jnp.minimum(groups * GROUP, n_held)
-    early = jnp.minimum(groups, 2)
+    early = jnp.minimum(groups, 4)
 
     def cut_of(group):
         return pl.ds(group * GROUP, GROUP)

time: 164 us -> 164 us (level); the launches traced: 161 us -> 163 us
  waiting for transfers between devices: 39.6 us -> 45.4 us
  starting transfers between devices: 44.4 us -> 41 us
    ppermute x24, waiting for transfers between devices: 36.3 us -> 43.7 us  [exchange(): return lax.ppermute(x, 'dev', [(i, i ^ bit) for i in range(devices)])]
    pallas_call x13, Pallas kernels: 48.3 us -> 42.7 us  [call(): pl.pallas_call(kernel, out_shape=out_shape, in_specs=in_specs, out_specs=...]
    ppermute x24, starting transfers between devices: 36.4 us -> 33.4 us  [exchange(): return lax.ppermute(x, 'dev', [(i, i ^ bit) for i in range(devices)])]
    pallas_call x2, Pallas kernels: 21.5 us -> 24.4 us  [after(): pl.pallas_call(functools.partial(after_kernel, layer, with_send), out_sha...]
    pallas_call x1, Pallas kernels: 5.07 us -> 7.21 us  [late(): pl.pallas_call(functools.partial(late_kernel, layer), out_shape=shape_of(...]
    all_to_all x2, waiting for transfers between devices: 3.39 us -> 1.7 us  [body(): incoming = all_to_all(outgoing)]
  transfers between devices with their start and end apart: 26 -> 26, of which waited for: 11 -> 13; matrix products, arithmetic and copies ran while one was open for 0% -> 0% of each run, Pallas kernels for 46% -> 45%
where the time goes in v9:
time: 164 us; the launch traced here: 163 us
  Pallas kernels  74.3 us (45%)
  waiting for transfers between devices  45.4 us (28%)
  starting transfers between devices  41 us (25%)
  between operations  1.9 us (1%)
    ppermute x24, waiting for transfers between devices, exchange(): return lax.ppermute(x, 'dev', [(i, i ^ bit) for i in range(devices)])  43.7 us
    pallas_call x13, Pallas kernels, call(): pl.pallas_call(kernel, out_shape=out_shape, in_specs=in_specs, out_specs=...  42.7 us
    ppermute x24, starting transfers between devices, exchange(): return lax.ppermute(x, 'dev', [(i, i ^ bit) for i in range(devices)])  33.4 us
    pallas_call x2, Pallas kernels, after(): pl.pallas_call(functools.partial(after_kernel, layer, with_send), out_sha...  24.4 us
    all_to_all x2, starting transfers between devices, body(): incoming = all_to_all(outgoing)  7.6 us
    pallas_call x1, Pallas kernels, late(): pl.pallas_call(functools.partial(late_kernel, layer), out_shape=shape_of(...  7.21 us
  transfers between devices with their start and end apart: 26, of which 13 were waited for; matrix products, arithmetic and copies ran while one was open for 0% of the time, Pallas kernels for 45%

profile of v9, /device:TPU:0, one launch (start us, length us, event | category | flops | bytes accessed | tf_op | source)
XLA Modules:
  0.0 163.2 jit_solution(4981786118301789121)
XLA Ops:
  0.6 4.1 %collective-permute-start.1 = (bf16[64,256]{1,0:T(8,128)(2,1)}, bf16[64,256]{1,0:T(8,128)(2,1)S(1)}, u32[]{:S(2)}, u32[]{:S(2)}) collective-permute-start(bf16[64,256]{1,0:T(8,128)(2,1)} %param.11), channel_id=1, source_target_pairs={{0,16},{1,17},{2,18},{3,19},{4,20},{5,21},{6,22},{7,23},{8,24},{9,... | collective-permute-start | bytes 98312 | tf_op jit(solution)/shard_map/ppermute | solution.py:788
  6.3 3.8 %pack.1 = bf16[32,128,256]{2,1,0:T(8,128)(2,1)} custom-call(s32[1,32]{1,0:T(1,128)} %chosen.3, bf16[32,128,256]{2,1,0:T(8,128)(2,1)} %bitcast.11), custom_call_target="tpu_custom_call" | custom-call | bytes 4194304 | tf_op jit(solution)/shard_map/pack/pallas_call | solution.py:30
  12.3 2.5 %collective-permute-start.5 = (bf16[256,256]{1,0:T(8,128)(2,1)S(1)}, bf16[256,256]{1,0:T(8,128)(2,1)S(1)}, u32[]{:S(2)}, u32[]{:S(2)}) collective-permute-start(bf16[256,256]{1,0:T(8,128)(2,1)S(1)} %constant_dynamic-update-slice_fusion), channel_id=1, source_target_pairs={{0,6},{1,7},{2,4},{3,5},{4,2},{5,3},{6,0},{7,1},{8,14},{9,15},{10,... | collective-permute-start | bytes 393224 | tf_op jit(solution)/shard_map/ppermute | solution.py:788
  15.8 3.6 %collective-permute-done.5 = bf16[256,256]{1,0:T(8,128)(2,1)S(1)} collective-permute-done((bf16[256,256]{1,0:T(8,128)(2,1)S(1)}, bf16[256,256]{1,0:T(8,128)(2,1)S(1)}, u32[]{:S(2)}, u32[]{:S(2)}) %collective-permute-start.5) | collective-permute-done | bytes 131104 | tf_op jit(solution)/shard_map/ppermute | solution.py:788
  20.4 3.6 %all-to-all-start = ((bf16[32,128,256]{2,1,0:T(8,128)(2,1)}), bf16[32,128,256]{2,1,0:T(8,128)(2,1)}, u32[]{:S(2)}, u32[]{:S(2)}) async-start(bf16[32,128,256]{2,1,0:T(8,128)(2,1)} %pack.1), calls=%async_computation | async-start | bytes 4194304 | tf_op jit(solution)/shard_map/all_to_all | solution.py:872
  26.1 5.7 %hub_first.1 = (bf16[16,128,256]{2,1,0:T(8,128)(2,1)S(1)}, bf16[256,256]{1,0:T(8,128)(2,1)S(1)}, f32[1024,256]{1,0:T(8,128)S(1)}, f32[1024,256]{1,0:T(8,128)S(1)}) custom-call(s32[8,256]{1,0:T(8,128)S(1)} %plan.1, s32[1]{0:T(128)S(6)} %copy.30.count, s32[1]{0:T(128)} %bitcast.position, s32[2048,1]{1,0:T(8,128)S(1)} %copy.16.place_col, ...), custom_call_target="tpu_custom_call" | custom-call | flops 2147483648 | bytes 14680064 | tf_op jit(solution)/shard_map/hub_first/pallas_call | solution.py:30
  32.0 2.5 %collective-permute-done.7.refs_0_ = f32[1024,256]{1,0:T(8,128)S(1)} collective-permute-done((f32[1024,256]{1,0:T(8,128)S(1)}, f32[1024,256]{1,0:T(8,128)S(1)}, u32[]{:S(2)}, u32[]{:S(2)}) %collective-permute-start.7) | collective-permute-done | bytes 1048608 | tf_op jit(solution)/shard_map/ppermute | solution.py:788
  36.6 2.1 %collective-permute-start.9 = (f32[256,256]{1,0:T(8,128)S(1)}, f32[256,256]{1,0:T(8,128)S(1)}, u32[]{:S(2)}, u32[]{:S(2)}) collective-permute-start(f32[256,256]{1,0:T(8,128)S(1)} %get-tuple-element.82), channel_id=1, source_target_pairs={{0,4},{1,5},{2,6},{3,7},{4,0},{5,1},{6,2},{7,3},{8,12},{9,13},{10,... | collective-permute-start | bytes 786440 | tf_op jit(solution)/shard_map/ppermute | solution.py:788
  38.9 10.0 %before.2 = (f32[32,128,256]{2,1,0:T(8,128)}, bf16[32,128,256]{2,1,0:T(8,128)(2,1)}) custom-call(s32[8,256]{1,0:T(8,128)} %copy-done.6, s32[1]{0:T(128)S(6)} %copy.30.count, bf16[16,128,256]{2,1,0:T(8,128)(2,1)} %copy-done.5, bf16[32,128,256]{2,1,0:T(8,128)(2,1)} %bitcast.13, bf16[144,128,128]{2,1,0:T(8,128)(2,1)} %tiles.3, bf16[2,256,2048]{2,1,0:T(8,128)(2,1)} %refs_4_.1, ...), custom_call_target="tpu_custom_call" | custom-call | flops 2863311616 | bytes 18874368 | tf_op jit(solution)/shard_map/before/pallas_call | solution.py:30
  50.4 8.9 %collective-permute-done.9.refs_2_ = f32[256,256]{1,0:T(8,128)S(1)} collective-permute-done((f32[256,256]{1,0:T(8,128)S(1)}, f32[256,256]{1,0:T(8,128)S(1)}, u32[]{:S(2)}, u32[]{:S(2)}) %collective-permute-start.9) | collective-permute-done | bytes 262176 | tf_op jit(solution)/shard_map/ppermute | solution.py:788
  59.4 5.2 %collective-permute-start.11 = (bf16[256,256]{1,0:T(8,128)(2,1)S(1)}, bf16[256,256]{1,0:T(8,128)(2,1)S(1)}, u32[]{:S(2)}, u32[]{:S(2)}) collective-permute-start(bf16[256,256]{1,0:T(8,128)(2,1)S(1)} %total.2.refs_0_), channel_id=1, source_target_pairs={{0,8},{1,9},{2,10},{3,11},{4,12},{5,13},{6,14},{7,15},{8,0},{9,1},... | collective-permute-start | bytes 393224 | tf_op jit(solution)/shard_map/ppermute | solution.py:788
  64.6 5.0 %collective-permute-done.11.refs_1_ = bf16[256,256]{1,0:T(8,128)(2,1)S(1)} collective-permute-done((bf16[256,256]{1,0:T(8,128)(2,1)S(1)}, bf16[256,256]{1,0:T(8,128)(2,1)S(1)}, u32[]{:S(2)}, u32[]{:S(2)}) %collective-permute-start.11) | collective-permute-done | bytes 131104 | tf_op jit(solution)/shard_map/ppermute | solution.py:788
  69.7 8.9 %collective-permute-done.12.refs_1_ = bf16[256,256]{1,0:T(8,128)(2,1)S(1)} collective-permute-done((bf16[256,256]{1,0:T(8,128)(2,1)S(1)}, bf16[256,256]{1,0:T(8,128)(2,1)S(1)}, u32[]{:S(2)}, u32[]{:S(2)}) %collective-permute-start.12) | collective-permute-done | bytes 131104 | tf_op jit(solution)/shard_map/ppermute | solution.py:788
  79.7 2.2 %collective-permute-start.15 = (bf16[256,256]{1,0:T(8,128)(2,1)S(1)}, bf16[256,256]{1,0:T(8,128)(2,1)S(1)}, u32[]{:S(2)}, u32[]{:S(2)}) collective-permute-start(bf16[256,256]{1,0:T(8,128)(2,1)S(1)} %hub_network.2), channel_id=1, source_target_pairs={{0,6},{1,7},{2,4},{3,5},{4,2},{5,3},{6,0},{7,1},{8,14},{9,15},{10,... | collective-permute-start | bytes 393224 | tf_op jit(solution)/shard_map/ppermute | solution.py:788
  83.2 11.4 %after.2 = (bf16[32,128,256]{2,1,0:T(8,128)(2,1)}, f32[32,128,256]{2,1,0:T(8,128)}, bf16[32,128,256]{2,1,0:T(8,128)(2,1)}) custom-call(s32[8,256]{1,0:T(8,128)} %copy-done.6, f32[32,128,256]{2,1,0:T(8,128)} %get-tuple-element.90.base, bf16[32,128,256]{2,1,0:T(8,128)(2,1)} %get-tuple-element.91.done, ...), custom_call_target="tpu_custom_call", output_to_operand_aliasing={{0}: (2, {}), {1}: (1, {})} | custom-call | flops 8589934592 | bytes 16777216 | tf_op jit(solution)/shard_map/after/pallas_call | solution.py:701
  94.6 4.0 %all-to-all-start.1 = ((bf16[32,128,256]{2,1,0:T(8,128)(2,1)}), bf16[32,128,256]{2,1,0:T(8,128)(2,1)}, u32[]{:S(2)}, u32[]{:S(2)}) async-start(bf16[32,128,256]{2,1,0:T(8,128)(2,1)} %get-tuple-element.111), calls=%async_computation.1 | async-start | bytes 4194304 | tf_op jit(solution)/shard_map/all_to_all | solution.py:887
  98.9 7.2 %late.1.own_hbm.own_in = bf16[32,128,256]{2,1,0:T(8,128)(2,1)} custom-call(s32[8,256]{1,0:T(8,128)} %copy-done.6, f32[32,128,256]{2,1,0:T(8,128)} %get-tuple-element.99.sums, bf16[32,128,256]{2,1,0:T(8,128)(2,1)} %get-tuple-element.100.done, bf16[2,256,2048]{2,1,0:T(8,128)(2,1)} %refs_4_.1, bf16[2,2048,256]{2,1,0:T(8,128)(2,1)} %refs_5_.1), custom_call_target="tpu_custom_call", output_to_operand_aliasing={{}: (2, {})} | custom-call | flops 2147483648 | bytes 5242880 | tf_op jit(solution)/shard_map/late/pallas_call | solution.py:763
  106.2 9.7 %hub_second.1 = (bf16[16,128,256]{2,1,0:T(8,128)(2,1)S(1)}, bf16[64,256]{1,0:T(8,128)(2,1)S(1)}, f32[1024,256]{1,0:T(8,128)S(1)}, f32[1024,256]{1,0:T(8,128)S(1)}) custom-call(s32[8,256]{1,0:T(8,128)S(1)} %copy-done.7, s32[1]{0:T(128)S(6)} %copy.30.count, s32[1]{0:T(128)} %bitcast.position, s32[1,2048]{1,0:T(1,128)S(1)} %bitcast.8, ...), custom_call_target="tpu_custom_call" | custom-call | flops 2147483648 | bytes 14680064 | tf_op jit(solution)/shard_map/hub_second/pallas_call | solution.py:30
  116.0 2.6 %collective-permute-done.17.refs_0_ = f32[1024,256]{1,0:T(8,128)S(1)} collective-permute-done((f32[1024,256]{1,0:T(8,128)S(1)}, f32[1024,256]{1,0:T(8,128)S(1)}, u32[]{:S(2)}, u32[]{:S(2)}) %collective-permute-start.17) | collective-permute-done | bytes 1048608 | tf_op jit(solution)/shard_map/ppermute | solution.py:788
  119.6 2.4 %collective-permute-start.19 = (f32[256,256]{1,0:T(8,128)S(1)}, f32[256,256]{1,0:T(8,128)S(1)}, u32[]{:S(2)}, u32[]{:S(2)}) collective-permute-start(f32[256,256]{1,0:T(8,128)S(1)} %get-tuple-element.107), channel_id=1, source_target_pairs={{0,4},{1,5},{2,6},{3,7},{4,0},{5,1},{6,2},{7,3},{8,12},{9,13},{10,... | collective-permute-start | bytes 786440 | tf_op jit(solution)/shard_map/ppermute | solution.py:788
  122.4 9.5 %before.3 = (f32[32,128,256]{2,1,0:T(8,128)}, bf16[32,128,256]{2,1,0:T(8,128)(2,1)}) custom-call(s32[8,256]{1,0:T(8,128)} %copy-done.6, s32[1]{0:T(128)S(6)} %copy.30.count, bf16[16,128,256]{2,1,0:T(8,128)(2,1)} %copy-done.4, bf16[32,128,256]{2,1,0:T(8,128)(2,1)} %late.1.own_hbm.own_in, bf16[144,128,128]{2,1,0:T(8,128)(2,1)} %tiles.3, ...), custom_call_target="tpu_custom_call" | custom-call | flops 2863311616 | bytes 18874368 | tf_op jit(solution)/shard_map/before/pallas_call | solution.py:30
  132.7 6.4 %collective-permute-done.19.refs_1_ = f32[256,256]{1,0:T(8,128)S(1)} collective-permute-done((f32[256,256]{1,0:T(8,128)S(1)}, f32[256,256]{1,0:T(8,128)S(1)}, u32[]{:S(2)}, u32[]{:S(2)}) %collective-permute-start.19) | collective-permute-done | bytes 262176 | tf_op jit(solution)/shard_map/ppermute | solution.py:788
  139.2 4.5 %collective-permute-start.21 = (bf16[64,256]{1,0:T(8,128)(2,1)S(1)}, bf16[64,256]{1,0:T(8,128)(2,1)S(1)}, u32[]{:S(2)}, u32[]{:S(2)}) collective-permute-start(bf16[64,256]{1,0:T(8,128)(2,1)S(1)} %get-tuple-element.117), channel_id=1, source_target_pairs={{0,8},{1,9},{2,10},{3,11},{4,12},{5,13},{6,14},{7,15},{8,0},{9,1},... | collective-permute-start | bytes 98312 | tf_op jit(solution)/shard_map/ppermute | solution.py:788
  148.5 13.0 %after.3 = bf16[32,128,256]{2,1,0:T(8,128)(2,1)} custom-call(s32[8,256]{1,0:T(8,128)} %copy-done.6, f32[32,128,256]{2,1,0:T(8,128)} %get-tuple-element.109.base, bf16[32,128,256]{2,1,0:T(8,128)(2,1)} %get-tuple-element.110.done, bf16[32,128,256]{2,1,0:T(8,128)(2,1)} %all-to-all-done.1.incoming, ...), custom_call_target="tpu_custom_call", output_to_operand_aliasing={{}: (2, {})} | custom-call | flops 8589934592 | bytes 16777216 | tf_op jit(solution)/shard_map/after/pallas_call | solution.py:701
  (84 shorter events, 22.5 us)
Async XLA Ops:
  0.6 9.5 %collective-permute-start.1 = (bf16[64,256]{1,0:T(8,128)(2,1)}, bf16[64,256]{1,0:T(8,128)(2,1)S(1)}, u32[]{:S(2)}, u32[]{:S(2)}) collective-permute-start(bf16[64,256]{1,0:T(8,128)(2,1)} %param.11), channel_id=1, source_target_pairs={{0,16},{1,17},{2,18},{3,19},{4,20},{5,21},{6,22},{7,23},{8,24},{9,... | collective-permute-start | bytes 98312 | tf_op jit(solution)/shard_map/ppermute | solution.py:788
  4.7 5.4 %collective-permute-start = (bf16[64,256]{1,0:T(8,128)(2,1)}, bf16[64,256]{1,0:T(8,128)(2,1)S(1)}, u32[]{:S(2)}, u32[]{:S(2)}) collective-permute-start(bf16[64,256]{1,0:T(8,128)(2,1)} %param.11), channel_id=1, source_target_pairs={{0,8},{1,9},{2,10},{3,11},{4,12},{5,13},{6,14},{7,15},{8,0},{9,1},... | collective-permute-start | bytes 98312 | tf_op jit(solution)/shard_map/ppermute | solution.py:788
  6.3 5.9 %collective-permute-start.2 = (bf16[64,256]{1,0:T(8,128)(2,1)}, bf16[64,256]{1,0:T(8,128)(2,1)S(1)}, u32[]{:S(2)}, u32[]{:S(2)}) collective-permute-start(bf16[64,256]{1,0:T(8,128)(2,1)} %param.11), channel_id=1, source_target_pairs={{0,24},{1,25},{2,26},{3,27},{4,28},{5,29},{6,30},{7,31},{8,16},{9,... | collective-permute-start | bytes 98312 | tf_op jit(solution)/shard_map/ppermute | solution.py:788
  12.3 7.2 %collective-permute-start.5 = (bf16[256,256]{1,0:T(8,128)(2,1)S(1)}, bf16[256,256]{1,0:T(8,128)(2,1)S(1)}, u32[]{:S(2)}, u32[]{:S(2)}) collective-permute-start(bf16[256,256]{1,0:T(8,128)(2,1)S(1)} %constant_dynamic-update-slice_fusion), channel_id=1, source_target_pairs={{0,6},{1,7},{2,4},{3,5},{4,2},{5,3},{6,0},{7,1},{8,14},{9,15},{10,... | collective-permute-start | bytes 393224 | tf_op jit(solution)/shard_map/ppermute | solution.py:788
  14.8 5.6 %collective-permute-start.4 = (bf16[256,256]{1,0:T(8,128)(2,1)S(1)}, bf16[256,256]{1,0:T(8,128)(2,1)S(1)}, u32[]{:S(2)}, u32[]{:S(2)}) collective-permute-start(bf16[256,256]{1,0:T(8,128)(2,1)S(1)} %constant_dynamic-update-slice_fusion), channel_id=1, source_target_pairs={{0,4},{1,5},{2,6},{3,7},{4,0},{5,1},{6,2},{7,3},{8,12},{9,13},{10,... | collective-permute-start | bytes 393224 | tf_op jit(solution)/shard_map/ppermute | solution.py:788
  15.3 5.1 %collective-permute-start.3 = (bf16[256,256]{1,0:T(8,128)(2,1)S(1)}, bf16[256,256]{1,0:T(8,128)(2,1)S(1)}, u32[]{:S(2)}, u32[]{:S(2)}) collective-permute-start(bf16[256,256]{1,0:T(8,128)(2,1)S(1)} %constant_dynamic-update-slice_fusion), channel_id=1, source_target_pairs={{0,2},{1,3},{2,0},{3,1},{4,6},{5,7},{6,4},{7,5},{8,10},{9,11},{10,... | collective-permute-start | bytes 393224 | tf_op jit(solution)/shard_map/ppermute | solution.py:788
  20.4 62.8 %all-to-all-start = ((bf16[32,128,256]{2,1,0:T(8,128)(2,1)}), bf16[32,128,256]{2,1,0:T(8,128)(2,1)}, u32[]{:S(2)}, u32[]{:S(2)}) async-start(bf16[32,128,256]{2,1,0:T(8,128)(2,1)} %pack.1), calls=%async_computation | async-start | bytes 4194304 | tf_op jit(solution)/shard_map/all_to_all | solution.py:872
  31.8 2.7 %collective-permute-start.7 = (f32[1024,256]{1,0:T(8,128)S(1)}, f32[1024,256]{1,0:T(8,128)S(1)}, u32[]{:S(2)}, u32[]{:S(2)}) collective-permute-start(f32[1024,256]{1,0:T(8,128)S(1)} %get-tuple-element.80), channel_id=1, source_target_pairs={{0,1},{1,0},{2,3},{3,2},{4,5},{5,4},{6,7},{7,6},{8,9},{9,8},{10,11... | collective-permute-start | bytes 3145736 | tf_op jit(solution)/shard_map/ppermute | solution.py:788
  35.4 15.0 %collective-permute-start.8 = (f32[256,256]{1,0:T(8,128)}, f32[256,256]{1,0:T(8,128)S(1)}, u32[]{:S(2)}, u32[]{:S(2)}) collective-permute-start(f32[256,256]{1,0:T(8,128)} %get-tuple-element.81), channel_id=1, source_target_pairs={{0,2},{1,3},{2,0},{3,1},{4,6},{5,7},{6,4},{7,5},{8,10},{9,11},{10,... | collective-permute-start | bytes 786440 | tf_op jit(solution)/shard_map/ppermute | solution.py:788
  36.6 22.7 %collective-permute-start.9 = (f32[256,256]{1,0:T(8,128)S(1)}, f32[256,256]{1,0:T(8,128)S(1)}, u32[]{:S(2)}, u32[]{:S(2)}) collective-permute-start(f32[256,256]{1,0:T(8,128)S(1)} %get-tuple-element.82), channel_id=1, source_target_pairs={{0,4},{1,5},{2,6},{3,7},{4,0},{5,1},{6,2},{7,3},{8,12},{9,13},{10,... | collective-permute-start | bytes 786440 | tf_op jit(solution)/shard_map/ppermute | solution.py:788
  38.8 20.5 %collective-permute-start.10 = (f32[256,256]{1,0:T(8,128)S(1)}, f32[256,256]{1,0:T(8,128)S(1)}, u32[]{:S(2)}, u32[]{:S(2)}) collective-permute-start(f32[256,256]{1,0:T(8,128)S(1)} %get-tuple-element.83), channel_id=1, source_target_pairs={{0,6},{1,7},{2,4},{3,5},{4,2},{5,3},{6,0},{7,1},{8,14},{9,15},{10,... | collective-permute-start | bytes 786440 | tf_op jit(solution)/shard_map/ppermute | solution.py:788
  59.4 10.2 %collective-permute-start.11 = (bf16[256,256]{1,0:T(8,128)(2,1)S(1)}, bf16[256,256]{1,0:T(8,128)(2,1)S(1)}, u32[]{:S(2)}, u32[]{:S(2)}) collective-permute-start(bf16[256,256]{1,0:T(8,128)(2,1)S(1)} %total.2.refs_0_), channel_id=1, source_target_pairs={{0,8},{1,9},{2,10},{3,11},{4,12},{5,13},{6,14},{7,15},{8,0},{9,1},... | collective-permute-start | bytes 393224 | tf_op jit(solution)/shard_map/ppermute | solution.py:788
  69.6 8.9 %collective-permute-start.12 = (bf16[256,256]{1,0:T(8,128)(2,1)S(1)}, bf16[256,256]{1,0:T(8,128)(2,1)S(1)}, u32[]{:S(2)}, u32[]{:S(2)}) collective-permute-start(bf16[256,256]{1,0:T(8,128)(2,1)S(1)} %total.3.refs_0_), channel_id=1, source_target_pairs={{0,16},{1,17},{2,18},{3,19},{4,20},{5,21},{6,22},{7,23},{8,24},{9,... | collective-permute-start | bytes 393224 | tf_op jit(solution)/shard_map/ppermute | solution.py:788
  79.7 14.9 %collective-permute-start.15 = (bf16[256,256]{1,0:T(8,128)(2,1)S(1)}, bf16[256,256]{1,0:T(8,128)(2,1)S(1)}, u32[]{:S(2)}, u32[]{:S(2)}) collective-permute-start(bf16[256,256]{1,0:T(8,128)(2,1)S(1)} %hub_network.2), channel_id=1, source_target_pairs={{0,6},{1,7},{2,4},{3,5},{4,2},{5,3},{6,0},{7,1},{8,14},{9,15},{10,... | collective-permute-start | bytes 393224 | tf_op jit(solution)/shard_map/ppermute | solution.py:788
  81.9 12.7 %collective-permute-start.14 = (bf16[256,256]{1,0:T(8,128)(2,1)S(1)}, bf16[256,256]{1,0:T(8,128)(2,1)S(1)}, u32[]{:S(2)}, u32[]{:S(2)}) collective-permute-start(bf16[256,256]{1,0:T(8,128)(2,1)S(1)} %hub_network.2), channel_id=1, source_target_pairs={{0,4},{1,5},{2,6},{3,7},{4,0},{5,1},{6,2},{7,3},{8,12},{9,13},{10,... | collective-permute-start | bytes 393224 | tf_op jit(solution)/shard_map/ppermute | solution.py:788
  82.4 12.2 %collective-permute-start.13 = (bf16[256,256]{1,0:T(8,128)(2,1)S(1)}, bf16[256,256]{1,0:T(8,128)(2,1)S(1)}, u32[]{:S(2)}, u32[]{:S(2)}) collective-permute-start(bf16[256,256]{1,0:T(8,128)(2,1)S(1)} %hub_network.2), channel_id=1, source_target_pairs={{0,2},{1,3},{2,0},{3,1},{4,6},{5,7},{6,4},{7,5},{8,10},{9,11},{10,... | collective-permute-start | bytes 393224 | tf_op jit(solution)/shard_map/ppermute | solution.py:788
  94.6 53.9 %all-to-all-start.1 = ((bf16[32,128,256]{2,1,0:T(8,128)(2,1)}), bf16[32,128,256]{2,1,0:T(8,128)(2,1)}, u32[]{:S(2)}, u32[]{:S(2)}) async-start(bf16[32,128,256]{2,1,0:T(8,128)(2,1)} %get-tuple-element.111), calls=%async_computation.1 | async-start | bytes 4194304 | tf_op jit(solution)/shard_map/all_to_all | solution.py:887
  98.7 7.5 %collective-permute-start.16 = (bf16[1024,256]{1,0:T(8,128)(2,1)S(1)}, bf16[1024,256]{1,0:T(8,128)(2,1)S(1)}, u32[]{:S(2)}, u32[]{:S(2)}) collective-permute-start(bf16[1024,256]{1,0:T(8,128)(2,1)S(1)} %constant_dynamic-update-slice_fusion.8.half0), channel_id=1, source_target_pairs={{0,1},{1,0},{2,3},{3,2},{4,5},{5,4},{6,7},{7,6},{8,9},{9,8},{10,11... | collective-permute-start | bytes 1572872 | tf_op jit(solution)/shard_map/ppermute | solution.py:788
  118.9 13.8 %collective-permute-start.18 = (f32[256,256]{1,0:T(8,128)S(1)}, f32[256,256]{1,0:T(8,128)S(1)}, u32[]{:S(2)}, u32[]{:S(2)}) collective-permute-start(f32[256,256]{1,0:T(8,128)S(1)} %get-tuple-element.106), channel_id=1, source_target_pairs={{0,2},{1,3},{2,0},{3,1},{4,6},{5,7},{6,4},{7,5},{8,10},{9,11},{10,... | collective-permute-start | bytes 786440 | tf_op jit(solution)/shard_map/ppermute | solution.py:788
  119.6 19.5 %collective-permute-start.19 = (f32[256,256]{1,0:T(8,128)S(1)}, f32[256,256]{1,0:T(8,128)S(1)}, u32[]{:S(2)}, u32[]{:S(2)}) collective-permute-start(f32[256,256]{1,0:T(8,128)S(1)} %get-tuple-element.107), channel_id=1, source_target_pairs={{0,4},{1,5},{2,6},{3,7},{4,0},{5,1},{6,2},{7,3},{8,12},{9,13},{10,... | collective-permute-start | bytes 786440 | tf_op jit(solution)/shard_map/ppermute | solution.py:788
  122.0 17.2 %collective-permute-start.20 = (f32[256,256]{1,0:T(8,128)S(1)}, f32[256,256]{1,0:T(8,128)S(1)}, u32[]{:S(2)}, u32[]{:S(2)}) collective-permute-start(f32[256,256]{1,0:T(8,128)S(1)} %get-tuple-element.108), channel_id=1, source_target_pairs={{0,6},{1,7},{2,4},{3,5},{4,2},{5,3},{6,0},{7,1},{8,14},{9,15},{10,... | collective-permute-start | bytes 786440 | tf_op jit(solution)/shard_map/ppermute | solution.py:788
  139.2 22.3 %collective-permute-start.21 = (bf16[64,256]{1,0:T(8,128)(2,1)S(1)}, bf16[64,256]{1,0:T(8,128)(2,1)S(1)}, u32[]{:S(2)}, u32[]{:S(2)}) collective-permute-start(bf16[64,256]{1,0:T(8,128)(2,1)S(1)} %get-tuple-element.117), channel_id=1, source_target_pairs={{0,8},{1,9},{2,10},{3,11},{4,12},{5,13},{6,14},{7,15},{8,0},{9,1},... | collective-permute-start | bytes 98312 | tf_op jit(solution)/shard_map/ppermute | solution.py:788
  143.7 17.8 %collective-permute-start.22 = (bf16[64,256]{1,0:T(8,128)(2,1)S(1)}, bf16[64,256]{1,0:T(8,128)(2,1)S(1)}, u32[]{:S(2)}, u32[]{:S(2)}) collective-permute-start(bf16[64,256]{1,0:T(8,128)(2,1)S(1)} %get-tuple-element.118), channel_id=1, source_target_pairs={{0,16},{1,17},{2,18},{3,19},{4,20},{5,21},{6,22},{7,23},{8,24},{9,... | collective-permute-start | bytes 98312 | tf_op jit(solution)/shard_map/ppermute | solution.py:788
  145.4 16.1 %collective-permute-start.23 = (bf16[64,256]{1,0:T(8,128)(2,1)S(1)}, bf16[64,256]{1,0:T(8,128)(2,1)S(1)}, u32[]{:S(2)}, u32[]{:S(2)}) collective-permute-start(bf16[64,256]{1,0:T(8,128)(2,1)S(1)} %get-tuple-element.119), channel_id=1, source_target_pairs={{0,24},{1,25},{2,26},{3,27},{4,28},{5,29},{6,30},{7,31},{8,16},{9,... | collective-permute-start | bytes 98312 | tf_op jit(solution)/shard_map/ppermute | solution.py:788
  (15 other events, 150.9 us)
